TPU v7x, 256 devices: a whole 4x4x8 slice. The times are simulated.
256 devices in a mesh: gx: 64 (over y, z, core), gy: 4 (over x).
Axes of the slice: x: 4, y: 4, z: 8, core: 2. Of those that a mesh axis runs over, the one named last changes fastest.
Arguments:
- state: float32 [256, 1048576], P(('gx', 'gy')), may hold values from -6 to 6
- locations: int32 [1024], replicated, may hold values from 0 to 1048575, as said below
- tile_mask: int32 [2048, 1024], P(('gx', 'gy')), may hold values from 0 to 1, as said below
- plan: int32 [1024], replicated, may hold values from 0 to 1023, each once
- obs_value: float32 [1024], replicated, may hold values from -6 to 6
- obs_error: float32 [1024], replicated, may hold values from 0.2 to 2
Outputs:
- analysis: float32 [256, 1048576], P(('gx', 'gy'))
Inputs may be any that keep to these rules, and one draw needn't show every extreme that they name: `locations`: observations with an even index lie anywhere in the grid; those with an odd index gather in 8 clusters of tiles. tile_mask is 1 only where the tile lies within 4 tiles, counted cyclically, of the tile that holds the observed variable.
All inputs are finite; a program needn't handle non-finite values.
Results may differ from a plain program's by a relative error of at most 0.0003.
Values sent between devices are 32-bit elements; how exact they have to be, the bound alone decides.
No kernel may reach another device: no remote copies, remote signals or barrier semaphores. Data moves between devices by JAX's collectives and lax.ppermute only.
A program may use at most 64 MiB of HBM per device.

v0:
```python
import jax
import jax.numpy as jnp
from jax import lax
from jax.sharding import PartitionSpec as P

BATCH_OBS = 256
BATCHES = 4


epsilon = 1e-06


def passed_along(value, axis, by):
    peers = lax.axis_size(axis)
    return lax.ppermute(value, axis, [(i, (i + by) % peers) for i in range(peers)])


def adjust(prior_rows, obs_values, obs_errors):
    members = prior_rows.shape[0]
    average = jnp.mean(prior_rows, axis=0)
    obs_anomaly = prior_rows - average[None, :]
    spread = jnp.sum(obs_anomaly * obs_anomaly, axis=0) / (members - 1) + epsilon
    shrink = jnp.sqrt(obs_errors / (spread + obs_errors))
    post_mean = (average * obs_errors + obs_values * spread) / (spread + obs_errors)
    increments = (shrink - 1.0)[None, :] * obs_anomaly + (post_mean - average)[None, :]
    obs_gains = 1.0 / ((members - 1) * spread)
    return (obs_anomaly, increments, obs_gains)


def update_tile(tile_block, tile_weights, obs_anomaly, increments):
    anomaly = tile_block - jnp.mean(tile_block, axis=0)[None, :]
    covariance = lax.dot_general(
        anomaly,
        obs_anomaly,
        (((0,), (0,)), ((), ())),
        precision=lax.Precision.HIGHEST,
        preferred_element_type=jnp.float32,
    )
    coefficient = covariance * tile_weights[None, :]
    return tile_block + lax.dot_general(
        increments,
        coefficient,
        (((1,), (1,)), ((), ())),
        precision=lax.Precision.HIGHEST,
        preferred_element_type=jnp.float32,
    )


def regress(ensemble, weights, obs_anomaly, increments):
    members, per_device = ensemble.shape
    tiles_here, obs_count = weights.shape
    tile_width = per_device // tiles_here
    blocks = ensemble.reshape(members, tiles_here, tile_width).transpose(1, 0, 2)

    def visit(operands):
        tile_block, tile_weights = operands
        return lax.cond(
            jnp.any(tile_weights > 0),
            lambda: update_tile(tile_block, tile_weights, obs_anomaly, increments),
            lambda: tile_block,
        )

    updated = lax.map(visit, (blocks, weights))
    return updated.transpose(1, 0, 2).reshape(members, per_device)


def gather_priors(columns):
    total = columns
    total = total + passed_along(columns, ("gx", "gy"), 1)
    total = total + passed_along(columns, ("gx", "gy"), -1)
    return total


def shards(state, locations, tile_mask, plan, obs_value, obs_error):
    wide_size = lax.axis_size("gx")
    narrow_size = lax.axis_size("gy")
    members_here, total_vars = state.shape
    per_device = total_vars // (wide_size * narrow_size)
    shaped = state.reshape(members_here, wide_size, narrow_size, per_device)
    arrived = lax.all_to_all(
        lax.all_to_all(shaped, "gx", split_axis=1, concat_axis=0, tiled=True),
        "gy",
        split_axis=2,
        concat_axis=0,
        tiled=True,
    )
    ensemble = arrived.reshape(-1, per_device)
    first_var = (lax.axis_index("gx") * narrow_size + lax.axis_index("gy")) * per_device
    for batch_step in range(BATCHES):
        picked = plan[batch_step * BATCH_OBS : (batch_step + 1) * BATCH_OBS]
        offset = locations[picked] - first_var
        inside = (offset >= 0) & (offset < per_device)
        clipped = jnp.clip(offset, 0, per_device - 1)
        columns = jnp.where(inside[None, :], jnp.take(ensemble, clipped, axis=1), 0.0)
        prior_rows = gather_priors(columns)
        obs_anomaly, increments, obs_gains = adjust(
            prior_rows, obs_value[picked], obs_error[picked]
        )
        weights = tile_mask[:, picked].astype(jnp.float32) * obs_gains[None, :]
        ensemble = regress(ensemble, weights, obs_anomaly, increments)
    blocks = ensemble.reshape(narrow_size, wide_size, members_here, 1, 1, per_device)
    returned = lax.all_to_all(
        lax.all_to_all(blocks, "gx", split_axis=1, concat_axis=3, tiled=True),
        "gy",
        split_axis=0,
        concat_axis=4,
        tiled=True,
    )
    return returned.reshape(members_here, total_vars)


def solution(mesh):
    placed = (P(("gx", "gy"), None), P(), P(("gx", "gy"), None), P(), P(), P())
    return jax.shard_map(
        shards, mesh=mesh, in_specs=placed, out_specs=P(("gx", "gy"), None), check_vma=False
    )
```

profile of v0, /device:TPU:1, one launch (start us, length us, event | category | flops | bytes accessed | tf_op | source)
XLA Modules:
  0.0 635.2 jit_solution(18345050026841521951)
XLA Ops:
  0.6 34.2 %reduce.3 = f32[1048576]{0:T(1024)} reduce(f32[1,1048576]{1,0:T(1,128)} %param.24, f32[]{:T(128)} %broadcast.516), dimensions={0}, to_apply=%param.24.reduce_sub_computation.3 | reduce | bytes 8388612 | tf_op args[0]
  34.8 5.3 reshape.192
  40.1 109.3 %all_to_all.54 = f32[1,64,4,4096]{3,2,0,1:T(4,128)S(1)} all-to-all(f32[1,64,4,4096]{3,2,0,1:T(4,128)} %bitcast.149), channel_id=1, replica_groups=mesh['gx'=64,'gy'=4] {'gx'}, dimensions={1} | all-to-all | bytes 8388608 | tf_op jit(solution)/shard_map/all_to_all | solution.py:81
  149.4 4.4 copy.71
  153.9 5.3 all-to-all-start.1
  159.2 1.4 gather_fusion.9
  160.6 1.4 gather_fusion.8
  162.0 1.4 gather_fusion.11
  163.4 1.4 gather_fusion.10
  164.7 1.4 gather_fusion.7
  166.1 1.4 gather_fusion.5
  167.5 1.4 gather_fusion.13
  168.9 1.4 gather_fusion.12
  170.2 1.4 gather_fusion.3
  174.0 1.4 gather_fusion.1
  175.4 32.3 %all-to-all-done.1 = f32[64,1,4,4096]{3,0,1,2:T(8,128)} async-done(((f32[64,1,4,4096]{3,0,1,2:T(8,128)}), f32[64,1,4,4096]{3,0,1,2:T(8,128)}, u32[]{:S(2)}, u32[]{:S(2)}) %all-to-all-start.1) | async-done | bytes 4194336 | tf_op jit(solution)/shard_map/all_to_all | solution.py:80
  207.7 5.6 copy.72
  213.3 3.2 gather_fusion.16
  216.6 2.1 collective-permute-start.1
  219.3 8.0 %copy.93 = f32[32,8,8,512]{3,2,1,0:T(8,128)} copy(f32[32,8,8,512]{3,1,2,0:T(8,128)} %bitcast.53) | data formatting | bytes 8388608
  227.3 2.1 collective-permute-done
  230.4 2.3 broadcast.295.clone.2
  232.7 51.7 %while.40 = (s32[]{:T(128)}, f32[8,256,512]{1,2,0:T(8,128)}, f32[8,256]{1,0:T(8,128)S(1)}, f32[8,256,512]{2,0,1:T(8,128)}, f32[256,256]{1,0:T(8,128)S(1)}, /*index=5*/f32[256,256]{1,0:T(8,128)S(1)}, s32[]{:T(128)}) while((s32[]{:T(128)}, f32[8,256,512]{1,2,0:T(8,128)}, f32[8,256]{1,0:T(8,128)S(1)}, f32[8,256,512]{2,0,1:T(8,128)}, ...), condition=%wide.region_7.9_spmd, body=%wide.region_2.8_spmd.sunk | while | flops 805831168 | bytes 6828179 | solution.py:63
  233.9 2.7 constant_dynamic-slice_fusion.11
  237.1 1.6 conditional.8
  240.8 2.7 constant_dynamic-slice_fusion.11
  244.0 1.6 conditional.8
  247.6 2.7 constant_dynamic-slice_fusion.11
  250.8 1.6 conditional.8
  254.5 2.7 constant_dynamic-slice_fusion.11
  257.7 1.6 conditional.8
  261.3 2.7 constant_dynamic-slice_fusion.11
  264.5 1.6 conditional.8
  268.2 2.7 constant_dynamic-slice_fusion.11
  273.4 2.7 constant_dynamic-slice_fusion.11
  276.7 1.6 conditional.8
  280.3 2.7 constant_dynamic-slice_fusion.11
  284.4 3.2 gather_fusion.17
  289.4 5.9 collective-permute-done.3
  296.9 2.4 broadcast.295.clone.1
  299.3 26.7 %while.41 = (s32[]{:T(128)}, f32[8,256,512]{1,2,0:T(8,128)}, f32[8,256]{1,0:T(8,128)S(1)}, f32[8,256,512]{1,2,0:T(8,128)}, f32[256,256]{1,0:T(8,128)S(1)}, /*index=5*/f32[256,256]{1,0:T(8,128)S(1)}, s32[]{:T(128)}) while((s32[]{:T(128)}, f32[8,256,512]{1,2,0:T(8,128)}, f32[8,256]{1,0:T(8,128)S(1)}, f32[8,256,512]{1,2,0:T(8,128)}, ...), condition=%wide.region_15.17_spmd, body=%wide.region_10.16_spmd.sunk | while | flops 805831168 | bytes 5779603 | solution.py:63
  300.5 1.1 dynamic-slice_bitcast_fusion.6
  303.6 1.1 dynamic-slice_bitcast_fusion.6
  323.6 1.6 conditional.9
  326.0 3.2 gather_fusion.18
  329.4 10.3 %collective-permute-start.4 = (f32[256,256]{0,1:T(8,128)S(1)}, f32[256,256]{0,1:T(8,128)S(1)}, u32[]{:S(2)}, u32[]{:S(2)}) collective-permute-start(f32[256,256]{0,1:T(8,128)S(1)} %bitcast_select_fusion.1), channel_id=1, source_target_pairs={{0,1},{1,2},{2,3},{3,4},{4,5},{5,6},{6,7},{7,8},{8,9},{9,10},{10,1... | collective-permute-start | bytes 786440 | tf_op jit(solution)/shard_map/ppermute | solution.py:15
  339.7 3.6 collective-permute-done.5
  344.4 2.3 broadcast.295.clone
  346.7 26.9 %while.42 = (s32[]{:T(128)}, f32[8,256,512]{1,2,0:T(8,128)}, f32[8,256]{1,0:T(8,128)S(1)}, f32[8,256,512]{1,2,0:T(8,128)}, f32[256,256]{1,0:T(8,128)S(1)}, /*index=5*/f32[256,256]{1,0:T(8,128)S(1)}, s32[]{:T(128)}) while((s32[]{:T(128)}, f32[8,256,512]{1,2,0:T(8,128)}, f32[8,256]{1,0:T(8,128)S(1)}, f32[8,256,512]{1,2,0:T(8,128)}, ...), condition=%wide.region_23.25_spmd, body=%wide.region_18.24_spmd.sunk | while | flops 805831168 | bytes 5779603 | solution.py:63
  373.6 3.2 gather_fusion.19
  376.9 7.1 %collective-permute-start.7 = (f32[256,256]{0,1:T(8,128)S(1)}, f32[256,256]{0,1:T(8,128)S(1)}, u32[]{:S(2)}, u32[]{:S(2)}) collective-permute-start(f32[256,256]{0,1:T(8,128)S(1)} %bitcast_select_fusion), channel_id=1, source_target_pairs={{0,255},{1,0},{2,1},{3,2},{4,3},{5,4},{6,5},{7,6},{8,7},{9,8},{10,... | collective-permute-start | bytes 786440 | tf_op jit(solution)/shard_map/ppermute | solution.py:15
  384.0 1.6 collective-permute-start.6
  385.5 1.4 gather_fusion.15
  386.9 1.4 gather_fusion.14
  389.9 19.0 %collective-permute-done.6 = f32[256,256]{0,1:T(8,128)S(1)} collective-permute-done((f32[256,256]{0,1:T(8,128)S(1)}, f32[256,256]{0,1:T(8,128)S(1)}, u32[]{:S(2)}, u32[]{:S(2)}) %collective-permute-start.6) | collective-permute-done | bytes 262176 | tf_op jit(solution)/shard_map/ppermute | solution.py:15
  410.0 2.4 broadcast.295
  412.3 25.8 %while.43 = (s32[]{:T(128)}, f32[8,256,512]{1,2,0:T(8,128)}, f32[8,256]{1,0:T(8,128)S(1)}, f32[8,256,512]{1,2,0:T(8,128)}, f32[256,256]{1,0:T(8,128)S(1)}, /*index=5*/f32[256,256]{1,0:T(8,128)S(1)}, s32[]{:T(128)}) while((s32[]{:T(128)}, f32[8,256,512]{1,2,0:T(8,128)}, f32[8,256]{1,0:T(8,128)S(1)}, f32[8,256,512]{1,2,0:T(8,128)}, ...), condition=%wide.region_31.33_spmd, body=%wide.region_26.32_spmd.sunk | while | flops 805831168 | bytes 5779603 | solution.py:63
  438.1 8.0 %reshape.386 = f32[4,64,1,1,1,4096]{1,0,5,4,3,2:T(4,128)} reshape(f32[256,8,512]{0,2,1:T(8,128)} %bitcast.148) | data formatting | bytes 8388608 | tf_op jit(solution)/shard_map/reshape;reshape | solution.py:101
  446.2 8.6 %copy.87 = f32[4,64,1,1,1,4096]{5,0,4,3,2,1:T(4,128)} copy(f32[4,64,1,1,1,4096]{1,0,5,4,3,2:T(4,128)} %reshape.386) | data formatting | bytes 8388608 | tf_op jit(solution)/shard_map/reshape;reshape | solution.py:101
  454.8 111.1 %all_to_all.55 = f32[4,64,1,1,1,4096]{5,0,4,3,2,1:T(4,128)S(1)} all-to-all(f32[4,64,1,1,1,4096]{5,0,4,3,2,1:T(4,128)} %copy.87), channel_id=1, replica_groups=mesh['gx'=64,'gy'=4] {'gx'}, dimensions={1} | all-to-all | bytes 8388608 | tf_op jit(solution)/shard_map/all_to_all | solution.py:103
  565.8 2.4 copy.88
  568.2 52.1 %all_to_all.56 = f32[4,1,1,64,1,4096]{5,3,4,2,1,0:T(8,128)S(1)} all-to-all(f32[4,1,1,64,1,4096]{5,3,4,2,1,0:T(8,128)S(1)} %copy.88), channel_id=1, replica_groups=mesh['gx'=64,'gy'=4] {'gy'}, dimensions={0} | all-to-all | bytes 8388608 | tf_op jit(solution)/shard_map/all_to_all | solution.py:102
  620.3 4.6 copy.89
  624.9 9.9 %reshape.197 = f32[1,1048576]{1,0:T(1,128)} reshape(f32[1,1,1,64,4,1,4096]{6,4,3,5,2,1,0:T(4,128)} %copy.89) | data formatting | bytes 8388608 | tf_op jit(solution)/shard_map/reshape | solution.py:109
  (256 shorter events, 99.1 us)
Async XLA Ops:
  0.0 164.7 %copy-start = (s32[1024]{0:T(1024)S(1)}, s32[1024]{0:T(1024)}, u32[]{:S(2)}) copy-start(s32[1024]{0:T(1024)} %param.25) | copy-start | bytes 12292
  153.9 5.3 copy-start.5
  153.9 5.3 copy-start.2
  153.9 6.7 %copy-start.3 = (f32[1024]{0:T(1024)S(1)}, f32[1024]{0:T(1024)}, u32[]{:S(2)}) copy-start(f32[1024]{0:T(1024)} %param.29) | copy-start | bytes 12292
  153.9 53.9 %all-to-all-start.1 = ((f32[64,1,4,4096]{3,0,1,2:T(8,128)}), f32[64,1,4,4096]{3,0,1,2:T(8,128)}, u32[]{:S(2)}, u32[]{:S(2)}) async-start(f32[64,1,4,4096]{3,0,1,2:T(8,128)} %copy.71), calls=%async_computation.1 | async-start | bytes 8388608 | tf_op jit(solution)/shard_map/all_to_all | solution.py:80
  160.6 11.0 %copy-start.4 = (s32[8,1024]{1,0:T(8,128)S(1)}, s32[8,1024]{1,0:T(8,128)}, u32[]{:S(2)}) copy-start(s32[8,1024]{1,0:T(8,128)} %param.26) | copy-start | bytes 98308
  216.6 10.6 %collective-permute-start.1 = (f32[256,256]{0,1:T(8,128)S(1)}, f32[256,256]{0,1:T(8,128)S(1)}, u32[]{:S(2)}, u32[]{:S(2)}) collective-permute-start(f32[256,256]{0,1:T(8,128)S(1)} %bitcast_select_fusion.3), channel_id=1, source_target_pairs={{0,255},{1,0},{2,1},{3,2},{4,3},{5,4},{6,5},{7,6},{8,7},{9,8},{10,... | collective-permute-start | bytes 786440 | tf_op jit(solution)/shard_map/ppermute | solution.py:15
  218.7 10.6 %collective-permute-start = (f32[256,256]{0,1:T(8,128)S(1)}, f32[256,256]{0,1:T(8,128)S(1)}, u32[]{:S(2)}, u32[]{:S(2)}) collective-permute-start(f32[256,256]{0,1:T(8,128)S(1)} %bitcast_select_fusion.3), channel_id=1, source_target_pairs={{0,1},{1,2},{2,3},{3,4},{4,5},{5,6},{6,7},{7,8},{8,9},{9,10},{10,1... | collective-permute-start | bytes 786440 | tf_op jit(solution)/shard_map/ppermute | solution.py:15
  287.7 7.6 %collective-permute-start.3 = (f32[256,256]{0,1:T(8,128)S(1)}, f32[256,256]{0,1:T(8,128)S(1)}, u32[]{:S(2)}, u32[]{:S(2)}) collective-permute-start(f32[256,256]{0,1:T(8,128)S(1)} %bitcast_select_fusion.2), channel_id=1, source_target_pairs={{0,255},{1,0},{2,1},{3,2},{4,3},{5,4},{6,5},{7,6},{8,7},{9,8},{10,... | collective-permute-start | bytes 786440 | tf_op jit(solution)/shard_map/ppermute | solution.py:15
  288.6 7.2 %collective-permute-start.2 = (f32[256,256]{0,1:T(8,128)S(1)}, f32[256,256]{0,1:T(8,128)S(1)}, u32[]{:S(2)}, u32[]{:S(2)}) collective-permute-start(f32[256,256]{0,1:T(8,128)S(1)} %bitcast_select_fusion.2), channel_id=1, source_target_pairs={{0,1},{1,2},{2,3},{3,4},{4,5},{5,6},{6,7},{7,8},{8,9},{9,10},{10,1... | collective-permute-start | bytes 786440 | tf_op jit(solution)/shard_map/ppermute | solution.py:15
  329.3 14.0 %collective-permute-start.5 = (f32[256,256]{0,1:T(8,128)S(1)}, f32[256,256]{0,1:T(8,128)S(1)}, u32[]{:S(2)}, u32[]{:S(2)}) collective-permute-start(f32[256,256]{0,1:T(8,128)S(1)} %bitcast_select_fusion.1), channel_id=1, source_target_pairs={{0,255},{1,0},{2,1},{3,2},{4,3},{5,4},{6,5},{7,6},{8,7},{9,8},{10,... | collective-permute-start | bytes 786440 | tf_op jit(solution)/shard_map/ppermute | solution.py:15
  329.4 13.9 %collective-permute-start.4 = (f32[256,256]{0,1:T(8,128)S(1)}, f32[256,256]{0,1:T(8,128)S(1)}, u32[]{:S(2)}, u32[]{:S(2)}) collective-permute-start(f32[256,256]{0,1:T(8,128)S(1)} %bitcast_select_fusion.1), channel_id=1, source_target_pairs={{0,1},{1,2},{2,3},{3,4},{4,5},{5,6},{6,7},{7,8},{8,9},{9,10},{10,1... | collective-permute-start | bytes 786440 | tf_op jit(solution)/shard_map/ppermute | solution.py:15
  376.9 13.0 %collective-permute-start.7 = (f32[256,256]{0,1:T(8,128)S(1)}, f32[256,256]{0,1:T(8,128)S(1)}, u32[]{:S(2)}, u32[]{:S(2)}) collective-permute-start(f32[256,256]{0,1:T(8,128)S(1)} %bitcast_select_fusion), channel_id=1, source_target_pairs={{0,255},{1,0},{2,1},{3,2},{4,3},{5,4},{6,5},{7,6},{8,7},{9,8},{10,... | collective-permute-start | bytes 786440 | tf_op jit(solution)/shard_map/ppermute | solution.py:15
  384.0 24.9 %collective-permute-start.6 = (f32[256,256]{0,1:T(8,128)S(1)}, f32[256,256]{0,1:T(8,128)S(1)}, u32[]{:S(2)}, u32[]{:S(2)}) collective-permute-start(f32[256,256]{0,1:T(8,128)S(1)} %bitcast_select_fusion), channel_id=1, source_target_pairs={{0,1},{1,2},{2,3},{3,4},{4,5},{5,6},{6,7},{7,8},{8,9},{9,10},{10,1... | collective-permute-start | bytes 786440 | tf_op jit(solution)/shard_map/ppermute | solution.py:15
  620.3 14.6 %copy-start.1 = (s32[1024]{0:T(1024)S(1)}, s32[1024]{0:T(1024)}, u32[]{:S(2)}) copy-start(s32[1024]{0:T(1024)} %param.25) | copy-start | bytes 12292
where the time goes:
time: 646 us; the launch traced here: 635 us
  blocking collectives  272 us (42%)
  local copies, waits for them, and re-layouts  179 us (28%)
  waiting for transfers between devices  64.2 us (10%)
  other arithmetic  59.9 us (9%)
  starting transfers between devices  28.6 us (4%)
  loops' own time  20.6 us (3%)
  matrix products  9.69 us (2%)
    all_to_all x1, blocking collectives, shards(): lax.all_to_all(blocks, 'gx', split_axis=1, concat_axis=3, tiled=True)  111 us
    all_to_all x1, blocking collectives, shards(): lax.all_to_all(shaped, 'gx', split_axis=1, concat_axis=0, tiled=True)  109 us
    all_to_all x1, blocking collectives, shards(): lax.all_to_all(lax.all_to_all(blocks, 'gx', split_axis=1, concat_axis=3,...  52.1 us
    unnamed x1, other arithmetic  34.2 us
    all_to_all x1, waiting for transfers between devices, shards(): lax.all_to_all(lax.all_to_all(shaped, 'gx', split_axis=1, concat_axis=0,...  32.3 us
    ppermute x8, waiting for transfers between devices, passed_along(): lax.ppermute(value, axis, [(i, (i + by) % peers) for i in range(peers)])  31.9 us
    dynamic_update_slice x32, local copies, waits for them, and re-layouts, regress(): updated = lax.map(visit, (blocks, weights))  26.8 us
    squeeze x24, local copies, waits for them, and re-layouts, regress(): updated = lax.map(visit, (blocks, weights))  26 us
  transfers between devices with their start and end apart: 9, of which 7 were waited for; matrix products, arithmetic and copies ran while one was open for 4% of the time, Pallas kernels for 0%

commit v1 on v0

v1 whole, which is shorter than its diff:
```python
import functools

import jax
import jax.numpy as jnp
from jax import lax
from jax.experimental import pallas as pl
from jax.experimental.pallas import tpu as pltpu
from jax.sharding import Mesh, PartitionSpec as P

MEMBERS = 256
TILE = 512
NTILES = 2048
RADIUS = 4
WINDOW = 2 * RADIUS + 1
BATCH_OBS = 256
BATCHES = 4
NOBS = BATCH_OBS * BATCHES

ALL = ("y", "h", "l", "c", "x")
PEERS = ("y", "l", "c", "x")
GROUP = 64
SUMS = 4
RESIDUES = 16
SLICES = 4
LANES = 128
HALF = 64
OWN_TILES = NTILES // RESIDUES
PAIRS = OWN_TILES // 2
ROWS = NTILES * TILE // LANES
CHUNK = NOBS // 2 // SUMS

epsilon = 1e-06
f32 = jnp.float32
bf16 = jnp.bfloat16
i32 = jnp.int32

VMEM = pl.BlockSpec(memory_space=pltpu.VMEM)
SMEM = pl.BlockSpec(memory_space=pltpu.SMEM)


def kernel_params(mib):
    return pltpu.CompilerParams(vmem_limit_bytes=mib * 1024 * 1024)


def struct(shape, dtype=f32):
    return jax.ShapeDtypeStruct(shape, dtype)


def two_parts(value):
    high = value.astype(bf16)
    return high, (value - high.astype(f32)).astype(bf16)


def three_parts(value):
    high = value.astype(bf16)
    rest = value - high.astype(f32)
    middle = rest.astype(bf16)
    return high, middle, (rest - middle.astype(f32)).astype(bf16)


def dot(a, b):
    return lax.dot_general(a, b, (((1,), (0,)), ((), ())), preferred_element_type=f32)


def dot_parts(a_high, a_low, b_high, b_low):
    return dot(a_high, b_high) + dot(a_high, b_low) + dot(a_low, b_high)


def accurate_dot(a, b):
    return dot_parts(*two_parts(a), *two_parts(b))


def columns_kernel(plan_ref, locations_ref, state_ref, out_ref, picked_ref):
    lane = lax.broadcasted_iota(i32, (1, LANES), 1)

    def step(i, carry):
        base = pl.multiple_of(i * 8, 8)
        found = []
        for u in range(8):
            where = locations_ref[plan_ref[base + u]]
            row = state_ref[pl.ds(where >> 7, 1), :]
            found.append(jnp.where(lane == (where & (LANES - 1)), row, 0.0))
        picked_ref[pl.ds(base, 8), :] = jnp.concatenate(found, axis=0)
        return carry

    lax.fori_loop(0, NOBS // 8, step, 0, unroll=2)
    ones = jnp.ones((16, LANES), bf16)
    total = jnp.zeros((16, NOBS), f32)
    for part in three_parts(picked_ref[...]):
        total = total + lax.dot_general(ones, part, (((1,), (1,)), ((), ())), preferred_element_type=f32)
    for g in range(NOBS // LANES):
        out_ref[pl.ds(g, 1), :] = total[0:1, g * LANES : (g + 1) * LANES]


def own_columns(plan, locations, rows):
    return pl.pallas_call(
        columns_kernel,
        out_shape=struct((NOBS // LANES, LANES)),
        in_specs=[SMEM, SMEM, VMEM],
        out_specs=VMEM,
        scratch_shapes=[pltpu.VMEM((NOBS, LANES), f32)],
        compiler_params=kernel_params(24),
        cost_estimate=pl.CostEstimate(flops=10**6, bytes_accessed=8 * 2**20, transcendentals=0),
        name="own_columns",
    )(plan, locations, rows)


def spread_kernel(state_ref, first_ref, second_ref):
    low_lanes = lax.broadcasted_iota(i32, (PAIRS, LANES), 1) < HALF

    def step(d, carry):
        upper = state_ref[pl.ds(d, PAIRS, stride=GROUP), :]
        lower = state_ref[pl.ds(d + ROWS // 2, PAIRS, stride=GROUP), :]
        first_ref[d] = jnp.where(low_lanes, upper, lower)
        second_ref[d] = jnp.where(low_lanes, lower, upper)
        return carry

    lax.fori_loop(0, GROUP, step, 0)


def spread_out(rows):
    half = struct((GROUP, PAIRS, LANES))
    return pl.pallas_call(
        spread_kernel,
        out_shape=(half, half),
        in_specs=[VMEM],
        out_specs=(VMEM, VMEM),
        compiler_params=kernel_params(24),
        cost_estimate=pl.CostEstimate(flops=10**6, bytes_accessed=8 * 2**20, transcendentals=0),
        name="spread_out",
    )(rows)


def collect_kernel(first_ref, second_ref, state_ref):
    low_lanes = lax.broadcasted_iota(i32, (PAIRS, LANES), 1) < HALF

    def step(d, carry):
        first = first_ref[d]
        second = second_ref[d]
        state_ref[pl.ds(d, PAIRS, stride=GROUP), :] = jnp.where(low_lanes, first, second)
        state_ref[pl.ds(d + ROWS // 2, PAIRS, stride=GROUP), :] = jnp.where(low_lanes, second, first)
        return carry

    lax.fori_loop(0, GROUP, step, 0)


def collect(first, second):
    return pl.pallas_call(
        collect_kernel,
        out_shape=struct((ROWS, LANES)),
        in_specs=[VMEM, VMEM],
        out_specs=VMEM,
        compiler_params=kernel_params(24),
        cost_estimate=pl.CostEstimate(flops=10**6, bytes_accessed=8 * 2**20, transcendentals=0),
        name="collect",
    )(first, second)


def observation_kernel(
    position_ref, plan_ref, facts_ref, gathered_ref, masks_ref,
    anomalies_high_ref, anomalies_low_ref, increments_high_ref, increments_low_ref,
    links_high_ref, links_low_ref, column_facts_ref, row_facts_ref,
    ensemble_ref, increments_ref, one_hot_ref, facts_scratch, in_columns_ref,
):
    for d in range(SUMS):
        for g in range(NOBS // LANES):
            ensemble_ref[d * GROUP : (d + 1) * GROUP, g * LANES : (g + 1) * LANES] = gathered_ref[
                pl.ds(d * 8 + g, GROUP, stride=40), :
            ]
    for g in range(NOBS // LANES):
        facts_scratch[0:16, g * LANES : (g + 1) * LANES] = masks_ref[pl.ds(g, 16, stride=8), :]
    facts_scratch[16:24, :] = facts_ref[...]
    facts_scratch[24:128, :] = jnp.zeros((104, NOBS), f32)
    source = lax.broadcasted_iota(i32, (NOBS, NOBS), 0)
    one_hot_ref[...] = jnp.where(source == plan_ref[...], 1.0, 0.0).astype(bf16)
    high, middle, low = three_parts(facts_scratch[0:32, :])
    ordered = dot(high, one_hot_ref[...]) + dot(middle, one_hot_ref[...]) + dot(low, one_hot_ref[...])
    facts_scratch[0:32, :] = ordered
    for g in range(NOBS // LANES):
        in_columns_ref[g * LANES : (g + 1) * LANES, :] = facts_scratch[:, g * LANES : (g + 1) * LANES].T

    residue = position_ref[0]
    tile_row = facts_scratch[16:17, :].astype(i32)
    tile_column = in_columns_ref[:, 16:17].astype(i32)
    nth_row = (residue - tile_row + RADIUS) & (RESIDUES - 1)
    nth_column = (residue - tile_column + RADIUS) & (RESIDUES - 1)
    own_row = ((tile_row - RADIUS + nth_row) & (NTILES - 1)) >> 4
    own_column = ((tile_column - RADIUS + nth_column) & (NTILES - 1)) >> 4
    own_row = jnp.where(nth_row < WINDOW, own_row, -1)
    own_column = jnp.where(nth_column < WINDOW, own_column, -2)
    mask_column = jnp.zeros((NOBS, 1), f32)
    for n in range(WINDOW):
        mask_column = mask_column + jnp.where(nth_column == n, in_columns_ref[:, n : n + 1], 0.0)

    row_facts_ref[...] = jnp.broadcast_to(jnp.where(own_row < 0, -256, own_row & (PAIRS - 1)).astype(f32), (16, NOBS))
    lane = lax.broadcasted_iota(i32, (NOBS, LANES), 1)
    pair_column = jnp.where(own_column < 0, -256, own_column & (PAIRS - 1)).astype(f32)
    half_column = jnp.where(own_column >= PAIRS, 1.0, 0.0)

    for b in range(BATCHES):
        here = slice(b * BATCH_OBS, (b + 1) * BATCH_OBS)
        prior = ensemble_ref[:, here]
        average = jnp.sum(prior, axis=0, keepdims=True) / MEMBERS
        anomaly = prior - average
        spread = jnp.sum(anomaly * anomaly, axis=0, keepdims=True) / (MEMBERS - 1) + epsilon
        value = facts_scratch[17:18, here]
        error = facts_scratch[18:19, here]
        shrink = jnp.sqrt(error / (spread + error))
        moved = (average * error + value * spread) / (spread + error)
        increments = (shrink - 1.0) * anomaly + (moved - average)
        increments_ref[:, here] = increments
        turned = anomaly.T
        spread_column = jnp.sum(turned * turned, axis=1, keepdims=True) / (MEMBERS - 1) + epsilon
        gain_column = 1.0 / ((MEMBERS - 1) * spread_column)
        turned_high, turned_low = two_parts(turned)
        own_high = turned_high[:, 0:GROUP]
        own_low = turned_low[:, 0:GROUP]
        anomalies_high_ref[here, :] = jnp.concatenate([own_high] * 4, axis=1)
        anomalies_low_ref[here, :] = jnp.concatenate([own_low] * 4, axis=1)
        own_increments = two_parts(increments[0:GROUP, :])
        increments_high_ref[:, here] = own_increments[0]
        increments_low_ref[:, here] = own_increments[1]
        weight = mask_column[here] * gain_column
        column_facts_ref[here, :] = jnp.where(
            lane[here] == 0, weight, jnp.where(lane[here] == 1, pair_column[here], half_column[here])
        )
        if b > 0:
            before = b * BATCH_OBS
            links = accurate_dot(turned, increments_ref[:, 0:before])
            links = jnp.where(own_column[here] == own_row[:, 0:before], links * weight, 0.0)
            links_high, links_low = two_parts(links)
            links_high_ref[here, 0:before] = links_high
            links_low_ref[here, 0:before] = links_low
        if b < BATCHES - 1:
            after = slice((b + 1) * BATCH_OBS, NOBS)
            later = ensemble_ref[:, after]
            covariance = dot_parts(turned_high, turned_low, *two_parts(later))
            apart = (tile_row[:, after] - tile_column[here] + RADIUS) & (NTILES - 1)
            masks = jnp.zeros(apart.shape, f32)
            for n in range(WINDOW):
                masks = jnp.where(apart == n, in_columns_ref[here, n : n + 1], masks)
            ensemble_ref[:, after] = later + accurate_dot(increments, covariance * masks * gain_column)


def observations(position, plan, facts, gathered, masks):
    wide = struct((NOBS, 4 * GROUP), bf16)
    narrow = struct((GROUP, NOBS), bf16)
    links = struct((NOBS, NOBS), bf16)
    return pl.pallas_call(
        observation_kernel,
        out_shape=(wide, wide, narrow, narrow, links, links, struct((NOBS, LANES)), struct((16, NOBS))),
        in_specs=[SMEM, VMEM, VMEM, VMEM, VMEM],
        out_specs=(VMEM,) * 8,
        scratch_shapes=[
            pltpu.VMEM((MEMBERS, NOBS), f32),
            pltpu.VMEM((MEMBERS, NOBS), f32),
            pltpu.VMEM((NOBS, NOBS), bf16),
            pltpu.VMEM((128, NOBS), f32),
            pltpu.VMEM((NOBS, 128), f32),
        ],
        compiler_params=kernel_params(40),
        cost_estimate=pl.CostEstimate(flops=12 * 10**9, bytes_accessed=8 * 2**20, transcendentals=10**5),
        name="observations",
    )(position, plan, facts, gathered, masks)


def half_of(column_facts, second):
    half = column_facts[:, 2:3] > 0.5
    return jnp.logical_not(half) if second else half


def covariance_kernel(second, position_ref, block_ref, anomalies_high_ref, anomalies_low_ref, facts_ref, *refs):
    out_refs, (total_ref, pair_ref) = refs[:SUMS], refs[SUMS:]
    lane_block = lax.broadcasted_iota(i32, (NOBS, 4 * GROUP), 1) >> 6
    pair_ref[...] = (facts_ref[:, 1:2] - lane_block.astype(f32)).astype(bf16)
    total_ref[...] = jnp.zeros_like(total_ref)

    def step(g, carry):
        found = pair_ref[...] == jnp.full((NOBS, 4 * GROUP), (g * 4).astype(f32)).astype(bf16)
        zero = jnp.zeros((NOBS, 4 * GROUP), bf16)
        left_high = jnp.where(found, anomalies_high_ref[...], zero)
        left_low = jnp.where(found, anomalies_low_ref[...], zero)
        right = jnp.concatenate(
            [block_ref[pl.ds(g * 4 + u, GROUP, stride=PAIRS), :] for u in range(4)], axis=0
        )
        right_high, right_low = two_parts(right)
        both = dot(left_high, jnp.concatenate([right_high, right_low], axis=1))
        total_ref[...] += both[:, :LANES] + both[:, LANES:] + dot(left_low, right_high)
        return carry

    lax.fori_loop(0, PAIRS // 4, step, 0)
    total = total_ref[...]
    other = pltpu.roll(total, HALF, 1)
    half = half_of(facts_ref[...], second)
    low_lanes = lax.broadcasted_iota(i32, (NOBS // 2, LANES), 1) < HALF
    upper = jnp.where(half, other, total)[: NOBS // 2]
    lower = jnp.where(half, total, other)[NOBS // 2 :]
    total_ref[0 : NOBS // 2, :] = jnp.where(low_lanes, upper, lower)
    for d in range(SUMS):
        start = ((position_ref[1] + d) & (SUMS - 1)) * CHUNK
        out_refs[d][...] = total_ref[pl.ds(pl.multiple_of(start, CHUNK), CHUNK), :]


def covariances(second, position, block, anomalies_high, anomalies_low, facts):
    return pl.pallas_call(
        functools.partial(covariance_kernel, second),
        out_shape=(struct((CHUNK, LANES)),) * SUMS,
        in_specs=[SMEM] + [VMEM] * 4,
        out_specs=(VMEM,) * SUMS,
        scratch_shapes=[pltpu.VMEM((NOBS, LANES), f32), pltpu.VMEM((NOBS, 4 * GROUP), bf16)],
        compiler_params=kernel_params(24),
        cost_estimate=pl.CostEstimate(flops=3 * 10**9, bytes_accessed=4 * 2**20, transcendentals=0),
        name="covariances",
    )(position, block.reshape(GROUP * PAIRS, LANES), anomalies_high, anomalies_low, facts)


def update_kernel(
    second, position_ref, *refs
):
    sums_refs = refs[:SUMS]
    (block_ref, increments_high_ref, increments_low_ref, links_high_ref, links_low_ref,
     facts_ref, row_facts_ref, out_ref, sums_ref, coefficient_ref, right_ref) = refs[SUMS:]
    for d in range(SUMS):
        start = ((position_ref[1] - d) & (SUMS - 1)) * CHUNK
        sums_ref[pl.ds(pl.multiple_of(start, CHUNK), CHUNK), :] = sums_refs[d][...]
    packed = sums_ref[...]
    weight = facts_ref[:, 0:1]
    coefficient_ref[0 : NOBS // 2, :] = packed * weight[: NOBS // 2]
    coefficient_ref[NOBS // 2 :, :] = pltpu.roll(packed, HALF, 1) * weight[NOBS // 2 :]
    for b in range(1, BATCHES):
        here = slice(b * BATCH_OBS, (b + 1) * BATCH_OBS)
        before = slice(0, b * BATCH_OBS)
        coefficient_ref[here, :] += dot_parts(
            links_high_ref[here, before], links_low_ref[here, before], *two_parts(coefficient_ref[before, :])
        )
    coefficient = coefficient_ref[...]
    half = half_of(facts_ref[...], second)
    high_lanes = lax.broadcasted_iota(i32, (NOBS, LANES), 1) >= HALF
    placed = jnp.where(
        high_lanes,
        jnp.where(half, pltpu.roll(coefficient, HALF, 1), 0.0),
        jnp.where(half, 0.0, coefficient),
    )
    right_high, right_low = two_parts(placed)
    right_ref[:, :LANES] = right_high
    right_ref[:, LANES:] = right_low
    pair_row = row_facts_ref[...].astype(bf16)[0:1, :]

    def step(g, carry):
        highs, lows = [], []
        zero = jnp.zeros((GROUP, NOBS), bf16)
        for u in range(4):
            found = pair_row == jnp.full((1, NOBS), (g * 4 + u).astype(f32)).astype(bf16)
            found = jnp.broadcast_to(found, (GROUP, NOBS))
            highs.append(jnp.where(found, increments_high_ref[...], zero))
            lows.append(jnp.where(found, increments_low_ref[...], zero))
        both = dot(jnp.concatenate(highs, axis=0), right_ref[...])
        change = both[:, :LANES] + both[:, LANES:] + dot(jnp.concatenate(lows, axis=0), right_ref[:, :LANES])
        for u in range(4):
            rows = pl.ds(g * 4 + u, GROUP, stride=PAIRS)
            out_ref[rows, :] = block_ref[rows, :] + change[u * GROUP : (u + 1) * GROUP]
        return carry

    lax.fori_loop(0, PAIRS // 4, step, 0)


def updated(second, position, sums, block, increments_high, increments_low, links_high, links_low, facts, row_facts):
    out = pl.pallas_call(
        functools.partial(update_kernel, second),
        out_shape=struct((GROUP * PAIRS, LANES)),
        in_specs=[SMEM] + [VMEM] * (SUMS + 7),
        out_specs=VMEM,
        scratch_shapes=[
            pltpu.VMEM((NOBS // 2, LANES), f32),
            pltpu.VMEM((NOBS, LANES), f32),
            pltpu.VMEM((NOBS, 2 * LANES), bf16),
        ],
        compiler_params=kernel_params(32),
        cost_estimate=pl.CostEstimate(flops=4 * 10**9, bytes_accessed=8 * 2**20, transcendentals=0),
        name="updated",
    )(
        position, *sums, block.reshape(GROUP * PAIRS, LANES), increments_high, increments_low,
        links_high, links_low, facts, row_facts,
    )
    return out.reshape(GROUP, PAIRS, LANES)


def exchange(value):
    return lax.all_to_all(value, PEERS, 0, 0, tiled=True)


def passed_along(value, by):
    return lax.ppermute(value, "h", [(i, (i + by) % SUMS) for i in range(SUMS)])


def summed(parts):
    total = parts[0]
    for by in range(1, SUMS):
        total = total + passed_along(parts[by], by)
    return (total, *(passed_along(total, by) for by in range(1, SUMS)))


def shards(state, locations, tile_mask, plan, obs_value, obs_error):
    group_index = lax.axis_index(PEERS)
    position = jnp.stack([group_index // SLICES, lax.axis_index("h")]).astype(i32)
    rows = state.reshape(ROWS, LANES)

    tiles_here = tile_mask.shape[0]
    tiles = locations // TILE
    nth = jnp.arange(16, dtype=i32)[:, None]
    local = (tiles[None, :] - RADIUS + nth - lax.axis_index(ALL) * tiles_here) & (NTILES - 1)
    masks = jnp.zeros((16, NOBS), i32)
    for i in range(tiles_here):
        masks = masks + jnp.where((local == i) & (nth < WINDOW), tile_mask[i][None, :], 0)
    masks = exchange(masks.astype(f32).reshape(GROUP, 2, LANES)).sum(axis=0)

    columns = own_columns(plan, locations, rows)
    payload = jnp.concatenate(
        [columns, *(passed_along(columns, by) for by in range(1, SUMS)), masks, jnp.zeros((6, LANES), f32)], axis=0
    )
    gathered = exchange(jnp.broadcast_to(payload[None], (GROUP, 40, LANES)))

    first, second = spread_out(rows)
    first, gathered = lax.optimization_barrier((first, gathered))
    first = exchange(first)

    all_masks = gathered[:, 32:34, :]
    all_masks = all_masks + sum(passed_along(all_masks, by) for by in range(1, SUMS))
    facts = jnp.concatenate(
        [tiles.astype(f32)[None], obs_value[None], obs_error[None], jnp.zeros((5, NOBS), f32)], axis=0
    )
    (anomalies_high, anomalies_low, increments_high, increments_low, links_high, links_low, column_facts, row_facts) = (
        observations(
            position, plan[None], facts, gathered.reshape(GROUP * 40, LANES), all_masks.reshape(2 * GROUP, LANES)
        )
    )

    first, second = lax.optimization_barrier((first, second))
    second = exchange(second)

    def assimilated(is_second, block):
        parts = covariances(is_second, position, block, anomalies_high, anomalies_low, column_facts)
        return updated(
            is_second, position, summed(parts), block,
            increments_high, increments_low, links_high, links_low, column_facts, row_facts,
        )

    first = exchange(assimilated(False, first))
    second = exchange(assimilated(True, second))
    return collect(first, second).reshape(state.shape)


def solution(mesh):
    fine = Mesh(mesh.devices.reshape(4, 4, 2, 2, 4), ALL)
    placed = (P(ALL, None), P(), P(ALL, None), P(), P(), P())
    return jax.shard_map(shards, mesh=fine, in_specs=placed, out_specs=P(ALL, None), check_vma=False)
```

time: 646 us -> 301 us (0.47); the launches traced: 635 us -> 300 us
  blocking collectives: 272 us -> 72.4 us
  local copies, waits for them, and re-layouts: 179 us -> 16.4 us
  Pallas kernels: 0 us -> 62.3 us
  other arithmetic: 59.9 us -> 2.25 us
  starting transfers between devices: 28.6 us -> 78 us
  loops' own time: 20.6 us -> 0 us
  matrix products: 9.69 us -> 0 us
    all_to_all x3 -> x2, blocking collectives: 272 us -> 72.4 us  [exchange(): return lax.all_to_all(value, PEERS, 0, 0, tiled=True)]
    pallas_call x0 -> x8, Pallas kernels: none -> 62.3 us  [the longest x2 21.1 us: updated(): pl.pallas_call(functools.partial(update_kernel, second), out_shape=struct...]
    all_to_all x1 -> x4, starting transfers between devices: 5.28 us -> 40.3 us  [exchange(): return lax.all_to_all(value, PEERS, 0, 0, tiled=True)]
    unnamed x1 -> x0, other arithmetic: 34.2 us -> none
    gather x20 -> x0, local copies, waits for them, and re-layouts: 31.9 us -> none  [the longest x4 12.6 us: shards(): jnp.take(ensemble, clipped, axis=1)]
    dynamic_update_slice x32 -> x0, local copies, waits for them, and re-layouts: 26.8 us -> none  [regress(): updated = lax.map(visit, (blocks, weights))]
    squeeze x24 -> x0, local copies, waits for them, and re-layouts: 26 us -> none  [regress(): updated = lax.map(visit, (blocks, weights))]
    another operation x6 -> x0, local copies, waits for them, and re-layouts: 26 us -> none  [the longest x2 16.6 us: shards(): ensemble.reshape(narrow_size, wide_size, members_here, 1, 1, per_device)]
  transfers between devices with their start and end apart: 9 -> 22, of which waited for: 7 -> 12; matrix products, arithmetic and copies ran while one was open for 4% -> 0% of each run, Pallas kernels for 0% -> 19%
where the time goes in v1:
time: 301 us; the launch traced here: 300 us
  starting transfers between devices  78 us (26%)
  blocking collectives  72.4 us (24%)
  waiting for transfers between devices  68.3 us (23%)
  Pallas kernels  62.3 us (21%)
  local copies, waits for them, and re-layouts  16.4 us (5%)
    all_to_all x2, blocking collectives, exchange(): return lax.all_to_all(value, PEERS, 0, 0, tiled=True)  72.4 us
    ppermute x18, waiting for transfers between devices, passed_along(): return lax.ppermute(value, 'h', [(i, (i + by) % SUMS) for i in range(SUMS)])  56.7 us
    all_to_all x4, starting transfers between devices, exchange(): return lax.all_to_all(value, PEERS, 0, 0, tiled=True)  40.3 us
    ppermute x18, starting transfers between devices, passed_along(): return lax.ppermute(value, 'h', [(i, (i + by) % SUMS) for i in range(SUMS)])  37.7 us
    pallas_call x2, Pallas kernels, updated(): pl.pallas_call(functools.partial(update_kernel, second), out_shape=struct...  21.1 us
    pallas_call x2, Pallas kernels, covariances(): pl.pallas_call(functools.partial(covariance_kernel, second), out_shape=(s...  18.5 us
    unnamed x56, local copies, waits for them, and re-layouts  13.8 us
    all_to_all x4, waiting for transfers between devices, exchange(): return lax.all_to_all(value, PEERS, 0, 0, tiled=True)  11.6 us
  transfers between devices with their start and end apart: 22, of which 12 were waited for; matrix products, arithmetic and copies ran while one was open for 0% of the time, Pallas kernels for 19%

profile of v1, /device:TPU:1, one launch (start us, length us, event | category | flops | bytes accessed | tf_op | source)
XLA Modules:
  0.0 300.1 jit_solution(14693835866918395763)
XLA Ops:
  0.0 0.1 and.130
  0.1 0.1 and.131
  0.2 0.1 add.105
  0.3 0.7 fusion.12
  1.0 1.1 fusion.13
  2.1 1.2 fusion.7
  3.3 10.3 %all-to-all-start = ((f32[64,2,128]{2,1,0:T(2,128)}), f32[64,2,128]{2,1,0:T(2,128)S(1)}, u32[]{:S(2)}, u32[]{:S(2)}) async-start(f32[64,2,128]{2,1,0:T(2,128)} %fusion.7), calls=%async_computation | async-start | bytes 131072 | tf_op jit(solution)/shard_map/all_to_all | solution.py:389
  13.7 2.2 copy-done
  15.8 0.7 copy-done.9
  16.5 0.7 copy-done.10
  17.2 3.1 %own_columns.1 = f32[8,128]{1,0:T(8,128)S(1)} custom-call(s32[1024]{0:T(1024)S(1)} %copy-done.10, s32[1024]{0:T(1024)S(1)} %copy-done.9, f32[8192,128]{1,0:T(8,128)S(1)} %bitcast.65), custom_call_target="tpu_custom_call" | custom-call | flops 1000000 | bytes 8388608 | tf_op jit(solution)/shard_map/own_columns/pallas_call | solution.py:96
  20.3 5.1 %collective-permute-start.2 = (f32[8,128]{1,0:T(8,128)S(1)}, f32[8,128]{1,0:T(8,128)S(1)}, u32[]{:S(2)}, u32[]{:S(2)}) collective-permute-start(f32[8,128]{1,0:T(8,128)S(1)} %own_columns.1), channel_id=1, source_target_pairs={{0,48},{16,0},{32,16},{48,32},{1,49},{17,1},{33,17},{49,33},{2,50}... | collective-permute-start | bytes 12296 | tf_op jit(solution)/shard_map/ppermute | solution.py:393
  25.4 1.2 collective-permute-start.1
  26.6 2.1 collective-permute-start
  28.7 0.1 reduce_sum.9
  28.7 3.0 %collective-permute-done.1 = f32[8,128]{1,0:T(8,128)S(1)} collective-permute-done((f32[8,128]{1,0:T(8,128)S(1)}, f32[8,128]{1,0:T(8,128)S(1)}, u32[]{:S(2)}, u32[]{:S(2)}) %collective-permute-start.1) | collective-permute-done | bytes 4128 | tf_op jit(solution)/shard_map/ppermute | solution.py:393
  31.8 1.1 broadcast_in_dim.135
  32.9 10.3 %all-to-all-start.1 = ((f32[64,40,128]{2,1,0:T(8,128)}), f32[64,40,128]{2,1,0:T(8,128)S(1)}, u32[]{:S(2)}, u32[]{:S(2)}) async-start(f32[64,40,128]{2,1,0:T(8,128)} %broadcast_in_dim.135), calls=%async_computation.1 | async-start | bytes 2621440 | tf_op jit(solution)/shard_map/all_to_all | solution.py:389
  43.2 2.2 copy-done.1
  45.4 4.5 %spread_out.1 = (f32[64,64,128]{2,1,0:T(8,128)S(1)}, f32[64,64,128]{2,1,0:T(8,128)S(1)}) custom-call(f32[8192,128]{1,0:T(8,128)S(1)} %bitcast.66), custom_call_target="tpu_custom_call" | custom-call | flops 1000000 | bytes 8388608 | tf_op jit(solution)/shard_map/spread_out/pallas_call | solution.py:123
  50.0 1.3 copy-done.5
  51.3 11.6 %all-to-all-done.1 = f32[64,40,128]{2,1,0:T(8,128)S(1)} async-done(((f32[64,40,128]{2,1,0:T(8,128)}), f32[64,40,128]{2,1,0:T(8,128)S(1)}, u32[]{:S(2)}, u32[]{:S(2)}) %all-to-all-start.1) | async-done | bytes 1310752 | tf_op jit(solution)/shard_map/all_to_all | solution.py:389
  62.9 34.1 %all_to_all.30 = f32[64,64,128]{2,1,0:T(8,128)} all-to-all(f32[64,64,128]{2,1,0:T(8,128)S(1)} %get-tuple-element.28), channel_id=1, replica_groups=mesh['y'=4,'h'=4,'l'=2,'c'=2,'x'=4] {'y','l','c','x'}, dimensions={0} | all-to-all | bytes 4194304 | tf_op jit(solution)/shard_map/all_to_all | solution.py:389
  97.0 5.5 %all-to-all-start.4 = ((f32[64,64,128]{2,1,0:T(8,128)}), f32[64,64,128]{2,1,0:T(8,128)S(1)}, u32[]{:S(2)}, u32[]{:S(2)}) async-start(f32[64,64,128]{2,1,0:T(8,128)} %copy-done.5), calls=%async_computation.4 | async-start | bytes 4194304 | tf_op jit(solution)/shard_map/all_to_all | solution.py:389
  102.6 0.1 pad.3.clone
  102.7 0.1 maximum_maximum_fusion.facts_ref
  102.8 1.2 collective-permute-start.5
  104.0 2.8 collective-permute-start.4
  106.8 2.3 collective-permute-start.3
  109.1 0.1 pad_add_fusion.position_ref
  109.1 24.6 %collective-permute-done.4 = f32[64,2,128]{2,1,0:T(2,128)S(1)} collective-permute-done((f32[64,2,128]{2,1,0:T(2,128)S(1)}, f32[64,2,128]{2,1,0:T(2,128)S(1)}, u32[]{:S(2)}, u32[]{:S(2)}) %collective-permute-start.4) | collective-permute-done | bytes 65568 | tf_op jit(solution)/shard_map/ppermute | solution.py:393
  133.8 8.8 %observations.1 = (bf16[1024,256]{1,0:T(8,128)(2,1)S(1)}, bf16[1024,256]{1,0:T(8,128)(2,1)S(1)}, bf16[64,1024]{1,0:T(8,128)(2,1)S(1)}, bf16[64,1024]{1,0:T(8,128...) custom-call(s32[2]{0:T(128)S(1)} %pad_add_fusion.position_ref, ...), custom_call_target="tpu_custom_call" | custom-call | flops 12000000000 | bytes 8388608 | tf_op jit(solution)/shard_map/observations/pallas_call | solution.py:249
  142.7 9.2 %covariances.2 = (f32[128,128]{1,0:T(8,128)S(1)}, f32[128,128]{1,0:T(8,128)S(1)}, f32[128,128]{1,0:T(8,128)S(1)}, f32[128,128]{1,0:T(8,128)S(1)}) custom-call(s32[2]{0:T(128)S(1)} %pad_add_fusion.position_ref, f32[4096,128]{1,0:T(8,128)S(1)} %bitcast.69, bf16[1024,256]{1,0:T(8,128)(2,1)S(1)} %get-tuple-element.32.anomalies_high_ref, ...), custom_call_target="tpu_custom_call" | custom-call | flops 3000000000 | bytes 4194304 | tf_op jit(solution)/shard_map/covariances/pallas_call | solution.py:305
  151.9 0.1 collective-permute-start.6
  152.0 3.7 %collective-permute-start.7 = (f32[128,128]{1,0:T(8,128)S(1)}, f32[128,128]{1,0:T(8,128)S(1)}, u32[]{:S(2)}, u32[]{:S(2)}) collective-permute-start(f32[128,128]{1,0:T(8,128)S(1)} %get-tuple-element.37), channel_id=1, source_target_pairs={{0,32},{16,48},{32,0},{48,16},{1,33},{17,49},{33,1},{49,17},{2,34}... | collective-permute-start | bytes 196616 | tf_op jit(solution)/shard_map/ppermute | solution.py:393
  155.8 0.7 collective-permute-start.8
  156.5 1.0 collective-permute-done.6
  157.5 2.2 collective-permute-done.7
  159.8 0.3 collective-permute-done.8
  160.1 3.3 %collective-permute-start.11 = (f32[128,128]{1,0:T(8,128)S(1)}, f32[128,128]{1,0:T(8,128)S(1)}, u32[]{:S(2)}, u32[]{:S(2)}) collective-permute-start(f32[128,128]{1,0:T(8,128)S(1)} %add_add_fusion.1.refs_0_), channel_id=1, source_target_pairs={{0,48},{16,0},{32,16},{48,32},{1,49},{17,1},{33,17},{49,33},{2,50}... | collective-permute-start | bytes 196616 | tf_op jit(solution)/shard_map/ppermute | solution.py:393
  163.4 3.7 %collective-permute-start.10 = (f32[128,128]{1,0:T(8,128)S(1)}, f32[128,128]{1,0:T(8,128)S(1)}, u32[]{:S(2)}, u32[]{:S(2)}) collective-permute-start(f32[128,128]{1,0:T(8,128)S(1)} %add_add_fusion.1.refs_0_), channel_id=1, source_target_pairs={{0,32},{16,48},{32,0},{48,16},{1,33},{17,49},{33,1},{49,17},{2,34}... | collective-permute-start | bytes 196616 | tf_op jit(solution)/shard_map/ppermute | solution.py:393
  167.1 3.9 %collective-permute-done.10.refs_2_ = f32[128,128]{1,0:T(8,128)S(1)} collective-permute-done((f32[128,128]{1,0:T(8,128)S(1)}, f32[128,128]{1,0:T(8,128)S(1)}, u32[]{:S(2)}, u32[]{:S(2)}) %collective-permute-start.10) | collective-permute-done | bytes 65568 | tf_op jit(solution)/shard_map/ppermute | solution.py:393
  171.0 1.4 collective-permute-done.9.refs_1_
  172.4 10.6 %updated.2 = f32[4096,128]{1,0:T(8,128)S(1)} custom-call(s32[2]{0:T(128)S(1)} %pad_add_fusion.position_ref, f32[128,128]{1,0:T(8,128)S(1)} %add_add_fusion.1.refs_0_, f32[128,128]{1,0:T(8,128)S(1)} %collective-permute-done.9.refs_1_, f32[128,128]{1,0:T(8,128)S(1)} %collective-permute-done.10.refs_2_, f32[128,128]{1,0:T(8,128)S(1)} %collective-permute-done.11.refs_3_, ...), custom_call_target="tpu_custom_call" | custom-call | flops 4000000000 | bytes 8388608 | tf_op jit(solution)/shard_map/updated/pallas_call | solution.py:368
  183.0 1.3 copy-done.7
  184.3 1.4 copy-done.2
  185.6 14.2 %all-to-all-start.3 = ((f32[64,64,128]{2,1,0:T(8,128)}), f32[64,64,128]{2,1,0:T(8,128)S(1)}, u32[]{:S(2)}, u32[]{:S(2)}) async-start(f32[64,64,128]{2,1,0:T(8,128)} %bitcast.71), calls=%async_computation.3 | async-start | bytes 4194304 | tf_op jit(solution)/shard_map/all_to_all | solution.py:389
  199.9 1.6 copy-done.3
  201.5 1.0 copy-done.21
  202.5 9.2 %covariances.3 = (f32[128,128]{1,0:T(8,128)S(1)}, f32[128,128]{1,0:T(8,128)S(1)}, f32[128,128]{1,0:T(8,128)S(1)}, f32[128,128]{1,0:T(8,128)S(1)}) custom-call(s32[2]{0:T(128)S(1)} %pad_add_fusion.position_ref, f32[4096,128]{1,0:T(8,128)S(1)} %bitcast.67, bf16[1024,256]{1,0:T(8,128)(2,1)S(1)} %copy-done.19, bf16[1024,256]{1,0:T(8,128)(2,1)S(1)} %copy-done.21, ...), custom_call_target="tpu_custom_call" | custom-call | flops 3000000000 | bytes 4194304 | tf_op jit(solution)/shard_map/covariances/pallas_call | solution.py:305
  211.8 0.1 collective-permute-start.12
  211.9 3.2 %collective-permute-start.13 = (f32[128,128]{1,0:T(8,128)S(1)}, f32[128,128]{1,0:T(8,128)S(1)}, u32[]{:S(2)}, u32[]{:S(2)}) collective-permute-start(f32[128,128]{1,0:T(8,128)S(1)} %get-tuple-element.47), channel_id=1, source_target_pairs={{0,32},{16,48},{32,0},{48,16},{1,33},{17,49},{33,1},{49,17},{2,34}... | collective-permute-start | bytes 196616 | tf_op jit(solution)/shard_map/ppermute | solution.py:393
  215.0 3.5 %collective-permute-start.14 = (f32[128,128]{1,0:T(8,128)S(1)}, f32[128,128]{1,0:T(8,128)S(1)}, u32[]{:S(2)}, u32[]{:S(2)}) collective-permute-start(f32[128,128]{1,0:T(8,128)S(1)} %get-tuple-element.48), channel_id=1, source_target_pairs={{0,48},{16,0},{32,16},{48,32},{1,49},{17,1},{33,17},{49,33},{2,50}... | collective-permute-start | bytes 196616 | tf_op jit(solution)/shard_map/ppermute | solution.py:393
  218.5 7.4 %collective-permute-done.12 = f32[128,128]{1,0:T(8,128)S(1)} collective-permute-done((f32[128,128]{1,0:T(8,128)S(1)}, f32[128,128]{1,0:T(8,128)S(1)}, u32[]{:S(2)}, u32[]{:S(2)}) %collective-permute-start.12) | collective-permute-done | bytes 65568 | tf_op jit(solution)/shard_map/ppermute | solution.py:393
  225.9 5.8 %collective-permute-done.13 = f32[128,128]{1,0:T(8,128)S(1)} collective-permute-done((f32[128,128]{1,0:T(8,128)S(1)}, f32[128,128]{1,0:T(8,128)S(1)}, u32[]{:S(2)}, u32[]{:S(2)}) %collective-permute-start.13) | collective-permute-done | bytes 65568 | tf_op jit(solution)/shard_map/ppermute | solution.py:393
  231.7 0.1 collective-permute-start.17
  231.8 2.4 collective-permute-start.16
  234.1 2.3 collective-permute-start.15
  236.4 2.5 collective-permute-done.16.refs_2_
  238.9 4.6 %collective-permute-done.15.refs_1_ = f32[128,128]{1,0:T(8,128)S(1)} collective-permute-done((f32[128,128]{1,0:T(8,128)S(1)}, f32[128,128]{1,0:T(8,128)S(1)}, u32[]{:S(2)}, u32[]{:S(2)}) %collective-permute-start.15) | collective-permute-done | bytes 65568 | tf_op jit(solution)/shard_map/ppermute | solution.py:393
  243.6 10.6 %updated.3 = f32[4096,128]{1,0:T(8,128)S(1)} custom-call(s32[2]{0:T(128)S(1)} %pad_add_fusion.position_ref, f32[128,128]{1,0:T(8,128)S(1)} %add_add_fusion.refs_0_, f32[128,128]{1,0:T(8,128)S(1)} %collective-permute-done.15.refs_1_, f32[128,128]{1,0:T(8,128)S(1)} %collective-permute-done.16.refs_2_, f32[128,128]{1,0:T(8,128)S(1)} %collective-permute-done.17.refs_3_, ...), custom_call_target="tpu_custom_call" | custom-call | flops 4000000000 | bytes 8388608 | tf_op jit(solution)/shard_map/updated/pallas_call | solution.py:368
  254.2 1.3 copy-done.8
  255.5 38.3 %all_to_all.31.second_ref = f32[64,64,128]{2,1,0:T(8,128)S(1)} all-to-all(f32[64,64,128]{2,1,0:T(8,128)} %bitcast.72), channel_id=1, replica_groups=mesh['y'=4,'h'=4,'l'=2,'c'=2,'x'=4] {'y','l','c','x'}, dimensions={0} | all-to-all | bytes 4194304 | tf_op jit(solution)/shard_map/all_to_all | solution.py:389
  293.8 6.3 %collect.1 = f32[8192,128]{1,0:T(8,128)} custom-call(f32[64,64,128]{2,1,0:T(8,128)S(1)} %all-to-all-done.3.first_ref, f32[64,64,128]{2,1,0:T(8,128)S(1)} %all_to_all.31.second_ref), custom_call_target="tpu_custom_call" | custom-call | flops 1000000 | bytes 8388608 | tf_op jit(solution)/shard_map/collect/pallas_call | solution.py:148
  (66 shorter events, 0.3 us)
Async XLA Ops:
  3.3 25.4 %all-to-all-start = ((f32[64,2,128]{2,1,0:T(2,128)}), f32[64,2,128]{2,1,0:T(2,128)S(1)}, u32[]{:S(2)}, u32[]{:S(2)}) async-start(f32[64,2,128]{2,1,0:T(2,128)} %fusion.7), calls=%async_computation | async-start | bytes 131072 | tf_op jit(solution)/shard_map/all_to_all | solution.py:389
  13.6 2.2 copy-start
  15.8 0.7 copy-start.9
  16.5 0.7 copy-start.10
  20.3 8.5 %collective-permute-start.2 = (f32[8,128]{1,0:T(8,128)S(1)}, f32[8,128]{1,0:T(8,128)S(1)}, u32[]{:S(2)}, u32[]{:S(2)}) collective-permute-start(f32[8,128]{1,0:T(8,128)S(1)} %own_columns.1), channel_id=1, source_target_pairs={{0,48},{16,0},{32,16},{48,32},{1,49},{17,1},{33,17},{49,33},{2,50}... | collective-permute-start | bytes 12296 | tf_op jit(solution)/shard_map/ppermute | solution.py:393
  25.4 6.4 %collective-permute-start.1 = (f32[8,128]{1,0:T(8,128)S(1)}, f32[8,128]{1,0:T(8,128)S(1)}, u32[]{:S(2)}, u32[]{:S(2)}) collective-permute-start(f32[8,128]{1,0:T(8,128)S(1)} %own_columns.1), channel_id=1, source_target_pairs={{0,32},{16,48},{32,0},{48,16},{1,33},{17,49},{33,1},{49,17},{2,34}... | collective-permute-start | bytes 12296 | tf_op jit(solution)/shard_map/ppermute | solution.py:393
  26.6 5.2 %collective-permute-start = (f32[8,128]{1,0:T(8,128)S(1)}, f32[8,128]{1,0:T(8,128)S(1)}, u32[]{:S(2)}, u32[]{:S(2)}) collective-permute-start(f32[8,128]{1,0:T(8,128)S(1)} %own_columns.1), channel_id=1, source_target_pairs={{0,16},{16,32},{32,48},{48,0},{1,17},{17,33},{33,49},{49,1},{2,18}... | collective-permute-start | bytes 12296 | tf_op jit(solution)/shard_map/ppermute | solution.py:393
  32.9 29.9 %all-to-all-start.1 = ((f32[64,40,128]{2,1,0:T(8,128)}), f32[64,40,128]{2,1,0:T(8,128)S(1)}, u32[]{:S(2)}, u32[]{:S(2)}) async-start(f32[64,40,128]{2,1,0:T(8,128)} %broadcast_in_dim.135), calls=%async_computation.1 | async-start | bytes 2621440 | tf_op jit(solution)/shard_map/all_to_all | solution.py:389
  43.2 2.2 copy-start.1
  50.0 1.4 copy-start.5
  97.0 5.6 %copy-start.26 = (f32[1024]{0:T(1024)S(1)}, f32[1024]{0:T(1024)}, u32[]{:S(2)}) copy-start(f32[1024]{0:T(1024)} %param.11) | copy-start | bytes 12292
  97.0 5.6 %copy-start.27 = (f32[1024]{0:T(1024)S(1)}, f32[1024]{0:T(1024)}, u32[]{:S(2)}) copy-start(f32[1024]{0:T(1024)} %param.10) | copy-start | bytes 12292
  97.0 36.8 %copy-start.11 = (s32[1024]{0:T(1024)S(1)}, s32[1024]{0:T(1024)}, u32[]{:S(2)}) copy-start(s32[1024]{0:T(1024)} %plan_ref.1) | copy-start | bytes 12292
  97.0 87.2 %all-to-all-start.4 = ((f32[64,64,128]{2,1,0:T(8,128)}), f32[64,64,128]{2,1,0:T(8,128)S(1)}, u32[]{:S(2)}, u32[]{:S(2)}) async-start(f32[64,64,128]{2,1,0:T(8,128)} %copy-done.5), calls=%async_computation.4 | async-start | bytes 4194304 | tf_op jit(solution)/shard_map/all_to_all | solution.py:389
  102.8 6.4 %collective-permute-start.5 = (f32[64,2,128]{2,1,0:T(2,128)S(1)}, f32[64,2,128]{2,1,0:T(2,128)S(1)}, u32[]{:S(2)}, u32[]{:S(2)}) collective-permute-start(f32[64,2,128]{2,1,0:T(2,128)S(1)} %slice.35), channel_id=1, source_target_pairs={{0,48},{16,0},{32,16},{48,32},{1,49},{17,1},{33,17},{49,33},{2,50}... | collective-permute-start | bytes 196616 | tf_op jit(solution)/shard_map/ppermute | solution.py:393
  104.0 29.7 %collective-permute-start.4 = (f32[64,2,128]{2,1,0:T(2,128)S(1)}, f32[64,2,128]{2,1,0:T(2,128)S(1)}, u32[]{:S(2)}, u32[]{:S(2)}) collective-permute-start(f32[64,2,128]{2,1,0:T(2,128)S(1)} %slice.35), channel_id=1, source_target_pairs={{0,32},{16,48},{32,0},{48,16},{1,33},{17,49},{33,1},{49,17},{2,34}... | collective-permute-start | bytes 196616 | tf_op jit(solution)/shard_map/ppermute | solution.py:393
  106.8 26.9 %collective-permute-start.3 = (f32[64,2,128]{2,1,0:T(2,128)S(1)}, f32[64,2,128]{2,1,0:T(2,128)S(1)}, u32[]{:S(2)}, u32[]{:S(2)}) collective-permute-start(f32[64,2,128]{2,1,0:T(2,128)S(1)} %slice.35), channel_id=1, source_target_pairs={{0,16},{16,32},{32,48},{48,0},{1,17},{17,33},{33,49},{49,1},{2,18}... | collective-permute-start | bytes 196616 | tf_op jit(solution)/shard_map/ppermute | solution.py:393
  133.8 8.9 %copy-start.6 = (f32[64,64,128]{2,1,0:T(8,128)S(1)}, f32[64,64,128]{2,1,0:T(8,128)}, u32[]{:S(2)}) copy-start(f32[64,64,128]{2,1,0:T(8,128)} %all_to_all.30) | copy-start | bytes 6291460
  142.6 9.3 %copy-start.18 = (bf16[1024,256]{1,0:T(8,128)(2,1)}, bf16[1024,256]{1,0:T(8,128)(2,1)S(1)}, u32[]{:S(2)}) copy-start(bf16[1024,256]{1,0:T(8,128)(2,1)S(1)} %get-tuple-element.32.anomalies_high_ref) | copy-start | bytes 1572868
  142.6 9.3 %copy-start.20 = (bf16[1024,256]{1,0:T(8,128)(2,1)}, bf16[1024,256]{1,0:T(8,128)(2,1)S(1)}, u32[]{:S(2)}) copy-start(bf16[1024,256]{1,0:T(8,128)(2,1)S(1)} %get-tuple-element.33.anomalies_low_ref) | copy-start | bytes 1572868
  142.6 29.7 %copy-start.12 = (bf16[1024,1024]{1,0:T(8,128)(2,1)}, bf16[1024,1024]{1,0:T(8,128)(2,1)S(1)}, u32[]{:S(2)}) copy-start(bf16[1024,1024]{1,0:T(8,128)(2,1)S(1)} %get-tuple-element.41.refs_7_) | copy-start | bytes 6291460
  142.6 29.7 %copy-start.14 = (bf16[1024,1024]{1,0:T(8,128)(2,1)}, bf16[1024,1024]{1,0:T(8,128)(2,1)S(1)}, u32[]{:S(2)}) copy-start(bf16[1024,1024]{1,0:T(8,128)(2,1)S(1)} %get-tuple-element.42.refs_8_) | copy-start | bytes 6291460
  142.6 29.7 %copy-start.16 = (f32[1024,128]{1,0:T(8,128)}, f32[1024,128]{1,0:T(8,128)S(1)}, u32[]{:S(2)}) copy-start(f32[1024,128]{1,0:T(8,128)S(1)} %get-tuple-element.34.facts_ref.refs_9_) | copy-start | bytes 1572868
  142.7 29.7 %copy-start.22 = (bf16[64,1024]{1,0:T(8,128)(2,1)}, bf16[64,1024]{1,0:T(8,128)(2,1)S(1)}, u32[]{:S(2)}) copy-start(bf16[64,1024]{1,0:T(8,128)(2,1)S(1)} %get-tuple-element.40.refs_6_) | copy-start | bytes 393220
  142.7 29.7 %copy-start.24 = (f32[16,1024]{1,0:T(8,128)}, f32[16,1024]{1,0:T(8,128)S(1)}, u32[]{:S(2)}) copy-start(f32[16,1024]{1,0:T(8,128)S(1)} %get-tuple-element.43.refs_10_) | copy-start | bytes 196612
  151.9 5.6 %collective-permute-start.6 = (f32[128,128]{1,0:T(8,128)S(1)}, f32[128,128]{1,0:T(8,128)S(1)}, u32[]{:S(2)}, u32[]{:S(2)}) collective-permute-start(f32[128,128]{1,0:T(8,128)S(1)} %get-tuple-element.36), channel_id=1, source_target_pairs={{0,16},{16,32},{32,48},{48,0},{1,17},{17,33},{33,49},{49,1},{2,18}... | collective-permute-start | bytes 196616 | tf_op jit(solution)/shard_map/ppermute | solution.py:393
  152.0 7.7 %collective-permute-start.7 = (f32[128,128]{1,0:T(8,128)S(1)}, f32[128,128]{1,0:T(8,128)S(1)}, u32[]{:S(2)}, u32[]{:S(2)}) collective-permute-start(f32[128,128]{1,0:T(8,128)S(1)} %get-tuple-element.37), channel_id=1, source_target_pairs={{0,32},{16,48},{32,0},{48,16},{1,33},{17,49},{33,1},{49,17},{2,34}... | collective-permute-start | bytes 196616 | tf_op jit(solution)/shard_map/ppermute | solution.py:393
  155.8 4.3 %collective-permute-start.8 = (f32[128,128]{1,0:T(8,128)S(1)}, f32[128,128]{1,0:T(8,128)S(1)}, u32[]{:S(2)}, u32[]{:S(2)}) collective-permute-start(f32[128,128]{1,0:T(8,128)S(1)} %get-tuple-element.38), channel_id=1, source_target_pairs={{0,48},{16,0},{32,16},{48,32},{1,49},{17,1},{33,17},{49,33},{2,50}... | collective-permute-start | bytes 196616 | tf_op jit(solution)/shard_map/ppermute | solution.py:393
  160.1 7.0 %collective-permute-start.11 = (f32[128,128]{1,0:T(8,128)S(1)}, f32[128,128]{1,0:T(8,128)S(1)}, u32[]{:S(2)}, u32[]{:S(2)}) collective-permute-start(f32[128,128]{1,0:T(8,128)S(1)} %add_add_fusion.1.refs_0_), channel_id=1, source_target_pairs={{0,48},{16,0},{32,16},{48,32},{1,49},{17,1},{33,17},{49,33},{2,50}... | collective-permute-start | bytes 196616 | tf_op jit(solution)/shard_map/ppermute | solution.py:393
  163.4 7.5 %collective-permute-start.10 = (f32[128,128]{1,0:T(8,128)S(1)}, f32[128,128]{1,0:T(8,128)S(1)}, u32[]{:S(2)}, u32[]{:S(2)}) collective-permute-start(f32[128,128]{1,0:T(8,128)S(1)} %add_add_fusion.1.refs_0_), channel_id=1, source_target_pairs={{0,32},{16,48},{32,0},{48,16},{1,33},{17,49},{33,1},{49,17},{2,34}... | collective-permute-start | bytes 196616 | tf_op jit(solution)/shard_map/ppermute | solution.py:393
  167.1 5.2 %collective-permute-start.9 = (f32[128,128]{1,0:T(8,128)S(1)}, f32[128,128]{1,0:T(8,128)S(1)}, u32[]{:S(2)}, u32[]{:S(2)}) collective-permute-start(f32[128,128]{1,0:T(8,128)S(1)} %add_add_fusion.1.refs_0_), channel_id=1, source_target_pairs={{0,16},{16,32},{32,48},{48,0},{1,17},{17,33},{33,49},{49,1},{2,18}... | collective-permute-start | bytes 196616 | tf_op jit(solution)/shard_map/ppermute | solution.py:393
  182.9 1.3 copy-start.7
  184.3 1.4 copy-start.2
  185.6 14.2 %copy-start.17 = (f32[1024,128]{1,0:T(8,128)S(1)}, f32[1024,128]{1,0:T(8,128)}, u32[]{:S(2)}) copy-start(f32[1024,128]{1,0:T(8,128)} %copy-done.16) | copy-start | bytes 1572868
  185.6 14.2 %copy-start.19 = (bf16[1024,256]{1,0:T(8,128)(2,1)S(1)}, bf16[1024,256]{1,0:T(8,128)(2,1)}, u32[]{:S(2)}) copy-start(bf16[1024,256]{1,0:T(8,128)(2,1)} %copy-done.18) | copy-start | bytes 1572868
  185.6 69.9 %all-to-all-start.3 = ((f32[64,64,128]{2,1,0:T(8,128)}), f32[64,64,128]{2,1,0:T(8,128)S(1)}, u32[]{:S(2)}, u32[]{:S(2)}) async-start(f32[64,64,128]{2,1,0:T(8,128)} %bitcast.71), calls=%async_computation.3 | async-start | bytes 4194304 | tf_op jit(solution)/shard_map/all_to_all | solution.py:389
  199.9 1.6 copy-start.3
  201.4 1.0 copy-start.21
  202.5 41.1 %copy-start.4 = (f32[64,64,128]{2,1,0:T(8,128)S(1)}, f32[64,64,128]{2,1,0:T(8,128)}, u32[]{:S(2)}) copy-start(f32[64,64,128]{2,1,0:T(8,128)} %copy-done.2) | copy-start | bytes 6291460
  202.5 41.1 %copy-start.13 = (bf16[1024,1024]{1,0:T(8,128)(2,1)S(1)}, bf16[1024,1024]{1,0:T(8,128)(2,1)}, u32[]{:S(2)}) copy-start(bf16[1024,1024]{1,0:T(8,128)(2,1)} %copy-done.12) | copy-start | bytes 6291460
  202.5 41.1 %copy-start.15 = (bf16[1024,1024]{1,0:T(8,128)(2,1)S(1)}, bf16[1024,1024]{1,0:T(8,128)(2,1)}, u32[]{:S(2)}) copy-start(bf16[1024,1024]{1,0:T(8,128)(2,1)} %copy-done.14) | copy-start | bytes 6291460
  202.5 41.1 %copy-start.23 = (bf16[64,1024]{1,0:T(8,128)(2,1)S(1)}, bf16[64,1024]{1,0:T(8,128)(2,1)}, u32[]{:S(2)}) copy-start(bf16[64,1024]{1,0:T(8,128)(2,1)} %copy-done.22) | copy-start | bytes 393220
  202.5 41.1 %copy-start.25 = (f32[16,1024]{1,0:T(8,128)S(1)}, f32[16,1024]{1,0:T(8,128)}, u32[]{:S(2)}) copy-start(f32[16,1024]{1,0:T(8,128)} %copy-done.24) | copy-start | bytes 196612
  211.8 14.1 %collective-permute-start.12 = (f32[128,128]{1,0:T(8,128)S(1)}, f32[128,128]{1,0:T(8,128)S(1)}, u32[]{:S(2)}, u32[]{:S(2)}) collective-permute-start(f32[128,128]{1,0:T(8,128)S(1)} %get-tuple-element.46), channel_id=1, source_target_pairs={{0,16},{16,32},{32,48},{48,0},{1,17},{17,33},{33,49},{49,1},{2,18}... | collective-permute-start | bytes 196616 | tf_op jit(solution)/shard_map/ppermute | solution.py:393
  211.9 19.8 %collective-permute-start.13 = (f32[128,128]{1,0:T(8,128)S(1)}, f32[128,128]{1,0:T(8,128)S(1)}, u32[]{:S(2)}, u32[]{:S(2)}) collective-permute-start(f32[128,128]{1,0:T(8,128)S(1)} %get-tuple-element.47), channel_id=1, source_target_pairs={{0,32},{16,48},{32,0},{48,16},{1,33},{17,49},{33,1},{49,17},{2,34}... | collective-permute-start | bytes 196616 | tf_op jit(solution)/shard_map/ppermute | solution.py:393
  215.0 16.6 %collective-permute-start.14 = (f32[128,128]{1,0:T(8,128)S(1)}, f32[128,128]{1,0:T(8,128)S(1)}, u32[]{:S(2)}, u32[]{:S(2)}) collective-permute-start(f32[128,128]{1,0:T(8,128)S(1)} %get-tuple-element.48), channel_id=1, source_target_pairs={{0,48},{16,0},{32,16},{48,32},{1,49},{17,1},{33,17},{49,33},{2,50}... | collective-permute-start | bytes 196616 | tf_op jit(solution)/shard_map/ppermute | solution.py:393
  231.7 4.7 %collective-permute-start.17 = (f32[128,128]{1,0:T(8,128)S(1)}, f32[128,128]{1,0:T(8,128)S(1)}, u32[]{:S(2)}, u32[]{:S(2)}) collective-permute-start(f32[128,128]{1,0:T(8,128)S(1)} %add_add_fusion.refs_0_), channel_id=1, source_target_pairs={{0,48},{16,0},{32,16},{48,32},{1,49},{17,1},{33,17},{49,33},{2,50}... | collective-permute-start | bytes 196616 | tf_op jit(solution)/shard_map/ppermute | solution.py:393
  231.8 7.2 %collective-permute-start.16 = (f32[128,128]{1,0:T(8,128)S(1)}, f32[128,128]{1,0:T(8,128)S(1)}, u32[]{:S(2)}, u32[]{:S(2)}) collective-permute-start(f32[128,128]{1,0:T(8,128)S(1)} %add_add_fusion.refs_0_), channel_id=1, source_target_pairs={{0,32},{16,48},{32,0},{48,16},{1,33},{17,49},{33,1},{49,17},{2,34}... | collective-permute-start | bytes 196616 | tf_op jit(solution)/shard_map/ppermute | solution.py:393
  234.1 9.4 %collective-permute-start.15 = (f32[128,128]{1,0:T(8,128)S(1)}, f32[128,128]{1,0:T(8,128)S(1)}, u32[]{:S(2)}, u32[]{:S(2)}) collective-permute-start(f32[128,128]{1,0:T(8,128)S(1)} %add_add_fusion.refs_0_), channel_id=1, source_target_pairs={{0,16},{16,32},{32,48},{48,0},{1,17},{17,33},{33,49},{49,1},{2,18}... | collective-permute-start | bytes 196616 | tf_op jit(solution)/shard_map/ppermute | solution.py:393
  254.2 1.3 copy-start.8

commit v2 on v1

--- a/solution.py
+++ b/solution.py
@@ -17,8 +17,11 @@
 NOBS = BATCH_OBS * BATCHES
 
 ALL = ("y", "h", "l", "c", "x")
-PEERS = ("y", "l", "c", "x")
+PEERS = ("c", "y", "l", "x")
+CHIPS = ("y", "l", "x")
 GROUP = 64
+CORES = 2
+GROUP_CHIPS = GROUP // CORES
 SUMS = 4
 RESIDUES = 16
 SLICES = 4
@@ -157,18 +160,22 @@
 
 
 def observation_kernel(
-    position_ref, plan_ref, facts_ref, gathered_ref, masks_ref,
+    position_ref, plan_ref, facts_ref, own_ref, other_ref,
     anomalies_high_ref, anomalies_low_ref, increments_high_ref, increments_low_ref,
     links_high_ref, links_low_ref, column_facts_ref, row_facts_ref,
     ensemble_ref, increments_ref, one_hot_ref, facts_scratch, in_columns_ref,
 ):
+    core = position_ref[2]
     for d in range(SUMS):
-        for g in range(NOBS // LANES):
-            ensemble_ref[d * GROUP : (d + 1) * GROUP, g * LANES : (g + 1) * LANES] = gathered_ref[
-                pl.ds(d * 8 + g, GROUP, stride=40), :
-            ]
+        for gathered_ref, start in ((own_ref, core), (other_ref, 1 - core)):
+            rows = pl.ds(pl.multiple_of(d * GROUP + start * GROUP_CHIPS, GROUP_CHIPS), GROUP_CHIPS)
+            for g in range(NOBS // LANES):
+                ensemble_ref[rows, g * LANES : (g + 1) * LANES] = gathered_ref[
+                    pl.ds(d * 8 + g, GROUP_CHIPS, stride=40), :
+                ]
     for g in range(NOBS // LANES):
-        facts_scratch[0:16, g * LANES : (g + 1) * LANES] = masks_ref[pl.ds(g, 16, stride=8), :]
+        rows = pl.ds((g // 4) * 40 + 32 + g % 4, 16, stride=80)
+        facts_scratch[0:16, g * LANES : (g + 1) * LANES] = own_ref[rows, :] + other_ref[rows, :]
     facts_scratch[16:24, :] = facts_ref[...]
     facts_scratch[24:128, :] = jnp.zeros((104, NOBS), f32)
     source = lax.broadcasted_iota(i32, (NOBS, NOBS), 0)
@@ -242,7 +249,7 @@
             ensemble_ref[:, after] = later + accurate_dot(increments, covariance * masks * gain_column)
 
 
-def observations(position, plan, facts, gathered, masks):
+def observations(position, plan, facts, own, other):
     wide = struct((NOBS, 4 * GROUP), bf16)
     narrow = struct((GROUP, NOBS), bf16)
     links = struct((NOBS, NOBS), bf16)
@@ -261,7 +268,7 @@
         compiler_params=kernel_params(40),
         cost_estimate=pl.CostEstimate(flops=12 * 10**9, bytes_accessed=8 * 2**20, transcendentals=10**5),
         name="observations",
-    )(position, plan, facts, gathered, masks)
+    )(position, plan, facts, own, other)
 
 
 def half_of(column_facts, second):
@@ -385,8 +392,8 @@
     return out.reshape(GROUP, PAIRS, LANES)
 
 
-def exchange(value):
-    return lax.all_to_all(value, PEERS, 0, 0, tiled=True)
+def exchange(value, axes=PEERS):
+    return lax.all_to_all(value, axes, 0, 0, tiled=True)
 
 
 def passed_along(value, by):
@@ -401,8 +408,8 @@
 
 
 def shards(state, locations, tile_mask, plan, obs_value, obs_error):
-    group_index = lax.axis_index(PEERS)
-    position = jnp.stack([group_index // SLICES, lax.axis_index("h")]).astype(i32)
+    residue = lax.axis_index(PEERS) // SLICES
+    position = jnp.stack([residue, lax.axis_index("h"), lax.axis_index("c")]).astype(i32)
     rows = state.reshape(ROWS, LANES)
 
     tiles_here = tile_mask.shape[0]
@@ -412,41 +419,46 @@
     masks = jnp.zeros((16, NOBS), i32)
     for i in range(tiles_here):
         masks = masks + jnp.where((local == i) & (nth < WINDOW), tile_mask[i][None, :], 0)
-    masks = exchange(masks.astype(f32).reshape(GROUP, 2, LANES)).sum(axis=0)
+    masks = exchange(masks.astype(f32).reshape(GROUP_CHIPS, 4, LANES), CHIPS).sum(axis=0)
 
     columns = own_columns(plan, locations, rows)
+    mine = jnp.concatenate([columns, masks], axis=0)
+    all_four = [mine] + [passed_along(mine, by) for by in range(1, SUMS)]
     payload = jnp.concatenate(
-        [columns, *(passed_along(columns, by) for by in range(1, SUMS)), masks, jnp.zeros((6, LANES), f32)], axis=0
+        [*(each[0:8] for each in all_four), sum(each[8:12] for each in all_four), jnp.zeros((4, LANES), f32)], axis=0
     )
-    gathered = exchange(jnp.broadcast_to(payload[None], (GROUP, 40, LANES)))
-
     first, second = spread_out(rows)
-    first, gathered = lax.optimization_barrier((first, gathered))
+    first, _ = lax.optimization_barrier((first, masks))
     first = exchange(first)
-
-    all_masks = gathered[:, 32:34, :]
-    all_masks = all_masks + sum(passed_along(all_masks, by) for by in range(1, SUMS))
+    payload, first = lax.optimization_barrier((payload, first))
+    gathered = exchange(jnp.broadcast_to(payload[None], (GROUP_CHIPS, 40, LANES)), CHIPS)
+    second, gathered = lax.optimization_barrier((second, gathered))
+    second = exchange(second)
+
+    other = lax.ppermute(gathered, "c", [(0, 1), (1, 0)])
     facts = jnp.concatenate(
         [tiles.astype(f32)[None], obs_value[None], obs_error[None], jnp.zeros((5, NOBS), f32)], axis=0
     )
     (anomalies_high, anomalies_low, increments_high, increments_low, links_high, links_low, column_facts, row_facts) = (
         observations(
-            position, plan[None], facts, gathered.reshape(GROUP * 40, LANES), all_masks.reshape(2 * GROUP, LANES)
+            position, plan[None], facts, gathered.reshape(-1, LANES), other.reshape(-1, LANES)
         )
     )
 
-    first, second = lax.optimization_barrier((first, second))
-    second = exchange(second)
-
-    def assimilated(is_second, block):
-        parts = covariances(is_second, position, block, anomalies_high, anomalies_low, column_facts)
+    def covariance_parts(is_second, block):
+        return covariances(is_second, position, block, anomalies_high, anomalies_low, column_facts)
+
+    def update(is_second, sums, block):
         return updated(
-            is_second, position, summed(parts), block,
+            is_second, position, sums, block,
             increments_high, increments_low, links_high, links_low, column_facts, row_facts,
         )
 
-    first = exchange(assimilated(False, first))
-    second = exchange(assimilated(True, second))
+    first_sums = summed(covariance_parts(False, first))
+    second_parts = covariance_parts(True, second)
+    first_sums, second_parts = lax.optimization_barrier((first_sums, second_parts))
+    first = exchange(update(False, first_sums, first))
+    second = exchange(update(True, summed(second_parts), second))
     return collect(first, second).reshape(state.shape)
 
 

time: 301 us -> 268 us (0.89)
  waiting for transfers between devices: 68.3 us -> 52.2 us
  blocking collectives: 72.4 us -> 56.9 us
  starting transfers between devices: 78 us -> 72.4 us
  local copies, waits for them, and re-layouts: 16.4 us -> 20.8 us
    all_to_all x2, blocking collectives: 72.4 us -> 56.9 us  [exchange(): return lax.all_to_all(value, axes, 0, 0, tiled=True)]
    all_to_all x4, waiting for transfers between devices: 11.6 us -> 0.01 us  [exchange(): return lax.all_to_all(value, axes, 0, 0, tiled=True)]
    ppermute x18 -> x15, waiting for transfers between devices: 56.7 us -> 50.7 us  [passed_along(): return lax.ppermute(value, 'h', [(i, (i + by) % SUMS) for i in range(SUMS)])]
    unnamed x56 -> x64, local copies, waits for them, and re-layouts: 13.8 us -> 19.3 us
    all_to_all x4, starting transfers between devices: 40.3 us -> 35.2 us  [exchange(): return lax.all_to_all(value, axes, 0, 0, tiled=True)]
    ppermute x18 -> x15, starting transfers between devices: 37.7 us -> 36.6 us  [passed_along(): return lax.ppermute(value, 'h', [(i, (i + by) % SUMS) for i in range(SUMS)])]
  transfers between devices with their start and end apart: 22 -> 20, of which waited for: 12 -> 6; matrix products, arithmetic and copies ran while one was open for 0% -> 0% of each run, Pallas kernels for 19% -> 17%
where the time goes in v2:
time: 268 us; the launch traced here: 267 us
  starting transfers between devices  72.4 us (27%)
  Pallas kernels  62.5 us (23%)
  blocking collectives  56.9 us (21%)
  waiting for transfers between devices  52.2 us (19%)
  local copies, waits for them, and re-layouts  20.8 us (8%)
    all_to_all x2, blocking collectives, exchange(): return lax.all_to_all(value, axes, 0, 0, tiled=True)  56.9 us
    ppermute x15, waiting for transfers between devices, passed_along(): return lax.ppermute(value, 'h', [(i, (i + by) % SUMS) for i in range(SUMS)])  50.7 us
    ppermute x15, starting transfers between devices, passed_along(): return lax.ppermute(value, 'h', [(i, (i + by) % SUMS) for i in range(SUMS)])  36.6 us
    all_to_all x4, starting transfers between devices, exchange(): return lax.all_to_all(value, axes, 0, 0, tiled=True)  35.2 us
    pallas_call x2, Pallas kernels, updated(): pl.pallas_call(functools.partial(update_kernel, second), out_shape=struct...  21.2 us
    unnamed x64, local copies, waits for them, and re-layouts  19.3 us
    pallas_call x2, Pallas kernels, covariances(): pl.pallas_call(functools.partial(covariance_kernel, second), out_shape=(s...  18.5 us
    pallas_call x1, Pallas kernels, observations(): pl.pallas_call(observation_kernel, out_shape=(wide, wide, narrow, narrow,...  8.84 us
  transfers between devices with their start and end apart: 20, of which 6 were waited for; matrix products, arithmetic and copies ran while one was open for 0% of the time, Pallas kernels for 17%

profile of v2, /device:TPU:1, one launch (start us, length us, event | category | flops | bytes accessed | tf_op | source)
XLA Modules:
  0.0 267.1 jit_solution(17175512124087396024)
XLA Ops:
  0.0 0.1 and.130
  0.1 0.1 and.131
  0.2 0.1 add.109
  0.3 0.7 fusion.28
  1.0 1.1 fusion.29
  2.1 0.9 fusion.1
  3.0 9.2 %all-to-all-start = ((f32[32,4,128]{2,1,0:T(4,128)}), f32[32,4,128]{2,1,0:T(4,128)S(1)}, u32[]{:S(2)}, u32[]{:S(2)}) async-start(f32[32,4,128]{2,1,0:T(4,128)} %fusion.1), calls=%async_computation | async-start | bytes 131072 | tf_op jit(solution)/shard_map/all_to_all | solution.py:396
  12.2 0.0 copy-start
  12.2 2.2 copy-done
  14.4 4.5 %spread_out.1 = (f32[64,64,128]{2,1,0:T(8,128)S(1)}, f32[64,64,128]{2,1,0:T(8,128)S(1)}) custom-call(f32[8192,128]{1,0:T(8,128)S(1)} %bitcast.124), custom_call_target="tpu_custom_call" | custom-call | flops 1000000 | bytes 8388608 | tf_op jit(solution)/shard_map/spread_out/pallas_call | solution.py:126
  19.0 1.3 copy-done.7
  20.3 1.3 copy-done.9
  21.6 0.0 all-to-all-done
  21.7 0.0 copy-start.12
  21.7 9.7 %all-to-all-start.1 = ((f32[64,64,128]{2,1,0:T(8,128)}), f32[64,64,128]{2,1,0:T(8,128)S(1)}, u32[]{:S(2)}, u32[]{:S(2)}) async-start(f32[64,64,128]{2,1,0:T(8,128)} %copy-done.9), calls=%async_computation.1 | async-start | bytes 4194304 | tf_op jit(solution)/shard_map/all_to_all | solution.py:396
  31.4 0.0 copy-start.1
  31.4 2.2 copy-done.1
  33.6 3.1 %own_columns.1 = f32[8,128]{1,0:T(8,128)S(1)} custom-call(s32[1024]{0:T(1024)S(1)} %copy-done.12, s32[1024]{0:T(1024)S(1)} %copy-done.11, f32[8192,128]{1,0:T(8,128)S(1)} %bitcast.125), custom_call_target="tpu_custom_call" | custom-call | flops 1000000 | bytes 8388608 | tf_op jit(solution)/shard_map/own_columns/pallas_call | solution.py:99
  36.7 5.2 %collective-permute-start.2 = (f32[12,128]{1,0:T(8,128)S(1)}, f32[12,128]{1,0:T(8,128)S(1)}, u32[]{:S(2)}, u32[]{:S(2)}) collective-permute-start(f32[12,128]{1,0:T(8,128)S(1)} %pad_maximum_fusion), channel_id=1, source_target_pairs={{0,48},{16,0},{32,16},{48,32},{1,49},{17,1},{33,17},{49,33},{2,50}... | collective-permute-start | bytes 18440 | tf_op jit(solution)/shard_map/ppermute | solution.py:400
  41.8 1.2 collective-permute-start.1
  43.0 2.1 collective-permute-start
  45.1 15.6 %collective-permute-done.1 = f32[12,128]{1,0:T(8,128)S(1)} collective-permute-done((f32[12,128]{1,0:T(8,128)S(1)}, f32[12,128]{1,0:T(8,128)S(1)}, u32[]{:S(2)}, u32[]{:S(2)}) %collective-permute-start.1) | collective-permute-done | bytes 6176 | tf_op jit(solution)/shard_map/ppermute | solution.py:400
  60.7 0.0 collective-permute-done
  60.7 0.0 copy-start.4
  60.7 1.3 copy-done.4
  62.1 19.0 %all_to_all.30 = f32[32,40,128]{2,1,0:T(8,128)S(1)} all-to-all(f32[32,40,128]{2,1,0:T(8,128)S(1)} %broadcast_in_dim.140), channel_id=1, replica_groups=mesh['y'=4,'h'=4,'l'=2,'c'=2,'x'=4] {'y','l','x'}, dimensions={0} | all-to-all | bytes 1310720 | tf_op jit(solution)/shard_map/all_to_all | solution.py:396
  81.1 7.8 %all-to-all-start.3 = ((f32[64,64,128]{2,1,0:T(8,128)}), f32[64,64,128]{2,1,0:T(8,128)S(1)}, u32[]{:S(2)}, u32[]{:S(2)}) async-start(f32[64,64,128]{2,1,0:T(8,128)} %copy-done.7), calls=%async_computation.3 | async-start | bytes 4194304 | tf_op jit(solution)/shard_map/all_to_all | solution.py:396
  88.9 0.6 collective-permute-start.3
  89.6 0.1 pad.3.clone
  89.6 0.1 pad_add_fusion.position_ref
  89.7 0.1 maximum_maximum_fusion.facts_ref
  89.8 1.5 collective-permute-done.3
  91.3 8.8 %observations.1 = (bf16[1024,256]{1,0:T(8,128)(2,1)S(1)}, bf16[1024,256]{1,0:T(8,128)(2,1)S(1)}, bf16[64,1024]{1,0:T(8,128)(2,1)S(1)}, bf16[64,1024]{1,0:T(8,128...) custom-call(s32[3]{0:T(128)S(1)} %pad_add_fusion.position_ref, ...), custom_call_target="tpu_custom_call" | custom-call | flops 12000000000 | bytes 8388608 | tf_op jit(solution)/shard_map/observations/pallas_call | solution.py:256
  100.2 9.2 %covariances.2 = (f32[128,128]{1,0:T(8,128)S(1)}, f32[128,128]{1,0:T(8,128)S(1)}, f32[128,128]{1,0:T(8,128)S(1)}, f32[128,128]{1,0:T(8,128)S(1)}) custom-call(s32[3]{0:T(128)S(1)} %pad_add_fusion.position_ref, f32[4096,128]{1,0:T(8,128)S(1)} %bitcast.128, bf16[1024,256]{1,0:T(8,128)(2,1)S(1)} %get-tuple-element.42.anomalies_high_ref, ...), custom_call_target="tpu_custom_call" | custom-call | flops 3000000000 | bytes 4194304 | tf_op jit(solution)/shard_map/covariances/pallas_call | solution.py:312
  109.5 1.4 collective-permute-start.4
  111.0 1.1 collective-permute-start.5
  112.1 2.4 collective-permute-start.6
  114.4 0.7 collective-permute-done.4
  115.1 3.0 %collective-permute-done.5 = f32[128,128]{1,0:T(8,128)S(1)} collective-permute-done((f32[128,128]{1,0:T(8,128)S(1)}, f32[128,128]{1,0:T(8,128)S(1)}, u32[]{:S(2)}, u32[]{:S(2)}) %collective-permute-start.5) | collective-permute-done | bytes 65568 | tf_op jit(solution)/shard_map/ppermute | solution.py:400
  118.1 5.1 %collective-permute-start.9 = (f32[128,128]{1,0:T(8,128)S(1)}, f32[128,128]{1,0:T(8,128)S(1)}, u32[]{:S(2)}, u32[]{:S(2)}) collective-permute-start(f32[128,128]{1,0:T(8,128)S(1)} %add_add_fusion.1.refs_0_), channel_id=1, source_target_pairs={{0,48},{16,0},{32,16},{48,32},{1,49},{17,1},{33,17},{49,33},{2,50}... | collective-permute-start | bytes 196616 | tf_op jit(solution)/shard_map/ppermute | solution.py:400
  123.3 4.5 %collective-permute-start.8 = (f32[128,128]{1,0:T(8,128)S(1)}, f32[128,128]{1,0:T(8,128)S(1)}, u32[]{:S(2)}, u32[]{:S(2)}) collective-permute-start(f32[128,128]{1,0:T(8,128)S(1)} %add_add_fusion.1.refs_0_), channel_id=1, source_target_pairs={{0,32},{16,48},{32,0},{48,16},{1,33},{17,49},{33,1},{49,17},{2,34}... | collective-permute-start | bytes 196616 | tf_op jit(solution)/shard_map/ppermute | solution.py:400
  127.8 0.0 collective-permute-start.7
  127.8 1.4 copy-done.20
  129.2 1.0 copy-done.23
  130.2 1.0 copy-done.25
  131.3 9.2 %covariances.3 = (f32[128,128]{1,0:T(8,128)S(1)}, f32[128,128]{1,0:T(8,128)S(1)}, f32[128,128]{1,0:T(8,128)S(1)}, f32[128,128]{1,0:T(8,128)S(1)}) custom-call(s32[3]{0:T(128)S(1)} %pad_add_fusion.position_ref, f32[4096,128]{1,0:T(8,128)S(1)} %bitcast.126, bf16[1024,256]{1,0:T(8,128)(2,1)S(1)} %copy-done.23, bf16[1024,256]{1,0:T(8,128)(2,1)S(1)} %copy-done.25, ...), custom_call_target="tpu_custom_call" | custom-call | flops 3000000000 | bytes 4194304 | tf_op jit(solution)/shard_map/covariances/pallas_call | solution.py:312
  140.6 10.6 %updated.2 = f32[4096,128]{1,0:T(8,128)S(1)} custom-call(s32[3]{0:T(128)S(1)} %pad_add_fusion.position_ref, f32[128,128]{1,0:T(8,128)S(1)} %add_add_fusion.1.refs_0_, f32[128,128]{1,0:T(8,128)S(1)} %collective-permute-done.7.refs_1_, f32[128,128]{1,0:T(8,128)S(1)} %collective-permute-done.8.refs_2_, f32[128,128]{1,0:T(8,128)S(1)} %collective-permute-done.9.refs_3_, ...), custom_call_target="tpu_custom_call" | custom-call | flops 4000000000 | bytes 8388608 | tf_op jit(solution)/shard_map/updated/pallas_call | solution.py:375
  151.3 0.0 copy-start.8
  151.3 1.3 copy-done.8
  152.6 8.5 %all-to-all-start.4 = ((f32[64,64,128]{2,1,0:T(8,128)}), f32[64,64,128]{2,1,0:T(8,128)S(1)}, u32[]{:S(2)}, u32[]{:S(2)}) async-start(f32[64,64,128]{2,1,0:T(8,128)} %bitcast.130), calls=%async_computation.4 | async-start | bytes 4194304 | tf_op jit(solution)/shard_map/all_to_all | solution.py:396
  161.1 3.4 %collective-permute-start.10 = (f32[128,128]{1,0:T(8,128)S(1)}, f32[128,128]{1,0:T(8,128)S(1)}, u32[]{:S(2)}, u32[]{:S(2)}) collective-permute-start(f32[128,128]{1,0:T(8,128)S(1)} %get-tuple-element.64), channel_id=1, source_target_pairs={{0,16},{16,32},{32,48},{48,0},{1,17},{17,33},{33,49},{49,1},{2,18}... | collective-permute-start | bytes 196616 | tf_op jit(solution)/shard_map/ppermute | solution.py:400
  164.4 2.7 collective-permute-start.11
  167.1 0.7 collective-permute-start.12
  167.8 24.8 %collective-permute-done.10 = f32[128,128]{1,0:T(8,128)S(1)} collective-permute-done((f32[128,128]{1,0:T(8,128)S(1)}, f32[128,128]{1,0:T(8,128)S(1)}, u32[]{:S(2)}, u32[]{:S(2)}) %collective-permute-start.10) | collective-permute-done | bytes 65568 | tf_op jit(solution)/shard_map/ppermute | solution.py:400
  192.7 4.2 %collective-permute-start.15 = (f32[128,128]{1,0:T(8,128)S(1)}, f32[128,128]{1,0:T(8,128)S(1)}, u32[]{:S(2)}, u32[]{:S(2)}) collective-permute-start(f32[128,128]{1,0:T(8,128)S(1)} %add_add_fusion.refs_0_), channel_id=1, source_target_pairs={{0,48},{16,0},{32,16},{48,32},{1,49},{17,1},{33,17},{49,33},{2,50}... | collective-permute-start | bytes 196616 | tf_op jit(solution)/shard_map/ppermute | solution.py:400
  196.9 2.7 collective-permute-start.14
  199.5 6.6 %collective-permute-done.14.refs_2_ = f32[128,128]{1,0:T(8,128)S(1)} collective-permute-done((f32[128,128]{1,0:T(8,128)S(1)}, f32[128,128]{1,0:T(8,128)S(1)}, u32[]{:S(2)}, u32[]{:S(2)}) %collective-permute-start.14) | collective-permute-done | bytes 65568 | tf_op jit(solution)/shard_map/ppermute | solution.py:400
  206.2 1.6 copy-done.3
  207.7 1.6 copy-done.15
  209.3 1.6 copy-done.18
  210.9 10.6 %updated.3 = f32[4096,128]{1,0:T(8,128)S(1)} custom-call(s32[3]{0:T(128)S(1)} %pad_add_fusion.position_ref, f32[128,128]{1,0:T(8,128)S(1)} %add_add_fusion.refs_0_, f32[128,128]{1,0:T(8,128)S(1)} %collective-permute-done.13.refs_1_, f32[128,128]{1,0:T(8,128)S(1)} %collective-permute-done.14.refs_2_, f32[128,128]{1,0:T(8,128)S(1)} %collective-permute-done.15.refs_3_, ...), custom_call_target="tpu_custom_call" | custom-call | flops 4000000000 | bytes 8388608 | tf_op jit(solution)/shard_map/updated/pallas_call | solution.py:375
  221.6 1.3 copy-done.10
  222.9 37.9 %all_to_all.31.second_ref = f32[64,64,128]{2,1,0:T(8,128)S(1)} all-to-all(f32[64,64,128]{2,1,0:T(8,128)} %bitcast.131), channel_id=1, replica_groups=mesh['y'=4,'h'=4,'l'=2,'c'=2,'x'=4] {'c','y','l','x'}, dimensions={0} | all-to-all | bytes 4194304 | tf_op jit(solution)/shard_map/all_to_all | solution.py:396
  260.8 6.3 %collect.1 = f32[8192,128]{1,0:T(8,128)} custom-call(f32[64,64,128]{2,1,0:T(8,128)S(1)} %all-to-all-done.4.first_ref, f32[64,64,128]{2,1,0:T(8,128)S(1)} %all_to_all.31.second_ref), custom_call_target="tpu_custom_call" | custom-call | flops 1000000 | bytes 8388608 | tf_op jit(solution)/shard_map/collect/pallas_call | solution.py:151
  (73 shorter events, 0.3 us)
Async XLA Ops:
  3.0 18.6 %all-to-all-start = ((f32[32,4,128]{2,1,0:T(4,128)}), f32[32,4,128]{2,1,0:T(4,128)S(1)}, u32[]{:S(2)}, u32[]{:S(2)}) async-start(f32[32,4,128]{2,1,0:T(4,128)} %fusion.1), calls=%async_computation | async-start | bytes 131072 | tf_op jit(solution)/shard_map/all_to_all | solution.py:396
  12.2 2.2 copy-start
  19.0 1.3 copy-start.7
  20.3 1.3 copy-start.9
  21.7 9.7 %copy-start.11 = (s32[1024]{0:T(1024)S(1)}, s32[1024]{0:T(1024)}, u32[]{:S(2)}) copy-start(s32[1024]{0:T(1024)} %locations_ref.1) | copy-start | bytes 12292
  21.7 9.7 %copy-start.12 = (s32[1024]{0:T(1024)S(1)}, s32[1024]{0:T(1024)}, u32[]{:S(2)}) copy-start(s32[1024]{0:T(1024)} %plan_ref.1) | copy-start | bytes 12292
  21.7 39.0 %all-to-all-start.1 = ((f32[64,64,128]{2,1,0:T(8,128)}), f32[64,64,128]{2,1,0:T(8,128)S(1)}, u32[]{:S(2)}, u32[]{:S(2)}) async-start(f32[64,64,128]{2,1,0:T(8,128)} %copy-done.9), calls=%async_computation.1 | async-start | bytes 4194304 | tf_op jit(solution)/shard_map/all_to_all | solution.py:396
  31.4 2.2 copy-start.1
  36.7 8.5 %collective-permute-start.2 = (f32[12,128]{1,0:T(8,128)S(1)}, f32[12,128]{1,0:T(8,128)S(1)}, u32[]{:S(2)}, u32[]{:S(2)}) collective-permute-start(f32[12,128]{1,0:T(8,128)S(1)} %pad_maximum_fusion), channel_id=1, source_target_pairs={{0,48},{16,0},{32,16},{48,32},{1,49},{17,1},{33,17},{49,33},{2,50}... | collective-permute-start | bytes 18440 | tf_op jit(solution)/shard_map/ppermute | solution.py:400
  41.8 18.8 %collective-permute-start.1 = (f32[12,128]{1,0:T(8,128)S(1)}, f32[12,128]{1,0:T(8,128)S(1)}, u32[]{:S(2)}, u32[]{:S(2)}) collective-permute-start(f32[12,128]{1,0:T(8,128)S(1)} %pad_maximum_fusion), channel_id=1, source_target_pairs={{0,32},{16,48},{32,0},{48,16},{1,33},{17,49},{33,1},{49,17},{2,34}... | collective-permute-start | bytes 18440 | tf_op jit(solution)/shard_map/ppermute | solution.py:400
  43.0 17.7 %collective-permute-start = (f32[12,128]{1,0:T(8,128)S(1)}, f32[12,128]{1,0:T(8,128)S(1)}, u32[]{:S(2)}, u32[]{:S(2)}) collective-permute-start(f32[12,128]{1,0:T(8,128)S(1)} %pad_maximum_fusion), channel_id=1, source_target_pairs={{0,16},{16,32},{32,48},{48,0},{1,17},{17,33},{33,49},{49,1},{2,18}... | collective-permute-start | bytes 18440 | tf_op jit(solution)/shard_map/ppermute | solution.py:400
  60.7 1.3 copy-start.4
  81.1 8.6 %copy-start.30 = (f32[1024]{0:T(1024)S(1)}, f32[1024]{0:T(1024)}, u32[]{:S(2)}) copy-start(f32[1024]{0:T(1024)} %param.11) | copy-start | bytes 12292
  81.1 8.6 %copy-start.31 = (f32[1024]{0:T(1024)S(1)}, f32[1024]{0:T(1024)}, u32[]{:S(2)}) copy-start(f32[1024]{0:T(1024)} %param.10) | copy-start | bytes 12292
  81.1 46.7 %all-to-all-start.3 = ((f32[64,64,128]{2,1,0:T(8,128)}), f32[64,64,128]{2,1,0:T(8,128)S(1)}, u32[]{:S(2)}, u32[]{:S(2)}) async-start(f32[64,64,128]{2,1,0:T(8,128)} %copy-done.7), calls=%async_computation.3 | async-start | bytes 4194304 | tf_op jit(solution)/shard_map/all_to_all | solution.py:396
  88.9 2.4 collective-permute-start.3
  91.3 8.9 %copy-start.5 = (f32[64,64,128]{2,1,0:T(8,128)S(1)}, f32[64,64,128]{2,1,0:T(8,128)}, u32[]{:S(2)}) copy-start(f32[64,64,128]{2,1,0:T(8,128)} %copy-done.4) | copy-start | bytes 6291460
  100.2 9.3 %copy-start.13 = (bf16[1024,1024]{1,0:T(8,128)(2,1)}, bf16[1024,1024]{1,0:T(8,128)(2,1)S(1)}, u32[]{:S(2)}) copy-start(bf16[1024,1024]{1,0:T(8,128)(2,1)S(1)} %get-tuple-element.60.refs_7_) | copy-start | bytes 6291460
  100.2 9.3 %copy-start.16 = (bf16[1024,1024]{1,0:T(8,128)(2,1)}, bf16[1024,1024]{1,0:T(8,128)(2,1)S(1)}, u32[]{:S(2)}) copy-start(bf16[1024,1024]{1,0:T(8,128)(2,1)S(1)} %get-tuple-element.61.refs_8_) | copy-start | bytes 6291460
  100.2 9.3 %copy-start.19 = (f32[1024,128]{1,0:T(8,128)}, f32[1024,128]{1,0:T(8,128)S(1)}, u32[]{:S(2)}) copy-start(f32[1024,128]{1,0:T(8,128)S(1)} %get-tuple-element.44.facts_ref.refs_9_) | copy-start | bytes 1572868
  100.2 9.3 %copy-start.22 = (bf16[1024,256]{1,0:T(8,128)(2,1)}, bf16[1024,256]{1,0:T(8,128)(2,1)S(1)}, u32[]{:S(2)}) copy-start(bf16[1024,256]{1,0:T(8,128)(2,1)S(1)} %get-tuple-element.42.anomalies_high_ref) | copy-start | bytes 1572868
  100.2 9.3 %copy-start.24 = (bf16[1024,256]{1,0:T(8,128)(2,1)}, bf16[1024,256]{1,0:T(8,128)(2,1)S(1)}, u32[]{:S(2)}) copy-start(bf16[1024,256]{1,0:T(8,128)(2,1)S(1)} %get-tuple-element.43.anomalies_low_ref) | copy-start | bytes 1572868
  100.2 9.3 %copy-start.26 = (bf16[64,1024]{1,0:T(8,128)(2,1)}, bf16[64,1024]{1,0:T(8,128)(2,1)S(1)}, u32[]{:S(2)}) copy-start(bf16[64,1024]{1,0:T(8,128)(2,1)S(1)} %get-tuple-element.59.refs_6_) | copy-start | bytes 393220
  100.2 9.3 %copy-start.28 = (f32[16,1024]{1,0:T(8,128)}, f32[16,1024]{1,0:T(8,128)S(1)}, u32[]{:S(2)}) copy-start(f32[16,1024]{1,0:T(8,128)S(1)} %get-tuple-element.62.refs_10_) | copy-start | bytes 196612
  109.5 5.6 %collective-permute-start.4 = (f32[128,128]{1,0:T(8,128)S(1)}, f32[128,128]{1,0:T(8,128)S(1)}, u32[]{:S(2)}, u32[]{:S(2)}) collective-permute-start(f32[128,128]{1,0:T(8,128)S(1)} %get-tuple-element.46), channel_id=1, source_target_pairs={{0,16},{16,32},{32,48},{48,0},{1,17},{17,33},{33,49},{49,1},{2,18}... | collective-permute-start | bytes 196616 | tf_op jit(solution)/shard_map/ppermute | solution.py:400
  111.0 7.1 %collective-permute-start.5 = (f32[128,128]{1,0:T(8,128)S(1)}, f32[128,128]{1,0:T(8,128)S(1)}, u32[]{:S(2)}, u32[]{:S(2)}) collective-permute-start(f32[128,128]{1,0:T(8,128)S(1)} %get-tuple-element.47), channel_id=1, source_target_pairs={{0,32},{16,48},{32,0},{48,16},{1,33},{17,49},{33,1},{49,17},{2,34}... | collective-permute-start | bytes 196616 | tf_op jit(solution)/shard_map/ppermute | solution.py:400
  112.1 6.1 %collective-permute-start.6 = (f32[128,128]{1,0:T(8,128)S(1)}, f32[128,128]{1,0:T(8,128)S(1)}, u32[]{:S(2)}, u32[]{:S(2)}) collective-permute-start(f32[128,128]{1,0:T(8,128)S(1)} %get-tuple-element.48), channel_id=1, source_target_pairs={{0,48},{16,0},{32,16},{48,32},{1,49},{17,1},{33,17},{49,33},{2,50}... | collective-permute-start | bytes 196616 | tf_op jit(solution)/shard_map/ppermute | solution.py:400
  118.1 22.4 %collective-permute-start.9 = (f32[128,128]{1,0:T(8,128)S(1)}, f32[128,128]{1,0:T(8,128)S(1)}, u32[]{:S(2)}, u32[]{:S(2)}) collective-permute-start(f32[128,128]{1,0:T(8,128)S(1)} %add_add_fusion.1.refs_0_), channel_id=1, source_target_pairs={{0,48},{16,0},{32,16},{48,32},{1,49},{17,1},{33,17},{49,33},{2,50}... | collective-permute-start | bytes 196616 | tf_op jit(solution)/shard_map/ppermute | solution.py:400
  123.3 17.3 %collective-permute-start.8 = (f32[128,128]{1,0:T(8,128)S(1)}, f32[128,128]{1,0:T(8,128)S(1)}, u32[]{:S(2)}, u32[]{:S(2)}) collective-permute-start(f32[128,128]{1,0:T(8,128)S(1)} %add_add_fusion.1.refs_0_), channel_id=1, source_target_pairs={{0,32},{16,48},{32,0},{48,16},{1,33},{17,49},{33,1},{49,17},{2,34}... | collective-permute-start | bytes 196616 | tf_op jit(solution)/shard_map/ppermute | solution.py:400
  127.8 12.8 %collective-permute-start.7 = (f32[128,128]{1,0:T(8,128)S(1)}, f32[128,128]{1,0:T(8,128)S(1)}, u32[]{:S(2)}, u32[]{:S(2)}) collective-permute-start(f32[128,128]{1,0:T(8,128)S(1)} %add_add_fusion.1.refs_0_), channel_id=1, source_target_pairs={{0,16},{16,32},{32,48},{48,0},{1,17},{17,33},{33,49},{49,1},{2,18}... | collective-permute-start | bytes 196616 | tf_op jit(solution)/shard_map/ppermute | solution.py:400
  127.8 12.8 %copy-start.2 = (f32[64,64,128]{2,1,0:T(8,128)}, f32[64,64,128]{2,1,0:T(8,128)S(1)}, u32[]{:S(2)}) copy-start(f32[64,64,128]{2,1,0:T(8,128)S(1)} %all-to-all-done.3) | copy-start | bytes 6291460
  127.8 1.4 copy-start.20
  129.2 1.0 copy-start.23
  130.2 1.0 copy-start.25
  131.3 9.3 %copy-start.6 = (f32[64,64,128]{2,1,0:T(8,128)S(1)}, f32[64,64,128]{2,1,0:T(8,128)}, u32[]{:S(2)}) copy-start(f32[64,64,128]{2,1,0:T(8,128)} %copy-done.4) | copy-start | bytes 6291460
  131.3 9.3 %copy-start.14 = (bf16[1024,1024]{1,0:T(8,128)(2,1)S(1)}, bf16[1024,1024]{1,0:T(8,128)(2,1)}, u32[]{:S(2)}) copy-start(bf16[1024,1024]{1,0:T(8,128)(2,1)} %copy-done.13) | copy-start | bytes 6291460
  131.3 9.3 %copy-start.17 = (bf16[1024,1024]{1,0:T(8,128)(2,1)S(1)}, bf16[1024,1024]{1,0:T(8,128)(2,1)}, u32[]{:S(2)}) copy-start(bf16[1024,1024]{1,0:T(8,128)(2,1)} %copy-done.16) | copy-start | bytes 6291460
  131.3 9.3 %copy-start.21 = (f32[1024,128]{1,0:T(8,128)S(1)}, f32[1024,128]{1,0:T(8,128)}, u32[]{:S(2)}) copy-start(f32[1024,128]{1,0:T(8,128)} %copy-done.19) | copy-start | bytes 1572868
  131.3 9.3 %copy-start.27 = (bf16[64,1024]{1,0:T(8,128)(2,1)S(1)}, bf16[64,1024]{1,0:T(8,128)(2,1)}, u32[]{:S(2)}) copy-start(bf16[64,1024]{1,0:T(8,128)(2,1)} %copy-done.26) | copy-start | bytes 393220
  131.3 9.3 %copy-start.29 = (f32[16,1024]{1,0:T(8,128)S(1)}, f32[16,1024]{1,0:T(8,128)}, u32[]{:S(2)}) copy-start(f32[16,1024]{1,0:T(8,128)} %copy-done.28) | copy-start | bytes 196612
  151.3 1.3 copy-start.8
  152.6 70.3 %all-to-all-start.4 = ((f32[64,64,128]{2,1,0:T(8,128)}), f32[64,64,128]{2,1,0:T(8,128)S(1)}, u32[]{:S(2)}, u32[]{:S(2)}) async-start(f32[64,64,128]{2,1,0:T(8,128)} %bitcast.130), calls=%async_computation.4 | async-start | bytes 4194304 | tf_op jit(solution)/shard_map/all_to_all | solution.py:396
  161.1 31.6 %collective-permute-start.10 = (f32[128,128]{1,0:T(8,128)S(1)}, f32[128,128]{1,0:T(8,128)S(1)}, u32[]{:S(2)}, u32[]{:S(2)}) collective-permute-start(f32[128,128]{1,0:T(8,128)S(1)} %get-tuple-element.64), channel_id=1, source_target_pairs={{0,16},{16,32},{32,48},{48,0},{1,17},{17,33},{33,49},{49,1},{2,18}... | collective-permute-start | bytes 196616 | tf_op jit(solution)/shard_map/ppermute | solution.py:400
  164.4 28.2 %collective-permute-start.11 = (f32[128,128]{1,0:T(8,128)S(1)}, f32[128,128]{1,0:T(8,128)S(1)}, u32[]{:S(2)}, u32[]{:S(2)}) collective-permute-start(f32[128,128]{1,0:T(8,128)S(1)} %get-tuple-element.65), channel_id=1, source_target_pairs={{0,32},{16,48},{32,0},{48,16},{1,33},{17,49},{33,1},{49,17},{2,34}... | collective-permute-start | bytes 196616 | tf_op jit(solution)/shard_map/ppermute | solution.py:400
  167.1 25.6 %collective-permute-start.12 = (f32[128,128]{1,0:T(8,128)S(1)}, f32[128,128]{1,0:T(8,128)S(1)}, u32[]{:S(2)}, u32[]{:S(2)}) collective-permute-start(f32[128,128]{1,0:T(8,128)S(1)} %get-tuple-element.66), channel_id=1, source_target_pairs={{0,48},{16,0},{32,16},{48,32},{1,49},{17,1},{33,17},{49,33},{2,50}... | collective-permute-start | bytes 196616 | tf_op jit(solution)/shard_map/ppermute | solution.py:400
  192.7 6.9 %collective-permute-start.15 = (f32[128,128]{1,0:T(8,128)S(1)}, f32[128,128]{1,0:T(8,128)S(1)}, u32[]{:S(2)}, u32[]{:S(2)}) collective-permute-start(f32[128,128]{1,0:T(8,128)S(1)} %add_add_fusion.refs_0_), channel_id=1, source_target_pairs={{0,48},{16,0},{32,16},{48,32},{1,49},{17,1},{33,17},{49,33},{2,50}... | collective-permute-start | bytes 196616 | tf_op jit(solution)/shard_map/ppermute | solution.py:400
  196.9 9.3 %collective-permute-start.14 = (f32[128,128]{1,0:T(8,128)S(1)}, f32[128,128]{1,0:T(8,128)S(1)}, u32[]{:S(2)}, u32[]{:S(2)}) collective-permute-start(f32[128,128]{1,0:T(8,128)S(1)} %add_add_fusion.refs_0_), channel_id=1, source_target_pairs={{0,32},{16,48},{32,0},{48,16},{1,33},{17,49},{33,1},{49,17},{2,34}... | collective-permute-start | bytes 196616 | tf_op jit(solution)/shard_map/ppermute | solution.py:400
  199.5 6.6 %collective-permute-start.13 = (f32[128,128]{1,0:T(8,128)S(1)}, f32[128,128]{1,0:T(8,128)S(1)}, u32[]{:S(2)}, u32[]{:S(2)}) collective-permute-start(f32[128,128]{1,0:T(8,128)S(1)} %add_add_fusion.refs_0_), channel_id=1, source_target_pairs={{0,16},{16,32},{32,48},{48,0},{1,17},{17,33},{33,49},{49,1},{2,18}... | collective-permute-start | bytes 196616 | tf_op jit(solution)/shard_map/ppermute | solution.py:400
  206.2 1.6 copy-start.3
  207.7 1.6 copy-start.15
  209.3 1.6 copy-start.18
  221.5 1.4 copy-start.10

commit v3 on v2

--- a/solution.py
+++ b/solution.py
@@ -400,10 +400,14 @@
     return lax.ppermute(value, "h", [(i, (i + by) % SUMS) for i in range(SUMS)])
 
 
-def summed(parts):
+def scattered(parts):
     total = parts[0]
     for by in range(1, SUMS):
         total = total + passed_along(parts[by], by)
+    return total
+
+
+def shared(total):
     return (total, *(passed_along(total, by) for by in range(1, SUMS)))
 
 
@@ -454,11 +458,14 @@
             increments_high, increments_low, links_high, links_low, column_facts, row_facts,
         )
 
-    first_sums = summed(covariance_parts(False, first))
+    first_sums = shared(scattered(covariance_parts(False, first)))
     second_parts = covariance_parts(True, second)
     first_sums, second_parts = lax.optimization_barrier((first_sums, second_parts))
-    first = exchange(update(False, first_sums, first))
-    second = exchange(update(True, summed(second_parts), second))
+    first = update(False, first_sums, first)
+    first, second_total = lax.optimization_barrier((first, scattered(second_parts)))
+    second_sums = shared(second_total)
+    first = exchange(first)
+    second = exchange(update(True, second_sums, second))
     return collect(first, second).reshape(state.shape)
 
 

time: 268 us -> 259 us (0.966)
  waiting for transfers between devices: 52.2 us -> 47.4 us
  local copies, waits for them, and re-layouts: 20.8 us -> 17.6 us
    ppermute x15, waiting for transfers between devices: 50.7 us -> 45.9 us  [passed_along(): return lax.ppermute(value, 'h', [(i, (i + by) % SUMS) for i in range(SUMS)])]
    unnamed x64 -> x54, local copies, waits for them, and re-layouts: 19.3 us -> 16.1 us
    ppermute x15, starting transfers between devices: 36.6 us -> 33.6 us  [passed_along(): return lax.ppermute(value, 'h', [(i, (i + by) % SUMS) for i in range(SUMS)])]
  transfers between devices with their start and end apart: 20 -> 20, of which waited for: 6 -> 6; matrix products, arithmetic and copies ran while one was open for 0% -> 0% of each run, Pallas kernels for 17% -> 23%
where the time goes in v3:
time: 259 us; the launch traced here: 258 us
  starting transfers between devices  71.4 us (28%)
  Pallas kernels  64.6 us (25%)
  blocking collectives  54.9 us (21%)
  waiting for transfers between devices  47.4 us (18%)
  local copies, waits for them, and re-layouts  17.6 us (7%)
    all_to_all x2, blocking collectives, exchange(): return lax.all_to_all(value, axes, 0, 0, tiled=True)  54.9 us
    ppermute x15, waiting for transfers between devices, passed_along(): return lax.ppermute(value, 'h', [(i, (i + by) % SUMS) for i in range(SUMS)])  45.9 us
    all_to_all x4, starting transfers between devices, exchange(): return lax.all_to_all(value, axes, 0, 0, tiled=True)  37.1 us
    ppermute x15, starting transfers between devices, passed_along(): return lax.ppermute(value, 'h', [(i, (i + by) % SUMS) for i in range(SUMS)])  33.6 us
    pallas_call x2, Pallas kernels, updated(): pl.pallas_call(functools.partial(update_kernel, second), out_shape=struct...  22.1 us
    pallas_call x2, Pallas kernels, covariances(): pl.pallas_call(functools.partial(covariance_kernel, second), out_shape=(s...  19.7 us
    unnamed x54, local copies, waits for them, and re-layouts  16.1 us
    pallas_call x1, Pallas kernels, observations(): pl.pallas_call(observation_kernel, out_shape=(wide, wide, narrow, narrow,...  8.84 us
  transfers between devices with their start and end apart: 20, of which 6 were waited for; matrix products, arithmetic and copies ran while one was open for 0% of the time, Pallas kernels for 23%

profile of v3, /device:TPU:1, one launch (start us, length us, event | category | flops | bytes accessed | tf_op | source)
XLA Modules:
  0.0 258.1 jit_solution(1063834220398527540)
XLA Ops:
  0.0 0.1 and.130
  0.1 0.1 and.131
  0.2 0.1 add.109
  0.3 0.7 fusion.28
  1.0 1.1 fusion.29
  2.1 0.9 fusion.1
  3.0 9.2 %all-to-all-start = ((f32[32,4,128]{2,1,0:T(4,128)}), f32[32,4,128]{2,1,0:T(4,128)S(1)}, u32[]{:S(2)}, u32[]{:S(2)}) async-start(f32[32,4,128]{2,1,0:T(4,128)} %fusion.1), calls=%async_computation | async-start | bytes 131072 | tf_op jit(solution)/shard_map/all_to_all | solution.py:396
  12.2 0.0 copy-start
  12.2 2.2 copy-done
  14.4 4.5 %spread_out.1 = (f32[64,64,128]{2,1,0:T(8,128)S(1)}, f32[64,64,128]{2,1,0:T(8,128)S(1)}) custom-call(f32[8192,128]{1,0:T(8,128)S(1)} %bitcast.124), custom_call_target="tpu_custom_call" | custom-call | flops 1000000 | bytes 8388608 | tf_op jit(solution)/shard_map/spread_out/pallas_call | solution.py:126
  19.0 1.3 copy-done.2
  20.3 1.3 copy-done.4
  21.6 0.0 all-to-all-done
  21.7 0.0 copy-start.7
  21.7 9.7 %all-to-all-start.1 = ((f32[64,64,128]{2,1,0:T(8,128)}), f32[64,64,128]{2,1,0:T(8,128)S(1)}, u32[]{:S(2)}, u32[]{:S(2)}) async-start(f32[64,64,128]{2,1,0:T(8,128)} %copy-done.4), calls=%async_computation.1 | async-start | bytes 4194304 | tf_op jit(solution)/shard_map/all_to_all | solution.py:396
  31.4 0.0 copy-start.1
  31.4 2.2 copy-done.1
  33.6 3.1 %own_columns.1 = f32[8,128]{1,0:T(8,128)S(1)} custom-call(s32[1024]{0:T(1024)S(1)} %copy-done.7, s32[1024]{0:T(1024)S(1)} %copy-done.6, f32[8192,128]{1,0:T(8,128)S(1)} %bitcast.125), custom_call_target="tpu_custom_call" | custom-call | flops 1000000 | bytes 8388608 | tf_op jit(solution)/shard_map/own_columns/pallas_call | solution.py:99
  36.6 5.2 %collective-permute-start.2 = (f32[12,128]{1,0:T(8,128)S(1)}, f32[12,128]{1,0:T(8,128)S(1)}, u32[]{:S(2)}, u32[]{:S(2)}) collective-permute-start(f32[12,128]{1,0:T(8,128)S(1)} %pad_maximum_fusion), channel_id=1, source_target_pairs={{0,48},{16,0},{32,16},{48,32},{1,49},{17,1},{33,17},{49,33},{2,50}... | collective-permute-start | bytes 18440 | tf_op jit(solution)/shard_map/ppermute | solution.py:400
  41.8 1.2 collective-permute-start.1
  43.0 2.1 collective-permute-start
  45.1 15.6 %collective-permute-done.1 = f32[12,128]{1,0:T(8,128)S(1)} collective-permute-done((f32[12,128]{1,0:T(8,128)S(1)}, f32[12,128]{1,0:T(8,128)S(1)}, u32[]{:S(2)}, u32[]{:S(2)}) %collective-permute-start.1) | collective-permute-done | bytes 6176 | tf_op jit(solution)/shard_map/ppermute | solution.py:400
  60.7 0.0 collective-permute-done
  60.8 19.0 %all_to_all.30 = f32[32,40,128]{2,1,0:T(8,128)S(1)} all-to-all(f32[32,40,128]{2,1,0:T(8,128)S(1)} %broadcast_in_dim.140), channel_id=1, replica_groups=mesh['y'=4,'h'=4,'l'=2,'c'=2,'x'=4] {'y','l','x'}, dimensions={0} | all-to-all | bytes 1310720 | tf_op jit(solution)/shard_map/all_to_all | solution.py:396
  79.8 8.0 %all-to-all-start.3 = ((f32[64,64,128]{2,1,0:T(8,128)}), f32[64,64,128]{2,1,0:T(8,128)}, u32[]{:S(2)}, u32[]{:S(2)}) async-start(f32[64,64,128]{2,1,0:T(8,128)} %copy-done.2), calls=%async_computation.3 | async-start | bytes 4194304 | tf_op jit(solution)/shard_map/all_to_all | solution.py:396
  87.8 0.7 collective-permute-start.3
  88.5 0.1 pad.3.clone
  88.6 0.1 pad_add_fusion.position_ref
  88.7 0.1 maximum_maximum_fusion.facts_ref
  88.7 1.5 collective-permute-done.3
  90.2 8.8 %observations.1 = (bf16[1024,256]{1,0:T(8,128)(2,1)S(1)}, bf16[1024,256]{1,0:T(8,128)(2,1)S(1)}, bf16[64,1024]{1,0:T(8,128)(2,1)S(1)}, bf16[64,1024]{1,0:T(8,128...) custom-call(s32[3]{0:T(128)S(1)} %pad_add_fusion.position_ref, ...), custom_call_target="tpu_custom_call" | custom-call | flops 12000000000 | bytes 8388608 | tf_op jit(solution)/shard_map/observations/pallas_call | solution.py:256
  99.1 0.0 copy-start.8
  99.1 9.2 %covariances.2 = (f32[128,128]{1,0:T(8,128)S(1)}, f32[128,128]{1,0:T(8,128)S(1)}, f32[128,128]{1,0:T(8,128)S(1)}, f32[128,128]{1,0:T(8,128)S(1)}) custom-call(s32[3]{0:T(128)S(1)} %pad_add_fusion.position_ref, f32[4096,128]{1,0:T(8,128)S(1)} %bitcast.126, bf16[1024,256]{1,0:T(8,128)(2,1)S(1)} %get-tuple-element.44.anomalies_high_ref, ...), custom_call_target="tpu_custom_call" | custom-call | flops 3000000000 | bytes 4194304 | tf_op jit(solution)/shard_map/covariances/pallas_call | solution.py:312
  108.5 1.4 collective-permute-start.4
  109.9 1.1 collective-permute-start.5
  111.0 2.4 collective-permute-start.6
  113.3 2.0 collective-permute-done.4
  115.3 1.9 collective-permute-done.5
  117.2 4.9 %collective-permute-start.9 = (f32[128,128]{1,0:T(8,128)S(1)}, f32[128,128]{1,0:T(8,128)S(1)}, u32[]{:S(2)}, u32[]{:S(2)}) collective-permute-start(f32[128,128]{1,0:T(8,128)S(1)} %add_add_fusion.1.refs_0_), channel_id=1, source_target_pairs={{0,48},{16,0},{32,16},{48,32},{1,49},{17,1},{33,17},{49,33},{2,50}... | collective-permute-start | bytes 196616 | tf_op jit(solution)/shard_map/ppermute | solution.py:400
  122.2 4.5 %collective-permute-start.8 = (f32[128,128]{1,0:T(8,128)S(1)}, f32[128,128]{1,0:T(8,128)S(1)}, u32[]{:S(2)}, u32[]{:S(2)}) collective-permute-start(f32[128,128]{1,0:T(8,128)S(1)} %add_add_fusion.1.refs_0_), channel_id=1, source_target_pairs={{0,32},{16,48},{32,0},{48,16},{1,33},{17,49},{33,1},{49,17},{2,34}... | collective-permute-start | bytes 196616 | tf_op jit(solution)/shard_map/ppermute | solution.py:400
  126.6 0.0 collective-permute-start.7
  126.6 1.0 copy-done.15
  127.7 1.0 copy-done.18
  128.7 1.0 copy-done.20
  129.8 10.4 %covariances.3 = (f32[128,128]{1,0:T(8,128)S(1)}, f32[128,128]{1,0:T(8,128)S(1)}, f32[128,128]{1,0:T(8,128)S(1)}, f32[128,128]{1,0:T(8,128)S(1)}) custom-call(s32[3]{0:T(128)S(1)} %pad_add_fusion.position_ref, f32[4096,128]{1,0:T(8,128)} %bitcast.29.block_ref.refs_4_, bf16[1024,256]{1,0:T(8,128)(2,1)S(1)} %copy-done.18, bf16[1024,256]{1,0:T(8,128)(2,1)S(1)} %copy-done.20, ...), custom_call_target="tpu_custom_call" | custom-call | flops 3000000000 | bytes 4194304 | tf_op jit(solution)/shard_map/covariances/pallas_call | solution.py:312
  140.2 0.0 collective-permute-done.9.refs_3_
  140.2 0.0 collective-permute-done.8.refs_2_
  140.3 1.3 collective-permute-start.10
  141.5 4.4 %collective-permute-start.11 = (f32[128,128]{1,0:T(8,128)S(1)}, f32[128,128]{1,0:T(8,128)S(1)}, u32[]{:S(2)}, u32[]{:S(2)}) collective-permute-start(f32[128,128]{1,0:T(8,128)S(1)} %get-tuple-element.67), channel_id=1, source_target_pairs={{0,32},{16,48},{32,0},{48,16},{1,33},{17,49},{33,1},{49,17},{2,34}... | collective-permute-start | bytes 196616 | tf_op jit(solution)/shard_map/ppermute | solution.py:400
  146.0 0.1 collective-permute-start.12
  146.1 10.4 %updated.2 = f32[4096,128]{1,0:T(8,128)S(1)} custom-call(s32[3]{0:T(128)S(1)} %pad_add_fusion.position_ref, f32[128,128]{1,0:T(8,128)S(1)} %add_add_fusion.1.refs_0_, f32[128,128]{1,0:T(8,128)S(1)} %collective-permute-done.7.refs_1_, f32[128,128]{1,0:T(8,128)S(1)} %collective-permute-done.8.refs_2_, f32[128,128]{1,0:T(8,128)S(1)} %collective-permute-done.9.refs_3_, ...), custom_call_target="tpu_custom_call" | custom-call | flops 4000000000 | bytes 8388608 | tf_op jit(solution)/shard_map/updated/pallas_call | solution.py:375
  156.6 1.3 copy-done.3
  158.0 10.2 %all-to-all-start.4 = ((f32[64,64,128]{2,1,0:T(8,128)}), f32[64,64,128]{2,1,0:T(8,128)S(1)}, u32[]{:S(2)}, u32[]{:S(2)}) async-start(f32[64,64,128]{2,1,0:T(8,128)} %bitcast.128), calls=%async_computation.4 | async-start | bytes 4194304 | tf_op jit(solution)/shard_map/all_to_all | solution.py:396
  168.1 2.6 collective-permute-start.15
  170.7 2.5 collective-permute-start.14
  173.2 23.4 %collective-permute-done.14.refs_2_ = f32[128,128]{1,0:T(8,128)S(1)} collective-permute-done((f32[128,128]{1,0:T(8,128)S(1)}, f32[128,128]{1,0:T(8,128)S(1)}, u32[]{:S(2)}, u32[]{:S(2)}) %collective-permute-start.14) | collective-permute-done | bytes 65568 | tf_op jit(solution)/shard_map/ppermute | solution.py:400
  196.6 3.1 %collective-permute-done.13.refs_1_ = f32[128,128]{1,0:T(8,128)S(1)} collective-permute-done((f32[128,128]{1,0:T(8,128)S(1)}, f32[128,128]{1,0:T(8,128)S(1)}, u32[]{:S(2)}, u32[]{:S(2)}) %collective-permute-start.13) | collective-permute-done | bytes 65568 | tf_op jit(solution)/shard_map/ppermute | solution.py:400
  199.7 1.6 copy-done.10
  201.3 1.6 copy-done.13
  202.9 11.7 %updated.3 = f32[4096,128]{1,0:T(8,128)S(1)} custom-call(s32[3]{0:T(128)S(1)} %pad_add_fusion.position_ref, f32[128,128]{1,0:T(8,128)S(1)} %add_add_fusion.refs_0_, f32[128,128]{1,0:T(8,128)S(1)} %collective-permute-done.13.refs_1_, f32[128,128]{1,0:T(8,128)S(1)} %collective-permute-done.14.refs_2_, f32[128,128]{1,0:T(8,128)S(1)} %collective-permute-done.15.refs_3_, ...), custom_call_target="tpu_custom_call" | custom-call | flops 4000000000 | bytes 8388608 | tf_op jit(solution)/shard_map/updated/pallas_call | solution.py:375
  214.6 0.0 copy-start.5
  214.6 1.3 copy-done.5
  215.9 35.9 %all_to_all.31.second_ref = f32[64,64,128]{2,1,0:T(8,128)S(1)} all-to-all(f32[64,64,128]{2,1,0:T(8,128)} %bitcast.129), channel_id=1, replica_groups=mesh['y'=4,'h'=4,'l'=2,'c'=2,'x'=4] {'c','y','l','x'}, dimensions={0} | all-to-all | bytes 4194304 | tf_op jit(solution)/shard_map/all_to_all | solution.py:396
  251.8 6.3 %collect.1 = f32[8192,128]{1,0:T(8,128)} custom-call(f32[64,64,128]{2,1,0:T(8,128)S(1)} %all-to-all-done.4.first_ref, f32[64,64,128]{2,1,0:T(8,128)S(1)} %all_to_all.31.second_ref), custom_call_target="tpu_custom_call" | custom-call | flops 1000000 | bytes 8388608 | tf_op jit(solution)/shard_map/collect/pallas_call | solution.py:151
  (63 shorter events, 0.3 us)
Async XLA Ops:
  3.0 18.7 %all-to-all-start = ((f32[32,4,128]{2,1,0:T(4,128)}), f32[32,4,128]{2,1,0:T(4,128)S(1)}, u32[]{:S(2)}, u32[]{:S(2)}) async-start(f32[32,4,128]{2,1,0:T(4,128)} %fusion.1), calls=%async_computation | async-start | bytes 131072 | tf_op jit(solution)/shard_map/all_to_all | solution.py:396
  12.2 2.2 copy-start
  19.0 1.4 copy-start.2
  20.3 1.3 copy-start.4
  21.7 9.7 %copy-start.6 = (s32[1024]{0:T(1024)S(1)}, s32[1024]{0:T(1024)}, u32[]{:S(2)}) copy-start(s32[1024]{0:T(1024)} %locations_ref.1) | copy-start | bytes 12292
  21.7 9.7 %copy-start.7 = (s32[1024]{0:T(1024)S(1)}, s32[1024]{0:T(1024)}, u32[]{:S(2)}) copy-start(s32[1024]{0:T(1024)} %plan_ref.1) | copy-start | bytes 12292
  21.7 39.0 %all-to-all-start.1 = ((f32[64,64,128]{2,1,0:T(8,128)}), f32[64,64,128]{2,1,0:T(8,128)S(1)}, u32[]{:S(2)}, u32[]{:S(2)}) async-start(f32[64,64,128]{2,1,0:T(8,128)} %copy-done.4), calls=%async_computation.1 | async-start | bytes 4194304 | tf_op jit(solution)/shard_map/all_to_all | solution.py:396
  31.4 2.2 copy-start.1
  36.6 8.5 %collective-permute-start.2 = (f32[12,128]{1,0:T(8,128)S(1)}, f32[12,128]{1,0:T(8,128)S(1)}, u32[]{:S(2)}, u32[]{:S(2)}) collective-permute-start(f32[12,128]{1,0:T(8,128)S(1)} %pad_maximum_fusion), channel_id=1, source_target_pairs={{0,48},{16,0},{32,16},{48,32},{1,49},{17,1},{33,17},{49,33},{2,50}... | collective-permute-start | bytes 18440 | tf_op jit(solution)/shard_map/ppermute | solution.py:400
  41.8 18.8 %collective-permute-start.1 = (f32[12,128]{1,0:T(8,128)S(1)}, f32[12,128]{1,0:T(8,128)S(1)}, u32[]{:S(2)}, u32[]{:S(2)}) collective-permute-start(f32[12,128]{1,0:T(8,128)S(1)} %pad_maximum_fusion), channel_id=1, source_target_pairs={{0,32},{16,48},{32,0},{48,16},{1,33},{17,49},{33,1},{49,17},{2,34}... | collective-permute-start | bytes 18440 | tf_op jit(solution)/shard_map/ppermute | solution.py:400
  43.0 17.7 %collective-permute-start = (f32[12,128]{1,0:T(8,128)S(1)}, f32[12,128]{1,0:T(8,128)S(1)}, u32[]{:S(2)}, u32[]{:S(2)}) collective-permute-start(f32[12,128]{1,0:T(8,128)S(1)} %pad_maximum_fusion), channel_id=1, source_target_pairs={{0,16},{16,32},{32,48},{48,0},{1,17},{17,33},{33,49},{49,1},{2,18}... | collective-permute-start | bytes 18440 | tf_op jit(solution)/shard_map/ppermute | solution.py:400
  79.8 8.9 %copy-start.25 = (f32[1024]{0:T(1024)S(1)}, f32[1024]{0:T(1024)}, u32[]{:S(2)}) copy-start(f32[1024]{0:T(1024)} %param.11) | copy-start | bytes 12292
  79.8 8.9 %copy-start.26 = (f32[1024]{0:T(1024)S(1)}, f32[1024]{0:T(1024)}, u32[]{:S(2)}) copy-start(f32[1024]{0:T(1024)} %param.10) | copy-start | bytes 12292
  79.8 46.8 %all-to-all-start.3 = ((f32[64,64,128]{2,1,0:T(8,128)}), f32[64,64,128]{2,1,0:T(8,128)}, u32[]{:S(2)}, u32[]{:S(2)}) async-start(f32[64,64,128]{2,1,0:T(8,128)} %copy-done.2), calls=%async_computation.3 | async-start | bytes 4194304 | tf_op jit(solution)/shard_map/all_to_all | solution.py:396
  87.8 2.4 collective-permute-start.3
  99.1 9.3 %copy-start.8 = (bf16[1024,1024]{1,0:T(8,128)(2,1)}, bf16[1024,1024]{1,0:T(8,128)(2,1)S(1)}, u32[]{:S(2)}) copy-start(bf16[1024,1024]{1,0:T(8,128)(2,1)S(1)} %get-tuple-element.62.refs_7_) | copy-start | bytes 6291460
  99.1 9.3 %copy-start.11 = (bf16[1024,1024]{1,0:T(8,128)(2,1)}, bf16[1024,1024]{1,0:T(8,128)(2,1)S(1)}, u32[]{:S(2)}) copy-start(bf16[1024,1024]{1,0:T(8,128)(2,1)S(1)} %get-tuple-element.63.refs_8_) | copy-start | bytes 6291460
  99.1 9.3 %copy-start.14 = (f32[1024,128]{1,0:T(8,128)}, f32[1024,128]{1,0:T(8,128)S(1)}, u32[]{:S(2)}) copy-start(f32[1024,128]{1,0:T(8,128)S(1)} %get-tuple-element.46.facts_ref.refs_9_) | copy-start | bytes 1572868
  99.1 9.3 %copy-start.17 = (bf16[1024,256]{1,0:T(8,128)(2,1)}, bf16[1024,256]{1,0:T(8,128)(2,1)S(1)}, u32[]{:S(2)}) copy-start(bf16[1024,256]{1,0:T(8,128)(2,1)S(1)} %get-tuple-element.44.anomalies_high_ref) | copy-start | bytes 1572868
  99.1 9.3 %copy-start.19 = (bf16[1024,256]{1,0:T(8,128)(2,1)}, bf16[1024,256]{1,0:T(8,128)(2,1)S(1)}, u32[]{:S(2)}) copy-start(bf16[1024,256]{1,0:T(8,128)(2,1)S(1)} %get-tuple-element.45.anomalies_low_ref) | copy-start | bytes 1572868
  99.1 9.3 %copy-start.21 = (bf16[64,1024]{1,0:T(8,128)(2,1)}, bf16[64,1024]{1,0:T(8,128)(2,1)S(1)}, u32[]{:S(2)}) copy-start(bf16[64,1024]{1,0:T(8,128)(2,1)S(1)} %get-tuple-element.61.refs_6_) | copy-start | bytes 393220
  99.1 9.3 %copy-start.23 = (f32[16,1024]{1,0:T(8,128)}, f32[16,1024]{1,0:T(8,128)S(1)}, u32[]{:S(2)}) copy-start(f32[16,1024]{1,0:T(8,128)S(1)} %get-tuple-element.64.refs_10_) | copy-start | bytes 196612
  108.5 6.9 %collective-permute-start.4 = (f32[128,128]{1,0:T(8,128)S(1)}, f32[128,128]{1,0:T(8,128)S(1)}, u32[]{:S(2)}, u32[]{:S(2)}) collective-permute-start(f32[128,128]{1,0:T(8,128)S(1)} %get-tuple-element.48), channel_id=1, source_target_pairs={{0,16},{16,32},{32,48},{48,0},{1,17},{17,33},{33,49},{49,1},{2,18}... | collective-permute-start | bytes 196616 | tf_op jit(solution)/shard_map/ppermute | solution.py:400
  109.9 7.3 %collective-permute-start.5 = (f32[128,128]{1,0:T(8,128)S(1)}, f32[128,128]{1,0:T(8,128)S(1)}, u32[]{:S(2)}, u32[]{:S(2)}) collective-permute-start(f32[128,128]{1,0:T(8,128)S(1)} %get-tuple-element.49), channel_id=1, source_target_pairs={{0,32},{16,48},{32,0},{48,16},{1,33},{17,49},{33,1},{49,17},{2,34}... | collective-permute-start | bytes 196616 | tf_op jit(solution)/shard_map/ppermute | solution.py:400
  111.0 6.2 %collective-permute-start.6 = (f32[128,128]{1,0:T(8,128)S(1)}, f32[128,128]{1,0:T(8,128)S(1)}, u32[]{:S(2)}, u32[]{:S(2)}) collective-permute-start(f32[128,128]{1,0:T(8,128)S(1)} %get-tuple-element.50), channel_id=1, source_target_pairs={{0,48},{16,0},{32,16},{48,32},{1,49},{17,1},{33,17},{49,33},{2,50}... | collective-permute-start | bytes 196616 | tf_op jit(solution)/shard_map/ppermute | solution.py:400
  117.2 23.0 %collective-permute-start.9 = (f32[128,128]{1,0:T(8,128)S(1)}, f32[128,128]{1,0:T(8,128)S(1)}, u32[]{:S(2)}, u32[]{:S(2)}) collective-permute-start(f32[128,128]{1,0:T(8,128)S(1)} %add_add_fusion.1.refs_0_), channel_id=1, source_target_pairs={{0,48},{16,0},{32,16},{48,32},{1,49},{17,1},{33,17},{49,33},{2,50}... | collective-permute-start | bytes 196616 | tf_op jit(solution)/shard_map/ppermute | solution.py:400
  122.2 18.1 %collective-permute-start.8 = (f32[128,128]{1,0:T(8,128)S(1)}, f32[128,128]{1,0:T(8,128)S(1)}, u32[]{:S(2)}, u32[]{:S(2)}) collective-permute-start(f32[128,128]{1,0:T(8,128)S(1)} %add_add_fusion.1.refs_0_), channel_id=1, source_target_pairs={{0,32},{16,48},{32,0},{48,16},{1,33},{17,49},{33,1},{49,17},{2,34}... | collective-permute-start | bytes 196616 | tf_op jit(solution)/shard_map/ppermute | solution.py:400
  126.6 13.6 %collective-permute-start.7 = (f32[128,128]{1,0:T(8,128)S(1)}, f32[128,128]{1,0:T(8,128)S(1)}, u32[]{:S(2)}, u32[]{:S(2)}) collective-permute-start(f32[128,128]{1,0:T(8,128)S(1)} %add_add_fusion.1.refs_0_), channel_id=1, source_target_pairs={{0,16},{16,32},{32,48},{48,0},{1,17},{17,33},{33,49},{49,1},{2,18}... | collective-permute-start | bytes 196616 | tf_op jit(solution)/shard_map/ppermute | solution.py:400
  126.6 1.0 copy-start.15
  127.7 1.0 copy-start.18
  128.7 1.0 copy-start.20
  129.8 16.3 %copy-start.9 = (bf16[1024,1024]{1,0:T(8,128)(2,1)S(1)}, bf16[1024,1024]{1,0:T(8,128)(2,1)}, u32[]{:S(2)}) copy-start(bf16[1024,1024]{1,0:T(8,128)(2,1)} %copy-done.8) | copy-start | bytes 6291460
  129.8 16.3 %copy-start.12 = (bf16[1024,1024]{1,0:T(8,128)(2,1)S(1)}, bf16[1024,1024]{1,0:T(8,128)(2,1)}, u32[]{:S(2)}) copy-start(bf16[1024,1024]{1,0:T(8,128)(2,1)} %copy-done.11) | copy-start | bytes 6291460
  129.8 16.3 %copy-start.16 = (f32[1024,128]{1,0:T(8,128)S(1)}, f32[1024,128]{1,0:T(8,128)}, u32[]{:S(2)}) copy-start(f32[1024,128]{1,0:T(8,128)} %copy-done.14) | copy-start | bytes 1572868
  129.8 16.3 %copy-start.22 = (bf16[64,1024]{1,0:T(8,128)(2,1)S(1)}, bf16[64,1024]{1,0:T(8,128)(2,1)}, u32[]{:S(2)}) copy-start(bf16[64,1024]{1,0:T(8,128)(2,1)} %copy-done.21) | copy-start | bytes 393220
  129.8 16.3 %copy-start.24 = (f32[16,1024]{1,0:T(8,128)S(1)}, f32[16,1024]{1,0:T(8,128)}, u32[]{:S(2)}) copy-start(f32[16,1024]{1,0:T(8,128)} %copy-done.23) | copy-start | bytes 196612
  140.3 17.7 %collective-permute-start.10 = (f32[128,128]{1,0:T(8,128)S(1)}, f32[128,128]{1,0:T(8,128)S(1)}, u32[]{:S(2)}, u32[]{:S(2)}) collective-permute-start(f32[128,128]{1,0:T(8,128)S(1)} %get-tuple-element.66), channel_id=1, source_target_pairs={{0,16},{16,32},{32,48},{48,0},{1,17},{17,33},{33,49},{49,1},{2,18}... | collective-permute-start | bytes 196616 | tf_op jit(solution)/shard_map/ppermute | solution.py:400
  141.5 16.4 %collective-permute-start.11 = (f32[128,128]{1,0:T(8,128)S(1)}, f32[128,128]{1,0:T(8,128)S(1)}, u32[]{:S(2)}, u32[]{:S(2)}) collective-permute-start(f32[128,128]{1,0:T(8,128)S(1)} %get-tuple-element.67), channel_id=1, source_target_pairs={{0,32},{16,48},{32,0},{48,16},{1,33},{17,49},{33,1},{49,17},{2,34}... | collective-permute-start | bytes 196616 | tf_op jit(solution)/shard_map/ppermute | solution.py:400
  146.0 11.9 %collective-permute-start.12 = (f32[128,128]{1,0:T(8,128)S(1)}, f32[128,128]{1,0:T(8,128)S(1)}, u32[]{:S(2)}, u32[]{:S(2)}) collective-permute-start(f32[128,128]{1,0:T(8,128)S(1)} %get-tuple-element.68), channel_id=1, source_target_pairs={{0,48},{16,0},{32,16},{48,32},{1,49},{17,1},{33,17},{49,33},{2,50}... | collective-permute-start | bytes 196616 | tf_op jit(solution)/shard_map/ppermute | solution.py:400
  156.6 1.4 copy-start.3
  158.0 57.9 %all-to-all-start.4 = ((f32[64,64,128]{2,1,0:T(8,128)}), f32[64,64,128]{2,1,0:T(8,128)S(1)}, u32[]{:S(2)}, u32[]{:S(2)}) async-start(f32[64,64,128]{2,1,0:T(8,128)} %bitcast.128), calls=%async_computation.4 | async-start | bytes 4194304 | tf_op jit(solution)/shard_map/all_to_all | solution.py:396
  168.1 5.1 %collective-permute-start.15 = (f32[128,128]{1,0:T(8,128)S(1)}, f32[128,128]{1,0:T(8,128)S(1)}, u32[]{:S(2)}, u32[]{:S(2)}) collective-permute-start(f32[128,128]{1,0:T(8,128)S(1)} %add_add_fusion.refs_0_), channel_id=1, source_target_pairs={{0,48},{16,0},{32,16},{48,32},{1,49},{17,1},{33,17},{49,33},{2,50}... | collective-permute-start | bytes 196616 | tf_op jit(solution)/shard_map/ppermute | solution.py:400
  170.7 25.9 %collective-permute-start.14 = (f32[128,128]{1,0:T(8,128)S(1)}, f32[128,128]{1,0:T(8,128)S(1)}, u32[]{:S(2)}, u32[]{:S(2)}) collective-permute-start(f32[128,128]{1,0:T(8,128)S(1)} %add_add_fusion.refs_0_), channel_id=1, source_target_pairs={{0,32},{16,48},{32,0},{48,16},{1,33},{17,49},{33,1},{49,17},{2,34}... | collective-permute-start | bytes 196616 | tf_op jit(solution)/shard_map/ppermute | solution.py:400
  173.2 26.5 %collective-permute-start.13 = (f32[128,128]{1,0:T(8,128)S(1)}, f32[128,128]{1,0:T(8,128)S(1)}, u32[]{:S(2)}, u32[]{:S(2)}) collective-permute-start(f32[128,128]{1,0:T(8,128)S(1)} %add_add_fusion.refs_0_), channel_id=1, source_target_pairs={{0,16},{16,32},{32,48},{48,0},{1,17},{17,33},{33,49},{49,1},{2,18}... | collective-permute-start | bytes 196616 | tf_op jit(solution)/shard_map/ppermute | solution.py:400
  199.7 1.6 copy-start.10
  201.3 1.6 copy-start.13
  214.6 1.3 copy-start.5

commit v4 on v2

v4 whole, which is shorter than its diff:
```python
import functools

import jax
import jax.numpy as jnp
from jax import lax
from jax.experimental import pallas as pl
from jax.experimental.pallas import tpu as pltpu
from jax.sharding import Mesh, PartitionSpec as P

MEMBERS = 256
TILE = 512
NTILES = 2048
RADIUS = 4
WINDOW = 2 * RADIUS + 1
BATCH_OBS = 256
BATCHES = 4
NOBS = BATCH_OBS * BATCHES

ALL = ("y", "h", "l", "c", "x")
PEERS = ("c", "y", "l", "x")
CHIPS = ("y", "l", "x")
GROUP = 64
CORES = 2
GROUP_CHIPS = GROUP // CORES
SUMS = 4
RESIDUES = 16
SLICES = 4
LANES = 128
OWN_TILES = NTILES // RESIDUES
ROWS = NTILES * TILE // LANES
CHUNK = NOBS // SUMS
FOUR = 4
WIDE = FOUR * GROUP
GROUPS = OWN_TILES // FOUR
WINDOW_ROWS = 128
WINDOW_COLUMNS = 256
PADDED_ROWS = NOBS + WINDOW_ROWS
PADDED_COLUMNS = NOBS + WINDOW_COLUMNS
NOWHERE = -512
BLOCK_TILES = 16

epsilon = 1e-06
f32 = jnp.float32
bf16 = jnp.bfloat16
i32 = jnp.int32

VMEM = pl.BlockSpec(memory_space=pltpu.VMEM)
SMEM = pl.BlockSpec(memory_space=pltpu.SMEM)


def kernel_params(mib):
    return pltpu.CompilerParams(vmem_limit_bytes=mib * 1024 * 1024)


def struct(shape, dtype=f32):
    return jax.ShapeDtypeStruct(shape, dtype)


def two_parts(value):
    high = value.astype(bf16)
    return high, (value - high.astype(f32)).astype(bf16)


def three_parts(value):
    high = value.astype(bf16)
    rest = value - high.astype(f32)
    middle = rest.astype(bf16)
    return high, middle, (rest - middle.astype(f32)).astype(bf16)


def dot(a, b):
    return lax.dot_general(a, b, (((1,), (0,)), ((), ())), preferred_element_type=f32)


def dot_parts(a_high, a_low, b_high, b_low):
    return dot(a_high, b_high) + dot(a_high, b_low) + dot(a_low, b_high)


def accurate_dot(a, b):
    return dot_parts(*two_parts(a), *two_parts(b))


def columns_kernel(plan_ref, locations_ref, state_ref, out_ref, picked_ref):
    lane = lax.broadcasted_iota(i32, (1, LANES), 1)

    def step(i, carry):
        base = pl.multiple_of(i * 8, 8)
        found = []
        for u in range(8):
            where = locations_ref[plan_ref[base + u]]
            row = state_ref[pl.ds(where >> 7, 1), :]
            found.append(jnp.where(lane == (where & (LANES - 1)), row, 0.0))
        picked_ref[pl.ds(base, 8), :] = jnp.concatenate(found, axis=0)
        return carry

    lax.fori_loop(0, NOBS // 8, step, 0, unroll=2)
    ones = jnp.ones((16, LANES), bf16)
    total = jnp.zeros((16, NOBS), f32)
    for part in three_parts(picked_ref[...]):
        total = total + lax.dot_general(ones, part, (((1,), (1,)), ((), ())), preferred_element_type=f32)
    for g in range(NOBS // LANES):
        out_ref[pl.ds(g, 1), :] = total[0:1, g * LANES : (g + 1) * LANES]


def own_columns(plan, locations, rows):
    return pl.pallas_call(
        columns_kernel,
        out_shape=struct((NOBS // LANES, LANES)),
        in_specs=[SMEM, SMEM, VMEM],
        out_specs=VMEM,
        scratch_shapes=[pltpu.VMEM((NOBS, LANES), f32)],
        compiler_params=kernel_params(24),
        cost_estimate=pl.CostEstimate(flops=10**6, bytes_accessed=8 * 2**20, transcendentals=0),
        name="own_columns",
    )(plan, locations, rows)


def spread_kernel(state_ref, out_ref):
    for d in range(GROUP):
        out_ref[d] = state_ref[pl.ds(d, BLOCK_TILES, stride=GROUP), :]


def collect_kernel(in_ref, state_ref):
    for d in range(GROUP):
        state_ref[pl.ds(d, BLOCK_TILES, stride=GROUP), :] = in_ref[d]


def reordered(kernel, value, out_shape, name):
    by_device = pl.BlockSpec((GROUP, BLOCK_TILES, LANES), lambda i: (0, i, 0))
    by_row = pl.BlockSpec((GROUP * BLOCK_TILES, LANES), lambda i: (i, 0))
    specs = (by_row, by_device) if value.ndim == 2 else (by_device, by_row)
    return pl.pallas_call(
        kernel,
        grid=(OWN_TILES // BLOCK_TILES,),
        out_shape=struct(out_shape),
        in_specs=[specs[0]],
        out_specs=specs[1],
        compiler_params=kernel_params(16),
        cost_estimate=pl.CostEstimate(flops=10**6, bytes_accessed=8 * 2**20, transcendentals=0),
        name=name,
    )(value)


def spread_out(rows):
    return reordered(spread_kernel, rows, (GROUP, OWN_TILES, LANES), "spread_out")


def collect(blocks):
    return reordered(collect_kernel, blocks, (ROWS, LANES), "collect")


def observation_kernel(
    position_ref, plan_ref, facts_ref, own_ref, other_ref,
    anomalies_high_ref, anomalies_low_ref, tiles_ref, factors_high_ref, factors_low_ref, tile_rows_ref,
    ensemble_ref, increments_ref, one_hot_ref, facts_scratch, in_columns_ref,
    turned_ref, links_high_ref, links_low_ref, sort_ref, sort_back_ref,
):
    core = position_ref[2]
    for d in range(SUMS):
        for gathered_ref, start in ((own_ref, core), (other_ref, 1 - core)):
            rows = pl.ds(pl.multiple_of(d * GROUP + start * GROUP_CHIPS, GROUP_CHIPS), GROUP_CHIPS)
            for g in range(NOBS // LANES):
                ensemble_ref[rows, g * LANES : (g + 1) * LANES] = gathered_ref[
                    pl.ds(d * 8 + g, GROUP_CHIPS, stride=40), :
                ]
    for g in range(NOBS // LANES):
        rows = pl.ds((g // 4) * 40 + 32 + g % 4, 16, stride=80)
        facts_scratch[0:16, g * LANES : (g + 1) * LANES] = own_ref[rows, :] + other_ref[rows, :]
    facts_scratch[16:24, :] = facts_ref[...]
    facts_scratch[24:128, :] = jnp.zeros((104, NOBS), f32)
    source = lax.broadcasted_iota(i32, (NOBS, NOBS), 0)
    one_hot_ref[...] = jnp.where(source == plan_ref[...], 1.0, 0.0).astype(bf16)
    high, middle, low = three_parts(facts_scratch[0:32, :])
    ordered = dot(high, one_hot_ref[...]) + dot(middle, one_hot_ref[...]) + dot(low, one_hot_ref[...])
    facts_scratch[0:32, :] = ordered
    for g in range(NOBS // LANES):
        in_columns_ref[g * LANES : (g + 1) * LANES, :] = facts_scratch[:, g * LANES : (g + 1) * LANES].T

    residue = position_ref[0]
    tile_row = facts_scratch[16:17, :].astype(i32)
    tile_column = in_columns_ref[:, 16:17].astype(i32)
    nth_row = (residue - tile_row + RADIUS) & (RESIDUES - 1)
    nth_column = (residue - tile_column + RADIUS) & (RESIDUES - 1)
    own_row = ((tile_row - RADIUS + nth_row) & (NTILES - 1)) >> 4
    own_column = ((tile_column - RADIUS + nth_column) & (NTILES - 1)) >> 4
    own_row = jnp.where(nth_row < WINDOW, own_row, -1)
    own_column = jnp.where(nth_column < WINDOW, own_column, -2)
    mask_column = jnp.zeros((NOBS, 1), f32)
    for n in range(WINDOW):
        mask_column = mask_column + jnp.where(nth_column == n, in_columns_ref[:, n : n + 1], 0.0)

    mask_row = jnp.zeros((1, NOBS), f32)
    for n in range(WINDOW):
        mask_row = mask_row + jnp.where(nth_row == n, facts_scratch[n : n + 1, :], 0.0)

    key_row = jnp.where(own_row < 0, OWN_TILES, own_row) * NOBS + lax.broadcasted_iota(i32, (1, NOBS), 1)
    key_column = jnp.where(own_column < 0, OWN_TILES, own_column) * NOBS + lax.broadcasted_iota(i32, (NOBS, 1), 0)
    rank_row = jnp.sum(jnp.where(key_column < key_row, 1.0, 0.0), axis=0, keepdims=True).astype(i32)
    rank_column = jnp.sum(jnp.where(key_row < key_column, 1.0, 0.0), axis=1, keepdims=True).astype(i32)
    sort_ref[...] = jnp.where(source == rank_row, 1.0, 0.0).astype(bf16)
    to = lax.broadcasted_iota(i32, (NOBS, NOBS), 1)
    sort_back_ref[...] = jnp.where(to == rank_column, 1.0, 0.0).astype(bf16)

    gain_rows = []
    for b in range(BATCHES):
        here = slice(b * BATCH_OBS, (b + 1) * BATCH_OBS)
        prior = ensemble_ref[:, here]
        average = jnp.sum(prior, axis=0, keepdims=True) / MEMBERS
        anomaly = prior - average
        spread = jnp.sum(anomaly * anomaly, axis=0, keepdims=True) / (MEMBERS - 1) + epsilon
        value = facts_scratch[17:18, here]
        error = facts_scratch[18:19, here]
        shrink = jnp.sqrt(error / (spread + error))
        moved = (average * error + value * spread) / (spread + error)
        increments = (shrink - 1.0) * anomaly + (moved - average)
        increments_ref[:, here] = increments
        turned = anomaly.T
        spread_column = jnp.sum(turned * turned, axis=1, keepdims=True) / (MEMBERS - 1) + epsilon
        gain_column = 1.0 / ((MEMBERS - 1) * spread_column)
        turned_high, turned_low = two_parts(turned)
        turned_ref[here, :] = jnp.concatenate([turned_high[:, 0:GROUP], turned_low[:, 0:GROUP]], axis=1)
        gain_rows.append(1.0 / ((MEMBERS - 1) * spread))
        weight = mask_column[here] * gain_column
        if b > 0:
            before = b * BATCH_OBS
            links = accurate_dot(turned, increments_ref[:, 0:before])
            links = jnp.where(own_column[here] == own_row[:, 0:before], links * weight, 0.0)
            links_high, links_low = two_parts(links)
            links_high_ref[here, 0:before] = links_high
            links_low_ref[here, 0:before] = links_low
        if b < BATCHES - 1:
            after = slice((b + 1) * BATCH_OBS, NOBS)
            later = ensemble_ref[:, after]
            covariance = dot_parts(turned_high, turned_low, *two_parts(later))
            apart = (tile_row[:, after] - tile_column[here] + RADIUS) & (NTILES - 1)
            masks = jnp.zeros(apart.shape, f32)
            for n in range(WINDOW):
                masks = jnp.where(apart == n, in_columns_ref[here, n : n + 1], masks)
            ensemble_ref[:, after] = later + accurate_dot(increments, covariance * masks * gain_column)

    for b in reversed(range(BATCHES - 1)):
        here = slice(b * BATCH_OBS, (b + 1) * BATCH_OBS)
        after = slice((b + 1) * BATCH_OBS, NOBS)
        increments_ref[0:GROUP, here] += dot_parts(
            *two_parts(increments_ref[0:GROUP, after]), links_high_ref[after, here], links_low_ref[after, here]
        )
    factors = increments_ref[0:GROUP, :] * (mask_row * jnp.concatenate(gain_rows, axis=1))

    tile_here = jnp.where(own_column < 0, NOWHERE, own_column).astype(f32)
    tile_here = jnp.broadcast_to(tile_here, (NOBS, LANES)).astype(bf16)
    sorted_columns = dot(sort_ref[...], jnp.concatenate([turned_ref[...], tile_here], axis=1))
    high = sorted_columns[:, 0:GROUP].astype(bf16)
    low = sorted_columns[:, GROUP : 2 * GROUP].astype(bf16)
    anomalies_high_ref[0:NOBS, :] = jnp.concatenate([high] * FOUR, axis=1)
    anomalies_low_ref[0:NOBS, :] = jnp.concatenate([low] * FOUR, axis=1)
    nth_of_four = (lax.broadcasted_iota(i32, (NOBS, WIDE), 1) >> 6).astype(f32)
    tiles_ref[0:NOBS, :] = (sorted_columns[:, LANES : LANES + 1] - nth_of_four).astype(bf16)
    padding = slice(NOBS, PADDED_ROWS)
    anomalies_high_ref[padding, :] = jnp.zeros((WINDOW_ROWS, WIDE), bf16)
    anomalies_low_ref[padding, :] = jnp.zeros((WINDOW_ROWS, WIDE), bf16)
    tiles_ref[padding, :] = jnp.full((WINDOW_ROWS, WIDE), NOWHERE, bf16)

    factors_high, factors_low = two_parts(factors)
    tile_there = jnp.where(own_row < 0, NOWHERE, own_row).astype(f32)
    tile_there = jnp.broadcast_to(tile_there, (GROUP, NOBS)).astype(bf16)
    sorted_rows = dot(jnp.concatenate([factors_high, factors_low, tile_there], axis=0), sort_back_ref[...]).astype(bf16)
    factors_high_ref[:, 0:NOBS] = sorted_rows[0:GROUP]
    factors_low_ref[:, 0:NOBS] = sorted_rows[GROUP : 2 * GROUP]
    tile_rows_ref[:, 0:NOBS] = sorted_rows[2 * GROUP : 3 * GROUP]
    padding = slice(NOBS, PADDED_COLUMNS)
    factors_high_ref[:, padding] = jnp.zeros((GROUP, WINDOW_COLUMNS), bf16)
    factors_low_ref[:, padding] = jnp.zeros((GROUP, WINDOW_COLUMNS), bf16)
    tile_rows_ref[:, padding] = jnp.full((GROUP, WINDOW_COLUMNS), NOWHERE, bf16)


def observations(position, plan, facts, own, other):
    columns = struct((PADDED_ROWS, WIDE), bf16)
    factors = struct((GROUP, PADDED_COLUMNS), bf16)
    square = pltpu.VMEM((NOBS, NOBS), bf16)
    return pl.pallas_call(
        observation_kernel,
        out_shape=(columns, columns, columns, factors, factors, factors),
        in_specs=[SMEM, VMEM, VMEM, VMEM, VMEM],
        out_specs=(VMEM,) * 6,
        scratch_shapes=[
            pltpu.VMEM((MEMBERS, NOBS), f32),
            pltpu.VMEM((MEMBERS, NOBS), f32),
            square,
            pltpu.VMEM((128, NOBS), f32),
            pltpu.VMEM((NOBS, 128), f32),
            pltpu.VMEM((NOBS, 2 * GROUP), bf16),
            square,
            square,
            square,
            square,
        ],
        compiler_params=kernel_params(44),
        cost_estimate=pl.CostEstimate(flops=20 * 10**9, bytes_accessed=8 * 2**20, transcendentals=10**5),
        name="observations",
    )(position, plan, facts, own, other)


def for_windows(starts_ref, size, align, visit):
    def first(g):
        return starts_ref[g] & -align

    for g in range(GROUPS):
        visit(g, pl.multiple_of(first(g), align), True)

    def rest(g, carry):
        count = (starts_ref[g + 1] - first(g) + size - 1) // size

        def step(i, carry):
            visit(g, pl.multiple_of(first(g) + i * size, align), False)
            return carry

        return lax.fori_loop(1, count, step, carry)

    lax.fori_loop(0, GROUPS, rest, 0)


def number(value, shape):
    if isinstance(value, int):
        return jnp.full(shape, value, bf16)
    return jnp.full(shape, value.astype(f32)).astype(bf16)


def covariance_kernel(
    position_ref, starts_ref, block_ref, anomalies_high_ref, anomalies_low_ref, tiles_ref, *refs
):
    out_refs, (total_ref,) = refs[:SUMS], refs[SUMS:]
    total_ref[...] = jnp.zeros_like(total_ref)
    zero = jnp.zeros((WINDOW_ROWS, WIDE), bf16)

    def visit(g, start, is_first):
        rows = pl.ds(start, WINDOW_ROWS)
        found = tiles_ref[rows, :] == number(g * FOUR, (WINDOW_ROWS, WIDE))
        left = jnp.concatenate(
            [jnp.where(found, anomalies_high_ref[rows, :], zero), jnp.where(found, anomalies_low_ref[rows, :], zero)],
            axis=0,
        )
        right = jnp.concatenate(
            [block_ref[pl.ds(g * FOUR + u, GROUP, stride=OWN_TILES), :] for u in range(FOUR)], axis=0
        )
        both = dot(left, jnp.concatenate(two_parts(right), axis=1))
        both = both[:WINDOW_ROWS] + both[WINDOW_ROWS:]
        total_ref[rows, :] += both[:, :LANES] + both[:, LANES:]

    for_windows(starts_ref, WINDOW_ROWS, 16, visit)
    for d in range(SUMS):
        start = ((position_ref[1] + d) & (SUMS - 1)) * CHUNK
        out_refs[d][...] = total_ref[pl.ds(pl.multiple_of(start, CHUNK), CHUNK), :]


def covariances(position, starts, block, anomalies_high, anomalies_low, tiles):
    return pl.pallas_call(
        covariance_kernel,
        out_shape=(struct((CHUNK, LANES)),) * SUMS,
        in_specs=[SMEM, SMEM] + [VMEM] * 4,
        out_specs=(VMEM,) * SUMS,
        scratch_shapes=[pltpu.VMEM((PADDED_ROWS, LANES), f32)],
        compiler_params=kernel_params(24),
        cost_estimate=pl.CostEstimate(flops=3 * 10**9, bytes_accessed=4 * 2**20, transcendentals=0),
        name="covariances",
    )(position, starts, block.reshape(GROUP * OWN_TILES, LANES), anomalies_high, anomalies_low, tiles)


def update_kernel(position_ref, starts_ref, *refs):
    sums_refs = refs[:SUMS]
    block_ref, factors_high_ref, factors_low_ref, tile_rows_ref, out_ref, right_ref = refs[SUMS:]
    for d in range(SUMS):
        start = ((position_ref[1] - d) & (SUMS - 1)) * CHUNK
        right_ref[pl.ds(pl.multiple_of(start, CHUNK), CHUNK), :] = jnp.concatenate(two_parts(sums_refs[d][...]), axis=1)
    right_ref[NOBS:, :] = jnp.zeros((WINDOW_COLUMNS, 2 * LANES), bf16)
    zero = jnp.zeros((GROUP, WINDOW_COLUMNS), bf16)

    def visit(g, start, is_first):
        columns = pl.ds(start, WINDOW_COLUMNS)
        tiles = tile_rows_ref[:, columns]
        high = factors_high_ref[:, columns]
        low = factors_low_ref[:, columns]
        found = [tiles == number(g * FOUR + u, (GROUP, WINDOW_COLUMNS)) for u in range(FOUR)]
        left = [jnp.where(f, high, zero) for f in found] + [jnp.where(f, low, zero) for f in found]
        both = dot(jnp.concatenate(left, axis=0), right_ref[columns, :])
        both = both[:WIDE] + both[WIDE:]
        change = both[:, :LANES] + both[:, LANES:]
        for u in range(FOUR):
            rows = pl.ds(g * FOUR + u, GROUP, stride=OWN_TILES)
            before = block_ref if is_first else out_ref
            out_ref[rows, :] = before[rows, :] + change[u * GROUP : (u + 1) * GROUP]

    for_windows(starts_ref, WINDOW_COLUMNS, LANES, visit)


def updated(position, starts, sums, block, factors_high, factors_low, tile_rows):
    out = pl.pallas_call(
        update_kernel,
        out_shape=struct((GROUP * OWN_TILES, LANES)),
        in_specs=[SMEM, SMEM] + [VMEM] * (SUMS + 4),
        out_specs=VMEM,
        scratch_shapes=[pltpu.VMEM((PADDED_COLUMNS, 2 * LANES), bf16)],
        compiler_params=kernel_params(32),
        cost_estimate=pl.CostEstimate(flops=4 * 10**9, bytes_accessed=8 * 2**20, transcendentals=0),
        name="updated",
    )(position, starts, *sums, block.reshape(GROUP * OWN_TILES, LANES), factors_high, factors_low, tile_rows)
    return out.reshape(GROUP, OWN_TILES, LANES)


def exchange(value, axes=PEERS):
    return lax.all_to_all(value, axes, 0, 0, tiled=True)


def passed_along(value, by):
    return lax.ppermute(value, "h", [(i, (i + by) % SUMS) for i in range(SUMS)])


def shards(state, locations, tile_mask, plan, obs_value, obs_error):
    residue = lax.axis_index(PEERS) // SLICES
    position = jnp.stack([residue, lax.axis_index("h"), lax.axis_index("c")]).astype(i32)
    rows = state.reshape(ROWS, LANES)

    tiles_here = tile_mask.shape[0]
    tiles = locations // TILE
    nth = jnp.arange(16, dtype=i32)[:, None]
    local = (tiles[None, :] - RADIUS + nth - lax.axis_index(ALL) * tiles_here) & (NTILES - 1)
    masks = jnp.zeros((16, NOBS), i32)
    for i in range(tiles_here):
        masks = masks + jnp.where((local == i) & (nth < WINDOW), tile_mask[i][None, :], 0)
    masks = exchange(masks.astype(f32).reshape(GROUP_CHIPS, 4, LANES), CHIPS).sum(axis=0)

    columns = own_columns(plan, locations, rows)
    mine = jnp.concatenate([columns, masks], axis=0)
    all_four = [mine] + [passed_along(mine, by) for by in range(1, SUMS)]
    payload = jnp.concatenate(
        [*(each[0:8] for each in all_four), sum(each[8:12] for each in all_four), jnp.zeros((4, LANES), f32)], axis=0
    )
    gathered = exchange(jnp.broadcast_to(payload[None], (GROUP_CHIPS, 40, LANES)), CHIPS)
    other = lax.ppermute(gathered, "c", [(0, 1), (1, 0)])
    block, other = lax.optimization_barrier((spread_out(rows), other))
    block = exchange(block)

    facts = jnp.concatenate(
        [tiles.astype(f32)[None], obs_value[None], obs_error[None], jnp.zeros((5, NOBS), f32)], axis=0
    )
    anomalies_high, anomalies_low, sorted_tiles, factors_high, factors_low, tile_rows = observations(
        position, plan[None], facts, gathered.reshape(-1, LANES), other.reshape(-1, LANES)
    )
    nth_own = (residue - tiles + RADIUS) & (RESIDUES - 1)
    own_tile = jnp.where(nth_own < WINDOW, ((tiles - RADIUS + nth_own) & (NTILES - 1)) // RESIDUES, OWN_TILES)
    starts = jnp.sum(own_tile[None, :] < FOUR * jnp.arange(GROUPS + 1, dtype=i32)[:, None], axis=1, dtype=i32)

    parts = covariances(position, starts, block, anomalies_high, anomalies_low, sorted_tiles)
    total = parts[0]
    for by in range(1, SUMS):
        total = total + passed_along(parts[by], by)
    sums = [total] + [passed_along(total, by) for by in range(1, SUMS)]
    block = exchange(updated(position, starts, sums, block, factors_high, factors_low, tile_rows))
    return collect(block).reshape(state.shape)


def solution(mesh):
    fine = Mesh(mesh.devices.reshape(4, 4, 2, 2, 4), ALL)
    placed = (P(ALL, None), P(), P(ALL, None), P(), P(), P())
    return jax.shard_map(shards, mesh=fine, in_specs=placed, out_specs=P(ALL, None), check_vma=False)
```

time: 268 us -> 232 us (0.87)
  starting transfers between devices: 72.4 us -> 40 us
  Pallas kernels: 62.5 us -> 36.2 us
  blocking collectives: 56.9 us -> 81.2 us
  local copies, waits for them, and re-layouts: 20.8 us -> 10 us
  waiting for transfers between devices: 52.2 us -> 61.5 us
    all_to_all x4 -> x2, waiting for transfers between devices: 0.01 us -> 43.8 us  [exchange(): return lax.all_to_all(value, axes, 0, 0, tiled=True)]
    ppermute x15 -> x9, waiting for transfers between devices: 50.7 us -> 17.7 us  [passed_along(): return lax.ppermute(value, 'h', [(i, (i + by) % SUMS) for i in range(SUMS)])]
    pallas_call x7 -> x5, Pallas kernels: 59.4 us -> 33.1 us  [the longest x1 9.38 us: observations(): pl.pallas_call(observation_kernel, out_shape=(columns, columns, columns,...]
    all_to_all x2, blocking collectives: 56.9 us -> 81.2 us  [exchange(): return lax.all_to_all(value, axes, 0, 0, tiled=True)]
    all_to_all x4 -> x2, starting transfers between devices: 35.2 us -> 14.8 us  [exchange(): return lax.all_to_all(value, axes, 0, 0, tiled=True)]
    ppermute x15 -> x9, starting transfers between devices: 36.6 us -> 21.2 us  [passed_along(): return lax.ppermute(value, 'h', [(i, (i + by) % SUMS) for i in range(SUMS)])]
    unnamed x64 -> x20, local copies, waits for them, and re-layouts: 19.3 us -> 8.42 us
    ppermute x1, starting transfers between devices: 0.62 us -> 3.99 us  [shards(): other = lax.ppermute(gathered, 'c', [(0, 1), (1, 0)])]
  transfers between devices with their start and end apart: 20 -> 12, of which waited for: 6 -> 6; matrix products, arithmetic and copies ran while one was open for 0% -> 0% of each run, Pallas kernels for 17% -> 7%
where the time goes in v4:
time: 232 us; the launch traced here: 231 us
  blocking collectives  81.2 us (35%)
  waiting for transfers between devices  61.5 us (27%)
  starting transfers between devices  40 us (17%)
  Pallas kernels  36.2 us (16%)
  local copies, waits for them, and re-layouts  10 us (4%)
    all_to_all x2, blocking collectives, exchange(): return lax.all_to_all(value, axes, 0, 0, tiled=True)  81.2 us
    all_to_all x2, waiting for transfers between devices, exchange(): return lax.all_to_all(value, axes, 0, 0, tiled=True)  43.8 us
    ppermute x9, starting transfers between devices, passed_along(): return lax.ppermute(value, 'h', [(i, (i + by) % SUMS) for i in range(SUMS)])  21.2 us
    ppermute x9, waiting for transfers between devices, passed_along(): return lax.ppermute(value, 'h', [(i, (i + by) % SUMS) for i in range(SUMS)])  17.7 us
    all_to_all x2, starting transfers between devices, exchange(): return lax.all_to_all(value, axes, 0, 0, tiled=True)  14.8 us
    pallas_call x1, Pallas kernels, observations(): pl.pallas_call(observation_kernel, out_shape=(columns, columns, columns,...  9.38 us
    pallas_call x1, Pallas kernels, updated(): pl.pallas_call(update_kernel, out_shape=struct((GROUP * OWN_TILES, LANES)...  9.2 us
    unnamed x20, local copies, waits for them, and re-layouts  8.42 us
  transfers between devices with their start and end apart: 12, of which 6 were waited for; matrix products, arithmetic and copies ran while one was open for 0% of the time, Pallas kernels for 7%

profile of v4, /device:TPU:1, one launch (start us, length us, event | category | flops | bytes accessed | tf_op | source)
XLA Modules:
  0.0 231.2 jit_solution(1025316811217955045)
XLA Ops:
  0.0 1.2 fusion.32
  1.2 0.1 add.110
  1.3 0.1 and.151
  1.4 0.1 and.152
  1.5 0.7 fusion.31
  2.2 0.9 fusion.1
  3.1 9.2 %all-to-all-start = ((f32[32,4,128]{2,1,0:T(4,128)}), f32[32,4,128]{2,1,0:T(4,128)S(1)}, u32[]{:S(2)}, u32[]{:S(2)}) async-start(f32[32,4,128]{2,1,0:T(4,128)} %fusion.1), calls=%async_computation | async-start | bytes 131072 | tf_op jit(solution)/shard_map/all_to_all | solution.py:410
  12.3 0.0 copy-start
  12.4 2.2 copy-done
  14.5 0.0 copy-start.3
  14.5 0.7 copy-done.3
  15.2 0.0 copy-start.4
  15.2 0.7 copy-done.4
  15.9 3.1 %own_columns.1 = f32[8,128]{1,0:T(8,128)S(1)} custom-call(s32[1024]{0:T(1024)S(1)} %copy-done.4, s32[1024]{0:T(1024)S(1)} %copy-done.3, f32[8192,128]{1,0:T(8,128)S(1)} %bitcast.122), custom_call_target="tpu_custom_call" | custom-call | flops 1000000 | bytes 8388608 | tf_op jit(solution)/shard_map/own_columns/pallas_call | solution.py:106
  19.0 0.7 all-to-all-done
  19.7 3.1 %collective-permute-start = (f32[12,128]{1,0:T(8,128)S(1)}, f32[12,128]{1,0:T(8,128)S(1)}, u32[]{:S(2)}, u32[]{:S(2)}) collective-permute-start(f32[12,128]{1,0:T(8,128)S(1)} %pad_maximum_fusion), channel_id=1, source_target_pairs={{0,16},{16,32},{32,48},{48,0},{1,17},{17,33},{33,49},{49,1},{2,18}... | collective-permute-start | bytes 18440 | tf_op jit(solution)/shard_map/ppermute | solution.py:414
  22.8 4.2 %collective-permute-start.1 = (f32[12,128]{1,0:T(8,128)S(1)}, f32[12,128]{1,0:T(8,128)S(1)}, u32[]{:S(2)}, u32[]{:S(2)}) collective-permute-start(f32[12,128]{1,0:T(8,128)S(1)} %pad_maximum_fusion), channel_id=1, source_target_pairs={{0,32},{16,48},{32,0},{48,16},{1,33},{17,49},{33,1},{49,17},{2,34}... | collective-permute-start | bytes 18440 | tf_op jit(solution)/shard_map/ppermute | solution.py:414
  27.0 2.4 %collective-permute-start.2 = (f32[12,128]{1,0:T(8,128)S(1)}, f32[12,128]{1,0:T(8,128)S(1)}, u32[]{:S(2)}, u32[]{:S(2)}) collective-permute-start(f32[12,128]{1,0:T(8,128)S(1)} %pad_maximum_fusion), channel_id=1, source_target_pairs={{0,48},{16,0},{32,16},{48,32},{1,49},{17,1},{33,17},{49,33},{2,50}... | collective-permute-start | bytes 18440 | tf_op jit(solution)/shard_map/ppermute | solution.py:414
  29.4 0.0 collective-permute-done
  29.4 0.0 collective-permute-done.1
  29.4 1.0 collective-permute-done.2
  30.5 16.8 %all_to_all.20 = f32[32,40,128]{2,1,0:T(8,128)S(1)} all-to-all(f32[32,40,128]{2,1,0:T(8,128)S(1)} %broadcast_in_dim.142), channel_id=1, replica_groups=mesh['y'=4,'h'=4,'l'=2,'c'=2,'x'=4] {'y','l','x'}, dimensions={0} | all-to-all | bytes 1310720 | tf_op jit(solution)/shard_map/all_to_all | solution.py:410
  47.3 4.0 %collective-permute-start.3 = (f32[32,40,128]{2,1,0:T(8,128)S(1)}, f32[32,40,128]{2,1,0:T(8,128)S(1)}, u32[]{:S(2)}, u32[]{:S(2)}) collective-permute-start(f32[32,40,128]{2,1,0:T(8,128)S(1)} %all_to_all.20), channel_id=1, source_target_pairs={{0,4},{4,0},{1,5},{5,1},{2,6},{6,2},{3,7},{7,3},{8,12},{12,8},{9,1... | collective-permute-start | bytes 1966088 | tf_op jit(solution)/shard_map/ppermute | solution.py:438
  51.3 0.0 copy-start.1
  51.3 2.2 copy-done.1
  53.5 2.8 %spread_out.1 = f32[64,128,128]{2,1,0:T(8,128)S(1)} custom-call(f32[8192,128]{1,0:T(8,128)S(1)} %bitcast.123), custom_call_target="tpu_custom_call" | custom-call | flops 1000000 | bytes 8388608 | tf_op jit(solution)/shard_map/spread_out/pallas_call | solution.py:132
  56.3 0.0 copy-start.2
  56.3 2.0 copy-done.2
  58.3 0.0 copy-start.8
  58.3 0.0 copy-start.9
  58.3 0.0 copy-start.5
  58.3 0.0 collective-permute-done.3
  58.3 5.6 %all-to-all-start.2 = ((f32[64,128,128]{2,1,0:T(8,128)}), f32[64,128,128]{2,1,0:T(8,128)}, u32[]{:S(2)}, u32[]{:S(2)}) async-start(f32[64,128,128]{2,1,0:T(8,128)} %copy-done.2), calls=%async_computation.2 | async-start | bytes 8388608 | tf_op jit(solution)/shard_map/all_to_all | solution.py:410
  63.9 0.1 pad.3.clone
  64.0 0.1 pad_add_fusion.position_ref
  64.1 0.2 convert_reduce_fusion.starts_ref
  64.3 0.0 copy-done.8
  64.3 0.0 copy-done.9
  64.3 0.1 maximum_maximum_fusion.facts_ref
  64.3 0.0 copy-done.5
  64.3 9.4 %observations.1 = (bf16[1152,256]{1,0:T(8,128)(2,1)S(1)}, bf16[1152,256]{1,0:T(8,128)(2,1)S(1)}, bf16[1152,256]{1,0:T(8,128)(2,1)S(1)}, bf16[64,1280]{1,0:T(8,12...) custom-call(s32[3]{0:T(128)S(1)} %pad_add_fusion.position_ref, s32[1,1024]{1,0:T(1,128)S(1)} %bitcast.126, ...), custom_call_target="tpu_custom_call" | custom-call | flops 20000000000 | bytes 8388608 | tf_op jit(solution)/shard_map/observations/pallas_call | solution.py:280
  73.7 0.0 copy-start.6
  73.7 0.7 copy-done.6
  74.4 43.1 %all-to-all-done.2 = f32[64,128,128]{2,1,0:T(8,128)} async-done(((f32[64,128,128]{2,1,0:T(8,128)}), f32[64,128,128]{2,1,0:T(8,128)}, u32[]{:S(2)}, u32[]{:S(2)}) %all-to-all-start.2) | async-done | bytes 4194336 | tf_op jit(solution)/shard_map/all_to_all | solution.py:410
  117.6 0.0 copy-start.7
  117.6 6.2 %covariances.1 = (f32[256,128]{1,0:T(8,128)S(1)}, f32[256,128]{1,0:T(8,128)S(1)}, f32[256,128]{1,0:T(8,128)S(1)}, f32[256,128]{1,0:T(8,128)S(1)}) custom-call(s32[3]{0:T(128)S(1)} %pad_add_fusion.position_ref, s32[33]{0:T(128)S(1)} %convert_reduce_fusion.starts_ref, f32[8192,128]{1,0:T(8,128)} %bitcast.22.block_ref.refs_4_, ...), custom_call_target="tpu_custom_call" | custom-call | flops 3000000000 | bytes 4194304 | tf_op jit(solution)/shard_map/covariances/pallas_call | solution.py:356
  123.8 3.7 %collective-permute-start.6 = (f32[256,128]{1,0:T(8,128)S(1)}, f32[256,128]{1,0:T(8,128)S(1)}, u32[]{:S(2)}, u32[]{:S(2)}) collective-permute-start(f32[256,128]{1,0:T(8,128)S(1)} %get-tuple-element.25), channel_id=1, source_target_pairs={{0,48},{16,0},{32,16},{48,32},{1,49},{17,1},{33,17},{49,33},{2,50}... | collective-permute-start | bytes 393224 | tf_op jit(solution)/shard_map/ppermute | solution.py:414
  127.5 1.7 collective-permute-start.5
  129.2 0.5 collective-permute-start.4
  129.7 0.0 collective-permute-done.6
  129.7 9.8 %collective-permute-done.5 = f32[256,128]{1,0:T(8,128)S(1)} collective-permute-done((f32[256,128]{1,0:T(8,128)S(1)}, f32[256,128]{1,0:T(8,128)S(1)}, u32[]{:S(2)}, u32[]{:S(2)}) %collective-permute-start.5) | collective-permute-done | bytes 131104 | tf_op jit(solution)/shard_map/ppermute | solution.py:414
  139.4 0.0 collective-permute-done.4
  139.5 1.6 collective-permute-start.7
  141.0 3.8 %collective-permute-start.8 = (f32[256,128]{1,0:T(8,128)S(1)}, f32[256,128]{1,0:T(8,128)S(1)}, u32[]{:S(2)}, u32[]{:S(2)}) collective-permute-start(f32[256,128]{1,0:T(8,128)S(1)} %add_add_fusion.refs_0_), channel_id=1, source_target_pairs={{0,32},{16,48},{32,0},{48,16},{1,33},{17,49},{33,1},{49,17},{2,34}... | collective-permute-start | bytes 393224 | tf_op jit(solution)/shard_map/ppermute | solution.py:414
  144.8 0.3 collective-permute-start.9
  145.1 2.3 %collective-permute-done.7.refs_1_ = f32[256,128]{1,0:T(8,128)S(1)} collective-permute-done((f32[256,128]{1,0:T(8,128)S(1)}, f32[256,128]{1,0:T(8,128)S(1)}, u32[]{:S(2)}, u32[]{:S(2)}) %collective-permute-start.7) | collective-permute-done | bytes 131104 | tf_op jit(solution)/shard_map/ppermute | solution.py:414
  147.5 4.6 %collective-permute-done.8.refs_2_ = f32[256,128]{1,0:T(8,128)S(1)} collective-permute-done((f32[256,128]{1,0:T(8,128)S(1)}, f32[256,128]{1,0:T(8,128)S(1)}, u32[]{:S(2)}, u32[]{:S(2)}) %collective-permute-start.8) | collective-permute-done | bytes 131104 | tf_op jit(solution)/shard_map/ppermute | solution.py:414
  152.0 0.0 collective-permute-done.9.refs_3_
  152.1 0.0 copy-done.7
  152.1 9.2 %updated.1 = f32[8192,128]{1,0:T(8,128)S(1)} custom-call(s32[3]{0:T(128)S(1)} %pad_add_fusion.position_ref, s32[33]{0:T(128)S(1)} %convert_reduce_fusion.starts_ref, f32[256,128]{1,0:T(8,128)S(1)} %add_add_fusion.refs_0_, f32[256,128]{1,0:T(8,128)S(1)} %collective-permute-done.7.refs_1_, f32[256,128]{1,0:T(8,128)S(1)} %collective-permute-done.8.refs_2_, ...), custom_call_target="tpu_custom_call" | custom-call | flops 4000000000 | bytes 8388608 | tf_op jit(solution)/shard_map/updated/pallas_call | solution.py:396
  161.3 64.3 %all_to_all.21.in_ref = f32[64,128,128]{2,1,0:T(8,128)S(1)} all-to-all(f32[64,128,128]{2,1,0:T(8,128)S(1)} %bitcast.124), channel_id=1, replica_groups=mesh['y'=4,'h'=4,'l'=2,'c'=2,'x'=4] {'c','y','l','x'}, dimensions={0} | all-to-all | bytes 8388608 | tf_op jit(solution)/shard_map/all_to_all | solution.py:410
  225.6 5.6 %collect.1 = f32[8192,128]{1,0:T(8,128)} custom-call(f32[64,128,128]{2,1,0:T(8,128)S(1)} %all_to_all.21.in_ref), custom_call_target="tpu_custom_call" | custom-call | flops 1000000 | bytes 8388608 | tf_op jit(solution)/shard_map/collect/pallas_call | solution.py:132
  (14 shorter events, 0.2 us)
Async XLA Ops:
  3.1 16.6 %all-to-all-start = ((f32[32,4,128]{2,1,0:T(4,128)}), f32[32,4,128]{2,1,0:T(4,128)S(1)}, u32[]{:S(2)}, u32[]{:S(2)}) async-start(f32[32,4,128]{2,1,0:T(4,128)} %fusion.1), calls=%async_computation | async-start | bytes 131072 | tf_op jit(solution)/shard_map/all_to_all | solution.py:410
  12.3 2.2 copy-start
  14.5 0.7 copy-start.3
  15.2 0.7 copy-start.4
  19.7 9.7 %collective-permute-start = (f32[12,128]{1,0:T(8,128)S(1)}, f32[12,128]{1,0:T(8,128)S(1)}, u32[]{:S(2)}, u32[]{:S(2)}) collective-permute-start(f32[12,128]{1,0:T(8,128)S(1)} %pad_maximum_fusion), channel_id=1, source_target_pairs={{0,16},{16,32},{32,48},{48,0},{1,17},{17,33},{33,49},{49,1},{2,18}... | collective-permute-start | bytes 18440 | tf_op jit(solution)/shard_map/ppermute | solution.py:414
  22.8 6.6 %collective-permute-start.1 = (f32[12,128]{1,0:T(8,128)S(1)}, f32[12,128]{1,0:T(8,128)S(1)}, u32[]{:S(2)}, u32[]{:S(2)}) collective-permute-start(f32[12,128]{1,0:T(8,128)S(1)} %pad_maximum_fusion), channel_id=1, source_target_pairs={{0,32},{16,48},{32,0},{48,16},{1,33},{17,49},{33,1},{49,17},{2,34}... | collective-permute-start | bytes 18440 | tf_op jit(solution)/shard_map/ppermute | solution.py:414
  27.0 3.4 %collective-permute-start.2 = (f32[12,128]{1,0:T(8,128)S(1)}, f32[12,128]{1,0:T(8,128)S(1)}, u32[]{:S(2)}, u32[]{:S(2)}) collective-permute-start(f32[12,128]{1,0:T(8,128)S(1)} %pad_maximum_fusion), channel_id=1, source_target_pairs={{0,48},{16,0},{32,16},{48,32},{1,49},{17,1},{33,17},{49,33},{2,50}... | collective-permute-start | bytes 18440 | tf_op jit(solution)/shard_map/ppermute | solution.py:414
  47.3 11.0 %collective-permute-start.3 = (f32[32,40,128]{2,1,0:T(8,128)S(1)}, f32[32,40,128]{2,1,0:T(8,128)S(1)}, u32[]{:S(2)}, u32[]{:S(2)}) collective-permute-start(f32[32,40,128]{2,1,0:T(8,128)S(1)} %all_to_all.20), channel_id=1, source_target_pairs={{0,4},{4,0},{1,5},{5,1},{2,6},{6,2},{3,7},{7,3},{8,12},{12,8},{9,1... | collective-permute-start | bytes 1966088 | tf_op jit(solution)/shard_map/ppermute | solution.py:438
  51.3 2.2 copy-start.1
  56.3 2.0 copy-start.2
  58.3 5.9 %copy-start.8 = (f32[1024]{0:T(1024)S(1)}, f32[1024]{0:T(1024)}, u32[]{:S(2)}) copy-start(f32[1024]{0:T(1024)} %param.11) | copy-start | bytes 12292
  58.3 5.9 %copy-start.9 = (f32[1024]{0:T(1024)S(1)}, f32[1024]{0:T(1024)}, u32[]{:S(2)}) copy-start(f32[1024]{0:T(1024)} %param.10) | copy-start | bytes 12292
  58.3 6.0 %copy-start.5 = (s32[1024]{0:T(1024)S(1)}, s32[1024]{0:T(1024)}, u32[]{:S(2)}) copy-start(s32[1024]{0:T(1024)} %plan_ref.1) | copy-start | bytes 12292
  58.3 59.2 %all-to-all-start.2 = ((f32[64,128,128]{2,1,0:T(8,128)}), f32[64,128,128]{2,1,0:T(8,128)}, u32[]{:S(2)}, u32[]{:S(2)}) async-start(f32[64,128,128]{2,1,0:T(8,128)} %copy-done.2), calls=%async_computation.2 | async-start | bytes 8388608 | tf_op jit(solution)/shard_map/all_to_all | solution.py:410
  73.7 0.7 copy-start.6
  117.6 34.5 %copy-start.7 = (bf16[64,1280]{1,0:T(8,128)(2,1)S(1)}, bf16[64,1280]{1,0:T(8,128)(2,1)}, u32[]{:S(2)}) copy-start(bf16[64,1280]{1,0:T(8,128)(2,1)} %copy-done.6) | copy-start | bytes 491524
  123.8 5.9 %collective-permute-start.6 = (f32[256,128]{1,0:T(8,128)S(1)}, f32[256,128]{1,0:T(8,128)S(1)}, u32[]{:S(2)}, u32[]{:S(2)}) collective-permute-start(f32[256,128]{1,0:T(8,128)S(1)} %get-tuple-element.25), channel_id=1, source_target_pairs={{0,48},{16,0},{32,16},{48,32},{1,49},{17,1},{33,17},{49,33},{2,50}... | collective-permute-start | bytes 393224 | tf_op jit(solution)/shard_map/ppermute | solution.py:414
  127.5 11.9 %collective-permute-start.5 = (f32[256,128]{1,0:T(8,128)S(1)}, f32[256,128]{1,0:T(8,128)S(1)}, u32[]{:S(2)}, u32[]{:S(2)}) collective-permute-start(f32[256,128]{1,0:T(8,128)S(1)} %get-tuple-element.24), channel_id=1, source_target_pairs={{0,32},{16,48},{32,0},{48,16},{1,33},{17,49},{33,1},{49,17},{2,34}... | collective-permute-start | bytes 393224 | tf_op jit(solution)/shard_map/ppermute | solution.py:414
  129.2 10.3 %collective-permute-start.4 = (f32[256,128]{1,0:T(8,128)S(1)}, f32[256,128]{1,0:T(8,128)S(1)}, u32[]{:S(2)}, u32[]{:S(2)}) collective-permute-start(f32[256,128]{1,0:T(8,128)S(1)} %get-tuple-element.23), channel_id=1, source_target_pairs={{0,16},{16,32},{32,48},{48,0},{1,17},{17,33},{33,49},{49,1},{2,18}... | collective-permute-start | bytes 393224 | tf_op jit(solution)/shard_map/ppermute | solution.py:414
  139.5 8.0 %collective-permute-start.7 = (f32[256,128]{1,0:T(8,128)S(1)}, f32[256,128]{1,0:T(8,128)S(1)}, u32[]{:S(2)}, u32[]{:S(2)}) collective-permute-start(f32[256,128]{1,0:T(8,128)S(1)} %add_add_fusion.refs_0_), channel_id=1, source_target_pairs={{0,16},{16,32},{32,48},{48,0},{1,17},{17,33},{33,49},{49,1},{2,18}... | collective-permute-start | bytes 393224 | tf_op jit(solution)/shard_map/ppermute | solution.py:414
  141.0 11.0 %collective-permute-start.8 = (f32[256,128]{1,0:T(8,128)S(1)}, f32[256,128]{1,0:T(8,128)S(1)}, u32[]{:S(2)}, u32[]{:S(2)}) collective-permute-start(f32[256,128]{1,0:T(8,128)S(1)} %add_add_fusion.refs_0_), channel_id=1, source_target_pairs={{0,32},{16,48},{32,0},{48,16},{1,33},{17,49},{33,1},{49,17},{2,34}... | collective-permute-start | bytes 393224 | tf_op jit(solution)/shard_map/ppermute | solution.py:414
  144.8 7.2 %collective-permute-start.9 = (f32[256,128]{1,0:T(8,128)S(1)}, f32[256,128]{1,0:T(8,128)S(1)}, u32[]{:S(2)}, u32[]{:S(2)}) collective-permute-start(f32[256,128]{1,0:T(8,128)S(1)} %add_add_fusion.refs_0_), channel_id=1, source_target_pairs={{0,48},{16,0},{32,16},{48,32},{1,49},{17,1},{33,17},{49,33},{2,50}... | collective-permute-start | bytes 393224 | tf_op jit(solution)/shard_map/ppermute | solution.py:414

commit v5 on v4

--- a/solution.py
+++ b/solution.py
@@ -28,16 +28,18 @@
 LANES = 128
 OWN_TILES = NTILES // RESIDUES
 ROWS = NTILES * TILE // LANES
-CHUNK = NOBS // SUMS
-FOUR = 4
-WIDE = FOUR * GROUP
-GROUPS = OWN_TILES // FOUR
+EIGHT = 8
+WIDE = EIGHT * GROUP
+GROUPS = OWN_TILES // EIGHT
 WINDOW_ROWS = 128
 WINDOW_COLUMNS = 256
 PADDED_ROWS = NOBS + WINDOW_ROWS
 PADDED_COLUMNS = NOBS + WINDOW_COLUMNS
 NOWHERE = -512
 BLOCK_TILES = 16
+FIRST = 640
+FIRST_CHUNK = FIRST // SUMS
+REST_CHUNK = (NOBS - FIRST) // SUMS
 
 epsilon = 1e-06
 f32 = jnp.float32
@@ -121,8 +123,8 @@
 
 
 def collect_kernel(in_ref, state_ref):
-    for d in range(GROUP):
-        state_ref[pl.ds(d, BLOCK_TILES, stride=GROUP), :] = in_ref[d]
+    for a in range(BLOCK_TILES):
+        state_ref[a * GROUP : (a + 1) * GROUP, :] = in_ref[:, a, :]
 
 
 def reordered(kernel, value, out_shape, name):
@@ -251,10 +253,13 @@
     sorted_columns = dot(sort_ref[...], jnp.concatenate([turned_ref[...], tile_here], axis=1))
     high = sorted_columns[:, 0:GROUP].astype(bf16)
     low = sorted_columns[:, GROUP : 2 * GROUP].astype(bf16)
-    anomalies_high_ref[0:NOBS, :] = jnp.concatenate([high] * FOUR, axis=1)
-    anomalies_low_ref[0:NOBS, :] = jnp.concatenate([low] * FOUR, axis=1)
-    nth_of_four = (lax.broadcasted_iota(i32, (NOBS, WIDE), 1) >> 6).astype(f32)
-    tiles_ref[0:NOBS, :] = (sorted_columns[:, LANES : LANES + 1] - nth_of_four).astype(bf16)
+    replicate = jnp.where(
+        lax.broadcasted_iota(i32, (GROUP, WIDE), 1) >> 3 == lax.broadcasted_iota(i32, (GROUP, WIDE), 0), 1.0, 0.0
+    ).astype(bf16)
+    anomalies_high_ref[0:NOBS, :] = dot(high, replicate).astype(bf16)
+    anomalies_low_ref[0:NOBS, :] = dot(low, replicate).astype(bf16)
+    nth_of_eight = (lax.broadcasted_iota(i32, (NOBS, WIDE), 1) & (EIGHT - 1)).astype(f32)
+    tiles_ref[0:NOBS, :] = (sorted_columns[:, LANES : LANES + 1] - nth_of_eight).astype(bf16)
     padding = slice(NOBS, PADDED_ROWS)
     anomalies_high_ref[padding, :] = jnp.zeros((WINDOW_ROWS, WIDE), bf16)
     anomalies_low_ref[padding, :] = jnp.zeros((WINDOW_ROWS, WIDE), bf16)
@@ -263,23 +268,27 @@
     factors_high, factors_low = two_parts(factors)
     tile_there = jnp.where(own_row < 0, NOWHERE, own_row).astype(f32)
     tile_there = jnp.broadcast_to(tile_there, (GROUP, NOBS)).astype(bf16)
-    sorted_rows = dot(jnp.concatenate([factors_high, factors_low, tile_there], axis=0), sort_back_ref[...]).astype(bf16)
-    factors_high_ref[:, 0:NOBS] = sorted_rows[0:GROUP]
-    factors_low_ref[:, 0:NOBS] = sorted_rows[GROUP : 2 * GROUP]
-    tile_rows_ref[:, 0:NOBS] = sorted_rows[2 * GROUP : 3 * GROUP]
+    sorted_rows = dot(jnp.concatenate([factors_high, factors_low, tile_there], axis=0), sort_back_ref[...])
+    replicate = jnp.where(
+        lax.broadcasted_iota(i32, (WIDE, GROUP), 0) >> 3 == lax.broadcasted_iota(i32, (WIDE, GROUP), 1), 1.0, 0.0
+    ).astype(bf16)
+    factors_high_ref[:, 0:NOBS] = dot(replicate, sorted_rows[0:GROUP].astype(bf16)).astype(bf16)
+    factors_low_ref[:, 0:NOBS] = dot(replicate, sorted_rows[GROUP : 2 * GROUP].astype(bf16)).astype(bf16)
+    nth_of_eight = (lax.broadcasted_iota(i32, (16, NOBS), 0) & (EIGHT - 1)).astype(f32)
+    tile_rows_ref[:, 0:NOBS] = (sorted_rows[2 * GROUP : 2 * GROUP + 16] - nth_of_eight).astype(bf16)
     padding = slice(NOBS, PADDED_COLUMNS)
-    factors_high_ref[:, padding] = jnp.zeros((GROUP, WINDOW_COLUMNS), bf16)
-    factors_low_ref[:, padding] = jnp.zeros((GROUP, WINDOW_COLUMNS), bf16)
-    tile_rows_ref[:, padding] = jnp.full((GROUP, WINDOW_COLUMNS), NOWHERE, bf16)
+    factors_high_ref[:, padding] = jnp.zeros((WIDE, WINDOW_COLUMNS), bf16)
+    factors_low_ref[:, padding] = jnp.zeros((WIDE, WINDOW_COLUMNS), bf16)
+    tile_rows_ref[:, padding] = jnp.full((16, WINDOW_COLUMNS), NOWHERE, bf16)
 
 
 def observations(position, plan, facts, own, other):
     columns = struct((PADDED_ROWS, WIDE), bf16)
-    factors = struct((GROUP, PADDED_COLUMNS), bf16)
+    factors = struct((WIDE, PADDED_COLUMNS), bf16)
     square = pltpu.VMEM((NOBS, NOBS), bf16)
     return pl.pallas_call(
         observation_kernel,
-        out_shape=(columns, columns, columns, factors, factors, factors),
+        out_shape=(columns, columns, columns, factors, factors, struct((16, PADDED_COLUMNS), bf16)),
         in_specs=[SMEM, VMEM, VMEM, VMEM, VMEM],
         out_specs=(VMEM,) * 6,
         scratch_shapes=[
@@ -300,110 +309,127 @@
     )(position, plan, facts, own, other)
 
 
-def for_windows(starts_ref, size, align, visit):
-    def first(g):
-        return starts_ref[g] & -align
-
-    for g in range(GROUPS):
-        visit(g, pl.multiple_of(first(g), align), True)
-
-    def rest(g, carry):
-        count = (starts_ref[g + 1] - first(g) + size - 1) // size
-
-        def step(i, carry):
-            visit(g, pl.multiple_of(first(g) + i * size, align), False)
+def for_windows(starts_ref, groups, size, align, visit):
+    def start(g, i):
+        return pl.multiple_of((starts_ref[g] & -align) + i * size, align)
+
+    first_group = pl.program_id(0) * groups
+    for n in range(groups):
+        visit(n, first_group + n, start(first_group + n, 0), True)
+    for n in range(groups):
+        g = first_group + n
+        count = (starts_ref[g + 1] - (starts_ref[g] & -align) + size - 1) // size
+
+        def step(i, carry, n=n, g=g):
+            visit(n, g, start(g, i), False)
             return carry
 
-        return lax.fori_loop(1, count, step, carry)
-
-    lax.fori_loop(0, GROUPS, rest, 0)
-
-
-def number(value, shape):
-    if isinstance(value, int):
-        return jnp.full(shape, value, bf16)
-    return jnp.full(shape, value.astype(f32)).astype(bf16)
-
-
-def covariance_kernel(
-    position_ref, starts_ref, block_ref, anomalies_high_ref, anomalies_low_ref, tiles_ref, *refs
-):
-    out_refs, (total_ref,) = refs[:SUMS], refs[SUMS:]
-    total_ref[...] = jnp.zeros_like(total_ref)
+        lax.fori_loop(1, count, step, 0)
+
+
+def first_tile(g, shape):
+    return jnp.full(shape, (g * EIGHT).astype(f32)).astype(bf16)
+
+
+COVARIANCE_GROUPS = 4
+
+
+def covariance_kernel(position_ref, starts_ref, block_ref, anomalies_high_ref, anomalies_low_ref, tiles_ref, *refs):
+    out_refs, (total_ref,) = refs[: 2 * SUMS], refs[2 * SUMS :]
+
+    @pl.when(pl.program_id(0) == 0)
+    def _():
+        total_ref[...] = jnp.zeros_like(total_ref)
+
     zero = jnp.zeros((WINDOW_ROWS, WIDE), bf16)
 
-    def visit(g, start, is_first):
+    def visit(n, g, start, is_first):
         rows = pl.ds(start, WINDOW_ROWS)
-        found = tiles_ref[rows, :] == number(g * FOUR, (WINDOW_ROWS, WIDE))
+        found = tiles_ref[rows, :] == first_tile(g, (WINDOW_ROWS, WIDE))
         left = jnp.concatenate(
             [jnp.where(found, anomalies_high_ref[rows, :], zero), jnp.where(found, anomalies_low_ref[rows, :], zero)],
             axis=0,
         )
-        right = jnp.concatenate(
-            [block_ref[pl.ds(g * FOUR + u, GROUP, stride=OWN_TILES), :] for u in range(FOUR)], axis=0
-        )
+        right = block_ref[:, n * EIGHT : (n + 1) * EIGHT, :].reshape(WIDE, LANES)
         both = dot(left, jnp.concatenate(two_parts(right), axis=1))
         both = both[:WINDOW_ROWS] + both[WINDOW_ROWS:]
         total_ref[rows, :] += both[:, :LANES] + both[:, LANES:]
 
-    for_windows(starts_ref, WINDOW_ROWS, 16, visit)
-    for d in range(SUMS):
-        start = ((position_ref[1] + d) & (SUMS - 1)) * CHUNK
-        out_refs[d][...] = total_ref[pl.ds(pl.multiple_of(start, CHUNK), CHUNK), :]
+    for_windows(starts_ref, COVARIANCE_GROUPS, WINDOW_ROWS, 16, visit)
+
+    @pl.when(pl.program_id(0) == pl.num_programs(0) - 1)
+    def _():
+        for d in range(SUMS):
+            to = (position_ref[1] + d) & (SUMS - 1)
+            start = pl.multiple_of(to * FIRST_CHUNK, 16)
+            out_refs[d][...] = total_ref[pl.ds(start, FIRST_CHUNK), :]
+            start = pl.multiple_of(FIRST + to * REST_CHUNK, 16)
+            out_refs[SUMS + d][...] = total_ref[pl.ds(start, REST_CHUNK), :]
 
 
 def covariances(position, starts, block, anomalies_high, anomalies_low, tiles):
+    steps = GROUPS // COVARIANCE_GROUPS
     return pl.pallas_call(
         covariance_kernel,
-        out_shape=(struct((CHUNK, LANES)),) * SUMS,
-        in_specs=[SMEM, SMEM] + [VMEM] * 4,
-        out_specs=(VMEM,) * SUMS,
+        grid=(steps,),
+        out_shape=(struct((FIRST_CHUNK, LANES)),) * SUMS + (struct((REST_CHUNK, LANES)),) * SUMS,
+        in_specs=[SMEM, SMEM, pl.BlockSpec((GROUP, OWN_TILES // steps, LANES), lambda i: (0, i, 0))] + [VMEM] * 3,
+        out_specs=(VMEM,) * (2 * SUMS),
         scratch_shapes=[pltpu.VMEM((PADDED_ROWS, LANES), f32)],
         compiler_params=kernel_params(24),
         cost_estimate=pl.CostEstimate(flops=3 * 10**9, bytes_accessed=4 * 2**20, transcendentals=0),
         name="covariances",
-    )(position, starts, block.reshape(GROUP * OWN_TILES, LANES), anomalies_high, anomalies_low, tiles)
+    )(position, starts, block, anomalies_high, anomalies_low, tiles)
+
+
+UPDATE_GROUPS = 2
 
 
 def update_kernel(position_ref, starts_ref, *refs):
-    sums_refs = refs[:SUMS]
-    block_ref, factors_high_ref, factors_low_ref, tile_rows_ref, out_ref, right_ref = refs[SUMS:]
-    for d in range(SUMS):
-        start = ((position_ref[1] - d) & (SUMS - 1)) * CHUNK
-        right_ref[pl.ds(pl.multiple_of(start, CHUNK), CHUNK), :] = jnp.concatenate(two_parts(sums_refs[d][...]), axis=1)
-    right_ref[NOBS:, :] = jnp.zeros((WINDOW_COLUMNS, 2 * LANES), bf16)
-    zero = jnp.zeros((GROUP, WINDOW_COLUMNS), bf16)
-
-    def visit(g, start, is_first):
+    sums_refs = refs[: 2 * SUMS]
+    block_ref, factors_high_ref, factors_low_ref, tile_rows_ref, out_ref, right_ref = refs[2 * SUMS :]
+
+    @pl.when(pl.program_id(0) == 0)
+    def _():
+        for d in range(SUMS):
+            of = (position_ref[1] - d) & (SUMS - 1)
+            start = pl.multiple_of(of * FIRST_CHUNK, 16)
+            right_ref[pl.ds(start, FIRST_CHUNK), :] = jnp.concatenate(two_parts(sums_refs[d][...]), axis=1)
+            start = pl.multiple_of(FIRST + of * REST_CHUNK, 16)
+            right_ref[pl.ds(start, REST_CHUNK), :] = jnp.concatenate(two_parts(sums_refs[SUMS + d][...]), axis=1)
+        right_ref[NOBS:, :] = jnp.zeros((WINDOW_COLUMNS, 2 * LANES), bf16)
+
+    def visit(n, g, start, is_first):
         columns = pl.ds(start, WINDOW_COLUMNS)
-        tiles = tile_rows_ref[:, columns]
-        high = factors_high_ref[:, columns]
-        low = factors_low_ref[:, columns]
-        found = [tiles == number(g * FOUR + u, (GROUP, WINDOW_COLUMNS)) for u in range(FOUR)]
-        left = [jnp.where(f, high, zero) for f in found] + [jnp.where(f, low, zero) for f in found]
+        found = tile_rows_ref[:, columns] == first_tile(g, (16, WINDOW_COLUMNS))
+        found = jnp.where(found, jnp.ones((16, WINDOW_COLUMNS), bf16), jnp.zeros((16, WINDOW_COLUMNS), bf16))
+        left = [
+            (ref[:, columns].reshape(WIDE // 16, 16, WINDOW_COLUMNS) * found[None]).reshape(WIDE, WINDOW_COLUMNS)
+            for ref in (factors_high_ref, factors_low_ref)
+        ]
         both = dot(jnp.concatenate(left, axis=0), right_ref[columns, :])
         both = both[:WIDE] + both[WIDE:]
-        change = both[:, :LANES] + both[:, LANES:]
-        for u in range(FOUR):
-            rows = pl.ds(g * FOUR + u, GROUP, stride=OWN_TILES)
-            before = block_ref if is_first else out_ref
-            out_ref[rows, :] = before[rows, :] + change[u * GROUP : (u + 1) * GROUP]
-
-    for_windows(starts_ref, WINDOW_COLUMNS, LANES, visit)
+        change = (both[:, :LANES] + both[:, LANES:]).reshape(GROUP, EIGHT, LANES)
+        here = slice(n * EIGHT, (n + 1) * EIGHT)
+        out_ref[:, here, :] = (block_ref if is_first else out_ref)[:, here, :] + change
+
+    for_windows(starts_ref, UPDATE_GROUPS, WINDOW_COLUMNS, LANES, visit)
 
 
 def updated(position, starts, sums, block, factors_high, factors_low, tile_rows):
-    out = pl.pallas_call(
+    steps = GROUPS // UPDATE_GROUPS
+    by_tiles = pl.BlockSpec((GROUP, OWN_TILES // steps, LANES), lambda i: (0, i, 0))
+    return pl.pallas_call(
         update_kernel,
-        out_shape=struct((GROUP * OWN_TILES, LANES)),
-        in_specs=[SMEM, SMEM] + [VMEM] * (SUMS + 4),
-        out_specs=VMEM,
+        grid=(steps,),
+        out_shape=struct((GROUP, OWN_TILES, LANES)),
+        in_specs=[SMEM, SMEM] + [VMEM] * (2 * SUMS) + [by_tiles] + [VMEM] * 3,
+        out_specs=by_tiles,
         scratch_shapes=[pltpu.VMEM((PADDED_COLUMNS, 2 * LANES), bf16)],
-        compiler_params=kernel_params(32),
+        compiler_params=kernel_params(24),
         cost_estimate=pl.CostEstimate(flops=4 * 10**9, bytes_accessed=8 * 2**20, transcendentals=0),
         name="updated",
-    )(position, starts, *sums, block.reshape(GROUP * OWN_TILES, LANES), factors_high, factors_low, tile_rows)
-    return out.reshape(GROUP, OWN_TILES, LANES)
+    )(position, starts, *sums, block, factors_high, factors_low, tile_rows)
 
 
 def exchange(value, axes=PEERS):
@@ -412,6 +438,13 @@
 
 def passed_along(value, by):
     return lax.ppermute(value, "h", [(i, (i + by) % SUMS) for i in range(SUMS)])
+
+
+def summed(parts):
+    total = parts[0]
+    for by in range(1, SUMS):
+        total = total + passed_along(parts[by], by)
+    return (total, *(passed_along(total, by) for by in range(1, SUMS)))
 
 
 def shards(state, locations, tile_mask, plan, obs_value, obs_error):
@@ -434,9 +467,10 @@
     payload = jnp.concatenate(
         [*(each[0:8] for each in all_four), sum(each[8:12] for each in all_four), jnp.zeros((4, LANES), f32)], axis=0
     )
+    block, payload = lax.optimization_barrier((spread_out(rows), payload))
     gathered = exchange(jnp.broadcast_to(payload[None], (GROUP_CHIPS, 40, LANES)), CHIPS)
     other = lax.ppermute(gathered, "c", [(0, 1), (1, 0)])
-    block, other = lax.optimization_barrier((spread_out(rows), other))
+    block, other = lax.optimization_barrier((block, other))
     block = exchange(block)
 
     facts = jnp.concatenate(
@@ -447,13 +481,13 @@
     )
     nth_own = (residue - tiles + RADIUS) & (RESIDUES - 1)
     own_tile = jnp.where(nth_own < WINDOW, ((tiles - RADIUS + nth_own) & (NTILES - 1)) // RESIDUES, OWN_TILES)
-    starts = jnp.sum(own_tile[None, :] < FOUR * jnp.arange(GROUPS + 1, dtype=i32)[:, None], axis=1, dtype=i32)
+    starts = jnp.sum(own_tile[None, :] < EIGHT * jnp.arange(GROUPS + 1, dtype=i32)[:, None], axis=1, dtype=i32)
+    nth_all = (jnp.arange(RESIDUES, dtype=i32)[:, None] - tiles[None, :] + RADIUS) & (RESIDUES - 1)
+    most = jnp.max(jnp.sum(nth_all < WINDOW, axis=1, dtype=i32))
 
     parts = covariances(position, starts, block, anomalies_high, anomalies_low, sorted_tiles)
-    total = parts[0]
-    for by in range(1, SUMS):
-        total = total + passed_along(parts[by], by)
-    sums = [total] + [passed_along(total, by) for by in range(1, SUMS)]
+    rest = lax.cond(most > FIRST, summed, lambda parts: parts, parts[SUMS:])
+    sums = summed(parts[:SUMS]) + tuple(rest)
     block = exchange(updated(position, starts, sums, block, factors_high, factors_low, tile_rows))
     return collect(block).reshape(state.shape)
 

time: 232 us -> 225 us (0.970)
  waiting for transfers between devices: 61.5 us -> 49.9 us
  local copies, waits for them, and re-layouts: 10 us -> 18.7 us
  Pallas kernels: 36.2 us -> 33.4 us
    unnamed x20 -> x32, local copies, waits for them, and re-layouts: 8.42 us -> 17.2 us
    ppermute x9, waiting for transfers between devices: 17.7 us -> 10.5 us  [passed_along(): return lax.ppermute(value, 'h', [(i, (i + by) % SUMS) for i in range(SUMS)])]
    all_to_all x2, waiting for transfers between devices: 43.8 us -> 37.7 us  [exchange(): return lax.all_to_all(value, axes, 0, 0, tiled=True)]
    pallas_call x2, Pallas kernels: 15.4 us -> 12 us  [the longest x1 7.06 us: updated(): pl.pallas_call(update_kernel, grid=(steps,), out_shape=struct((GROUP, OWN...]
  transfers between devices with their start and end apart: 12 -> 12, of which waited for: 6 -> 7; matrix products, arithmetic and copies ran while one was open for 0% -> 1% of each run, Pallas kernels for 7% -> 7%
where the time goes in v5:
time: 225 us; the launch traced here: 224 us
  blocking collectives  79.7 us (35%)
  waiting for transfers between devices  49.9 us (22%)
  starting transfers between devices  38.8 us (17%)
  Pallas kernels  33.4 us (15%)
  local copies, waits for them, and re-layouts  18.7 us (8%)
  other arithmetic  2.82 us (1%)
    all_to_all x2, blocking collectives, exchange(): return lax.all_to_all(value, axes, 0, 0, tiled=True)  79.7 us
    all_to_all x2, waiting for transfers between devices, exchange(): return lax.all_to_all(value, axes, 0, 0, tiled=True)  37.7 us
    ppermute x9, starting transfers between devices, passed_along(): return lax.ppermute(value, 'h', [(i, (i + by) % SUMS) for i in range(SUMS)])  20.2 us
    unnamed x32, local copies, waits for them, and re-layouts  17.2 us
    all_to_all x2, starting transfers between devices, exchange(): return lax.all_to_all(value, axes, 0, 0, tiled=True)  14.8 us
    pallas_call x1, Pallas kernels, observations(): pl.pallas_call(observation_kernel, out_shape=(columns, columns, columns,...  10.7 us
    ppermute x9, waiting for transfers between devices, passed_along(): return lax.ppermute(value, 'h', [(i, (i + by) % SUMS) for i in range(SUMS)])  10.5 us
    pallas_call x2, Pallas kernels, reordered(): pl.pallas_call(kernel, grid=(OWN_TILES // BLOCK_TILES,), out_shape=struct...  7.56 us
  transfers between devices with their start and end apart: 12, of which 7 were waited for; matrix products, arithmetic and copies ran while one was open for 1% of the time, Pallas kernels for 7%

profile of v5, /device:TPU:1, one launch (start us, length us, event | category | flops | bytes accessed | tf_op | source)
XLA Modules:
  0.0 224.0 jit_solution(16505832828908359791)
XLA Ops:
  0.0 0.1 and.157
  0.1 0.1 and.158
  0.2 0.1 add.124
  0.3 1.1 fusion.32
  1.4 0.7 add_select_fusion.1
  2.1 0.9 fusion.1
  3.0 9.2 %all-to-all-start = ((f32[32,4,128]{2,1,0:T(4,128)}), f32[32,4,128]{2,1,0:T(4,128)S(1)}, u32[]{:S(2)}, u32[]{:S(2)}) async-start(f32[32,4,128]{2,1,0:T(4,128)} %fusion.1), calls=%async_computation | async-start | bytes 131072 | tf_op jit(solution)/shard_map/all_to_all | solution.py:436
  12.3 0.0 copy-start
  12.3 2.2 copy-done
  14.4 0.0 copy-start.3
  14.4 0.7 copy-done.3
  15.1 0.7 copy-done.4
  15.8 3.1 %own_columns.1 = f32[8,128]{1,0:T(8,128)S(1)} custom-call(s32[1024]{0:T(1024)S(1)} %copy-done.4, s32[1024]{0:T(1024)S(1)} %copy-done.3, f32[8192,128]{1,0:T(8,128)S(1)} %bitcast.120), custom_call_target="tpu_custom_call" | custom-call | flops 1000000 | bytes 8388608 | tf_op jit(solution)/shard_map/own_columns/pallas_call | solution.py:108
  18.9 0.7 all-to-all-done
  19.6 5.2 %collective-permute-start.8 = (f32[12,128]{1,0:T(8,128)S(1)}, f32[12,128]{1,0:T(8,128)S(1)}, u32[]{:S(2)}, u32[]{:S(2)}) collective-permute-start(f32[12,128]{1,0:T(8,128)S(1)} %pad_maximum_fusion), channel_id=1, source_target_pairs={{0,48},{16,0},{32,16},{48,32},{1,49},{17,1},{33,17},{49,33},{2,50}... | collective-permute-start | bytes 18440 | tf_op jit(solution)/shard_map/ppermute | solution.py:440
  24.8 1.2 collective-permute-start.7
  26.0 2.1 collective-permute-start.6
  28.1 2.2 copy-done.1
  30.3 2.8 %spread_out.1 = f32[64,128,128]{2,1,0:T(8,128)S(1)} custom-call(f32[8192,128]{1,0:T(8,128)S(1)} %bitcast.121), custom_call_target="tpu_custom_call" | custom-call | flops 1000000 | bytes 8388608 | tf_op jit(solution)/shard_map/spread_out/pallas_call | solution.py:134
  33.1 0.0 copy-start.2
  33.1 2.0 copy-done.2
  35.1 0.0 collective-permute-done.8
  35.1 0.0 collective-permute-done.7
  35.1 0.0 collective-permute-done.6
  35.2 16.8 %all_to_all.20 = f32[32,40,128]{2,1,0:T(8,128)S(1)} all-to-all(f32[32,40,128]{2,1,0:T(8,128)S(1)} %broadcast_in_dim.144), channel_id=1, replica_groups=mesh['y'=4,'h'=4,'l'=2,'c'=2,'x'=4] {'y','l','x'}, dimensions={0} | all-to-all | bytes 1310720 | tf_op jit(solution)/shard_map/all_to_all | solution.py:436
  52.0 3.7 %collective-permute-start.9 = (f32[32,40,128]{2,1,0:T(8,128)S(1)}, f32[32,40,128]{2,1,0:T(8,128)S(1)}, u32[]{:S(2)}, u32[]{:S(2)}) collective-permute-start(f32[32,40,128]{2,1,0:T(8,128)S(1)} %all_to_all.20), channel_id=1, source_target_pairs={{0,4},{4,0},{1,5},{5,1},{2,6},{6,2},{3,7},{7,3},{8,12},{12,8},{9,1... | collective-permute-start | bytes 1966088 | tf_op jit(solution)/shard_map/ppermute | solution.py:472
  55.7 1.7 collective-permute-done.9
  57.5 5.6 %all-to-all-start.2 = ((f32[64,128,128]{2,1,0:T(8,128)}), f32[64,128,128]{2,1,0:T(8,128)}, u32[]{:S(2)}, u32[]{:S(2)}) async-start(f32[64,128,128]{2,1,0:T(8,128)} %copy-done.2), calls=%async_computation.2 | async-start | bytes 8388608 | tf_op jit(solution)/shard_map/all_to_all | solution.py:436
  63.1 0.1 convert_reduce_fusion.1
  63.2 0.6 reduce_max.9
  64.4 0.1 pad.3.clone
  64.5 0.1 pad_add_fusion.position_ref
  64.6 0.2 convert_reduce_fusion.starts_ref
  64.8 0.0 copy-done.14
  64.8 0.0 copy-done.15
  64.8 0.1 maximum_maximum_fusion.facts_ref
  64.9 0.0 copy-done.5
  64.9 10.7 %observations.1 = (bf16[1152,512]{1,0:T(8,128)(2,1)S(1)}, bf16[1152,512]{1,0:T(8,128)(2,1)S(1)}, bf16[1152,512]{1,0:T(8,128)(2,1)S(1)}, bf16[512,1280]{1,0:T(8,1...) custom-call(s32[3]{0:T(128)S(1)} %pad_add_fusion.position_ref, s32[1,1024]{1,0:T(1,128)S(1)} %bitcast.123, ...), custom_call_target="tpu_custom_call" | custom-call | flops 20000000000 | bytes 8388608 | tf_op jit(solution)/shard_map/observations/pallas_call | solution.py:289
  75.6 0.0 copy-start.6
  75.6 1.1 copy-done.6
  76.7 1.0 copy-done.8
  77.8 1.0 copy-done.10
  78.8 1.1 copy-done.12
  79.9 37.0 %all-to-all-done.2.block_ref.refs_8_ = f32[64,128,128]{2,1,0:T(8,128)} async-done(((f32[64,128,128]{2,1,0:T(8,128)}), f32[64,128,128]{2,1,0:T(8,128)}, u32[]{:S(2)}, u32[]{:S(2)}) %all-to-all-start.2) | async-done | bytes 4194336 | tf_op jit(solution)/shard_map/all_to_all | solution.py:436
  116.9 1.3 copy-done.9
  118.2 1.3 copy-done.11
  119.5 1.3 copy-done.13
  120.7 4.9 %covariances.1 = (f32[160,128]{1,0:T(8,128)S(1)}, f32[160,128]{1,0:T(8,128)S(1)}, f32[160,128]{1,0:T(8,128)S(1)}, f32[160,128]{1,0:T(8,128)S(1)}, f32[96,128]{1,...) custom-call(s32[3]{0:T(128)S(1)} %pad_add_fusion.position_ref, ...), custom_call_target="tpu_custom_call" | custom-call | flops 3000000000 | bytes 4194304 | tf_op jit(solution)/shard_map/covariances/pallas_call | solution.py:372
  125.7 2.4 %collective-permute-start.10 = (f32[160,128]{1,0:T(8,128)S(1)}, f32[160,128]{1,0:T(8,128)S(1)}, u32[]{:S(2)}, u32[]{:S(2)}) collective-permute-start(f32[160,128]{1,0:T(8,128)S(1)} %get-tuple-element.55), channel_id=1, source_target_pairs={{0,16},{16,32},{32,48},{48,0},{1,17},{17,33},{33,49},{49,1},{2,18}... | collective-permute-start | bytes 245768 | tf_op jit(solution)/shard_map/ppermute | solution.py:440
  128.1 1.2 collective-permute-start.11
  129.2 2.4 %collective-permute-start.12 = (f32[160,128]{1,0:T(8,128)S(1)}, f32[160,128]{1,0:T(8,128)S(1)}, u32[]{:S(2)}, u32[]{:S(2)}) collective-permute-start(f32[160,128]{1,0:T(8,128)S(1)} %get-tuple-element.57), channel_id=1, source_target_pairs={{0,48},{16,0},{32,16},{48,32},{1,49},{17,1},{33,17},{49,33},{2,50}... | collective-permute-start | bytes 245768 | tf_op jit(solution)/shard_map/ppermute | solution.py:440
  131.6 0.0 collective-permute-done.10
  131.6 3.8 %collective-permute-done.11 = f32[160,128]{1,0:T(8,128)S(1)} collective-permute-done((f32[160,128]{1,0:T(8,128)S(1)}, f32[160,128]{1,0:T(8,128)S(1)}, u32[]{:S(2)}, u32[]{:S(2)}) %collective-permute-start.11) | collective-permute-done | bytes 81952 | tf_op jit(solution)/shard_map/ppermute | solution.py:440
  135.4 0.0 collective-permute-done.12
  135.4 2.8 %collective-permute-start.15 = (f32[160,128]{1,0:T(8,128)S(1)}, f32[160,128]{1,0:T(8,128)S(1)}, u32[]{:S(2)}, u32[]{:S(2)}) collective-permute-start(f32[160,128]{1,0:T(8,128)S(1)} %add_add_fusion.1.refs_0_), channel_id=1, source_target_pairs={{0,48},{16,0},{32,16},{48,32},{1,49},{17,1},{33,17},{49,33},{2,50}... | collective-permute-start | bytes 245768 | tf_op jit(solution)/shard_map/ppermute | solution.py:440
  138.3 2.9 %collective-permute-start.14 = (f32[160,128]{1,0:T(8,128)S(1)}, f32[160,128]{1,0:T(8,128)S(1)}, u32[]{:S(2)}, u32[]{:S(2)}) collective-permute-start(f32[160,128]{1,0:T(8,128)S(1)} %add_add_fusion.1.refs_0_), channel_id=1, source_target_pairs={{0,32},{16,48},{32,0},{48,16},{1,33},{17,49},{33,1},{49,17},{2,34}... | collective-permute-start | bytes 245768 | tf_op jit(solution)/shard_map/ppermute | solution.py:440
  141.2 0.0 collective-permute-start.13
  141.2 3.3 %collective-permute-done.15.refs_3_ = f32[160,128]{1,0:T(8,128)S(1)} collective-permute-done((f32[160,128]{1,0:T(8,128)S(1)}, f32[160,128]{1,0:T(8,128)S(1)}, u32[]{:S(2)}, u32[]{:S(2)}) %collective-permute-start.15) | collective-permute-done | bytes 81952 | tf_op jit(solution)/shard_map/ppermute | solution.py:440
  144.5 1.7 collective-permute-done.14.refs_2_
  146.2 1.7 collective-permute-done.13.refs_1_
  147.9 1.3 copy-done.7
  149.2 7.1 %updated.1 = f32[64,128,128]{2,1,0:T(8,128)S(1)} custom-call(s32[3]{0:T(128)S(1)} %pad_add_fusion.position_ref, s32[17]{0:T(128)S(1)} %convert_reduce_fusion.starts_ref, f32[160,128]{1,0:T(8,128)S(1)} %add_add_fusion.1.refs_0_, f32[160,128]{1,0:T(8,128)S(1)} %collective-permute-done.13.refs_1_, f32[160,128]{1,0:T(8,128)S(1)} %collective-permute-done.14.refs_2_, ...), custom_call_target="tpu_custom_call" | custom-call | flops 4000000000 | bytes 8388608 | tf_op jit(solution)/shard_map/updated/pallas_call | solution.py:422
  156.3 62.9 %all_to_all.21.in_ref = f32[64,128,128]{2,1,0:T(8,128)S(1)} all-to-all(f32[64,128,128]{2,1,0:T(8,128)S(1)} %updated.1), channel_id=1, replica_groups=mesh['y'=4,'h'=4,'l'=2,'c'=2,'x'=4] {'c','y','l','x'}, dimensions={0} | all-to-all | bytes 8388608 | tf_op jit(solution)/shard_map/all_to_all | solution.py:436
  219.2 4.8 %collect.1 = f32[8192,128]{1,0:T(8,128)} custom-call(f32[64,128,128]{2,1,0:T(8,128)S(1)} %all_to_all.21.in_ref), custom_call_target="tpu_custom_call" | custom-call | flops 1000000 | bytes 8388608 | tf_op jit(solution)/shard_map/collect/pallas_call | solution.py:134
  (27 shorter events, 0.2 us)
Async XLA Ops:
  3.0 16.6 %all-to-all-start = ((f32[32,4,128]{2,1,0:T(4,128)}), f32[32,4,128]{2,1,0:T(4,128)S(1)}, u32[]{:S(2)}, u32[]{:S(2)}) async-start(f32[32,4,128]{2,1,0:T(4,128)} %fusion.1), calls=%async_computation | async-start | bytes 131072 | tf_op jit(solution)/shard_map/all_to_all | solution.py:436
  12.3 2.2 copy-start
  14.4 0.7 copy-start.3
  15.1 0.7 copy-start.4
  19.6 15.5 %collective-permute-start.8 = (f32[12,128]{1,0:T(8,128)S(1)}, f32[12,128]{1,0:T(8,128)S(1)}, u32[]{:S(2)}, u32[]{:S(2)}) collective-permute-start(f32[12,128]{1,0:T(8,128)S(1)} %pad_maximum_fusion), channel_id=1, source_target_pairs={{0,48},{16,0},{32,16},{48,32},{1,49},{17,1},{33,17},{49,33},{2,50}... | collective-permute-start | bytes 18440 | tf_op jit(solution)/shard_map/ppermute | solution.py:440
  24.8 10.3 %collective-permute-start.7 = (f32[12,128]{1,0:T(8,128)S(1)}, f32[12,128]{1,0:T(8,128)S(1)}, u32[]{:S(2)}, u32[]{:S(2)}) collective-permute-start(f32[12,128]{1,0:T(8,128)S(1)} %pad_maximum_fusion), channel_id=1, source_target_pairs={{0,32},{16,48},{32,0},{48,16},{1,33},{17,49},{33,1},{49,17},{2,34}... | collective-permute-start | bytes 18440 | tf_op jit(solution)/shard_map/ppermute | solution.py:440
  26.0 9.1 %collective-permute-start.6 = (f32[12,128]{1,0:T(8,128)S(1)}, f32[12,128]{1,0:T(8,128)S(1)}, u32[]{:S(2)}, u32[]{:S(2)}) collective-permute-start(f32[12,128]{1,0:T(8,128)S(1)} %pad_maximum_fusion), channel_id=1, source_target_pairs={{0,16},{16,32},{32,48},{48,0},{1,17},{17,33},{33,49},{49,1},{2,18}... | collective-permute-start | bytes 18440 | tf_op jit(solution)/shard_map/ppermute | solution.py:440
  28.1 2.2 copy-start.1
  33.1 2.0 copy-start.2
  52.0 12.8 %copy-start.14 = (f32[1024]{0:T(1024)S(1)}, f32[1024]{0:T(1024)}, u32[]{:S(2)}) copy-start(f32[1024]{0:T(1024)} %param.13) | copy-start | bytes 12292
  52.0 12.8 %copy-start.15 = (f32[1024]{0:T(1024)S(1)}, f32[1024]{0:T(1024)}, u32[]{:S(2)}) copy-start(f32[1024]{0:T(1024)} %param.12) | copy-start | bytes 12292
  52.0 12.9 %copy-start.5 = (s32[1024]{0:T(1024)S(1)}, s32[1024]{0:T(1024)}, u32[]{:S(2)}) copy-start(s32[1024]{0:T(1024)} %plan_ref.1) | copy-start | bytes 12292
  52.0 5.4 %collective-permute-start.9 = (f32[32,40,128]{2,1,0:T(8,128)S(1)}, f32[32,40,128]{2,1,0:T(8,128)S(1)}, u32[]{:S(2)}, u32[]{:S(2)}) collective-permute-start(f32[32,40,128]{2,1,0:T(8,128)S(1)} %all_to_all.20), channel_id=1, source_target_pairs={{0,4},{4,0},{1,5},{5,1},{2,6},{6,2},{3,7},{7,3},{8,12},{12,8},{9,1... | collective-permute-start | bytes 1966088 | tf_op jit(solution)/shard_map/ppermute | solution.py:472
  57.5 59.4 %all-to-all-start.2 = ((f32[64,128,128]{2,1,0:T(8,128)}), f32[64,128,128]{2,1,0:T(8,128)}, u32[]{:S(2)}, u32[]{:S(2)}) async-start(f32[64,128,128]{2,1,0:T(8,128)} %copy-done.2), calls=%async_computation.2 | async-start | bytes 8388608 | tf_op jit(solution)/shard_map/all_to_all | solution.py:436
  75.6 1.1 copy-start.6
  76.7 1.0 copy-start.8
  77.8 1.0 copy-start.10
  78.8 1.1 copy-start.12
  116.9 1.3 copy-start.9
  118.2 1.3 copy-start.11
  119.5 1.3 copy-start.13
  125.7 6.0 %collective-permute-start.10 = (f32[160,128]{1,0:T(8,128)S(1)}, f32[160,128]{1,0:T(8,128)S(1)}, u32[]{:S(2)}, u32[]{:S(2)}) collective-permute-start(f32[160,128]{1,0:T(8,128)S(1)} %get-tuple-element.55), channel_id=1, source_target_pairs={{0,16},{16,32},{32,48},{48,0},{1,17},{17,33},{33,49},{49,1},{2,18}... | collective-permute-start | bytes 245768 | tf_op jit(solution)/shard_map/ppermute | solution.py:440
  128.1 7.4 %collective-permute-start.11 = (f32[160,128]{1,0:T(8,128)S(1)}, f32[160,128]{1,0:T(8,128)S(1)}, u32[]{:S(2)}, u32[]{:S(2)}) collective-permute-start(f32[160,128]{1,0:T(8,128)S(1)} %get-tuple-element.56), channel_id=1, source_target_pairs={{0,32},{16,48},{32,0},{48,16},{1,33},{17,49},{33,1},{49,17},{2,34}... | collective-permute-start | bytes 245768 | tf_op jit(solution)/shard_map/ppermute | solution.py:440
  129.2 6.2 %collective-permute-start.12 = (f32[160,128]{1,0:T(8,128)S(1)}, f32[160,128]{1,0:T(8,128)S(1)}, u32[]{:S(2)}, u32[]{:S(2)}) collective-permute-start(f32[160,128]{1,0:T(8,128)S(1)} %get-tuple-element.57), channel_id=1, source_target_pairs={{0,48},{16,0},{32,16},{48,32},{1,49},{17,1},{33,17},{49,33},{2,50}... | collective-permute-start | bytes 245768 | tf_op jit(solution)/shard_map/ppermute | solution.py:440
  135.4 9.1 %collective-permute-start.15 = (f32[160,128]{1,0:T(8,128)S(1)}, f32[160,128]{1,0:T(8,128)S(1)}, u32[]{:S(2)}, u32[]{:S(2)}) collective-permute-start(f32[160,128]{1,0:T(8,128)S(1)} %add_add_fusion.1.refs_0_), channel_id=1, source_target_pairs={{0,48},{16,0},{32,16},{48,32},{1,49},{17,1},{33,17},{49,33},{2,50}... | collective-permute-start | bytes 245768 | tf_op jit(solution)/shard_map/ppermute | solution.py:440
  138.3 7.9 %collective-permute-start.14 = (f32[160,128]{1,0:T(8,128)S(1)}, f32[160,128]{1,0:T(8,128)S(1)}, u32[]{:S(2)}, u32[]{:S(2)}) collective-permute-start(f32[160,128]{1,0:T(8,128)S(1)} %add_add_fusion.1.refs_0_), channel_id=1, source_target_pairs={{0,32},{16,48},{32,0},{48,16},{1,33},{17,49},{33,1},{49,17},{2,34}... | collective-permute-start | bytes 245768 | tf_op jit(solution)/shard_map/ppermute | solution.py:440
  141.2 6.7 %collective-permute-start.13 = (f32[160,128]{1,0:T(8,128)S(1)}, f32[160,128]{1,0:T(8,128)S(1)}, u32[]{:S(2)}, u32[]{:S(2)}) collective-permute-start(f32[160,128]{1,0:T(8,128)S(1)} %add_add_fusion.1.refs_0_), channel_id=1, source_target_pairs={{0,16},{16,32},{32,48},{48,0},{1,17},{17,33},{33,49},{49,1},{2,18}... | collective-permute-start | bytes 245768 | tf_op jit(solution)/shard_map/ppermute | solution.py:440
  147.9 1.3 copy-start.7

commit v6 on v5

--- a/solution.py
+++ b/solution.py
@@ -35,6 +35,9 @@
 WINDOW_COLUMNS = 256
 PADDED_ROWS = NOBS + WINDOW_ROWS
 PADDED_COLUMNS = NOBS + WINDOW_COLUMNS
+LOW = slice(WIDE, 2 * WIDE)
+TILES = slice(2 * WIDE, 2 * WIDE + LANES)
+TILE_ROWS = slice(2 * WIDE, 2 * WIDE + 16)
 NOWHERE = -512
 BLOCK_TILES = 16
 FIRST = 640
@@ -80,6 +83,36 @@
 
 def accurate_dot(a, b):
     return dot_parts(*two_parts(a), *two_parts(b))
+
+
+def masks_kernel(position_ref, locations_ref, tile_mask_ref, out_ref):
+    tiles_here = tile_mask_ref.shape[0]
+    first = position_ref[3] * tiles_here
+    per_row = NOBS // LANES
+    relative = (locations_ref[...] >> 9) - RADIUS - first
+    masks = [
+        jnp.concatenate([tile_mask_ref[i : i + 1, g * LANES : (g + 1) * LANES] for g in range(per_row)], axis=0)
+        for i in range(tiles_here)
+    ]
+    for n in range(16):
+        local = (relative + n) & (NTILES - 1)
+        found = jnp.zeros((per_row, LANES), i32)
+        if n < WINDOW:
+            for i in range(tiles_here):
+                found = jnp.where(local == i, masks[i], found)
+        out_ref[n * per_row : (n + 1) * per_row, :] = found.astype(f32)
+
+
+def own_masks(position, locations, tile_mask):
+    return pl.pallas_call(
+        masks_kernel,
+        out_shape=struct((16 * NOBS // LANES, LANES)),
+        in_specs=[SMEM, VMEM, VMEM],
+        out_specs=VMEM,
+        compiler_params=kernel_params(4),
+        cost_estimate=pl.CostEstimate(flops=10**5, bytes_accessed=10**5, transcendentals=0),
+        name="own_masks",
+    )(position, locations, tile_mask)
 
 
 def columns_kernel(plan_ref, locations_ref, state_ref, out_ref, picked_ref):
@@ -123,8 +156,9 @@
 
 
 def collect_kernel(in_ref, state_ref):
+    rows_ref = in_ref.reshape(GROUP * BLOCK_TILES, LANES)
     for a in range(BLOCK_TILES):
-        state_ref[a * GROUP : (a + 1) * GROUP, :] = in_ref[:, a, :]
+        state_ref[a * GROUP : (a + 1) * GROUP, :] = rows_ref[pl.ds(a, GROUP, stride=BLOCK_TILES), :]
 
 
 def reordered(kernel, value, out_shape, name):
@@ -153,7 +187,7 @@
 
 def observation_kernel(
     position_ref, plan_ref, facts_ref, own_ref, other_ref,
-    anomalies_high_ref, anomalies_low_ref, tiles_ref, factors_high_ref, factors_low_ref, tile_rows_ref,
+    columns_ref, factors_ref,
     ensemble_ref, increments_ref, one_hot_ref, facts_scratch, in_columns_ref,
     turned_ref, links_high_ref, links_low_ref, sort_ref, sort_back_ref,
 ):
@@ -256,14 +290,12 @@
     replicate = jnp.where(
         lax.broadcasted_iota(i32, (GROUP, WIDE), 1) >> 3 == lax.broadcasted_iota(i32, (GROUP, WIDE), 0), 1.0, 0.0
     ).astype(bf16)
-    anomalies_high_ref[0:NOBS, :] = dot(high, replicate).astype(bf16)
-    anomalies_low_ref[0:NOBS, :] = dot(low, replicate).astype(bf16)
-    nth_of_eight = (lax.broadcasted_iota(i32, (NOBS, WIDE), 1) & (EIGHT - 1)).astype(f32)
-    tiles_ref[0:NOBS, :] = (sorted_columns[:, LANES : LANES + 1] - nth_of_eight).astype(bf16)
-    padding = slice(NOBS, PADDED_ROWS)
-    anomalies_high_ref[padding, :] = jnp.zeros((WINDOW_ROWS, WIDE), bf16)
-    anomalies_low_ref[padding, :] = jnp.zeros((WINDOW_ROWS, WIDE), bf16)
-    tiles_ref[padding, :] = jnp.full((WINDOW_ROWS, WIDE), NOWHERE, bf16)
+    columns_ref[0:NOBS, 0:WIDE] = dot(high, replicate).astype(bf16)
+    columns_ref[0:NOBS, LOW] = dot(low, replicate).astype(bf16)
+    nth_of_eight = (lax.broadcasted_iota(i32, (NOBS, LANES), 1) & (EIGHT - 1)).astype(f32)
+    columns_ref[0:NOBS, TILES] = (sorted_columns[:, LANES : LANES + 1] - nth_of_eight).astype(bf16)
+    columns_ref[NOBS:, 0 : 2 * WIDE] = jnp.zeros((WINDOW_ROWS, 2 * WIDE), bf16)
+    columns_ref[NOBS:, TILES] = jnp.full((WINDOW_ROWS, LANES), NOWHERE, bf16)
 
     factors_high, factors_low = two_parts(factors)
     tile_there = jnp.where(own_row < 0, NOWHERE, own_row).astype(f32)
@@ -272,25 +304,23 @@
     replicate = jnp.where(
         lax.broadcasted_iota(i32, (WIDE, GROUP), 0) >> 3 == lax.broadcasted_iota(i32, (WIDE, GROUP), 1), 1.0, 0.0
     ).astype(bf16)
-    factors_high_ref[:, 0:NOBS] = dot(replicate, sorted_rows[0:GROUP].astype(bf16)).astype(bf16)
-    factors_low_ref[:, 0:NOBS] = dot(replicate, sorted_rows[GROUP : 2 * GROUP].astype(bf16)).astype(bf16)
+    factors_ref[0:WIDE, 0:NOBS] = dot(replicate, sorted_rows[0:GROUP].astype(bf16)).astype(bf16)
+    factors_ref[LOW, 0:NOBS] = dot(replicate, sorted_rows[GROUP : 2 * GROUP].astype(bf16)).astype(bf16)
     nth_of_eight = (lax.broadcasted_iota(i32, (16, NOBS), 0) & (EIGHT - 1)).astype(f32)
-    tile_rows_ref[:, 0:NOBS] = (sorted_rows[2 * GROUP : 2 * GROUP + 16] - nth_of_eight).astype(bf16)
-    padding = slice(NOBS, PADDED_COLUMNS)
-    factors_high_ref[:, padding] = jnp.zeros((WIDE, WINDOW_COLUMNS), bf16)
-    factors_low_ref[:, padding] = jnp.zeros((WIDE, WINDOW_COLUMNS), bf16)
-    tile_rows_ref[:, padding] = jnp.full((16, WINDOW_COLUMNS), NOWHERE, bf16)
+    factors_ref[TILE_ROWS, 0:NOBS] = (sorted_rows[2 * GROUP : 2 * GROUP + 16] - nth_of_eight).astype(bf16)
+    factors_ref[0 : 2 * WIDE, NOBS:] = jnp.zeros((2 * WIDE, WINDOW_COLUMNS), bf16)
+    factors_ref[TILE_ROWS, NOBS:] = jnp.full((16, WINDOW_COLUMNS), NOWHERE, bf16)
 
 
 def observations(position, plan, facts, own, other):
-    columns = struct((PADDED_ROWS, WIDE), bf16)
-    factors = struct((WIDE, PADDED_COLUMNS), bf16)
+    columns = struct((PADDED_ROWS, 2 * WIDE + LANES), bf16)
+    factors = struct((2 * WIDE + 16, PADDED_COLUMNS), bf16)
     square = pltpu.VMEM((NOBS, NOBS), bf16)
     return pl.pallas_call(
         observation_kernel,
-        out_shape=(columns, columns, columns, factors, factors, struct((16, PADDED_COLUMNS), bf16)),
+        out_shape=(columns, factors),
         in_specs=[SMEM, VMEM, VMEM, VMEM, VMEM],
-        out_specs=(VMEM,) * 6,
+        out_specs=(VMEM,) * 2,
         scratch_shapes=[
             pltpu.VMEM((MEMBERS, NOBS), f32),
             pltpu.VMEM((MEMBERS, NOBS), f32),
@@ -334,24 +364,30 @@
 COVARIANCE_GROUPS = 4
 
 
-def covariance_kernel(position_ref, starts_ref, block_ref, anomalies_high_ref, anomalies_low_ref, tiles_ref, *refs):
+def covariance_kernel(position_ref, starts_ref, block_ref, columns_ref, *refs):
     out_refs, (total_ref,) = refs[: 2 * SUMS], refs[2 * SUMS :]
 
     @pl.when(pl.program_id(0) == 0)
     def _():
         total_ref[...] = jnp.zeros_like(total_ref)
 
-    zero = jnp.zeros((WINDOW_ROWS, WIDE), bf16)
+    zero = jnp.zeros((WINDOW_ROWS, LANES), bf16)
 
     def visit(n, g, start, is_first):
         rows = pl.ds(start, WINDOW_ROWS)
-        found = tiles_ref[rows, :] == first_tile(g, (WINDOW_ROWS, WIDE))
-        left = jnp.concatenate(
-            [jnp.where(found, anomalies_high_ref[rows, :], zero), jnp.where(found, anomalies_low_ref[rows, :], zero)],
-            axis=0,
-        )
+        found = columns_ref[rows, TILES] == first_tile(g, (WINDOW_ROWS, LANES))
+        left = [
+            jnp.concatenate(
+                [
+                    jnp.where(found, columns_ref[rows, part * WIDE + n * LANES : part * WIDE + (n + 1) * LANES], zero)
+                    for n in range(WIDE // LANES)
+                ],
+                axis=1,
+            )
+            for part in range(2)
+        ]
         right = block_ref[:, n * EIGHT : (n + 1) * EIGHT, :].reshape(WIDE, LANES)
-        both = dot(left, jnp.concatenate(two_parts(right), axis=1))
+        both = dot(jnp.concatenate(left, axis=0), jnp.concatenate(two_parts(right), axis=1))
         both = both[:WINDOW_ROWS] + both[WINDOW_ROWS:]
         total_ref[rows, :] += both[:, :LANES] + both[:, LANES:]
 
@@ -367,19 +403,19 @@
             out_refs[SUMS + d][...] = total_ref[pl.ds(start, REST_CHUNK), :]
 
 
-def covariances(position, starts, block, anomalies_high, anomalies_low, tiles):
+def covariances(position, starts, block, columns):
     steps = GROUPS // COVARIANCE_GROUPS
     return pl.pallas_call(
         covariance_kernel,
         grid=(steps,),
         out_shape=(struct((FIRST_CHUNK, LANES)),) * SUMS + (struct((REST_CHUNK, LANES)),) * SUMS,
-        in_specs=[SMEM, SMEM, pl.BlockSpec((GROUP, OWN_TILES // steps, LANES), lambda i: (0, i, 0))] + [VMEM] * 3,
+        in_specs=[SMEM, SMEM, pl.BlockSpec((GROUP, OWN_TILES // steps, LANES), lambda i: (0, i, 0)), VMEM],
         out_specs=(VMEM,) * (2 * SUMS),
         scratch_shapes=[pltpu.VMEM((PADDED_ROWS, LANES), f32)],
         compiler_params=kernel_params(24),
         cost_estimate=pl.CostEstimate(flops=3 * 10**9, bytes_accessed=4 * 2**20, transcendentals=0),
         name="covariances",
-    )(position, starts, block, anomalies_high, anomalies_low, tiles)
+    )(position, starts, block, columns)
 
 
 UPDATE_GROUPS = 2
@@ -387,7 +423,7 @@
 
 def update_kernel(position_ref, starts_ref, *refs):
     sums_refs = refs[: 2 * SUMS]
-    block_ref, factors_high_ref, factors_low_ref, tile_rows_ref, out_ref, right_ref = refs[2 * SUMS :]
+    block_ref, factors_ref, out_ref, right_ref = refs[2 * SUMS :]
 
     @pl.when(pl.program_id(0) == 0)
     def _():
@@ -401,11 +437,11 @@
 
     def visit(n, g, start, is_first):
         columns = pl.ds(start, WINDOW_COLUMNS)
-        found = tile_rows_ref[:, columns] == first_tile(g, (16, WINDOW_COLUMNS))
+        found = factors_ref[TILE_ROWS, columns] == first_tile(g, (16, WINDOW_COLUMNS))
         found = jnp.where(found, jnp.ones((16, WINDOW_COLUMNS), bf16), jnp.zeros((16, WINDOW_COLUMNS), bf16))
         left = [
-            (ref[:, columns].reshape(WIDE // 16, 16, WINDOW_COLUMNS) * found[None]).reshape(WIDE, WINDOW_COLUMNS)
-            for ref in (factors_high_ref, factors_low_ref)
+            (factors_ref[part, columns].reshape(WIDE // 16, 16, WINDOW_COLUMNS) * found[None]).reshape(WIDE, WINDOW_COLUMNS)
+            for part in (slice(0, WIDE), LOW)
         ]
         both = dot(jnp.concatenate(left, axis=0), right_ref[columns, :])
         both = both[:WIDE] + both[WIDE:]
@@ -416,20 +452,20 @@
     for_windows(starts_ref, UPDATE_GROUPS, WINDOW_COLUMNS, LANES, visit)
 
 
-def updated(position, starts, sums, block, factors_high, factors_low, tile_rows):
+def updated(position, starts, sums, block, factors):
     steps = GROUPS // UPDATE_GROUPS
     by_tiles = pl.BlockSpec((GROUP, OWN_TILES // steps, LANES), lambda i: (0, i, 0))
     return pl.pallas_call(
         update_kernel,
         grid=(steps,),
         out_shape=struct((GROUP, OWN_TILES, LANES)),
-        in_specs=[SMEM, SMEM] + [VMEM] * (2 * SUMS) + [by_tiles] + [VMEM] * 3,
+        in_specs=[SMEM, SMEM] + [VMEM] * (2 * SUMS) + [by_tiles, VMEM],
         out_specs=by_tiles,
         scratch_shapes=[pltpu.VMEM((PADDED_COLUMNS, 2 * LANES), bf16)],
         compiler_params=kernel_params(24),
         cost_estimate=pl.CostEstimate(flops=4 * 10**9, bytes_accessed=8 * 2**20, transcendentals=0),
         name="updated",
-    )(position, starts, *sums, block, factors_high, factors_low, tile_rows)
+    )(position, starts, *sums, block, factors)
 
 
 def exchange(value, axes=PEERS):
@@ -449,26 +485,21 @@
 
 def shards(state, locations, tile_mask, plan, obs_value, obs_error):
     residue = lax.axis_index(PEERS) // SLICES
-    position = jnp.stack([residue, lax.axis_index("h"), lax.axis_index("c")]).astype(i32)
+    position = jnp.stack([residue, lax.axis_index("h"), lax.axis_index("c"), lax.axis_index(ALL)]).astype(i32)
     rows = state.reshape(ROWS, LANES)
 
-    tiles_here = tile_mask.shape[0]
+    masks = own_masks(position, locations.reshape(-1, LANES), tile_mask)
+    masks = exchange(masks.reshape(GROUP_CHIPS, 4, LANES), CHIPS).sum(axis=0)
     tiles = locations // TILE
-    nth = jnp.arange(16, dtype=i32)[:, None]
-    local = (tiles[None, :] - RADIUS + nth - lax.axis_index(ALL) * tiles_here) & (NTILES - 1)
-    masks = jnp.zeros((16, NOBS), i32)
-    for i in range(tiles_here):
-        masks = masks + jnp.where((local == i) & (nth < WINDOW), tile_mask[i][None, :], 0)
-    masks = exchange(masks.astype(f32).reshape(GROUP_CHIPS, 4, LANES), CHIPS).sum(axis=0)
-
-    columns = own_columns(plan, locations, rows)
-    mine = jnp.concatenate([columns, masks], axis=0)
+
+    observed = own_columns(plan, locations, rows)
+    mine = jnp.concatenate([observed, masks], axis=0)
     all_four = [mine] + [passed_along(mine, by) for by in range(1, SUMS)]
     payload = jnp.concatenate(
         [*(each[0:8] for each in all_four), sum(each[8:12] for each in all_four), jnp.zeros((4, LANES), f32)], axis=0
     )
-    block, payload = lax.optimization_barrier((spread_out(rows), payload))
     gathered = exchange(jnp.broadcast_to(payload[None], (GROUP_CHIPS, 40, LANES)), CHIPS)
+    block, gathered = lax.optimization_barrier((spread_out(rows), gathered))
     other = lax.ppermute(gathered, "c", [(0, 1), (1, 0)])
     block, other = lax.optimization_barrier((block, other))
     block = exchange(block)
@@ -476,7 +507,7 @@
     facts = jnp.concatenate(
         [tiles.astype(f32)[None], obs_value[None], obs_error[None], jnp.zeros((5, NOBS), f32)], axis=0
     )
-    anomalies_high, anomalies_low, sorted_tiles, factors_high, factors_low, tile_rows = observations(
+    columns, factors = observations(
         position, plan[None], facts, gathered.reshape(-1, LANES), other.reshape(-1, LANES)
     )
     nth_own = (residue - tiles + RADIUS) & (RESIDUES - 1)
@@ -485,10 +516,10 @@
     nth_all = (jnp.arange(RESIDUES, dtype=i32)[:, None] - tiles[None, :] + RADIUS) & (RESIDUES - 1)
     most = jnp.max(jnp.sum(nth_all < WINDOW, axis=1, dtype=i32))
 
-    parts = covariances(position, starts, block, anomalies_high, anomalies_low, sorted_tiles)
+    parts = covariances(position, starts, block, columns)
     rest = lax.cond(most > FIRST, summed, lambda parts: parts, parts[SUMS:])
     sums = summed(parts[:SUMS]) + tuple(rest)
-    block = exchange(updated(position, starts, sums, block, factors_high, factors_low, tile_rows))
+    block = exchange(updated(position, starts, sums, block, factors))
     return collect(block).reshape(state.shape)
 
 

time: 225 us -> 218 us (0.969)
  blocking collectives: 79.7 us -> 60.1 us
  starting transfers between devices: 38.8 us -> 50.8 us
  waiting for transfers between devices: 49.9 us -> 54.7 us
  local copies, waits for them, and re-layouts: 18.7 us -> 15 us
    all_to_all x2 -> x1, blocking collectives: 79.7 us -> 60.1 us  [exchange(): return lax.all_to_all(value, axes, 0, 0, tiled=True)]
    all_to_all x2 -> x3, starting transfers between devices: 14.8 us -> 21.9 us  [exchange(): return lax.all_to_all(value, axes, 0, 0, tiled=True)]
    ppermute x9, starting transfers between devices: 20.2 us -> 24.9 us  [passed_along(): return lax.ppermute(value, 'h', [(i, (i + by) % SUMS) for i in range(SUMS)])]
    all_to_all x2 -> x3, waiting for transfers between devices: 37.7 us -> 41.7 us  [exchange(): return lax.all_to_all(value, axes, 0, 0, tiled=True)]
    unnamed x32 -> x30, local copies, waits for them, and re-layouts: 17.2 us -> 14.1 us
    pallas_call x1 -> x2, Pallas kernels: 10.7 us -> 11.9 us  [the longest x1 10.7 us: observations(): pl.pallas_call(observation_kernel, out_shape=(columns, factors), in_specs...]
  transfers between devices with their start and end apart: 12 -> 13, of which waited for: 7 -> 9; matrix products, arithmetic and copies ran while one was open for 1% -> 1% of each run, Pallas kernels for 7% -> 8%
where the time goes in v6:
time: 218 us; the launch traced here: 217 us
  blocking collectives  60.1 us (28%)
  waiting for transfers between devices  54.7 us (25%)
  starting transfers between devices  50.8 us (23%)
  Pallas kernels  34.2 us (16%)
  local copies, waits for them, and re-layouts  15 us (7%)
    all_to_all x1, blocking collectives, exchange(): return lax.all_to_all(value, axes, 0, 0, tiled=True)  60.1 us
    all_to_all x3, waiting for transfers between devices, exchange(): return lax.all_to_all(value, axes, 0, 0, tiled=True)  41.7 us
    ppermute x9, starting transfers between devices, passed_along(): return lax.ppermute(value, 'h', [(i, (i + by) % SUMS) for i in range(SUMS)])  24.9 us
    all_to_all x3, starting transfers between devices, exchange(): return lax.all_to_all(value, axes, 0, 0, tiled=True)  21.9 us
    unnamed x30, local copies, waits for them, and re-layouts  14.1 us
    ppermute x9, waiting for transfers between devices, passed_along(): return lax.ppermute(value, 'h', [(i, (i + by) % SUMS) for i in range(SUMS)])  11.3 us
    pallas_call x1, Pallas kernels, observations(): pl.pallas_call(observation_kernel, out_shape=(columns, factors), in_specs...  10.7 us
    pallas_call x1, Pallas kernels, updated(): pl.pallas_call(update_kernel, grid=(steps,), out_shape=struct((GROUP, OWN...  7.11 us
  transfers between devices with their start and end apart: 13, of which 9 were waited for; matrix products, arithmetic and copies ran while one was open for 1% of the time, Pallas kernels for 8%

profile of v6, /device:TPU:1, one launch (start us, length us, event | category | flops | bytes accessed | tf_op | source)
XLA Modules:
  0.0 216.8 jit_solution(14283579376980885116)
XLA Ops:
  0.0 0.1 pad_add_fusion.position_ref
  0.1 0.0 copy-start.3
  0.1 0.7 copy-done.3
  0.8 0.0 copy-start.6
  0.8 0.8 copy-done.6
  1.5 1.2 own_masks.1
  2.7 9.2 %all-to-all-start = ((f32[32,4,128]{2,1,0:T(4,128)}), f32[32,4,128]{2,1,0:T(4,128)S(1)}, u32[]{:S(2)}, u32[]{:S(2)}) async-start(f32[32,4,128]{2,1,0:T(4,128)} %bitcast.6), calls=%async_computation | async-start | bytes 131072 | tf_op jit(solution)/shard_map/all_to_all | solution.py:472
  12.0 0.0 copy-start
  12.0 2.2 %copy-done = f32[1,1048576]{1,0:T(1,128)S(1)} copy-done((f32[1,1048576]{1,0:T(1,128)S(1)}, f32[1,1048576]{1,0:T(1,128)}, u32[]{:S(2)}) %copy-start) | copy-done | bytes 4194328
  14.2 0.0 copy-start.4
  14.2 0.7 copy-done.4
  14.8 0.0 copy-start.7
  14.8 0.7 copy-done.7
  15.5 3.1 %own_columns.1 = f32[8,128]{1,0:T(8,128)S(1)} custom-call(s32[1024]{0:T(1024)S(1)} %copy-done.7, s32[1024]{0:T(1024)S(1)} %copy-done.4, f32[8192,128]{1,0:T(8,128)S(1)} %bitcast.14), custom_call_target="tpu_custom_call" | custom-call | flops 1000000 | bytes 8388608 | tf_op jit(solution)/shard_map/own_columns/pallas_call | solution.py:141
  18.6 0.7 all-to-all-done
  19.3 5.2 %collective-permute-start.8 = (f32[12,128]{1,0:T(8,128)S(1)}, f32[12,128]{1,0:T(8,128)S(1)}, u32[]{:S(2)}, u32[]{:S(2)}) collective-permute-start(f32[12,128]{1,0:T(8,128)S(1)} %pad_maximum_fusion), channel_id=1, source_target_pairs={{0,48},{16,0},{32,16},{48,32},{1,49},{17,1},{33,17},{49,33},{2,50}... | collective-permute-start | bytes 18440 | tf_op jit(solution)/shard_map/ppermute | solution.py:476
  24.5 1.2 collective-permute-start.7
  25.7 2.1 collective-permute-start.6
  27.8 0.0 collective-permute-done.8
  27.8 3.1 %collective-permute-done.7 = f32[12,128]{1,0:T(8,128)S(1)} collective-permute-done((f32[12,128]{1,0:T(8,128)S(1)}, f32[12,128]{1,0:T(8,128)S(1)}, u32[]{:S(2)}, u32[]{:S(2)}) %collective-permute-start.7) | collective-permute-done | bytes 6176 | tf_op jit(solution)/shard_map/ppermute | solution.py:476
  31.0 0.0 collective-permute-done.6
  31.0 0.9 broadcast_in_dim.34
  31.9 7.0 %all-to-all-start.1 = ((f32[32,40,128]{2,1,0:T(8,128)}), f32[32,40,128]{2,1,0:T(8,128)S(1)}, u32[]{:S(2)}, u32[]{:S(2)}) async-start(f32[32,40,128]{2,1,0:T(8,128)} %broadcast_in_dim.34), calls=%async_computation.1 | async-start | bytes 1310720 | tf_op jit(solution)/shard_map/all_to_all | solution.py:472
  38.9 0.0 copy-start.1
  39.0 2.2 %copy-done.1 = f32[1,1048576]{1,0:T(1,128)S(1)} copy-done((f32[1,1048576]{1,0:T(1,128)S(1)}, f32[1,1048576]{1,0:T(1,128)}, u32[]{:S(2)}) %copy-start.1) | copy-done | bytes 4194328
  41.1 2.8 %spread_out.1 = f32[64,128,128]{2,1,0:T(8,128)S(1)} custom-call(f32[8192,128]{1,0:T(8,128)S(1)} %bitcast.15), custom_call_target="tpu_custom_call" | custom-call | flops 1000000 | bytes 8388608 | tf_op jit(solution)/shard_map/spread_out/pallas_call | solution.py:168
  43.9 0.0 copy-start.2
  43.9 2.0 copy-done.2
  46.0 2.7 %all-to-all-done.1 = f32[32,40,128]{2,1,0:T(8,128)S(1)} async-done(((f32[32,40,128]{2,1,0:T(8,128)}), f32[32,40,128]{2,1,0:T(8,128)S(1)}, u32[]{:S(2)}, u32[]{:S(2)}) %all-to-all-start.1) | async-done | bytes 655392 | tf_op jit(solution)/shard_map/all_to_all | solution.py:472
  48.6 4.0 %collective-permute-start.9 = (f32[32,40,128]{2,1,0:T(8,128)S(1)}, f32[32,40,128]{2,1,0:T(8,128)S(1)}, u32[]{:S(2)}, u32[]{:S(2)}) collective-permute-start(f32[32,40,128]{2,1,0:T(8,128)S(1)} %all-to-all-done.1), channel_id=1, source_target_pairs={{0,4},{4,0},{1,5},{5,1},{2,6},{6,2},{3,7},{7,3},{8,12},{12,8},{9,1... | collective-permute-start | bytes 1966088 | tf_op jit(solution)/shard_map/ppermute | solution.py:503
  52.6 1.7 collective-permute-done.9
  54.4 5.6 %all-to-all-start.2 = ((f32[64,128,128]{2,1,0:T(8,128)}), f32[64,128,128]{2,1,0:T(8,128)}, u32[]{:S(2)}, u32[]{:S(2)}) async-start(f32[64,128,128]{2,1,0:T(8,128)} %copy-done.2), calls=%async_computation.2 | async-start | bytes 8388608 | tf_op jit(solution)/shard_map/all_to_all | solution.py:472
  60.0 0.0 copy-done.5
  60.0 0.1 convert_reduce_fusion.1
  60.2 0.6 reduce_max.9
  61.3 0.1 pad.3.clone
  61.4 0.2 convert_reduce_fusion.starts_ref
  61.6 0.0 copy-done.13
  61.6 0.0 copy-done.14
  61.6 0.1 maximum_maximum_fusion.facts_ref
  61.7 0.0 copy-done.8
  61.7 10.7 %observations.1 = (bf16[1152,1152]{1,0:T(8,128)(2,1)S(1)}, bf16[1040,1280]{1,0:T(8,128)(2,1)S(1)}) custom-call(s32[4]{0:T(128)S(1)} %pad_add_fusion.position_ref, s32[1,1024]{1,0:T(1,128)S(1)} %bitcast.18, f32[8,1024]{1,0:T(8,128)S(1)} %maximum_maximum_fusion.facts_ref, f32[1280,128]{1,0:T(8,128)S(1)} %bitcast.16, f32[1280,128]{1,0:T(8,128)S(1)} %bitcast.19), custom_call_target="tpu_custom_call" | custom-call | flops 20000000000 | bytes 8388608 | tf_op jit(solution)/shard_map/observations/pallas_call | solution.py:319
  72.4 0.0 copy-start.9
  72.4 1.5 copy-done.9
  73.9 1.6 copy-done.11
  75.5 38.3 %all-to-all-done.2.block_ref.refs_8_ = f32[64,128,128]{2,1,0:T(8,128)} async-done(((f32[64,128,128]{2,1,0:T(8,128)}), f32[64,128,128]{2,1,0:T(8,128)}, u32[]{:S(2)}, u32[]{:S(2)}) %all-to-all-start.2) | async-done | bytes 4194336 | tf_op jit(solution)/shard_map/all_to_all | solution.py:472
  113.8 1.7 copy-done.12
  115.5 5.2 %covariances.1 = (f32[160,128]{1,0:T(8,128)S(1)}, f32[160,128]{1,0:T(8,128)S(1)}, f32[160,128]{1,0:T(8,128)S(1)}, f32[160,128]{1,0:T(8,128)S(1)}, f32[96,128]{1,...) custom-call(s32[4]{0:T(128)S(1)} %pad_add_fusion.position_ref, ...), custom_call_target="tpu_custom_call" | custom-call | flops 3000000000 | bytes 4194304 | tf_op jit(solution)/shard_map/covariances/pallas_call | solution.py:408
  120.7 0.4 collective-permute-start.10
  121.1 3.4 %collective-permute-start.11 = (f32[160,128]{1,0:T(8,128)S(1)}, f32[160,128]{1,0:T(8,128)S(1)}, u32[]{:S(2)}, u32[]{:S(2)}) collective-permute-start(f32[160,128]{1,0:T(8,128)S(1)} %get-tuple-element.50), channel_id=1, source_target_pairs={{0,32},{16,48},{32,0},{48,16},{1,33},{17,49},{33,1},{49,17},{2,34}... | collective-permute-start | bytes 245768 | tf_op jit(solution)/shard_map/ppermute | solution.py:476
  124.5 3.5 %collective-permute-start.12 = (f32[160,128]{1,0:T(8,128)S(1)}, f32[160,128]{1,0:T(8,128)S(1)}, u32[]{:S(2)}, u32[]{:S(2)}) collective-permute-start(f32[160,128]{1,0:T(8,128)S(1)} %get-tuple-element.51), channel_id=1, source_target_pairs={{0,48},{16,0},{32,16},{48,32},{1,49},{17,1},{33,17},{49,33},{2,50}... | collective-permute-start | bytes 245768 | tf_op jit(solution)/shard_map/ppermute | solution.py:476
  128.0 0.0 collective-permute-done.10
  128.1 0.3 collective-permute-done.11
  128.4 1.2 collective-permute-done.12
  129.6 6.7 %collective-permute-start.15 = (f32[160,128]{1,0:T(8,128)S(1)}, f32[160,128]{1,0:T(8,128)S(1)}, u32[]{:S(2)}, u32[]{:S(2)}) collective-permute-start(f32[160,128]{1,0:T(8,128)S(1)} %add_add_fusion.1.refs_0_), channel_id=1, source_target_pairs={{0,48},{16,0},{32,16},{48,32},{1,49},{17,1},{33,17},{49,33},{2,50}... | collective-permute-start | bytes 245768 | tf_op jit(solution)/shard_map/ppermute | solution.py:476
  136.3 2.4 %collective-permute-start.14 = (f32[160,128]{1,0:T(8,128)S(1)}, f32[160,128]{1,0:T(8,128)S(1)}, u32[]{:S(2)}, u32[]{:S(2)}) collective-permute-start(f32[160,128]{1,0:T(8,128)S(1)} %add_add_fusion.1.refs_0_), channel_id=1, source_target_pairs={{0,32},{16,48},{32,0},{48,16},{1,33},{17,49},{33,1},{49,17},{2,34}... | collective-permute-start | bytes 245768 | tf_op jit(solution)/shard_map/ppermute | solution.py:476
  138.7 0.0 collective-permute-start.13
  138.7 0.9 collective-permute-done.15.refs_3_
  139.6 5.8 %collective-permute-done.14.refs_2_ = f32[160,128]{1,0:T(8,128)S(1)} collective-permute-done((f32[160,128]{1,0:T(8,128)S(1)}, f32[160,128]{1,0:T(8,128)S(1)}, u32[]{:S(2)}, u32[]{:S(2)}) %collective-permute-start.14) | collective-permute-done | bytes 81952 | tf_op jit(solution)/shard_map/ppermute | solution.py:476
  145.4 0.0 collective-permute-done.13.refs_1_
  145.4 0.0 copy-done.10
  145.4 7.1 %updated.1 = f32[64,128,128]{2,1,0:T(8,128)S(1)} custom-call(s32[4]{0:T(128)S(1)} %pad_add_fusion.position_ref, s32[17]{0:T(128)S(1)} %convert_reduce_fusion.starts_ref, f32[160,128]{1,0:T(8,128)S(1)} %add_add_fusion.1.refs_0_, f32[160,128]{1,0:T(8,128)S(1)} %collective-permute-done.13.refs_1_, f32[160,128]{1,0:T(8,128)S(1)} %collective-permute-done.14.refs_2_, ...), custom_call_target="tpu_custom_call" | custom-call | flops 4000000000 | bytes 8388608 | tf_op jit(solution)/shard_map/updated/pallas_call | solution.py:458
  152.5 60.1 %all_to_all.20.in_ref = f32[64,128,128]{2,1,0:T(8,128)S(1)} all-to-all(f32[64,128,128]{2,1,0:T(8,128)S(1)} %updated.1), channel_id=1, replica_groups=mesh['y'=4,'h'=4,'l'=2,'c'=2,'x'=4] {'c','y','l','x'}, dimensions={0} | all-to-all | bytes 8388608 | tf_op jit(solution)/shard_map/all_to_all | solution.py:472
  212.6 4.2 %collect.1 = f32[8192,128]{1,0:T(8,128)} custom-call(f32[64,128,128]{2,1,0:T(8,128)S(1)} %all_to_all.20.in_ref), custom_call_target="tpu_custom_call" | custom-call | flops 1000000 | bytes 8388608 | tf_op jit(solution)/shard_map/collect/pallas_call | solution.py:168
  (20 shorter events, 0.2 us)
Async XLA Ops:
  0.1 0.7 copy-start.3
  0.8 0.8 copy-start.6
  2.7 16.6 %all-to-all-start = ((f32[32,4,128]{2,1,0:T(4,128)}), f32[32,4,128]{2,1,0:T(4,128)S(1)}, u32[]{:S(2)}, u32[]{:S(2)}) async-start(f32[32,4,128]{2,1,0:T(4,128)} %bitcast.6), calls=%async_computation | async-start | bytes 131072 | tf_op jit(solution)/shard_map/all_to_all | solution.py:472
  12.0 2.2 %copy-start = (f32[1,1048576]{1,0:T(1,128)S(1)}, f32[1,1048576]{1,0:T(1,128)}, u32[]{:S(2)}) copy-start(f32[1,1048576]{1,0:T(1,128)} %param.8) | copy-start | bytes 12582916
  14.2 0.7 copy-start.4
  14.8 0.7 copy-start.7
  19.3 8.5 %collective-permute-start.8 = (f32[12,128]{1,0:T(8,128)S(1)}, f32[12,128]{1,0:T(8,128)S(1)}, u32[]{:S(2)}, u32[]{:S(2)}) collective-permute-start(f32[12,128]{1,0:T(8,128)S(1)} %pad_maximum_fusion), channel_id=1, source_target_pairs={{0,48},{16,0},{32,16},{48,32},{1,49},{17,1},{33,17},{49,33},{2,50}... | collective-permute-start | bytes 18440 | tf_op jit(solution)/shard_map/ppermute | solution.py:476
  24.5 6.4 %collective-permute-start.7 = (f32[12,128]{1,0:T(8,128)S(1)}, f32[12,128]{1,0:T(8,128)S(1)}, u32[]{:S(2)}, u32[]{:S(2)}) collective-permute-start(f32[12,128]{1,0:T(8,128)S(1)} %pad_maximum_fusion), channel_id=1, source_target_pairs={{0,32},{16,48},{32,0},{48,16},{1,33},{17,49},{33,1},{49,17},{2,34}... | collective-permute-start | bytes 18440 | tf_op jit(solution)/shard_map/ppermute | solution.py:476
  25.7 5.3 %collective-permute-start.6 = (f32[12,128]{1,0:T(8,128)S(1)}, f32[12,128]{1,0:T(8,128)S(1)}, u32[]{:S(2)}, u32[]{:S(2)}) collective-permute-start(f32[12,128]{1,0:T(8,128)S(1)} %pad_maximum_fusion), channel_id=1, source_target_pairs={{0,16},{16,32},{32,48},{48,0},{1,17},{17,33},{33,49},{49,1},{2,18}... | collective-permute-start | bytes 18440 | tf_op jit(solution)/shard_map/ppermute | solution.py:476
  31.9 16.8 %all-to-all-start.1 = ((f32[32,40,128]{2,1,0:T(8,128)}), f32[32,40,128]{2,1,0:T(8,128)S(1)}, u32[]{:S(2)}, u32[]{:S(2)}) async-start(f32[32,40,128]{2,1,0:T(8,128)} %broadcast_in_dim.34), calls=%async_computation.1 | async-start | bytes 1310720 | tf_op jit(solution)/shard_map/all_to_all | solution.py:472
  38.9 2.2 %copy-start.1 = (f32[1,1048576]{1,0:T(1,128)S(1)}, f32[1,1048576]{1,0:T(1,128)}, u32[]{:S(2)}) copy-start(f32[1,1048576]{1,0:T(1,128)} %param.8) | copy-start | bytes 12582916
  43.9 2.0 copy-start.2
  46.0 14.0 %copy-start.5 = (s32[1024]{0:T(1024)S(1)}, s32[1024]{0:T(1024)}, u32[]{:S(2)}) copy-start(s32[1024]{0:T(1024)} %locations_ref.1) | copy-start | bytes 12292
  46.0 15.6 %copy-start.13 = (f32[1024]{0:T(1024)S(1)}, f32[1024]{0:T(1024)}, u32[]{:S(2)}) copy-start(f32[1024]{0:T(1024)} %param.13) | copy-start | bytes 12292
  46.0 15.6 %copy-start.14 = (f32[1024]{0:T(1024)S(1)}, f32[1024]{0:T(1024)}, u32[]{:S(2)}) copy-start(f32[1024]{0:T(1024)} %param.12) | copy-start | bytes 12292
  46.0 15.7 %copy-start.8 = (s32[1024]{0:T(1024)S(1)}, s32[1024]{0:T(1024)}, u32[]{:S(2)}) copy-start(s32[1024]{0:T(1024)} %plan_ref.1) | copy-start | bytes 12292
  48.6 5.7 %collective-permute-start.9 = (f32[32,40,128]{2,1,0:T(8,128)S(1)}, f32[32,40,128]{2,1,0:T(8,128)S(1)}, u32[]{:S(2)}, u32[]{:S(2)}) collective-permute-start(f32[32,40,128]{2,1,0:T(8,128)S(1)} %all-to-all-done.1), channel_id=1, source_target_pairs={{0,4},{4,0},{1,5},{5,1},{2,6},{6,2},{3,7},{7,3},{8,12},{12,8},{9,1... | collective-permute-start | bytes 1966088 | tf_op jit(solution)/shard_map/ppermute | solution.py:503
  54.4 59.4 %all-to-all-start.2 = ((f32[64,128,128]{2,1,0:T(8,128)}), f32[64,128,128]{2,1,0:T(8,128)}, u32[]{:S(2)}, u32[]{:S(2)}) async-start(f32[64,128,128]{2,1,0:T(8,128)} %copy-done.2), calls=%async_computation.2 | async-start | bytes 8388608 | tf_op jit(solution)/shard_map/all_to_all | solution.py:472
  72.4 1.5 copy-start.9
  73.9 1.6 copy-start.11
  113.8 1.8 copy-start.12
  115.5 29.8 %copy-start.10 = (bf16[1040,1280]{1,0:T(8,128)(2,1)S(1)}, bf16[1040,1280]{1,0:T(8,128)(2,1)}, u32[]{:S(2)}) copy-start(bf16[1040,1280]{1,0:T(8,128)(2,1)} %copy-done.9) | copy-start | bytes 7987204
  120.7 7.4 %collective-permute-start.10 = (f32[160,128]{1,0:T(8,128)S(1)}, f32[160,128]{1,0:T(8,128)S(1)}, u32[]{:S(2)}, u32[]{:S(2)}) collective-permute-start(f32[160,128]{1,0:T(8,128)S(1)} %get-tuple-element.49), channel_id=1, source_target_pairs={{0,16},{16,32},{32,48},{48,0},{1,17},{17,33},{33,49},{49,1},{2,18}... | collective-permute-start | bytes 245768 | tf_op jit(solution)/shard_map/ppermute | solution.py:476
  121.1 7.2 %collective-permute-start.11 = (f32[160,128]{1,0:T(8,128)S(1)}, f32[160,128]{1,0:T(8,128)S(1)}, u32[]{:S(2)}, u32[]{:S(2)}) collective-permute-start(f32[160,128]{1,0:T(8,128)S(1)} %get-tuple-element.50), channel_id=1, source_target_pairs={{0,32},{16,48},{32,0},{48,16},{1,33},{17,49},{33,1},{49,17},{2,34}... | collective-permute-start | bytes 245768 | tf_op jit(solution)/shard_map/ppermute | solution.py:476
  124.5 5.0 %collective-permute-start.12 = (f32[160,128]{1,0:T(8,128)S(1)}, f32[160,128]{1,0:T(8,128)S(1)}, u32[]{:S(2)}, u32[]{:S(2)}) collective-permute-start(f32[160,128]{1,0:T(8,128)S(1)} %get-tuple-element.51), channel_id=1, source_target_pairs={{0,48},{16,0},{32,16},{48,32},{1,49},{17,1},{33,17},{49,33},{2,50}... | collective-permute-start | bytes 245768 | tf_op jit(solution)/shard_map/ppermute | solution.py:476
  129.6 10.1 %collective-permute-start.15 = (f32[160,128]{1,0:T(8,128)S(1)}, f32[160,128]{1,0:T(8,128)S(1)}, u32[]{:S(2)}, u32[]{:S(2)}) collective-permute-start(f32[160,128]{1,0:T(8,128)S(1)} %add_add_fusion.1.refs_0_), channel_id=1, source_target_pairs={{0,48},{16,0},{32,16},{48,32},{1,49},{17,1},{33,17},{49,33},{2,50}... | collective-permute-start | bytes 245768 | tf_op jit(solution)/shard_map/ppermute | solution.py:476
  136.3 9.1 %collective-permute-start.14 = (f32[160,128]{1,0:T(8,128)S(1)}, f32[160,128]{1,0:T(8,128)S(1)}, u32[]{:S(2)}, u32[]{:S(2)}) collective-permute-start(f32[160,128]{1,0:T(8,128)S(1)} %add_add_fusion.1.refs_0_), channel_id=1, source_target_pairs={{0,32},{16,48},{32,0},{48,16},{1,33},{17,49},{33,1},{49,17},{2,34}... | collective-permute-start | bytes 245768 | tf_op jit(solution)/shard_map/ppermute | solution.py:476
  138.7 6.7 %collective-permute-start.13 = (f32[160,128]{1,0:T(8,128)S(1)}, f32[160,128]{1,0:T(8,128)S(1)}, u32[]{:S(2)}, u32[]{:S(2)}) collective-permute-start(f32[160,128]{1,0:T(8,128)S(1)} %add_add_fusion.1.refs_0_), channel_id=1, source_target_pairs={{0,16},{16,32},{32,48},{48,0},{1,17},{17,33},{33,49},{49,1},{2,18}... | collective-permute-start | bytes 245768 | tf_op jit(solution)/shard_map/ppermute | solution.py:476

commit v7 on v6

--- a/solution.py
+++ b/solution.py
@@ -187,9 +187,8 @@
 
 def observation_kernel(
     position_ref, plan_ref, facts_ref, own_ref, other_ref,
-    columns_ref, factors_ref,
-    ensemble_ref, increments_ref, one_hot_ref, facts_scratch, in_columns_ref,
-    turned_ref, links_high_ref, links_low_ref, sort_ref, sort_back_ref,
+    columns_ref, turned_high_ref, turned_low_ref, increments_ref, column_facts_ref, row_facts_ref,
+    ensemble_ref, one_hot_ref, facts_scratch, in_columns_ref, own_turned_ref,
 ):
     core = position_ref[2]
     for d in range(SUMS):
@@ -231,11 +230,10 @@
 
     key_row = jnp.where(own_row < 0, OWN_TILES, own_row) * NOBS + lax.broadcasted_iota(i32, (1, NOBS), 1)
     key_column = jnp.where(own_column < 0, OWN_TILES, own_column) * NOBS + lax.broadcasted_iota(i32, (NOBS, 1), 0)
+    lane = lax.broadcasted_iota(i32, (NOBS, LANES), 1)
     rank_row = jnp.sum(jnp.where(key_column < key_row, 1.0, 0.0), axis=0, keepdims=True).astype(i32)
-    rank_column = jnp.sum(jnp.where(key_row < key_column, 1.0, 0.0), axis=1, keepdims=True).astype(i32)
+    sort_ref = one_hot_ref
     sort_ref[...] = jnp.where(source == rank_row, 1.0, 0.0).astype(bf16)
-    to = lax.broadcasted_iota(i32, (NOBS, NOBS), 1)
-    sort_back_ref[...] = jnp.where(to == rank_column, 1.0, 0.0).astype(bf16)
 
     gain_rows = []
     for b in range(BATCHES):
@@ -254,16 +252,13 @@
         spread_column = jnp.sum(turned * turned, axis=1, keepdims=True) / (MEMBERS - 1) + epsilon
         gain_column = 1.0 / ((MEMBERS - 1) * spread_column)
         turned_high, turned_low = two_parts(turned)
-        turned_ref[here, :] = jnp.concatenate([turned_high[:, 0:GROUP], turned_low[:, 0:GROUP]], axis=1)
+        turned_high_ref[here, :] = turned_high
+        turned_low_ref[here, :] = turned_low
+        own_turned_ref[here, :] = jnp.concatenate([turned_high[:, 0:GROUP], turned_low[:, 0:GROUP]], axis=1)
         gain_rows.append(1.0 / ((MEMBERS - 1) * spread))
-        weight = mask_column[here] * gain_column
-        if b > 0:
-            before = b * BATCH_OBS
-            links = accurate_dot(turned, increments_ref[:, 0:before])
-            links = jnp.where(own_column[here] == own_row[:, 0:before], links * weight, 0.0)
-            links_high, links_low = two_parts(links)
-            links_high_ref[here, 0:before] = links_high
-            links_low_ref[here, 0:before] = links_low
+        column_facts_ref[here, :] = jnp.where(
+            lane[here] == 0, mask_column[here] * gain_column, own_column[here].astype(f32)
+        )
         if b < BATCHES - 1:
             after = slice((b + 1) * BATCH_OBS, NOBS)
             later = ensemble_ref[:, after]
@@ -274,17 +269,12 @@
                 masks = jnp.where(apart == n, in_columns_ref[here, n : n + 1], masks)
             ensemble_ref[:, after] = later + accurate_dot(increments, covariance * masks * gain_column)
 
-    for b in reversed(range(BATCHES - 1)):
-        here = slice(b * BATCH_OBS, (b + 1) * BATCH_OBS)
-        after = slice((b + 1) * BATCH_OBS, NOBS)
-        increments_ref[0:GROUP, here] += dot_parts(
-            *two_parts(increments_ref[0:GROUP, after]), links_high_ref[after, here], links_low_ref[after, here]
-        )
-    factors = increments_ref[0:GROUP, :] * (mask_row * jnp.concatenate(gain_rows, axis=1))
+    row_facts_ref[0:8, :] = jnp.broadcast_to(mask_row * jnp.concatenate(gain_rows, axis=1), (8, NOBS))
+    row_facts_ref[8:16, :] = jnp.broadcast_to(own_row.astype(f32), (8, NOBS))
 
     tile_here = jnp.where(own_column < 0, NOWHERE, own_column).astype(f32)
     tile_here = jnp.broadcast_to(tile_here, (NOBS, LANES)).astype(bf16)
-    sorted_columns = dot(sort_ref[...], jnp.concatenate([turned_ref[...], tile_here], axis=1))
+    sorted_columns = dot(sort_ref[...], jnp.concatenate([own_turned_ref[...], tile_here], axis=1))
     high = sorted_columns[:, 0:GROUP].astype(bf16)
     low = sorted_columns[:, GROUP : 2 * GROUP].astype(bf16)
     replicate = jnp.where(
@@ -296,6 +286,59 @@
     columns_ref[0:NOBS, TILES] = (sorted_columns[:, LANES : LANES + 1] - nth_of_eight).astype(bf16)
     columns_ref[NOBS:, 0 : 2 * WIDE] = jnp.zeros((WINDOW_ROWS, 2 * WIDE), bf16)
     columns_ref[NOBS:, TILES] = jnp.full((WINDOW_ROWS, LANES), NOWHERE, bf16)
+
+
+def observations(position, plan, facts, own, other):
+    turned = struct((NOBS, MEMBERS), bf16)
+    return pl.pallas_call(
+        observation_kernel,
+        out_shape=(
+            struct((PADDED_ROWS, 2 * WIDE + LANES), bf16), turned, turned,
+            struct((MEMBERS, NOBS)), struct((NOBS, LANES)), struct((16, NOBS)),
+        ),
+        in_specs=[SMEM, VMEM, VMEM, VMEM, VMEM],
+        out_specs=(VMEM,) * 6,
+        scratch_shapes=[
+            pltpu.VMEM((MEMBERS, NOBS), f32),
+            pltpu.VMEM((NOBS, NOBS), bf16),
+            pltpu.VMEM((128, NOBS), f32),
+            pltpu.VMEM((NOBS, 128), f32),
+            pltpu.VMEM((NOBS, 2 * GROUP), bf16),
+        ],
+        compiler_params=kernel_params(32),
+        cost_estimate=pl.CostEstimate(flops=8 * 10**9, bytes_accessed=8 * 2**20, transcendentals=10**5),
+        name="observations",
+    )(position, plan, facts, own, other)
+
+
+def factors_kernel(
+    turned_high_ref, turned_low_ref, all_increments_ref, column_facts_ref, row_facts_ref,
+    factors_ref,
+    increments_ref, links_high_ref, links_low_ref, sort_back_ref,
+):
+    own_row = row_facts_ref[8:9, :].astype(i32)
+    own_column = column_facts_ref[:, 1:2].astype(i32)
+    for b in range(1, BATCHES):
+        here = slice(b * BATCH_OBS, (b + 1) * BATCH_OBS)
+        before = slice(0, b * BATCH_OBS)
+        links = dot_parts(turned_high_ref[here, :], turned_low_ref[here, :], *two_parts(all_increments_ref[:, before]))
+        links = jnp.where(own_column[here] == own_row[:, before], links * column_facts_ref[here, 0:1], 0.0)
+        links_high, links_low = two_parts(links)
+        links_high_ref[here, before] = links_high
+        links_low_ref[here, before] = links_low
+    increments_ref[...] = all_increments_ref[0:GROUP, :]
+    for b in reversed(range(BATCHES - 1)):
+        here = slice(b * BATCH_OBS, (b + 1) * BATCH_OBS)
+        after = slice((b + 1) * BATCH_OBS, NOBS)
+        increments_ref[:, here] += dot_parts(
+            *two_parts(increments_ref[:, after]), links_high_ref[after, here], links_low_ref[after, here]
+        )
+    factors = increments_ref[...] * row_facts_ref[0:1, :]
+    key_row = jnp.where(own_row < 0, OWN_TILES, own_row) * NOBS + lax.broadcasted_iota(i32, (1, NOBS), 1)
+    key_column = jnp.where(own_column < 0, OWN_TILES, own_column) * NOBS + lax.broadcasted_iota(i32, (NOBS, 1), 0)
+    rank_column = jnp.sum(jnp.where(key_row < key_column, 1.0, 0.0), axis=1, keepdims=True).astype(i32)
+    to = lax.broadcasted_iota(i32, (NOBS, NOBS), 1)
+    sort_back_ref[...] = jnp.where(to == rank_column, 1.0, 0.0).astype(bf16)
 
     factors_high, factors_low = two_parts(factors)
     tile_there = jnp.where(own_row < 0, NOWHERE, own_row).astype(f32)
@@ -312,31 +355,18 @@
     factors_ref[TILE_ROWS, NOBS:] = jnp.full((16, WINDOW_COLUMNS), NOWHERE, bf16)
 
 
-def observations(position, plan, facts, own, other):
-    columns = struct((PADDED_ROWS, 2 * WIDE + LANES), bf16)
-    factors = struct((2 * WIDE + 16, PADDED_COLUMNS), bf16)
+def factors_of(turned_high, turned_low, increments, column_facts, row_facts):
     square = pltpu.VMEM((NOBS, NOBS), bf16)
     return pl.pallas_call(
-        observation_kernel,
-        out_shape=(columns, factors),
-        in_specs=[SMEM, VMEM, VMEM, VMEM, VMEM],
-        out_specs=(VMEM,) * 2,
-        scratch_shapes=[
-            pltpu.VMEM((MEMBERS, NOBS), f32),
-            pltpu.VMEM((MEMBERS, NOBS), f32),
-            square,
-            pltpu.VMEM((128, NOBS), f32),
-            pltpu.VMEM((NOBS, 128), f32),
-            pltpu.VMEM((NOBS, 2 * GROUP), bf16),
-            square,
-            square,
-            square,
-            square,
-        ],
-        compiler_params=kernel_params(44),
-        cost_estimate=pl.CostEstimate(flops=20 * 10**9, bytes_accessed=8 * 2**20, transcendentals=10**5),
-        name="observations",
-    )(position, plan, facts, own, other)
+        factors_kernel,
+        out_shape=struct((2 * WIDE + 16, PADDED_COLUMNS), bf16),
+        in_specs=[VMEM] * 5,
+        out_specs=VMEM,
+        scratch_shapes=[pltpu.VMEM((GROUP, NOBS), f32), square, square, square],
+        compiler_params=kernel_params(32),
+        cost_estimate=pl.CostEstimate(flops=8 * 10**9, bytes_accessed=6 * 2**20, transcendentals=0),
+        name="factors",
+    )(turned_high, turned_low, increments, column_facts, row_facts)
 
 
 def for_windows(starts_ref, groups, size, align, visit):
@@ -492,22 +522,21 @@
     masks = exchange(masks.reshape(GROUP_CHIPS, 4, LANES), CHIPS).sum(axis=0)
     tiles = locations // TILE
 
-    observed = own_columns(plan, locations, rows)
-    mine = jnp.concatenate([observed, masks], axis=0)
+    block, masks = lax.optimization_barrier((spread_out(rows), masks))
+    block = exchange(block)
+    mine = jnp.concatenate([own_columns(plan, locations, rows), masks], axis=0)
     all_four = [mine] + [passed_along(mine, by) for by in range(1, SUMS)]
     payload = jnp.concatenate(
         [*(each[0:8] for each in all_four), sum(each[8:12] for each in all_four), jnp.zeros((4, LANES), f32)], axis=0
     )
+    block, payload = lax.optimization_barrier((block, payload))
     gathered = exchange(jnp.broadcast_to(payload[None], (GROUP_CHIPS, 40, LANES)), CHIPS)
-    block, gathered = lax.optimization_barrier((spread_out(rows), gathered))
     other = lax.ppermute(gathered, "c", [(0, 1), (1, 0)])
-    block, other = lax.optimization_barrier((block, other))
-    block = exchange(block)
 
     facts = jnp.concatenate(
         [tiles.astype(f32)[None], obs_value[None], obs_error[None], jnp.zeros((5, NOBS), f32)], axis=0
     )
-    columns, factors = observations(
+    columns, *for_factors = observations(
         position, plan[None], facts, gathered.reshape(-1, LANES), other.reshape(-1, LANES)
     )
     nth_own = (residue - tiles + RADIUS) & (RESIDUES - 1)
@@ -519,7 +548,7 @@
     parts = covariances(position, starts, block, columns)
     rest = lax.cond(most > FIRST, summed, lambda parts: parts, parts[SUMS:])
     sums = summed(parts[:SUMS]) + tuple(rest)
-    block = exchange(updated(position, starts, sums, block, factors))
+    block = exchange(updated(position, starts, sums, block, factors_of(*for_factors)))
     return collect(block).reshape(state.shape)
 
 

time: 218 us -> 220 us (level)
  blocking collectives: 60.1 us -> 76.6 us
  starting transfers between devices: 50.8 us -> 40.8 us
  local copies, waits for them, and re-layouts: 15 us -> 9.04 us
  Pallas kernels: 34.2 us -> 37.4 us
    all_to_all x3 -> x2, waiting for transfers between devices: 41.7 us -> 0.33 us  [exchange(): return lax.all_to_all(value, axes, 0, 0, tiled=True)]
    ppermute x9, waiting for transfers between devices: 11.3 us -> 52.6 us  [passed_along(): return lax.ppermute(value, 'h', [(i, (i + by) % SUMS) for i in range(SUMS)])]
    all_to_all x1 -> x2, blocking collectives: 60.1 us -> 76.6 us  [exchange(): return lax.all_to_all(value, axes, 0, 0, tiled=True)]
    ppermute x9, starting transfers between devices: 24.9 us -> 19.3 us  [passed_along(): return lax.ppermute(value, 'h', [(i, (i + by) % SUMS) for i in range(SUMS)])]
    unnamed x30 -> x22, local copies, waits for them, and re-layouts: 14.1 us -> 8.88 us
    all_to_all x3 -> x2, starting transfers between devices: 21.9 us -> 18.8 us  [exchange(): return lax.all_to_all(value, axes, 0, 0, tiled=True)]
    pallas_call x1 -> x2, Pallas kernels: 10.7 us -> 13.9 us  [the longest x1 10.4 us: observations(): pl.pallas_call(observation_kernel, out_shape=(struct((PADDED_ROWS, 2 * WI...]
  transfers between devices with their start and end apart: 13 -> 12, of which waited for: 9 -> 6; matrix products, arithmetic and copies ran while one was open for 1% -> 1% of each run, Pallas kernels for 8% -> 4%
where the time goes in v7:
time: 220 us; the launch traced here: 219 us
  blocking collectives  76.6 us (35%)
  waiting for transfers between devices  52.9 us (24%)
  starting transfers between devices  40.8 us (19%)
  Pallas kernels  37.4 us (17%)
  local copies, waits for them, and re-layouts  9.04 us (4%)
    all_to_all x2, blocking collectives, exchange(): return lax.all_to_all(value, axes, 0, 0, tiled=True)  76.6 us
    ppermute x9, waiting for transfers between devices, passed_along(): return lax.ppermute(value, 'h', [(i, (i + by) % SUMS) for i in range(SUMS)])  52.6 us
    ppermute x9, starting transfers between devices, passed_along(): return lax.ppermute(value, 'h', [(i, (i + by) % SUMS) for i in range(SUMS)])  19.3 us
    all_to_all x2, starting transfers between devices, exchange(): return lax.all_to_all(value, axes, 0, 0, tiled=True)  18.8 us
    pallas_call x1, Pallas kernels, observations(): pl.pallas_call(observation_kernel, out_shape=(struct((PADDED_ROWS, 2 * WI...  10.4 us
    unnamed x22, local copies, waits for them, and re-layouts  8.88 us
    pallas_call x1, Pallas kernels, updated(): pl.pallas_call(update_kernel, grid=(steps,), out_shape=struct((GROUP, OWN...  7.09 us
    pallas_call x2, Pallas kernels, reordered(): pl.pallas_call(kernel, grid=(OWN_TILES // BLOCK_TILES,), out_shape=struct...  7 us
  transfers between devices with their start and end apart: 12, of which 6 were waited for; matrix products, arithmetic and copies ran while one was open for 1% of the time, Pallas kernels for 4%

profile of v7, /device:TPU:1, one launch (start us, length us, event | category | flops | bytes accessed | tf_op | source)
XLA Modules:
  0.0 218.8 jit_solution(16544256615412838958)
XLA Ops:
  0.0 0.1 pad_add_fusion.position_ref
  0.1 0.0 copy-start.3
  0.1 0.7 copy-done.3
  0.8 0.0 copy-start.5
  0.8 0.8 copy-done.5
  1.5 1.2 own_masks.1
  2.7 9.2 %all-to-all-start = ((f32[32,4,128]{2,1,0:T(4,128)}), f32[32,4,128]{2,1,0:T(4,128)S(1)}, u32[]{:S(2)}, u32[]{:S(2)}) async-start(f32[32,4,128]{2,1,0:T(4,128)} %bitcast.6), calls=%async_computation | async-start | bytes 131072 | tf_op jit(solution)/shard_map/all_to_all | solution.py:502
  12.0 0.0 copy-start
  12.0 2.2 copy-done
  14.1 2.8 %spread_out.1 = f32[64,128,128]{2,1,0:T(8,128)S(1)} custom-call(f32[8192,128]{1,0:T(8,128)S(1)} %bitcast.14), custom_call_target="tpu_custom_call" | custom-call | flops 1000000 | bytes 8388608 | tf_op jit(solution)/shard_map/spread_out/pallas_call | solution.py:168
  16.9 0.0 copy-start.2
  17.0 2.0 copy-done.2
  19.0 0.3 all-to-all-done
  19.3 0.0 copy-start.4
  19.3 0.0 copy-start.6
  19.3 9.5 %all-to-all-start.1 = ((f32[64,128,128]{2,1,0:T(8,128)}), f32[64,128,128]{2,1,0:T(8,128)}, u32[]{:S(2)}, u32[]{:S(2)}) async-start(f32[64,128,128]{2,1,0:T(8,128)} %copy-done.2), calls=%async_computation.1 | async-start | bytes 8388608 | tf_op jit(solution)/shard_map/all_to_all | solution.py:502
  28.9 0.0 copy-done.4
  28.9 0.0 copy-done.6
  28.9 0.0 copy-start.1
  28.9 2.2 copy-done.1
  31.1 0.0 copy-start.9
  31.1 0.0 copy-start.10
  31.1 3.1 %own_columns.1 = f32[8,128]{1,0:T(8,128)S(1)} custom-call(s32[1024]{0:T(1024)S(1)} %copy-done.6, s32[1024]{0:T(1024)S(1)} %copy-done.4, f32[8192,128]{1,0:T(8,128)S(1)} %bitcast.15), custom_call_target="tpu_custom_call" | custom-call | flops 1000000 | bytes 8388608 | tf_op jit(solution)/shard_map/own_columns/pallas_call | solution.py:141
  34.2 5.2 %collective-permute-start.8 = (f32[12,128]{1,0:T(8,128)S(1)}, f32[12,128]{1,0:T(8,128)S(1)}, u32[]{:S(2)}, u32[]{:S(2)}) collective-permute-start(f32[12,128]{1,0:T(8,128)S(1)} %pad_maximum_fusion), channel_id=1, source_target_pairs={{0,48},{16,0},{32,16},{48,32},{1,49},{17,1},{33,17},{49,33},{2,50}... | collective-permute-start | bytes 18440 | tf_op jit(solution)/shard_map/ppermute | solution.py:506
  39.4 1.2 collective-permute-start.7
  40.5 2.1 collective-permute-start.6
  42.6 0.0 collective-permute-done.8
  42.6 43.5 %collective-permute-done.7 = f32[12,128]{1,0:T(8,128)S(1)} collective-permute-done((f32[12,128]{1,0:T(8,128)S(1)}, f32[12,128]{1,0:T(8,128)S(1)}, u32[]{:S(2)}, u32[]{:S(2)}) %collective-permute-start.7) | collective-permute-done | bytes 6176 | tf_op jit(solution)/shard_map/ppermute | solution.py:506
  86.1 0.0 collective-permute-done.6
  86.2 0.0 all-to-all-done.1.block_ref.refs_8_
  86.2 18.7 %all_to_all.20 = f32[32,40,128]{2,1,0:T(8,128)S(1)} all-to-all(f32[32,40,128]{2,1,0:T(8,128)S(1)} %broadcast_in_dim.39), channel_id=1, replica_groups=mesh['y'=4,'h'=4,'l'=2,'c'=2,'x'=4] {'y','l','x'}, dimensions={0} | all-to-all | bytes 1310720 | tf_op jit(solution)/shard_map/all_to_all | solution.py:502
  104.9 2.7 %collective-permute-start.9 = (f32[32,40,128]{2,1,0:T(8,128)S(1)}, f32[32,40,128]{2,1,0:T(8,128)S(1)}, u32[]{:S(2)}, u32[]{:S(2)}) collective-permute-start(f32[32,40,128]{2,1,0:T(8,128)S(1)} %all_to_all.20), channel_id=1, source_target_pairs={{0,4},{4,0},{1,5},{5,1},{2,6},{6,2},{3,7},{7,3},{8,12},{12,8},{9,1... | collective-permute-start | bytes 1966088 | tf_op jit(solution)/shard_map/ppermute | solution.py:534
  107.6 0.1 convert_reduce_fusion.1
  107.8 0.6 reduce_max.9
  109.1 0.1 pad.3.clone
  109.1 0.2 convert_reduce_fusion.starts_ref
  109.3 0.0 copy-done.9
  109.3 0.0 copy-done.10
  109.3 0.1 maximum_maximum_fusion.facts_ref
  109.4 0.0 collective-permute-done.9
  109.4 10.4 %observations.1 = (bf16[1152,1152]{1,0:T(8,128)(2,1)S(1)}, bf16[1024,256]{1,0:T(8,128)(2,1)S(1)}, bf16[1024,256]{1,0:T(8,128)(2,1)S(1)}, f32[256,1024]{1,0:T(8,1...) custom-call(s32[4]{0:T(128)S(1)} %pad_add_fusion.position_ref, s32[1,1024]{1,0:T(1,128)S(1)} %bitcast.18, ...), custom_call_target="tpu_custom_call" | custom-call | flops 8000000000 | bytes 8388608 | tf_op jit(solution)/shard_map/observations/pallas_call | solution.py:293
  119.8 0.0 copy-start.7
  119.8 5.2 %covariances.1 = (f32[160,128]{1,0:T(8,128)S(1)}, f32[160,128]{1,0:T(8,128)S(1)}, f32[160,128]{1,0:T(8,128)S(1)}, f32[160,128]{1,0:T(8,128)S(1)}, f32[96,128]{1,...) custom-call(s32[4]{0:T(128)S(1)} %pad_add_fusion.position_ref, ...), custom_call_target="tpu_custom_call" | custom-call | flops 3000000000 | bytes 4194304 | tf_op jit(solution)/shard_map/covariances/pallas_call | solution.py:438
  125.0 0.0 copy-done.7
  125.0 0.6 collective-permute-start.10
  125.6 1.9 collective-permute-start.11
  127.5 2.1 collective-permute-start.12
  129.6 2.5 %collective-permute-done.10 = f32[160,128]{1,0:T(8,128)S(1)} collective-permute-done((f32[160,128]{1,0:T(8,128)S(1)}, f32[160,128]{1,0:T(8,128)S(1)}, u32[]{:S(2)}, u32[]{:S(2)}) %collective-permute-start.10) | collective-permute-done | bytes 81952 | tf_op jit(solution)/shard_map/ppermute | solution.py:506
  132.1 1.9 collective-permute-done.11
  134.1 2.9 %collective-permute-done.12 = f32[160,128]{1,0:T(8,128)S(1)} collective-permute-done((f32[160,128]{1,0:T(8,128)S(1)}, f32[160,128]{1,0:T(8,128)S(1)}, u32[]{:S(2)}, u32[]{:S(2)}) %collective-permute-start.12) | collective-permute-done | bytes 81952 | tf_op jit(solution)/shard_map/ppermute | solution.py:506
  137.0 1.8 collective-permute-start.15
  138.8 4.4 %collective-permute-start.14 = (f32[160,128]{1,0:T(8,128)S(1)}, f32[160,128]{1,0:T(8,128)S(1)}, u32[]{:S(2)}, u32[]{:S(2)}) collective-permute-start(f32[160,128]{1,0:T(8,128)S(1)} %add_add_fusion.1.refs_0_), channel_id=1, source_target_pairs={{0,32},{16,48},{32,0},{48,16},{1,33},{17,49},{33,1},{49,17},{2,34}... | collective-permute-start | bytes 245768 | tf_op jit(solution)/shard_map/ppermute | solution.py:506
  143.2 0.1 collective-permute-start.13
  143.2 0.0 copy-start.8
  143.2 1.0 copy-done.8
  144.3 3.5 %factors.1.refs_9_ = bf16[1040,1280]{1,0:T(8,128)(2,1)S(1)} custom-call(bf16[1024,256]{1,0:T(8,128)(2,1)S(1)} %get-tuple-element.64.turned_high_ref, bf16[1024,256]{1,0:T(8,128)(2,1)S(1)} %get-tuple-element.65.turned_low_ref, f32[256,1024]{1,0:T(8,128)S(1)} %get-tuple-element.66.all_increments_ref, f32[1024,128]{1,0:T(8,128)S(1)} %copy-done.8, ...), custom_call_target="tpu_custom_call" | custom-call | flops 8000000000 | bytes 6291456 | tf_op jit(solution)/shard_map/factors/pallas_call | solution.py:360
  147.8 0.0 collective-permute-done.15.refs_3_
  147.8 0.0 collective-permute-done.14.refs_2_
  147.8 1.8 collective-permute-done.13.refs_1_
  149.6 7.1 %updated.1 = f32[64,128,128]{2,1,0:T(8,128)S(1)} custom-call(s32[4]{0:T(128)S(1)} %pad_add_fusion.position_ref, s32[17]{0:T(128)S(1)} %convert_reduce_fusion.starts_ref, f32[160,128]{1,0:T(8,128)S(1)} %add_add_fusion.1.refs_0_, f32[160,128]{1,0:T(8,128)S(1)} %collective-permute-done.13.refs_1_, f32[160,128]{1,0:T(8,128)S(1)} %collective-permute-done.14.refs_2_, ...), custom_call_target="tpu_custom_call" | custom-call | flops 4000000000 | bytes 8388608 | tf_op jit(solution)/shard_map/updated/pallas_call | solution.py:488
  156.7 57.9 %all_to_all.21.in_ref = f32[64,128,128]{2,1,0:T(8,128)S(1)} all-to-all(f32[64,128,128]{2,1,0:T(8,128)S(1)} %updated.1), channel_id=1, replica_groups=mesh['y'=4,'h'=4,'l'=2,'c'=2,'x'=4] {'c','y','l','x'}, dimensions={0} | all-to-all | bytes 8388608 | tf_op jit(solution)/shard_map/all_to_all | solution.py:502
  214.6 4.2 %collect.1 = f32[8192,128]{1,0:T(8,128)} custom-call(f32[64,128,128]{2,1,0:T(8,128)S(1)} %all_to_all.21.in_ref), custom_call_target="tpu_custom_call" | custom-call | flops 1000000 | bytes 8388608 | tf_op jit(solution)/shard_map/collect/pallas_call | solution.py:168
  (14 shorter events, 0.2 us)
Async XLA Ops:
  0.1 0.7 copy-start.3
  0.8 0.8 copy-start.5
  2.7 16.6 %all-to-all-start = ((f32[32,4,128]{2,1,0:T(4,128)}), f32[32,4,128]{2,1,0:T(4,128)S(1)}, u32[]{:S(2)}, u32[]{:S(2)}) async-start(f32[32,4,128]{2,1,0:T(4,128)} %bitcast.6), calls=%async_computation | async-start | bytes 131072 | tf_op jit(solution)/shard_map/all_to_all | solution.py:502
  12.0 2.2 %copy-start = (f32[1,1048576]{1,0:T(1,128)S(1)}, f32[1,1048576]{1,0:T(1,128)}, u32[]{:S(2)}) copy-start(f32[1,1048576]{1,0:T(1,128)} %param.8) | copy-start | bytes 12582916
  16.9 2.0 copy-start.2
  19.3 9.6 %copy-start.4 = (s32[1024]{0:T(1024)S(1)}, s32[1024]{0:T(1024)}, u32[]{:S(2)}) copy-start(s32[1024]{0:T(1024)} %locations_ref.1) | copy-start | bytes 12292
  19.3 9.6 %copy-start.6 = (s32[1024]{0:T(1024)S(1)}, s32[1024]{0:T(1024)}, u32[]{:S(2)}) copy-start(s32[1024]{0:T(1024)} %plan_ref.1) | copy-start | bytes 12292
  19.3 66.8 %all-to-all-start.1 = ((f32[64,128,128]{2,1,0:T(8,128)}), f32[64,128,128]{2,1,0:T(8,128)}, u32[]{:S(2)}, u32[]{:S(2)}) async-start(f32[64,128,128]{2,1,0:T(8,128)} %copy-done.2), calls=%async_computation.1 | async-start | bytes 8388608 | tf_op jit(solution)/shard_map/all_to_all | solution.py:502
  28.9 2.2 %copy-start.1 = (f32[1,1048576]{1,0:T(1,128)S(1)}, f32[1,1048576]{1,0:T(1,128)}, u32[]{:S(2)}) copy-start(f32[1,1048576]{1,0:T(1,128)} %param.8) | copy-start | bytes 12582916
  31.1 78.2 %copy-start.9 = (f32[1024]{0:T(1024)S(1)}, f32[1024]{0:T(1024)}, u32[]{:S(2)}) copy-start(f32[1024]{0:T(1024)} %param.13) | copy-start | bytes 12292
  31.1 78.2 %copy-start.10 = (f32[1024]{0:T(1024)S(1)}, f32[1024]{0:T(1024)}, u32[]{:S(2)}) copy-start(f32[1024]{0:T(1024)} %param.12) | copy-start | bytes 12292
  34.2 8.5 %collective-permute-start.8 = (f32[12,128]{1,0:T(8,128)S(1)}, f32[12,128]{1,0:T(8,128)S(1)}, u32[]{:S(2)}, u32[]{:S(2)}) collective-permute-start(f32[12,128]{1,0:T(8,128)S(1)} %pad_maximum_fusion), channel_id=1, source_target_pairs={{0,48},{16,0},{32,16},{48,32},{1,49},{17,1},{33,17},{49,33},{2,50}... | collective-permute-start | bytes 18440 | tf_op jit(solution)/shard_map/ppermute | solution.py:506
  39.4 46.8 %collective-permute-start.7 = (f32[12,128]{1,0:T(8,128)S(1)}, f32[12,128]{1,0:T(8,128)S(1)}, u32[]{:S(2)}, u32[]{:S(2)}) collective-permute-start(f32[12,128]{1,0:T(8,128)S(1)} %pad_maximum_fusion), channel_id=1, source_target_pairs={{0,32},{16,48},{32,0},{48,16},{1,33},{17,49},{33,1},{49,17},{2,34}... | collective-permute-start | bytes 18440 | tf_op jit(solution)/shard_map/ppermute | solution.py:506
  40.5 45.6 %collective-permute-start.6 = (f32[12,128]{1,0:T(8,128)S(1)}, f32[12,128]{1,0:T(8,128)S(1)}, u32[]{:S(2)}, u32[]{:S(2)}) collective-permute-start(f32[12,128]{1,0:T(8,128)S(1)} %pad_maximum_fusion), channel_id=1, source_target_pairs={{0,16},{16,32},{32,48},{48,0},{1,17},{17,33},{33,49},{49,1},{2,18}... | collective-permute-start | bytes 18440 | tf_op jit(solution)/shard_map/ppermute | solution.py:506
  104.9 4.5 %collective-permute-start.9 = (f32[32,40,128]{2,1,0:T(8,128)S(1)}, f32[32,40,128]{2,1,0:T(8,128)S(1)}, u32[]{:S(2)}, u32[]{:S(2)}) collective-permute-start(f32[32,40,128]{2,1,0:T(8,128)S(1)} %all_to_all.20), channel_id=1, source_target_pairs={{0,4},{4,0},{1,5},{5,1},{2,6},{6,2},{3,7},{7,3},{8,12},{12,8},{9,1... | collective-permute-start | bytes 1966088 | tf_op jit(solution)/shard_map/ppermute | solution.py:534
  119.8 5.2 %copy-start.7 = (f32[1024,128]{1,0:T(8,128)}, f32[1024,128]{1,0:T(8,128)S(1)}, u32[]{:S(2)}) copy-start(f32[1024,128]{1,0:T(8,128)S(1)} %get-tuple-element.67.column_facts_ref) | copy-start | bytes 1572868
  125.0 7.1 %collective-permute-start.10 = (f32[160,128]{1,0:T(8,128)S(1)}, f32[160,128]{1,0:T(8,128)S(1)}, u32[]{:S(2)}, u32[]{:S(2)}) collective-permute-start(f32[160,128]{1,0:T(8,128)S(1)} %get-tuple-element.53), channel_id=1, source_target_pairs={{0,16},{16,32},{32,48},{48,0},{1,17},{17,33},{33,49},{49,1},{2,18}... | collective-permute-start | bytes 245768 | tf_op jit(solution)/shard_map/ppermute | solution.py:506
  125.6 8.5 %collective-permute-start.11 = (f32[160,128]{1,0:T(8,128)S(1)}, f32[160,128]{1,0:T(8,128)S(1)}, u32[]{:S(2)}, u32[]{:S(2)}) collective-permute-start(f32[160,128]{1,0:T(8,128)S(1)} %get-tuple-element.54), channel_id=1, source_target_pairs={{0,32},{16,48},{32,0},{48,16},{1,33},{17,49},{33,1},{49,17},{2,34}... | collective-permute-start | bytes 245768 | tf_op jit(solution)/shard_map/ppermute | solution.py:506
  127.5 9.5 %collective-permute-start.12 = (f32[160,128]{1,0:T(8,128)S(1)}, f32[160,128]{1,0:T(8,128)S(1)}, u32[]{:S(2)}, u32[]{:S(2)}) collective-permute-start(f32[160,128]{1,0:T(8,128)S(1)} %get-tuple-element.55), channel_id=1, source_target_pairs={{0,48},{16,0},{32,16},{48,32},{1,49},{17,1},{33,17},{49,33},{2,50}... | collective-permute-start | bytes 245768 | tf_op jit(solution)/shard_map/ppermute | solution.py:506
  137.0 10.8 %collective-permute-start.15 = (f32[160,128]{1,0:T(8,128)S(1)}, f32[160,128]{1,0:T(8,128)S(1)}, u32[]{:S(2)}, u32[]{:S(2)}) collective-permute-start(f32[160,128]{1,0:T(8,128)S(1)} %add_add_fusion.1.refs_0_), channel_id=1, source_target_pairs={{0,48},{16,0},{32,16},{48,32},{1,49},{17,1},{33,17},{49,33},{2,50}... | collective-permute-start | bytes 245768 | tf_op jit(solution)/shard_map/ppermute | solution.py:506
  138.8 9.0 %collective-permute-start.14 = (f32[160,128]{1,0:T(8,128)S(1)}, f32[160,128]{1,0:T(8,128)S(1)}, u32[]{:S(2)}, u32[]{:S(2)}) collective-permute-start(f32[160,128]{1,0:T(8,128)S(1)} %add_add_fusion.1.refs_0_), channel_id=1, source_target_pairs={{0,32},{16,48},{32,0},{48,16},{1,33},{17,49},{33,1},{49,17},{2,34}... | collective-permute-start | bytes 245768 | tf_op jit(solution)/shard_map/ppermute | solution.py:506
  143.2 6.4 %collective-permute-start.13 = (f32[160,128]{1,0:T(8,128)S(1)}, f32[160,128]{1,0:T(8,128)S(1)}, u32[]{:S(2)}, u32[]{:S(2)}) collective-permute-start(f32[160,128]{1,0:T(8,128)S(1)} %add_add_fusion.1.refs_0_), channel_id=1, source_target_pairs={{0,16},{16,32},{32,48},{48,0},{1,17},{17,33},{33,49},{49,1},{2,18}... | collective-permute-start | bytes 245768 | tf_op jit(solution)/shard_map/ppermute | solution.py:506
  143.2 1.0 copy-start.8

commit v8 on v6

--- a/solution.py
+++ b/solution.py
@@ -51,6 +51,7 @@
 
 VMEM = pl.BlockSpec(memory_space=pltpu.VMEM)
 SMEM = pl.BlockSpec(memory_space=pltpu.SMEM)
+ANY = pl.BlockSpec(memory_space=pl.ANY)
 
 
 def kernel_params(mib):
@@ -155,34 +156,58 @@
         out_ref[d] = state_ref[pl.ds(d, BLOCK_TILES, stride=GROUP), :]
 
 
-def collect_kernel(in_ref, state_ref):
-    rows_ref = in_ref.reshape(GROUP * BLOCK_TILES, LANES)
-    for a in range(BLOCK_TILES):
-        state_ref[a * GROUP : (a + 1) * GROUP, :] = rows_ref[pl.ds(a, GROUP, stride=BLOCK_TILES), :]
-
-
-def reordered(kernel, value, out_shape, name):
-    by_device = pl.BlockSpec((GROUP, BLOCK_TILES, LANES), lambda i: (0, i, 0))
-    by_row = pl.BlockSpec((GROUP * BLOCK_TILES, LANES), lambda i: (i, 0))
-    specs = (by_row, by_device) if value.ndim == 2 else (by_device, by_row)
-    return pl.pallas_call(
-        kernel,
+def spread_out(rows):
+    return pl.pallas_call(
+        spread_kernel,
         grid=(OWN_TILES // BLOCK_TILES,),
-        out_shape=struct(out_shape),
-        in_specs=[specs[0]],
-        out_specs=specs[1],
+        out_shape=struct((GROUP, OWN_TILES, LANES)),
+        in_specs=[pl.BlockSpec((GROUP * BLOCK_TILES, LANES), lambda i: (i, 0))],
+        out_specs=pl.BlockSpec((GROUP, BLOCK_TILES, LANES), lambda i: (0, i, 0)),
         compiler_params=kernel_params(16),
         cost_estimate=pl.CostEstimate(flops=10**6, bytes_accessed=8 * 2**20, transcendentals=0),
-        name=name,
-    )(value)
-
-
-def spread_out(rows):
-    return reordered(spread_kernel, rows, (GROUP, OWN_TILES, LANES), "spread_out")
+        name="spread_out",
+    )(rows)
+
+
+PIECES = 8
+
+
+def collect_kernel(in_ref, state_ref, held_ref, in_sems, out_sems):
+    devices = GROUP // PIECES
+    arriving = [
+        pltpu.make_async_copy(
+            in_ref.at[pl.ds(n * devices, devices)], held_ref.at[pl.ds(n * devices, devices)], in_sems.at[n]
+        )
+        for n in range(PIECES)
+    ]
+    leaving = [
+        pltpu.make_async_copy(held_ref.at[d], state_ref.at[:, d, :], out_sems.at[d]) for d in range(GROUP)
+    ]
+    for copy in arriving:
+        copy.start()
+    for n in range(PIECES):
+        arriving[n].wait()
+        for copy in leaving[n * devices : (n + 1) * devices]:
+            copy.start()
+    for copy in leaving:
+        copy.wait()
 
 
 def collect(blocks):
-    return reordered(collect_kernel, blocks, (ROWS, LANES), "collect")
+    return pl.pallas_call(
+        collect_kernel,
+        out_shape=struct((OWN_TILES, GROUP, LANES)),
+        in_specs=[ANY],
+        out_specs=ANY,
+        scratch_shapes=[
+            pltpu.VMEM((GROUP, OWN_TILES, LANES), f32),
+            pltpu.SemaphoreType.DMA((PIECES,)),
+            pltpu.SemaphoreType.DMA((GROUP,)),
+        ],
+        compiler_params=kernel_params(60),
+        cost_estimate=pl.CostEstimate(flops=10**6, bytes_accessed=8 * 2**20, transcendentals=0),
+        name="collect",
+    )(blocks)
 
 
 def observation_kernel(
@@ -343,39 +368,58 @@
     def start(g, i):
         return pl.multiple_of((starts_ref[g] & -align) + i * size, align)
 
-    first_group = pl.program_id(0) * groups
-    for n in range(groups):
-        visit(n, first_group + n, start(first_group + n, 0), True)
-    for n in range(groups):
-        g = first_group + n
+    for g in groups:
+        visit(g, start(g, 0))
+    return functools.partial(for_rest, starts_ref, groups, size, align, visit, start)
+
+
+def for_rest(starts_ref, groups, size, align, visit, start):
+    for g in groups:
         count = (starts_ref[g + 1] - (starts_ref[g] & -align) + size - 1) // size
 
-        def step(i, carry, n=n, g=g):
-            visit(n, g, start(g, i), False)
+        def step(i, carry, g=g):
+            visit(g, start(g, i))
             return carry
 
         lax.fori_loop(1, count, step, 0)
 
 
-def first_tile(g, shape):
-    return jnp.full(shape, (g * EIGHT).astype(f32)).astype(bf16)
-
-
-COVARIANCE_GROUPS = 4
-
-
-def covariance_kernel(position_ref, starts_ref, block_ref, columns_ref, *refs):
-    out_refs, (total_ref,) = refs[: 2 * SUMS], refs[2 * SUMS :]
-
-    @pl.when(pl.program_id(0) == 0)
-    def _():
-        total_ref[...] = jnp.zeros_like(total_ref)
-
+COVARIANCE_PIECES = 2
+UPDATE_PIECES = 4
+
+
+def piece_copies(pieces, from_ref, to_ref, sems):
+    tiles = OWN_TILES // pieces
+    return [
+        pltpu.make_async_copy(
+            from_ref.at[:, pl.ds(n * tiles, tiles), :], to_ref.at[:, pl.ds(n * tiles, tiles), :], sems.at[n]
+        )
+        for n in range(pieces)
+    ]
+
+
+def piece_groups(pieces, n):
+    groups = GROUPS // pieces
+    return range(n * groups, (n + 1) * groups)
+
+
+def covariance_kernel(position_ref, starts_ref, block_ref, columns_in_ref, *refs):
+    out_refs, (total_ref, held_ref, columns_ref, sems, columns_sems) = refs[: 2 * SUMS], refs[2 * SUMS :]
+    usual = FIRST + WINDOW_ROWS
+    columns_copy, more_copy = (
+        pltpu.make_async_copy(columns_in_ref.at[rows], columns_ref.at[rows], columns_sems.at[n])
+        for n, rows in enumerate((pl.ds(0, usual), pl.ds(usual, PADDED_ROWS - usual)))
+    )
+    columns_copy.start()
+    arriving = piece_copies(COVARIANCE_PIECES, block_ref, held_ref, sems)
+    for copy in arriving:
+        copy.start()
+    total_ref[...] = jnp.zeros_like(total_ref)
     zero = jnp.zeros((WINDOW_ROWS, LANES), bf16)
 
-    def visit(n, g, start, is_first):
+    def visit(g, start):
         rows = pl.ds(start, WINDOW_ROWS)
-        found = columns_ref[rows, TILES] == first_tile(g, (WINDOW_ROWS, LANES))
+        found = columns_ref[rows, TILES] == jnp.full((WINDOW_ROWS, LANES), g * EIGHT, bf16)
         left = [
             jnp.concatenate(
                 [
@@ -386,82 +430,99 @@
             )
             for part in range(2)
         ]
-        right = block_ref[:, n * EIGHT : (n + 1) * EIGHT, :].reshape(WIDE, LANES)
+        right = held_ref[:, g * EIGHT : (g + 1) * EIGHT, :].reshape(WIDE, LANES)
         both = dot(jnp.concatenate(left, axis=0), jnp.concatenate(two_parts(right), axis=1))
         both = both[:WINDOW_ROWS] + both[WINDOW_ROWS:]
         total_ref[rows, :] += both[:, :LANES] + both[:, LANES:]
 
-    for_windows(starts_ref, COVARIANCE_GROUPS, WINDOW_ROWS, 16, visit)
-
-    @pl.when(pl.program_id(0) == pl.num_programs(0) - 1)
+    columns_copy.wait()
+
+    @pl.when(starts_ref[GROUPS] > FIRST)
     def _():
-        for d in range(SUMS):
-            to = (position_ref[1] + d) & (SUMS - 1)
-            start = pl.multiple_of(to * FIRST_CHUNK, 16)
-            out_refs[d][...] = total_ref[pl.ds(start, FIRST_CHUNK), :]
-            start = pl.multiple_of(FIRST + to * REST_CHUNK, 16)
-            out_refs[SUMS + d][...] = total_ref[pl.ds(start, REST_CHUNK), :]
+        more_copy.start()
+        more_copy.wait()
+
+    rest = []
+    for n in range(COVARIANCE_PIECES):
+        arriving[n].wait()
+        rest.append(for_windows(starts_ref, piece_groups(COVARIANCE_PIECES, n), WINDOW_ROWS, 16, visit))
+    for windows in rest:
+        windows()
+    for d in range(SUMS):
+        to = (position_ref[1] + d) & (SUMS - 1)
+        start = pl.multiple_of(to * FIRST_CHUNK, 16)
+        out_refs[d][...] = total_ref[pl.ds(start, FIRST_CHUNK), :]
+        start = pl.multiple_of(FIRST + to * REST_CHUNK, 16)
+        out_refs[SUMS + d][...] = total_ref[pl.ds(start, REST_CHUNK), :]
 
 
 def covariances(position, starts, block, columns):
-    steps = GROUPS // COVARIANCE_GROUPS
     return pl.pallas_call(
         covariance_kernel,
-        grid=(steps,),
         out_shape=(struct((FIRST_CHUNK, LANES)),) * SUMS + (struct((REST_CHUNK, LANES)),) * SUMS,
-        in_specs=[SMEM, SMEM, pl.BlockSpec((GROUP, OWN_TILES // steps, LANES), lambda i: (0, i, 0)), VMEM],
+        in_specs=[SMEM, SMEM, ANY, ANY],
         out_specs=(VMEM,) * (2 * SUMS),
-        scratch_shapes=[pltpu.VMEM((PADDED_ROWS, LANES), f32)],
-        compiler_params=kernel_params(24),
-        cost_estimate=pl.CostEstimate(flops=3 * 10**9, bytes_accessed=4 * 2**20, transcendentals=0),
+        scratch_shapes=[
+            pltpu.VMEM((PADDED_ROWS, LANES), f32),
+            pltpu.VMEM((GROUP, OWN_TILES, LANES), f32),
+            pltpu.VMEM((PADDED_ROWS, 2 * WIDE + LANES), bf16),
+            pltpu.SemaphoreType.DMA((COVARIANCE_PIECES,)),
+            pltpu.SemaphoreType.DMA((2,)),
+        ],
+        compiler_params=kernel_params(60),
+        cost_estimate=pl.CostEstimate(flops=3 * 10**9, bytes_accessed=7 * 2**20, transcendentals=0),
         name="covariances",
     )(position, starts, block, columns)
 
 
-UPDATE_GROUPS = 2
-
-
 def update_kernel(position_ref, starts_ref, *refs):
     sums_refs = refs[: 2 * SUMS]
-    block_ref, factors_ref, out_ref, right_ref = refs[2 * SUMS :]
-
-    @pl.when(pl.program_id(0) == 0)
-    def _():
-        for d in range(SUMS):
-            of = (position_ref[1] - d) & (SUMS - 1)
-            start = pl.multiple_of(of * FIRST_CHUNK, 16)
-            right_ref[pl.ds(start, FIRST_CHUNK), :] = jnp.concatenate(two_parts(sums_refs[d][...]), axis=1)
-            start = pl.multiple_of(FIRST + of * REST_CHUNK, 16)
-            right_ref[pl.ds(start, REST_CHUNK), :] = jnp.concatenate(two_parts(sums_refs[SUMS + d][...]), axis=1)
-        right_ref[NOBS:, :] = jnp.zeros((WINDOW_COLUMNS, 2 * LANES), bf16)
-
-    def visit(n, g, start, is_first):
+    block_ref, factors_ref, out_ref, right_ref, held_ref, in_sems, out_sems = refs[2 * SUMS :]
+    arriving = piece_copies(UPDATE_PIECES, block_ref, held_ref, in_sems)
+    leaving = piece_copies(UPDATE_PIECES, held_ref, out_ref, out_sems)
+    for copy in arriving:
+        copy.start()
+    for d in range(SUMS):
+        of = (position_ref[1] - d) & (SUMS - 1)
+        start = pl.multiple_of(of * FIRST_CHUNK, 16)
+        right_ref[pl.ds(start, FIRST_CHUNK), :] = jnp.concatenate(two_parts(sums_refs[d][...]), axis=1)
+        start = pl.multiple_of(FIRST + of * REST_CHUNK, 16)
+        right_ref[pl.ds(start, REST_CHUNK), :] = jnp.concatenate(two_parts(sums_refs[SUMS + d][...]), axis=1)
+    right_ref[NOBS:, :] = jnp.zeros((WINDOW_COLUMNS, 2 * LANES), bf16)
+
+    def visit(g, start):
         columns = pl.ds(start, WINDOW_COLUMNS)
-        found = factors_ref[TILE_ROWS, columns] == first_tile(g, (16, WINDOW_COLUMNS))
-        found = jnp.where(found, jnp.ones((16, WINDOW_COLUMNS), bf16), jnp.zeros((16, WINDOW_COLUMNS), bf16))
+        shape = (16, WINDOW_COLUMNS)
+        found = factors_ref[TILE_ROWS, columns] == jnp.full(shape, g * EIGHT, bf16)
+        found = jnp.where(found, jnp.ones(shape, bf16), jnp.zeros(shape, bf16))
         left = [
             (factors_ref[part, columns].reshape(WIDE // 16, 16, WINDOW_COLUMNS) * found[None]).reshape(WIDE, WINDOW_COLUMNS)
             for part in (slice(0, WIDE), LOW)
         ]
         both = dot(jnp.concatenate(left, axis=0), right_ref[columns, :])
         both = both[:WIDE] + both[WIDE:]
-        change = (both[:, :LANES] + both[:, LANES:]).reshape(GROUP, EIGHT, LANES)
-        here = slice(n * EIGHT, (n + 1) * EIGHT)
-        out_ref[:, here, :] = (block_ref if is_first else out_ref)[:, here, :] + change
-
-    for_windows(starts_ref, UPDATE_GROUPS, WINDOW_COLUMNS, LANES, visit)
+        held_ref[:, g * EIGHT : (g + 1) * EIGHT, :] += (both[:, :LANES] + both[:, LANES:]).reshape(GROUP, EIGHT, LANES)
+
+    for n in range(UPDATE_PIECES):
+        arriving[n].wait()
+        for_windows(starts_ref, piece_groups(UPDATE_PIECES, n), WINDOW_COLUMNS, LANES, visit)()
+        leaving[n].start()
+    for copy in leaving:
+        copy.wait()
 
 
 def updated(position, starts, sums, block, factors):
-    steps = GROUPS // UPDATE_GROUPS
-    by_tiles = pl.BlockSpec((GROUP, OWN_TILES // steps, LANES), lambda i: (0, i, 0))
     return pl.pallas_call(
         update_kernel,
-        grid=(steps,),
         out_shape=struct((GROUP, OWN_TILES, LANES)),
-        in_specs=[SMEM, SMEM] + [VMEM] * (2 * SUMS) + [by_tiles, VMEM],
-        out_specs=by_tiles,
-        scratch_shapes=[pltpu.VMEM((PADDED_COLUMNS, 2 * LANES), bf16)],
+        in_specs=[SMEM, SMEM] + [VMEM] * (2 * SUMS) + [ANY, VMEM],
+        out_specs=ANY,
+        scratch_shapes=[
+            pltpu.VMEM((PADDED_COLUMNS, 2 * LANES), bf16),
+            pltpu.VMEM((GROUP, OWN_TILES, LANES), f32),
+            pltpu.SemaphoreType.DMA((UPDATE_PIECES,)),
+            pltpu.SemaphoreType.DMA((UPDATE_PIECES,)),
+        ],
         compiler_params=kernel_params(24),
         cost_estimate=pl.CostEstimate(flops=4 * 10**9, bytes_accessed=8 * 2**20, transcendentals=0),
         name="updated",

time: 218 us -> 217 us (level)
    unnamed x30 -> x34, local copies, waits for them, and re-layouts: 14.1 us -> 12.3 us
  transfers between devices with their start and end apart: 13 -> 13, of which waited for: 9 -> 8; matrix products, arithmetic and copies ran while one was open for 1% -> 1% of each run, Pallas kernels for 8% -> 8%
where the time goes in v8:
time: 217 us
  blocking collectives  60.3 us (28%)
  waiting for transfers between devices  54.3 us (25%)
  starting transfers between devices  50.8 us (23%)
  Pallas kernels  34.3 us (16%)
  local copies, waits for them, and re-layouts  13.3 us (6%)
  other arithmetic  2.74 us (1%)
    all_to_all x1, blocking collectives, exchange(): return lax.all_to_all(value, axes, 0, 0, tiled=True)  60.3 us
    all_to_all x3, waiting for transfers between devices, exchange(): return lax.all_to_all(value, axes, 0, 0, tiled=True)  40.9 us
    ppermute x9, starting transfers between devices, passed_along(): return lax.ppermute(value, 'h', [(i, (i + by) % SUMS) for i in range(SUMS)])  24.9 us
    all_to_all x3, starting transfers between devices, exchange(): return lax.all_to_all(value, axes, 0, 0, tiled=True)  21.9 us
    unnamed x34, local copies, waits for them, and re-layouts  12.3 us
    ppermute x9, waiting for transfers between devices, passed_along(): return lax.ppermute(value, 'h', [(i, (i + by) % SUMS) for i in range(SUMS)])  11.6 us
    pallas_call x1, Pallas kernels, observations(): pl.pallas_call(observation_kernel, out_shape=(columns, factors), in_specs...  10.7 us
    pallas_call x1, Pallas kernels, updated(): pl.pallas_call(update_kernel, out_shape=struct((GROUP, OWN_TILES, LANES))...  6.49 us
  transfers between devices with their start and end apart: 13, of which 8 were waited for; matrix products, arithmetic and copies ran while one was open for 1% of the time, Pallas kernels for 8%

profile of v8, /device:TPU:1, one launch (start us, length us, event | category | flops | bytes accessed | tf_op | source)
XLA Modules:
  0.0 216.7 jit_solution(625902423939046578)
XLA Ops:
  0.0 0.1 pad_add_fusion.position_ref
  0.1 0.0 copy-start.9
  0.1 0.7 copy-done.3
  0.8 0.8 copy-done.6
  1.5 1.2 own_masks.1
  2.7 9.2 %all-to-all-start = ((f32[32,4,128]{2,1,0:T(4,128)}), f32[32,4,128]{2,1,0:T(4,128)S(1)}, u32[]{:S(2)}, u32[]{:S(2)}) async-start(f32[32,4,128]{2,1,0:T(4,128)} %bitcast.6), calls=%async_computation | async-start | bytes 131072 | tf_op jit(solution)/shard_map/all_to_all | solution.py:533
  12.0 0.0 copy-start
  12.0 2.2 %copy-done = f32[1,1048576]{1,0:T(1,128)S(1)} copy-done((f32[1,1048576]{1,0:T(1,128)S(1)}, f32[1,1048576]{1,0:T(1,128)}, u32[]{:S(2)}) %copy-start) | copy-done | bytes 4194328
  14.2 0.7 copy-done.4
  14.8 0.7 copy-done.7
  15.5 3.1 %own_columns.1 = f32[8,128]{1,0:T(8,128)S(1)} custom-call(s32[1024]{0:T(1024)S(1)} %copy-done.7, s32[1024]{0:T(1024)S(1)} %copy-done.4, f32[8192,128]{1,0:T(8,128)S(1)} %bitcast.14), custom_call_target="tpu_custom_call" | custom-call | flops 1000000 | bytes 8388608 | tf_op jit(solution)/shard_map/own_columns/pallas_call | solution.py:142
  18.6 0.7 all-to-all-done
  19.4 5.2 %collective-permute-start.8 = (f32[12,128]{1,0:T(8,128)S(1)}, f32[12,128]{1,0:T(8,128)S(1)}, u32[]{:S(2)}, u32[]{:S(2)}) collective-permute-start(f32[12,128]{1,0:T(8,128)S(1)} %pad_maximum_fusion), channel_id=1, source_target_pairs={{0,48},{16,0},{32,16},{48,32},{1,49},{17,1},{33,17},{49,33},{2,50}... | collective-permute-start | bytes 18440 | tf_op jit(solution)/shard_map/ppermute | solution.py:537
  24.5 1.2 collective-permute-start.7
  25.7 2.1 collective-permute-start.6
  27.8 0.0 collective-permute-done.8
  27.8 3.1 %collective-permute-done.7 = f32[12,128]{1,0:T(8,128)S(1)} collective-permute-done((f32[12,128]{1,0:T(8,128)S(1)}, f32[12,128]{1,0:T(8,128)S(1)}, u32[]{:S(2)}, u32[]{:S(2)}) %collective-permute-start.7) | collective-permute-done | bytes 6176 | tf_op jit(solution)/shard_map/ppermute | solution.py:537
  31.0 0.0 collective-permute-done.6
  31.0 0.9 broadcast_in_dim.34
  31.9 7.0 %all-to-all-start.1 = ((f32[32,40,128]{2,1,0:T(8,128)}), f32[32,40,128]{2,1,0:T(8,128)S(1)}, u32[]{:S(2)}, u32[]{:S(2)}) async-start(f32[32,40,128]{2,1,0:T(8,128)} %broadcast_in_dim.34), calls=%async_computation.1 | async-start | bytes 1310720 | tf_op jit(solution)/shard_map/all_to_all | solution.py:533
  38.9 0.0 copy-start.1
  39.0 2.2 %copy-done.1 = f32[1,1048576]{1,0:T(1,128)S(1)} copy-done((f32[1,1048576]{1,0:T(1,128)S(1)}, f32[1,1048576]{1,0:T(1,128)}, u32[]{:S(2)}) %copy-start.1) | copy-done | bytes 4194328
  41.1 2.8 %spread_out.1 = f32[64,128,128]{2,1,0:T(8,128)S(1)} custom-call(f32[8192,128]{1,0:T(8,128)S(1)} %bitcast.15), custom_call_target="tpu_custom_call" | custom-call | flops 1000000 | bytes 8388608 | tf_op jit(solution)/shard_map/spread_out/pallas_call | solution.py:160
  43.9 0.0 copy-start.2
  44.0 2.0 copy-done.2
  46.0 2.7 %all-to-all-done.1 = f32[32,40,128]{2,1,0:T(8,128)S(1)} async-done(((f32[32,40,128]{2,1,0:T(8,128)}), f32[32,40,128]{2,1,0:T(8,128)S(1)}, u32[]{:S(2)}, u32[]{:S(2)}) %all-to-all-start.1) | async-done | bytes 655392 | tf_op jit(solution)/shard_map/all_to_all | solution.py:533
  48.7 4.0 %collective-permute-start.9 = (f32[32,40,128]{2,1,0:T(8,128)S(1)}, f32[32,40,128]{2,1,0:T(8,128)S(1)}, u32[]{:S(2)}, u32[]{:S(2)}) collective-permute-start(f32[32,40,128]{2,1,0:T(8,128)S(1)} %all-to-all-done.1), channel_id=1, source_target_pairs={{0,4},{4,0},{1,5},{5,1},{2,6},{6,2},{3,7},{7,3},{8,12},{12,8},{9,1... | collective-permute-start | bytes 1966088 | tf_op jit(solution)/shard_map/ppermute | solution.py:564
  52.6 1.7 collective-permute-done.9
  54.4 5.6 %all-to-all-start.2 = ((f32[64,128,128]{2,1,0:T(8,128)}), f32[64,128,128]{2,1,0:T(8,128)}, u32[]{:S(2)}, u32[]{:S(2)}) async-start(f32[64,128,128]{2,1,0:T(8,128)} %copy-done.2), calls=%async_computation.2 | async-start | bytes 8388608 | tf_op jit(solution)/shard_map/all_to_all | solution.py:533
  60.0 0.0 copy-done.5
  60.0 0.1 convert_reduce_fusion.1
  60.2 0.7 reduce_max.9
  61.5 0.1 pad.3.clone
  61.6 0.8 convert_reduce_fusion.starts_ref
  62.4 0.0 copy-done.15
  62.4 0.0 copy-done.16
  62.4 0.1 maximum_maximum_fusion.facts_ref
  62.5 0.0 copy-done.9
  62.5 0.0 copy-done.8
  62.5 10.7 %observations.1 = (bf16[1152,1152]{1,0:T(8,128)(2,1)S(1)}, bf16[1040,1280]{1,0:T(8,128)(2,1)S(1)}) custom-call(s32[4]{0:T(128)S(1)} %pad_add_fusion.position_ref, s32[1,1024]{1,0:T(1,128)S(1)} %bitcast.18, f32[8,1024]{1,0:T(8,128)S(1)} %maximum_maximum_fusion.facts_ref, f32[1280,128]{1,0:T(8,128)S(1)} %bitcast.16, f32[1280,128]{1,0:T(8,128)S(1)} %bitcast.19), custom_call_target="tpu_custom_call" | custom-call | flops 20000000000 | bytes 8388608 | tf_op jit(solution)/shard_map/observations/pallas_call | solution.py:344
  73.2 0.0 copy-start.12
  73.2 1.5 copy-done.12
  74.7 1.6 copy-done.14
  76.3 37.5 %all-to-all-done.2.block_ref.refs_8_ = f32[64,128,128]{2,1,0:T(8,128)} async-done(((f32[64,128,128]{2,1,0:T(8,128)}), f32[64,128,128]{2,1,0:T(8,128)}, u32[]{:S(2)}, u32[]{:S(2)}) %all-to-all-start.2) | async-done | bytes 4194336 | tf_op jit(solution)/shard_map/all_to_all | solution.py:533
  113.8 5.9 %covariances.1 = (f32[160,128]{1,0:T(8,128)}, f32[160,128]{1,0:T(8,128)}, f32[160,128]{1,0:T(8,128)}, f32[160,128]{1,0:T(8,128)}, f32[96,128]{1,0:T(8,128)S(1)},...) custom-call(s32[4]{0:T(128)} %copy-done.9, s32[17]{0:T(128)} %convert_reduce_fusion.starts_ref, ...), custom_call_target="tpu_custom_call" | custom-call | flops 3000000000 | bytes 7340032 | tf_op jit(solution)/shard_map/covariances/pallas_call | solution.py:460
  119.8 0.5 collective-permute-start.10
  120.3 3.4 %collective-permute-start.11 = (f32[160,128]{1,0:T(8,128)}, f32[160,128]{1,0:T(8,128)S(1)}, u32[]{:S(2)}, u32[]{:S(2)}) collective-permute-start(f32[160,128]{1,0:T(8,128)} %get-tuple-element.50), channel_id=1, source_target_pairs={{0,32},{16,48},{32,0},{48,16},{1,33},{17,49},{33,1},{49,17},{2,34}... | collective-permute-start | bytes 245768 | tf_op jit(solution)/shard_map/ppermute | solution.py:537
  123.7 3.5 %collective-permute-start.12 = (f32[160,128]{1,0:T(8,128)}, f32[160,128]{1,0:T(8,128)S(1)}, u32[]{:S(2)}, u32[]{:S(2)}) collective-permute-start(f32[160,128]{1,0:T(8,128)} %get-tuple-element.51), channel_id=1, source_target_pairs={{0,48},{16,0},{32,16},{48,32},{1,49},{17,1},{33,17},{49,33},{2,50}... | collective-permute-start | bytes 245768 | tf_op jit(solution)/shard_map/ppermute | solution.py:537
  127.2 0.0 collective-permute-done.10
  127.2 0.5 collective-permute-done.11
  127.7 1.3 collective-permute-done.12
  129.0 0.9 add_add_fusion.1.refs_0_
  129.9 6.6 %collective-permute-start.15 = (f32[160,128]{1,0:T(8,128)S(1)}, f32[160,128]{1,0:T(8,128)S(1)}, u32[]{:S(2)}, u32[]{:S(2)}) collective-permute-start(f32[160,128]{1,0:T(8,128)S(1)} %add_add_fusion.1.refs_0_), channel_id=1, source_target_pairs={{0,48},{16,0},{32,16},{48,32},{1,49},{17,1},{33,17},{49,33},{2,50}... | collective-permute-start | bytes 245768 | tf_op jit(solution)/shard_map/ppermute | solution.py:537
  136.5 2.4 %collective-permute-start.14 = (f32[160,128]{1,0:T(8,128)S(1)}, f32[160,128]{1,0:T(8,128)S(1)}, u32[]{:S(2)}, u32[]{:S(2)}) collective-permute-start(f32[160,128]{1,0:T(8,128)S(1)} %add_add_fusion.1.refs_0_), channel_id=1, source_target_pairs={{0,32},{16,48},{32,0},{48,16},{1,33},{17,49},{33,1},{49,17},{2,34}... | collective-permute-start | bytes 245768 | tf_op jit(solution)/shard_map/ppermute | solution.py:537
  138.9 0.0 collective-permute-start.13
  138.9 0.0 collective-permute-done.15.refs_3_
  138.9 6.7 %collective-permute-done.14.refs_2_ = f32[160,128]{1,0:T(8,128)S(1)} collective-permute-done((f32[160,128]{1,0:T(8,128)S(1)}, f32[160,128]{1,0:T(8,128)S(1)}, u32[]{:S(2)}, u32[]{:S(2)}) %collective-permute-start.14) | collective-permute-done | bytes 81952 | tf_op jit(solution)/shard_map/ppermute | solution.py:537
  145.6 0.0 collective-permute-done.13.refs_1_
  145.6 0.0 copy-done.10
  145.6 0.0 copy-done.11
  145.6 0.0 copy-done.13
  145.6 6.5 %updated.1 = f32[64,128,128]{2,1,0:T(8,128)S(1)} custom-call(s32[4]{0:T(128)S(1)} %copy-done.10, s32[17]{0:T(128)S(1)} %copy-done.11, f32[160,128]{1,0:T(8,128)S(1)} %add_add_fusion.1.refs_0_, f32[160,128]{1,0:T(8,128)S(1)} %collective-permute-done.13.refs_1_, f32[160,128]{1,0:T(8,128)S(1)} %collective-permute-done.14.refs_2_, ...), custom_call_target="tpu_custom_call" | custom-call | flops 4000000000 | bytes 8388608 | tf_op jit(solution)/shard_map/updated/pallas_call | solution.py:515
  152.1 60.3 %all_to_all.20.in_ref = f32[64,128,128]{2,1,0:T(8,128)} all-to-all(f32[64,128,128]{2,1,0:T(8,128)S(1)} %updated.1), channel_id=1, replica_groups=mesh['y'=4,'h'=4,'l'=2,'c'=2,'x'=4] {'c','y','l','x'}, dimensions={0} | all-to-all | bytes 8388608 | tf_op jit(solution)/shard_map/all_to_all | solution.py:533
  212.4 4.1 %collect.1 = f32[128,64,128]{2,1,0:T(8,128)} custom-call(f32[64,128,128]{2,1,0:T(8,128)} %all_to_all.20.in_ref), custom_call_target="tpu_custom_call" | custom-call | flops 1000000 | bytes 8388608 | tf_op jit(solution)/shard_map/collect/pallas_call | solution.py:197
  (24 shorter events, 0.1 us)
Async XLA Ops:
  0.1 62.4 %copy-start.9 = (s32[4]{0:T(128)}, s32[4]{0:T(128)S(1)}, u32[]{:S(2)}) copy-start(s32[4]{0:T(128)S(1)} %pad_add_fusion.position_ref) | copy-start | bytes 52
  0.1 0.7 copy-start.3
  0.8 0.8 copy-start.6
  2.7 16.6 %all-to-all-start = ((f32[32,4,128]{2,1,0:T(4,128)}), f32[32,4,128]{2,1,0:T(4,128)S(1)}, u32[]{:S(2)}, u32[]{:S(2)}) async-start(f32[32,4,128]{2,1,0:T(4,128)} %bitcast.6), calls=%async_computation | async-start | bytes 131072 | tf_op jit(solution)/shard_map/all_to_all | solution.py:533
  12.0 2.2 %copy-start = (f32[1,1048576]{1,0:T(1,128)S(1)}, f32[1,1048576]{1,0:T(1,128)}, u32[]{:S(2)}) copy-start(f32[1,1048576]{1,0:T(1,128)} %param.8) | copy-start | bytes 12582916
  14.2 0.7 copy-start.4
  14.8 0.7 copy-start.7
  19.4 8.5 %collective-permute-start.8 = (f32[12,128]{1,0:T(8,128)S(1)}, f32[12,128]{1,0:T(8,128)S(1)}, u32[]{:S(2)}, u32[]{:S(2)}) collective-permute-start(f32[12,128]{1,0:T(8,128)S(1)} %pad_maximum_fusion), channel_id=1, source_target_pairs={{0,48},{16,0},{32,16},{48,32},{1,49},{17,1},{33,17},{49,33},{2,50}... | collective-permute-start | bytes 18440 | tf_op jit(solution)/shard_map/ppermute | solution.py:537
  24.5 6.4 %collective-permute-start.7 = (f32[12,128]{1,0:T(8,128)S(1)}, f32[12,128]{1,0:T(8,128)S(1)}, u32[]{:S(2)}, u32[]{:S(2)}) collective-permute-start(f32[12,128]{1,0:T(8,128)S(1)} %pad_maximum_fusion), channel_id=1, source_target_pairs={{0,32},{16,48},{32,0},{48,16},{1,33},{17,49},{33,1},{49,17},{2,34}... | collective-permute-start | bytes 18440 | tf_op jit(solution)/shard_map/ppermute | solution.py:537
  25.7 5.3 %collective-permute-start.6 = (f32[12,128]{1,0:T(8,128)S(1)}, f32[12,128]{1,0:T(8,128)S(1)}, u32[]{:S(2)}, u32[]{:S(2)}) collective-permute-start(f32[12,128]{1,0:T(8,128)S(1)} %pad_maximum_fusion), channel_id=1, source_target_pairs={{0,16},{16,32},{32,48},{48,0},{1,17},{17,33},{33,49},{49,1},{2,18}... | collective-permute-start | bytes 18440 | tf_op jit(solution)/shard_map/ppermute | solution.py:537
  31.9 16.8 %all-to-all-start.1 = ((f32[32,40,128]{2,1,0:T(8,128)}), f32[32,40,128]{2,1,0:T(8,128)S(1)}, u32[]{:S(2)}, u32[]{:S(2)}) async-start(f32[32,40,128]{2,1,0:T(8,128)} %broadcast_in_dim.34), calls=%async_computation.1 | async-start | bytes 1310720 | tf_op jit(solution)/shard_map/all_to_all | solution.py:533
  38.9 2.2 %copy-start.1 = (f32[1,1048576]{1,0:T(1,128)S(1)}, f32[1,1048576]{1,0:T(1,128)}, u32[]{:S(2)}) copy-start(f32[1,1048576]{1,0:T(1,128)} %param.8) | copy-start | bytes 12582916
  43.9 2.0 copy-start.2
  46.0 14.0 %copy-start.5 = (s32[1024]{0:T(1024)S(1)}, s32[1024]{0:T(1024)}, u32[]{:S(2)}) copy-start(s32[1024]{0:T(1024)} %locations_ref.1) | copy-start | bytes 12292
  46.0 16.4 %copy-start.15 = (f32[1024]{0:T(1024)S(1)}, f32[1024]{0:T(1024)}, u32[]{:S(2)}) copy-start(f32[1024]{0:T(1024)} %param.13) | copy-start | bytes 12292
  46.0 16.4 %copy-start.16 = (f32[1024]{0:T(1024)S(1)}, f32[1024]{0:T(1024)}, u32[]{:S(2)}) copy-start(f32[1024]{0:T(1024)} %param.12) | copy-start | bytes 12292
  46.0 16.5 %copy-start.8 = (s32[1024]{0:T(1024)S(1)}, s32[1024]{0:T(1024)}, u32[]{:S(2)}) copy-start(s32[1024]{0:T(1024)} %plan_ref.1) | copy-start | bytes 12292
  48.7 5.7 %collective-permute-start.9 = (f32[32,40,128]{2,1,0:T(8,128)S(1)}, f32[32,40,128]{2,1,0:T(8,128)S(1)}, u32[]{:S(2)}, u32[]{:S(2)}) collective-permute-start(f32[32,40,128]{2,1,0:T(8,128)S(1)} %all-to-all-done.1), channel_id=1, source_target_pairs={{0,4},{4,0},{1,5},{5,1},{2,6},{6,2},{3,7},{7,3},{8,12},{12,8},{9,1... | collective-permute-start | bytes 1966088 | tf_op jit(solution)/shard_map/ppermute | solution.py:564
  54.4 59.4 %all-to-all-start.2 = ((f32[64,128,128]{2,1,0:T(8,128)}), f32[64,128,128]{2,1,0:T(8,128)}, u32[]{:S(2)}, u32[]{:S(2)}) async-start(f32[64,128,128]{2,1,0:T(8,128)} %copy-done.2), calls=%async_computation.2 | async-start | bytes 8388608 | tf_op jit(solution)/shard_map/all_to_all | solution.py:533
  73.2 1.5 copy-start.12
  74.7 1.6 copy-start.14
  113.8 31.8 %copy-start.10 = (s32[4]{0:T(128)S(1)}, s32[4]{0:T(128)}, u32[]{:S(2)}) copy-start(s32[4]{0:T(128)} %copy-done.9) | copy-start | bytes 52
  113.8 31.8 %copy-start.11 = (s32[17]{0:T(128)S(1)}, s32[17]{0:T(128)}, u32[]{:S(2)}) copy-start(s32[17]{0:T(128)} %convert_reduce_fusion.starts_ref) | copy-start | bytes 208
  113.8 31.8 %copy-start.13 = (bf16[1040,1280]{1,0:T(8,128)(2,1)S(1)}, bf16[1040,1280]{1,0:T(8,128)(2,1)}, u32[]{:S(2)}) copy-start(bf16[1040,1280]{1,0:T(8,128)(2,1)} %copy-done.12) | copy-start | bytes 7987204
  119.8 7.4 %collective-permute-start.10 = (f32[160,128]{1,0:T(8,128)}, f32[160,128]{1,0:T(8,128)S(1)}, u32[]{:S(2)}, u32[]{:S(2)}) collective-permute-start(f32[160,128]{1,0:T(8,128)} %get-tuple-element.49), channel_id=1, source_target_pairs={{0,16},{16,32},{32,48},{48,0},{1,17},{17,33},{33,49},{49,1},{2,18}... | collective-permute-start | bytes 245768 | tf_op jit(solution)/shard_map/ppermute | solution.py:537
  120.3 7.4 %collective-permute-start.11 = (f32[160,128]{1,0:T(8,128)}, f32[160,128]{1,0:T(8,128)S(1)}, u32[]{:S(2)}, u32[]{:S(2)}) collective-permute-start(f32[160,128]{1,0:T(8,128)} %get-tuple-element.50), channel_id=1, source_target_pairs={{0,32},{16,48},{32,0},{48,16},{1,33},{17,49},{33,1},{49,17},{2,34}... | collective-permute-start | bytes 245768 | tf_op jit(solution)/shard_map/ppermute | solution.py:537
  123.7 5.3 %collective-permute-start.12 = (f32[160,128]{1,0:T(8,128)}, f32[160,128]{1,0:T(8,128)S(1)}, u32[]{:S(2)}, u32[]{:S(2)}) collective-permute-start(f32[160,128]{1,0:T(8,128)} %get-tuple-element.51), channel_id=1, source_target_pairs={{0,48},{16,0},{32,16},{48,32},{1,49},{17,1},{33,17},{49,33},{2,50}... | collective-permute-start | bytes 245768 | tf_op jit(solution)/shard_map/ppermute | solution.py:537
  129.9 9.0 %collective-permute-start.15 = (f32[160,128]{1,0:T(8,128)S(1)}, f32[160,128]{1,0:T(8,128)S(1)}, u32[]{:S(2)}, u32[]{:S(2)}) collective-permute-start(f32[160,128]{1,0:T(8,128)S(1)} %add_add_fusion.1.refs_0_), channel_id=1, source_target_pairs={{0,48},{16,0},{32,16},{48,32},{1,49},{17,1},{33,17},{49,33},{2,50}... | collective-permute-start | bytes 245768 | tf_op jit(solution)/shard_map/ppermute | solution.py:537
  136.5 9.1 %collective-permute-start.14 = (f32[160,128]{1,0:T(8,128)S(1)}, f32[160,128]{1,0:T(8,128)S(1)}, u32[]{:S(2)}, u32[]{:S(2)}) collective-permute-start(f32[160,128]{1,0:T(8,128)S(1)} %add_add_fusion.1.refs_0_), channel_id=1, source_target_pairs={{0,32},{16,48},{32,0},{48,16},{1,33},{17,49},{33,1},{49,17},{2,34}... | collective-permute-start | bytes 245768 | tf_op jit(solution)/shard_map/ppermute | solution.py:537
  138.9 6.7 %collective-permute-start.13 = (f32[160,128]{1,0:T(8,128)S(1)}, f32[160,128]{1,0:T(8,128)S(1)}, u32[]{:S(2)}, u32[]{:S(2)}) collective-permute-start(f32[160,128]{1,0:T(8,128)S(1)} %add_add_fusion.1.refs_0_), channel_id=1, source_target_pairs={{0,16},{16,32},{32,48},{48,0},{1,17},{17,33},{33,49},{49,1},{2,18}... | collective-permute-start | bytes 245768 | tf_op jit(solution)/shard_map/ppermute | solution.py:537

commit v9 on v8

--- a/solution.py
+++ b/solution.py
@@ -449,7 +449,7 @@
     for windows in rest:
         windows()
     for d in range(SUMS):
-        to = (position_ref[1] + d) & (SUMS - 1)
+        to = position_ref[1] ^ d
         start = pl.multiple_of(to * FIRST_CHUNK, 16)
         out_refs[d][...] = total_ref[pl.ds(start, FIRST_CHUNK), :]
         start = pl.multiple_of(FIRST + to * REST_CHUNK, 16)
@@ -483,7 +483,7 @@
     for copy in arriving:
         copy.start()
     for d in range(SUMS):
-        of = (position_ref[1] - d) & (SUMS - 1)
+        of = position_ref[1] ^ d
         start = pl.multiple_of(of * FIRST_CHUNK, 16)
         right_ref[pl.ds(start, FIRST_CHUNK), :] = jnp.concatenate(two_parts(sums_refs[d][...]), axis=1)
         start = pl.multiple_of(FIRST + of * REST_CHUNK, 16)
@@ -533,15 +533,15 @@
     return lax.all_to_all(value, axes, 0, 0, tiled=True)
 
 
-def passed_along(value, by):
-    return lax.ppermute(value, "h", [(i, (i + by) % SUMS) for i in range(SUMS)])
+def swapped(value, by):
+    return lax.ppermute(value, "h", [(i, i ^ by) for i in range(SUMS)])
 
 
 def summed(parts):
     total = parts[0]
     for by in range(1, SUMS):
-        total = total + passed_along(parts[by], by)
-    return (total, *(passed_along(total, by) for by in range(1, SUMS)))
+        total = total + swapped(parts[by], by)
+    return (total, *(swapped(total, by) for by in range(1, SUMS)))
 
 
 def shards(state, locations, tile_mask, plan, obs_value, obs_error):
@@ -555,7 +555,7 @@
 
     observed = own_columns(plan, locations, rows)
     mine = jnp.concatenate([observed, masks], axis=0)
-    all_four = [mine] + [passed_along(mine, by) for by in range(1, SUMS)]
+    all_four = [mine] + [swapped(mine, by) for by in range(1, SUMS)]
     payload = jnp.concatenate(
         [*(each[0:8] for each in all_four), sum(each[8:12] for each in all_four), jnp.zeros((4, LANES), f32)], axis=0
     )

time: 217 us -> 217 us (level)
  starting transfers between devices: 50.8 us -> 44.7 us
  blocking collectives: 60.3 us -> 63.8 us
  waiting for transfers between devices: 54.3 us -> 56.7 us
    ppermute x9, starting transfers between devices: 24.9 us -> 18.9 us  [swapped(): return lax.ppermute(value, 'h', [(i, i ^ by) for i in range(SUMS)])]
    all_to_all x1, blocking collectives: 60.3 us -> 63.8 us  [exchange(): return lax.all_to_all(value, axes, 0, 0, tiled=True)]
    ppermute x9, waiting for transfers between devices: 11.6 us -> 14 us  [swapped(): return lax.ppermute(value, 'h', [(i, i ^ by) for i in range(SUMS)])]
  transfers between devices with their start and end apart: 13 -> 13, of which waited for: 8 -> 9; matrix products, arithmetic and copies ran while one was open for 1% -> 1% of each run, Pallas kernels for 8% -> 8%
where the time goes in v9:
time: 217 us
  blocking collectives  63.8 us (29%)
  waiting for transfers between devices  56.7 us (26%)
  starting transfers between devices  44.7 us (21%)
  Pallas kernels  34.3 us (16%)
  local copies, waits for them, and re-layouts  13.3 us (6%)
  other arithmetic  2.74 us (1%)
    all_to_all x1, blocking collectives, exchange(): return lax.all_to_all(value, axes, 0, 0, tiled=True)  63.8 us
    all_to_all x3, waiting for transfers between devices, exchange(): return lax.all_to_all(value, axes, 0, 0, tiled=True)  40.9 us
    all_to_all x3, starting transfers between devices, exchange(): return lax.all_to_all(value, axes, 0, 0, tiled=True)  21.9 us
    ppermute x9, starting transfers between devices, swapped(): return lax.ppermute(value, 'h', [(i, i ^ by) for i in range(SUMS)])  18.9 us
    ppermute x9, waiting for transfers between devices, swapped(): return lax.ppermute(value, 'h', [(i, i ^ by) for i in range(SUMS)])  14 us
    unnamed x34, local copies, waits for them, and re-layouts  12.3 us
    pallas_call x1, Pallas kernels, observations(): pl.pallas_call(observation_kernel, out_shape=(columns, factors), in_specs...  10.7 us
    pallas_call x1, Pallas kernels, updated(): pl.pallas_call(update_kernel, out_shape=struct((GROUP, OWN_TILES, LANES))...  6.5 us
  transfers between devices with their start and end apart: 13, of which 9 were waited for; matrix products, arithmetic and copies ran while one was open for 1% of the time, Pallas kernels for 8%

profile of v9, /device:TPU:1, one launch (start us, length us, event | category | flops | bytes accessed | tf_op | source)
XLA Modules:
  0.0 216.6 jit_solution(5463371466795241320)
XLA Ops:
  0.0 0.1 pad_add_fusion.position_ref
  0.1 0.0 copy-start.9
  0.1 0.7 copy-done.3
  0.8 0.8 copy-done.6
  1.5 1.2 own_masks.1
  2.7 9.2 %all-to-all-start = ((f32[32,4,128]{2,1,0:T(4,128)}), f32[32,4,128]{2,1,0:T(4,128)S(1)}, u32[]{:S(2)}, u32[]{:S(2)}) async-start(f32[32,4,128]{2,1,0:T(4,128)} %bitcast.6), calls=%async_computation | async-start | bytes 131072 | tf_op jit(solution)/shard_map/all_to_all | solution.py:533
  12.0 0.0 copy-start
  12.0 2.2 %copy-done = f32[1,1048576]{1,0:T(1,128)S(1)} copy-done((f32[1,1048576]{1,0:T(1,128)S(1)}, f32[1,1048576]{1,0:T(1,128)}, u32[]{:S(2)}) %copy-start) | copy-done | bytes 4194328
  14.2 0.7 copy-done.4
  14.8 0.7 copy-done.7
  15.5 3.1 %own_columns.1 = f32[8,128]{1,0:T(8,128)S(1)} custom-call(s32[1024]{0:T(1024)S(1)} %copy-done.7, s32[1024]{0:T(1024)S(1)} %copy-done.4, f32[8192,128]{1,0:T(8,128)S(1)} %bitcast.14), custom_call_target="tpu_custom_call" | custom-call | flops 1000000 | bytes 8388608 | tf_op jit(solution)/shard_map/own_columns/pallas_call | solution.py:142
  18.6 0.7 all-to-all-done
  19.4 5.2 %collective-permute-start.8 = (f32[12,128]{1,0:T(8,128)S(1)}, f32[12,128]{1,0:T(8,128)S(1)}, u32[]{:S(2)}, u32[]{:S(2)}) collective-permute-start(f32[12,128]{1,0:T(8,128)S(1)} %pad_maximum_fusion), channel_id=1, source_target_pairs={{0,48},{16,32},{32,16},{48,0},{1,49},{17,33},{33,17},{49,1},{2,50}... | collective-permute-start | bytes 18440 | tf_op jit(solution)/shard_map/ppermute | solution.py:537
  24.6 1.2 collective-permute-start.7
  25.7 1.0 collective-permute-start.6
  26.7 0.0 collective-permute-done.8
  26.7 4.2 %collective-permute-done.7 = f32[12,128]{1,0:T(8,128)S(1)} collective-permute-done((f32[12,128]{1,0:T(8,128)S(1)}, f32[12,128]{1,0:T(8,128)S(1)}, u32[]{:S(2)}, u32[]{:S(2)}) %collective-permute-start.7) | collective-permute-done | bytes 6176 | tf_op jit(solution)/shard_map/ppermute | solution.py:537
  31.0 0.0 collective-permute-done.6
  31.0 0.9 broadcast_in_dim.34
  31.9 7.0 %all-to-all-start.1 = ((f32[32,40,128]{2,1,0:T(8,128)}), f32[32,40,128]{2,1,0:T(8,128)S(1)}, u32[]{:S(2)}, u32[]{:S(2)}) async-start(f32[32,40,128]{2,1,0:T(8,128)} %broadcast_in_dim.34), calls=%async_computation.1 | async-start | bytes 1310720 | tf_op jit(solution)/shard_map/all_to_all | solution.py:533
  39.0 0.0 copy-start.1
  39.0 2.2 %copy-done.1 = f32[1,1048576]{1,0:T(1,128)S(1)} copy-done((f32[1,1048576]{1,0:T(1,128)S(1)}, f32[1,1048576]{1,0:T(1,128)}, u32[]{:S(2)}) %copy-start.1) | copy-done | bytes 4194328
  41.2 2.8 %spread_out.1 = f32[64,128,128]{2,1,0:T(8,128)S(1)} custom-call(f32[8192,128]{1,0:T(8,128)S(1)} %bitcast.15), custom_call_target="tpu_custom_call" | custom-call | flops 1000000 | bytes 8388608 | tf_op jit(solution)/shard_map/spread_out/pallas_call | solution.py:160
  44.0 0.0 copy-start.2
  44.0 2.0 copy-done.2
  46.0 2.7 %all-to-all-done.1 = f32[32,40,128]{2,1,0:T(8,128)S(1)} async-done(((f32[32,40,128]{2,1,0:T(8,128)}), f32[32,40,128]{2,1,0:T(8,128)S(1)}, u32[]{:S(2)}, u32[]{:S(2)}) %all-to-all-start.1) | async-done | bytes 655392 | tf_op jit(solution)/shard_map/all_to_all | solution.py:533
  48.7 4.0 %collective-permute-start.9 = (f32[32,40,128]{2,1,0:T(8,128)S(1)}, f32[32,40,128]{2,1,0:T(8,128)S(1)}, u32[]{:S(2)}, u32[]{:S(2)}) collective-permute-start(f32[32,40,128]{2,1,0:T(8,128)S(1)} %all-to-all-done.1), channel_id=1, source_target_pairs={{0,4},{4,0},{1,5},{5,1},{2,6},{6,2},{3,7},{7,3},{8,12},{12,8},{9,1... | collective-permute-start | bytes 1966088 | tf_op jit(solution)/shard_map/ppermute | solution.py:564
  52.6 1.7 collective-permute-done.9
  54.4 5.6 %all-to-all-start.2 = ((f32[64,128,128]{2,1,0:T(8,128)}), f32[64,128,128]{2,1,0:T(8,128)}, u32[]{:S(2)}, u32[]{:S(2)}) async-start(f32[64,128,128]{2,1,0:T(8,128)} %copy-done.2), calls=%async_computation.2 | async-start | bytes 8388608 | tf_op jit(solution)/shard_map/all_to_all | solution.py:533
  60.0 0.0 copy-done.5
  60.0 0.1 convert_reduce_fusion.1
  60.2 0.7 reduce_max.9
  61.6 0.1 pad.3.clone
  61.6 0.8 convert_reduce_fusion.starts_ref
  62.4 0.0 copy-done.15
  62.4 0.0 copy-done.16
  62.4 0.1 maximum_maximum_fusion.facts_ref
  62.5 0.0 copy-done.9
  62.5 0.0 copy-done.8
  62.5 10.7 %observations.1 = (bf16[1152,1152]{1,0:T(8,128)(2,1)S(1)}, bf16[1040,1280]{1,0:T(8,128)(2,1)S(1)}) custom-call(s32[4]{0:T(128)S(1)} %pad_add_fusion.position_ref, s32[1,1024]{1,0:T(1,128)S(1)} %bitcast.18, f32[8,1024]{1,0:T(8,128)S(1)} %maximum_maximum_fusion.facts_ref, f32[1280,128]{1,0:T(8,128)S(1)} %bitcast.16, f32[1280,128]{1,0:T(8,128)S(1)} %bitcast.19), custom_call_target="tpu_custom_call" | custom-call | flops 20000000000 | bytes 8388608 | tf_op jit(solution)/shard_map/observations/pallas_call | solution.py:344
  73.2 0.0 copy-start.12
  73.2 1.5 copy-done.12
  74.7 1.6 copy-done.14
  76.3 37.5 %all-to-all-done.2.block_ref.refs_8_ = f32[64,128,128]{2,1,0:T(8,128)} async-done(((f32[64,128,128]{2,1,0:T(8,128)}), f32[64,128,128]{2,1,0:T(8,128)}, u32[]{:S(2)}, u32[]{:S(2)}) %all-to-all-start.2) | async-done | bytes 4194336 | tf_op jit(solution)/shard_map/all_to_all | solution.py:533
  113.8 5.9 %covariances.1 = (f32[160,128]{1,0:T(8,128)}, f32[160,128]{1,0:T(8,128)}, f32[160,128]{1,0:T(8,128)}, f32[160,128]{1,0:T(8,128)}, f32[96,128]{1,0:T(8,128)S(1)},...) custom-call(s32[4]{0:T(128)} %copy-done.9, s32[17]{0:T(128)} %convert_reduce_fusion.starts_ref, ...), custom_call_target="tpu_custom_call" | custom-call | flops 3000000000 | bytes 7340032 | tf_op jit(solution)/shard_map/covariances/pallas_call | solution.py:460
  119.7 1.3 collective-permute-start.10
  121.1 2.6 %collective-permute-start.11 = (f32[160,128]{1,0:T(8,128)}, f32[160,128]{1,0:T(8,128)S(1)}, u32[]{:S(2)}, u32[]{:S(2)}) collective-permute-start(f32[160,128]{1,0:T(8,128)} %get-tuple-element.50), channel_id=1, source_target_pairs={{0,32},{16,48},{32,0},{48,16},{1,33},{17,49},{33,1},{49,17},{2,34}... | collective-permute-start | bytes 245768 | tf_op jit(solution)/shard_map/ppermute | solution.py:537
  123.7 1.8 collective-permute-start.12
  125.5 0.0 collective-permute-done.10
  125.5 3.1 %collective-permute-done.11 = f32[160,128]{1,0:T(8,128)S(1)} collective-permute-done((f32[160,128]{1,0:T(8,128)}, f32[160,128]{1,0:T(8,128)S(1)}, u32[]{:S(2)}, u32[]{:S(2)}) %collective-permute-start.11) | collective-permute-done | bytes 81952 | tf_op jit(solution)/shard_map/ppermute | solution.py:537
  128.6 4.6 %collective-permute-done.12 = f32[160,128]{1,0:T(8,128)S(1)} collective-permute-done((f32[160,128]{1,0:T(8,128)}, f32[160,128]{1,0:T(8,128)S(1)}, u32[]{:S(2)}, u32[]{:S(2)}) %collective-permute-start.12) | collective-permute-done | bytes 81952 | tf_op jit(solution)/shard_map/ppermute | solution.py:537
  133.2 0.9 add_add_fusion.1.refs_0_
  134.1 0.1 collective-permute-start.15
  134.2 2.7 %collective-permute-start.14 = (f32[160,128]{1,0:T(8,128)S(1)}, f32[160,128]{1,0:T(8,128)S(1)}, u32[]{:S(2)}, u32[]{:S(2)}) collective-permute-start(f32[160,128]{1,0:T(8,128)S(1)} %add_add_fusion.1.refs_0_), channel_id=1, source_target_pairs={{0,32},{16,48},{32,0},{48,16},{1,33},{17,49},{33,1},{49,17},{2,34}... | collective-permute-start | bytes 245768 | tf_op jit(solution)/shard_map/ppermute | solution.py:537
  136.9 2.9 %collective-permute-start.13 = (f32[160,128]{1,0:T(8,128)S(1)}, f32[160,128]{1,0:T(8,128)S(1)}, u32[]{:S(2)}, u32[]{:S(2)}) collective-permute-start(f32[160,128]{1,0:T(8,128)S(1)} %add_add_fusion.1.refs_0_), channel_id=1, source_target_pairs={{0,16},{16,0},{32,48},{48,32},{1,17},{17,1},{33,49},{49,33},{2,18}... | collective-permute-start | bytes 245768 | tf_op jit(solution)/shard_map/ppermute | solution.py:537
  139.8 0.0 collective-permute-done.15.refs_3_
  139.8 1.8 collective-permute-done.14.refs_2_
  141.6 0.3 collective-permute-done.13.refs_1_
  142.0 0.0 copy-done.10
  142.0 0.0 copy-done.11
  142.0 0.0 copy-done.13
  142.0 6.5 %updated.1 = f32[64,128,128]{2,1,0:T(8,128)S(1)} custom-call(s32[4]{0:T(128)S(1)} %copy-done.10, s32[17]{0:T(128)S(1)} %copy-done.11, f32[160,128]{1,0:T(8,128)S(1)} %add_add_fusion.1.refs_0_, f32[160,128]{1,0:T(8,128)S(1)} %collective-permute-done.13.refs_1_, f32[160,128]{1,0:T(8,128)S(1)} %collective-permute-done.14.refs_2_, ...), custom_call_target="tpu_custom_call" | custom-call | flops 4000000000 | bytes 8388608 | tf_op jit(solution)/shard_map/updated/pallas_call | solution.py:515
  148.5 63.8 %all_to_all.20.in_ref = f32[64,128,128]{2,1,0:T(8,128)} all-to-all(f32[64,128,128]{2,1,0:T(8,128)S(1)} %updated.1), channel_id=1, replica_groups=mesh['y'=4,'h'=4,'l'=2,'c'=2,'x'=4] {'c','y','l','x'}, dimensions={0} | all-to-all | bytes 8388608 | tf_op jit(solution)/shard_map/all_to_all | solution.py:533
  212.3 4.1 %collect.1 = f32[128,64,128]{2,1,0:T(8,128)} custom-call(f32[64,128,128]{2,1,0:T(8,128)} %all_to_all.20.in_ref), custom_call_target="tpu_custom_call" | custom-call | flops 1000000 | bytes 8388608 | tf_op jit(solution)/shard_map/collect/pallas_call | solution.py:197
  (24 shorter events, 0.1 us)
Async XLA Ops:
  0.1 62.4 %copy-start.9 = (s32[4]{0:T(128)}, s32[4]{0:T(128)S(1)}, u32[]{:S(2)}) copy-start(s32[4]{0:T(128)S(1)} %pad_add_fusion.position_ref) | copy-start | bytes 52
  0.1 0.7 copy-start.3
  0.8 0.8 copy-start.6
  2.7 16.6 %all-to-all-start = ((f32[32,4,128]{2,1,0:T(4,128)}), f32[32,4,128]{2,1,0:T(4,128)S(1)}, u32[]{:S(2)}, u32[]{:S(2)}) async-start(f32[32,4,128]{2,1,0:T(4,128)} %bitcast.6), calls=%async_computation | async-start | bytes 131072 | tf_op jit(solution)/shard_map/all_to_all | solution.py:533
  12.0 2.2 %copy-start = (f32[1,1048576]{1,0:T(1,128)S(1)}, f32[1,1048576]{1,0:T(1,128)}, u32[]{:S(2)}) copy-start(f32[1,1048576]{1,0:T(1,128)} %param.8) | copy-start | bytes 12582916
  14.2 0.7 copy-start.4
  14.8 0.7 copy-start.7
  19.4 7.4 %collective-permute-start.8 = (f32[12,128]{1,0:T(8,128)S(1)}, f32[12,128]{1,0:T(8,128)S(1)}, u32[]{:S(2)}, u32[]{:S(2)}) collective-permute-start(f32[12,128]{1,0:T(8,128)S(1)} %pad_maximum_fusion), channel_id=1, source_target_pairs={{0,48},{16,32},{32,16},{48,0},{1,49},{17,33},{33,17},{49,1},{2,50}... | collective-permute-start | bytes 18440 | tf_op jit(solution)/shard_map/ppermute | solution.py:537
  24.6 6.4 %collective-permute-start.7 = (f32[12,128]{1,0:T(8,128)S(1)}, f32[12,128]{1,0:T(8,128)S(1)}, u32[]{:S(2)}, u32[]{:S(2)}) collective-permute-start(f32[12,128]{1,0:T(8,128)S(1)} %pad_maximum_fusion), channel_id=1, source_target_pairs={{0,32},{16,48},{32,0},{48,16},{1,33},{17,49},{33,1},{49,17},{2,34}... | collective-permute-start | bytes 18440 | tf_op jit(solution)/shard_map/ppermute | solution.py:537
  25.7 5.3 %collective-permute-start.6 = (f32[12,128]{1,0:T(8,128)S(1)}, f32[12,128]{1,0:T(8,128)S(1)}, u32[]{:S(2)}, u32[]{:S(2)}) collective-permute-start(f32[12,128]{1,0:T(8,128)S(1)} %pad_maximum_fusion), channel_id=1, source_target_pairs={{0,16},{16,0},{32,48},{48,32},{1,17},{17,1},{33,49},{49,33},{2,18}... | collective-permute-start | bytes 18440 | tf_op jit(solution)/shard_map/ppermute | solution.py:537
  31.9 16.8 %all-to-all-start.1 = ((f32[32,40,128]{2,1,0:T(8,128)}), f32[32,40,128]{2,1,0:T(8,128)S(1)}, u32[]{:S(2)}, u32[]{:S(2)}) async-start(f32[32,40,128]{2,1,0:T(8,128)} %broadcast_in_dim.34), calls=%async_computation.1 | async-start | bytes 1310720 | tf_op jit(solution)/shard_map/all_to_all | solution.py:533
  39.0 2.2 %copy-start.1 = (f32[1,1048576]{1,0:T(1,128)S(1)}, f32[1,1048576]{1,0:T(1,128)}, u32[]{:S(2)}) copy-start(f32[1,1048576]{1,0:T(1,128)} %param.8) | copy-start | bytes 12582916
  44.0 2.0 copy-start.2
  46.0 14.0 %copy-start.5 = (s32[1024]{0:T(1024)S(1)}, s32[1024]{0:T(1024)}, u32[]{:S(2)}) copy-start(s32[1024]{0:T(1024)} %locations_ref.1) | copy-start | bytes 12292
  46.0 16.4 %copy-start.15 = (f32[1024]{0:T(1024)S(1)}, f32[1024]{0:T(1024)}, u32[]{:S(2)}) copy-start(f32[1024]{0:T(1024)} %param.13) | copy-start | bytes 12292
  46.0 16.4 %copy-start.16 = (f32[1024]{0:T(1024)S(1)}, f32[1024]{0:T(1024)}, u32[]{:S(2)}) copy-start(f32[1024]{0:T(1024)} %param.12) | copy-start | bytes 12292
  46.0 16.5 %copy-start.8 = (s32[1024]{0:T(1024)S(1)}, s32[1024]{0:T(1024)}, u32[]{:S(2)}) copy-start(s32[1024]{0:T(1024)} %plan_ref.1) | copy-start | bytes 12292
  48.7 5.7 %collective-permute-start.9 = (f32[32,40,128]{2,1,0:T(8,128)S(1)}, f32[32,40,128]{2,1,0:T(8,128)S(1)}, u32[]{:S(2)}, u32[]{:S(2)}) collective-permute-start(f32[32,40,128]{2,1,0:T(8,128)S(1)} %all-to-all-done.1), channel_id=1, source_target_pairs={{0,4},{4,0},{1,5},{5,1},{2,6},{6,2},{3,7},{7,3},{8,12},{12,8},{9,1... | collective-permute-start | bytes 1966088 | tf_op jit(solution)/shard_map/ppermute | solution.py:564
  54.4 59.4 %all-to-all-start.2 = ((f32[64,128,128]{2,1,0:T(8,128)}), f32[64,128,128]{2,1,0:T(8,128)}, u32[]{:S(2)}, u32[]{:S(2)}) async-start(f32[64,128,128]{2,1,0:T(8,128)} %copy-done.2), calls=%async_computation.2 | async-start | bytes 8388608 | tf_op jit(solution)/shard_map/all_to_all | solution.py:533
  73.2 1.5 copy-start.12
  74.7 1.6 copy-start.14
  113.8 28.2 %copy-start.10 = (s32[4]{0:T(128)S(1)}, s32[4]{0:T(128)}, u32[]{:S(2)}) copy-start(s32[4]{0:T(128)} %copy-done.9) | copy-start | bytes 52
  113.8 28.2 %copy-start.11 = (s32[17]{0:T(128)S(1)}, s32[17]{0:T(128)}, u32[]{:S(2)}) copy-start(s32[17]{0:T(128)} %convert_reduce_fusion.starts_ref) | copy-start | bytes 208
  113.8 28.2 %copy-start.13 = (bf16[1040,1280]{1,0:T(8,128)(2,1)S(1)}, bf16[1040,1280]{1,0:T(8,128)(2,1)}, u32[]{:S(2)}) copy-start(bf16[1040,1280]{1,0:T(8,128)(2,1)} %copy-done.12) | copy-start | bytes 7987204
  119.7 5.7 %collective-permute-start.10 = (f32[160,128]{1,0:T(8,128)}, f32[160,128]{1,0:T(8,128)S(1)}, u32[]{:S(2)}, u32[]{:S(2)}) collective-permute-start(f32[160,128]{1,0:T(8,128)} %get-tuple-element.49), channel_id=1, source_target_pairs={{0,16},{16,0},{32,48},{48,32},{1,17},{17,1},{33,49},{49,33},{2,18}... | collective-permute-start | bytes 245768 | tf_op jit(solution)/shard_map/ppermute | solution.py:537
  121.1 7.5 %collective-permute-start.11 = (f32[160,128]{1,0:T(8,128)}, f32[160,128]{1,0:T(8,128)S(1)}, u32[]{:S(2)}, u32[]{:S(2)}) collective-permute-start(f32[160,128]{1,0:T(8,128)} %get-tuple-element.50), channel_id=1, source_target_pairs={{0,32},{16,48},{32,0},{48,16},{1,33},{17,49},{33,1},{49,17},{2,34}... | collective-permute-start | bytes 245768 | tf_op jit(solution)/shard_map/ppermute | solution.py:537
  123.7 9.5 %collective-permute-start.12 = (f32[160,128]{1,0:T(8,128)}, f32[160,128]{1,0:T(8,128)S(1)}, u32[]{:S(2)}, u32[]{:S(2)}) collective-permute-start(f32[160,128]{1,0:T(8,128)} %get-tuple-element.51), channel_id=1, source_target_pairs={{0,48},{16,32},{32,16},{48,0},{1,49},{17,33},{33,17},{49,1},{2,50}... | collective-permute-start | bytes 245768 | tf_op jit(solution)/shard_map/ppermute | solution.py:537
  134.1 5.7 %collective-permute-start.15 = (f32[160,128]{1,0:T(8,128)S(1)}, f32[160,128]{1,0:T(8,128)S(1)}, u32[]{:S(2)}, u32[]{:S(2)}) collective-permute-start(f32[160,128]{1,0:T(8,128)S(1)} %add_add_fusion.1.refs_0_), channel_id=1, source_target_pairs={{0,48},{16,32},{32,16},{48,0},{1,49},{17,33},{33,17},{49,1},{2,50}... | collective-permute-start | bytes 245768 | tf_op jit(solution)/shard_map/ppermute | solution.py:537
  134.2 7.4 %collective-permute-start.14 = (f32[160,128]{1,0:T(8,128)S(1)}, f32[160,128]{1,0:T(8,128)S(1)}, u32[]{:S(2)}, u32[]{:S(2)}) collective-permute-start(f32[160,128]{1,0:T(8,128)S(1)} %add_add_fusion.1.refs_0_), channel_id=1, source_target_pairs={{0,32},{16,48},{32,0},{48,16},{1,33},{17,49},{33,1},{49,17},{2,34}... | collective-permute-start | bytes 245768 | tf_op jit(solution)/shard_map/ppermute | solution.py:537
  136.9 5.0 %collective-permute-start.13 = (f32[160,128]{1,0:T(8,128)S(1)}, f32[160,128]{1,0:T(8,128)S(1)}, u32[]{:S(2)}, u32[]{:S(2)}) collective-permute-start(f32[160,128]{1,0:T(8,128)S(1)} %add_add_fusion.1.refs_0_), channel_id=1, source_target_pairs={{0,16},{16,0},{32,48},{48,32},{1,17},{17,1},{33,49},{49,33},{2,18}... | collective-permute-start | bytes 245768 | tf_op jit(solution)/shard_map/ppermute | solution.py:537

commit v10 on v9

--- a/solution.py
+++ b/solution.py
@@ -27,7 +27,6 @@
 SLICES = 4
 LANES = 128
 OWN_TILES = NTILES // RESIDUES
-ROWS = NTILES * TILE // LANES
 EIGHT = 8
 WIDE = EIGHT * GROUP
 GROUPS = OWN_TILES // EIGHT
@@ -39,7 +38,6 @@
 TILES = slice(2 * WIDE, 2 * WIDE + LANES)
 TILE_ROWS = slice(2 * WIDE, 2 * WIDE + 16)
 NOWHERE = -512
-BLOCK_TILES = 16
 FIRST = 640
 FIRST_CHUNK = FIRST // SUMS
 REST_CHUNK = (NOBS - FIRST) // SUMS
@@ -116,7 +114,26 @@
     )(position, locations, tile_mask)
 
 
-def columns_kernel(plan_ref, locations_ref, state_ref, out_ref, picked_ref):
+PIECES = 8
+
+
+def columns_kernel(
+    plan_ref, locations_ref, state_ref, out_ref, spread_ref, held_ref, picked_ref, in_sems, out_sems
+):
+    tiles = OWN_TILES // PIECES
+    arriving = [
+        pltpu.make_async_copy(
+            state_ref.at[pl.ds(n * tiles, tiles)], held_ref.at[pl.ds(n * tiles, tiles)], in_sems.at[n]
+        )
+        for n in range(PIECES)
+    ]
+    leaving = [pltpu.make_async_copy(held_ref.at[:, d, :], spread_ref.at[d], out_sems.at[d]) for d in range(GROUP)]
+    for copy in arriving:
+        copy.start()
+    for copy in arriving:
+        copy.wait()
+    for copy in leaving:
+        copy.start()
     lane = lax.broadcasted_iota(i32, (1, LANES), 1)
 
     def step(i, carry):
@@ -124,7 +141,7 @@
         found = []
         for u in range(8):
             where = locations_ref[plan_ref[base + u]]
-            row = state_ref[pl.ds(where >> 7, 1), :]
+            row = held_ref[where >> 13, pl.ds((where >> 7) & (GROUP - 1), 1), :]
             found.append(jnp.where(lane == (where & (LANES - 1)), row, 0.0))
         picked_ref[pl.ds(base, 8), :] = jnp.concatenate(found, axis=0)
         return carry
@@ -136,40 +153,26 @@
         total = total + lax.dot_general(ones, part, (((1,), (1,)), ((), ())), preferred_element_type=f32)
     for g in range(NOBS // LANES):
         out_ref[pl.ds(g, 1), :] = total[0:1, g * LANES : (g + 1) * LANES]
-
-
-def own_columns(plan, locations, rows):
+    for copy in leaving:
+        copy.wait()
+
+
+def own_columns_and_spread(plan, locations, state):
     return pl.pallas_call(
         columns_kernel,
-        out_shape=struct((NOBS // LANES, LANES)),
-        in_specs=[SMEM, SMEM, VMEM],
-        out_specs=VMEM,
-        scratch_shapes=[pltpu.VMEM((NOBS, LANES), f32)],
-        compiler_params=kernel_params(24),
+        out_shape=(struct((NOBS // LANES, LANES)), struct((GROUP, OWN_TILES, LANES))),
+        in_specs=[SMEM, SMEM, ANY],
+        out_specs=(VMEM, ANY),
+        scratch_shapes=[
+            pltpu.VMEM((OWN_TILES, GROUP, LANES), f32),
+            pltpu.VMEM((NOBS, LANES), f32),
+            pltpu.SemaphoreType.DMA((PIECES,)),
+            pltpu.SemaphoreType.DMA((GROUP,)),
+        ],
+        compiler_params=kernel_params(60),
         cost_estimate=pl.CostEstimate(flops=10**6, bytes_accessed=8 * 2**20, transcendentals=0),
         name="own_columns",
-    )(plan, locations, rows)
-
-
-def spread_kernel(state_ref, out_ref):
-    for d in range(GROUP):
-        out_ref[d] = state_ref[pl.ds(d, BLOCK_TILES, stride=GROUP), :]
-
-
-def spread_out(rows):
-    return pl.pallas_call(
-        spread_kernel,
-        grid=(OWN_TILES // BLOCK_TILES,),
-        out_shape=struct((GROUP, OWN_TILES, LANES)),
-        in_specs=[pl.BlockSpec((GROUP * BLOCK_TILES, LANES), lambda i: (i, 0))],
-        out_specs=pl.BlockSpec((GROUP, BLOCK_TILES, LANES), lambda i: (0, i, 0)),
-        compiler_params=kernel_params(16),
-        cost_estimate=pl.CostEstimate(flops=10**6, bytes_accessed=8 * 2**20, transcendentals=0),
-        name="spread_out",
-    )(rows)
-
-
-PIECES = 8
+    )(plan, locations, state.reshape(OWN_TILES, GROUP, LANES))
 
 
 def collect_kernel(in_ref, state_ref, held_ref, in_sems, out_sems):
@@ -547,20 +550,18 @@
 def shards(state, locations, tile_mask, plan, obs_value, obs_error):
     residue = lax.axis_index(PEERS) // SLICES
     position = jnp.stack([residue, lax.axis_index("h"), lax.axis_index("c"), lax.axis_index(ALL)]).astype(i32)
-    rows = state.reshape(ROWS, LANES)
 
     masks = own_masks(position, locations.reshape(-1, LANES), tile_mask)
     masks = exchange(masks.reshape(GROUP_CHIPS, 4, LANES), CHIPS).sum(axis=0)
     tiles = locations // TILE
 
-    observed = own_columns(plan, locations, rows)
+    observed, block = own_columns_and_spread(plan, locations, state)
     mine = jnp.concatenate([observed, masks], axis=0)
     all_four = [mine] + [swapped(mine, by) for by in range(1, SUMS)]
     payload = jnp.concatenate(
         [*(each[0:8] for each in all_four), sum(each[8:12] for each in all_four), jnp.zeros((4, LANES), f32)], axis=0
     )
     gathered = exchange(jnp.broadcast_to(payload[None], (GROUP_CHIPS, 40, LANES)), CHIPS)
-    block, gathered = lax.optimization_barrier((spread_out(rows), gathered))
     other = lax.ppermute(gathered, "c", [(0, 1), (1, 0)])
     block, other = lax.optimization_barrier((block, other))
     block = exchange(block)

time: 217 us -> 219 us (level)
  blocking collectives: 63.8 us -> 81.2 us
  local copies, waits for them, and re-layouts: 13.3 us -> 5.39 us
  starting transfers between devices: 44.7 us -> 37.7 us
  waiting for transfers between devices: 56.7 us -> 53.3 us
    all_to_all x1 -> x2, blocking collectives: 63.8 us -> 81.2 us  [exchange(): return lax.all_to_all(value, axes, 0, 0, tiled=True)]
    unnamed x34 -> x24, local copies, waits for them, and re-layouts: 12.3 us -> 4.55 us
    all_to_all x3 -> x2, starting transfers between devices: 21.9 us -> 15 us  [exchange(): return lax.all_to_all(value, axes, 0, 0, tiled=True)]
    all_to_all x3 -> x2, waiting for transfers between devices: 40.9 us -> 37.6 us  [exchange(): return lax.all_to_all(value, axes, 0, 0, tiled=True)]
    pallas_call x2 -> x1, Pallas kernels: 5.86 us -> 7.83 us  [own_columns_and_spread(): pl.pallas_call(columns_kernel, out_shape=(struct((NOBS // LANES, LANES)),...]
  transfers between devices with their start and end apart: 13 -> 12, of which waited for: 9 -> 7; matrix products, arithmetic and copies ran while one was open for 1% -> 1% of each run, Pallas kernels for 8% -> 9%
where the time goes in v10:
time: 219 us; the launch traced here: 218 us
  blocking collectives  81.2 us (37%)
  waiting for transfers between devices  53.3 us (24%)
  starting transfers between devices  37.7 us (17%)
  Pallas kernels  36.2 us (17%)
  local copies, waits for them, and re-layouts  5.39 us (2%)
  other arithmetic  3.38 us (2%)
    all_to_all x2, blocking collectives, exchange(): return lax.all_to_all(value, axes, 0, 0, tiled=True)  81.2 us
    all_to_all x2, waiting for transfers between devices, exchange(): return lax.all_to_all(value, axes, 0, 0, tiled=True)  37.6 us
    ppermute x9, starting transfers between devices, swapped(): return lax.ppermute(value, 'h', [(i, i ^ by) for i in range(SUMS)])  18.7 us
    all_to_all x2, starting transfers between devices, exchange(): return lax.all_to_all(value, axes, 0, 0, tiled=True)  15 us
    ppermute x9, waiting for transfers between devices, swapped(): return lax.ppermute(value, 'h', [(i, i ^ by) for i in range(SUMS)])  13.9 us
    pallas_call x1, Pallas kernels, observations(): pl.pallas_call(observation_kernel, out_shape=(columns, factors), in_specs...  10.7 us
    pallas_call x1, Pallas kernels, own_columns_and_spread(): pl.pallas_call(columns_kernel, out_shape=(struct((NOBS // LANES, LANES)),...  7.83 us
    pallas_call x1, Pallas kernels, updated(): pl.pallas_call(update_kernel, out_shape=struct((GROUP, OWN_TILES, LANES))...  6.5 us
  transfers between devices with their start and end apart: 12, of which 7 were waited for; matrix products, arithmetic and copies ran while one was open for 1% of the time, Pallas kernels for 9%

profile of v10, /device:TPU:1, one launch (start us, length us, event | category | flops | bytes accessed | tf_op | source)
XLA Modules:
  0.0 218.0 jit_solution(12224644156836734541)
XLA Ops:
  0.0 0.1 pad_add_fusion.position_ref
  0.1 0.0 copy-start.4
  0.1 0.0 copy-start
  0.1 0.7 copy-done
  0.8 0.0 copy-start.2
  0.8 0.8 copy-done.2
  1.5 1.2 own_masks.1
  2.7 9.2 %all-to-all-start = ((f32[32,4,128]{2,1,0:T(4,128)}), f32[32,4,128]{2,1,0:T(4,128)S(1)}, u32[]{:S(2)}, u32[]{:S(2)}) async-start(f32[32,4,128]{2,1,0:T(4,128)} %bitcast.6), calls=%async_computation | async-start | bytes 131072 | tf_op jit(solution)/shard_map/all_to_all | solution.py:536
  12.0 7.8 %own_columns.1 = (f32[8,128]{1,0:T(8,128)}, f32[64,128,128]{2,1,0:T(8,128)}) custom-call(s32[1024]{0:T(1024)} %plan_ref.1, s32[1024]{0:T(1024)} %locations_ref.1, f32[128,64,128]{2,1,0:T(8,128)} %bitcast.18), custom_call_target="tpu_custom_call" | custom-call | flops 1000000 | bytes 8388608 | tf_op jit(solution)/shard_map/own_columns/pallas_call | solution.py:161
  19.8 0.0 all-to-all-done
  19.9 0.7 pad_maximum_fusion
  20.5 5.1 %collective-permute-start.8 = (f32[12,128]{1,0:T(8,128)S(1)}, f32[12,128]{1,0:T(8,128)S(1)}, u32[]{:S(2)}, u32[]{:S(2)}) collective-permute-start(f32[12,128]{1,0:T(8,128)S(1)} %pad_maximum_fusion), channel_id=1, source_target_pairs={{0,48},{16,32},{32,16},{48,0},{1,49},{17,33},{33,17},{49,1},{2,50}... | collective-permute-start | bytes 18440 | tf_op jit(solution)/shard_map/ppermute | solution.py:540
  25.7 1.2 collective-permute-start.7
  26.8 0.9 collective-permute-start.6
  27.7 0.0 collective-permute-done.8
  27.8 4.3 %collective-permute-done.7 = f32[12,128]{1,0:T(8,128)S(1)} collective-permute-done((f32[12,128]{1,0:T(8,128)S(1)}, f32[12,128]{1,0:T(8,128)S(1)}, u32[]{:S(2)}, u32[]{:S(2)}) %collective-permute-start.7) | collective-permute-done | bytes 6176 | tf_op jit(solution)/shard_map/ppermute | solution.py:540
  32.1 0.0 collective-permute-done.6
  32.1 0.7 concatenate.10
  32.9 17.2 %all_to_all.20 = f32[32,40,128]{2,1,0:T(8,128)S(1)} all-to-all(f32[32,40,128]{2,1,0:T(8,128)S(1)} %broadcast_in_dim.34), channel_id=1, replica_groups=mesh['y'=4,'h'=4,'l'=2,'c'=2,'x'=4] {'y','l','x'}, dimensions={0} | all-to-all | bytes 1310720 | tf_op jit(solution)/shard_map/all_to_all | solution.py:536
  50.1 4.0 %collective-permute-start.9 = (f32[32,40,128]{2,1,0:T(8,128)S(1)}, f32[32,40,128]{2,1,0:T(8,128)S(1)}, u32[]{:S(2)}, u32[]{:S(2)}) collective-permute-start(f32[32,40,128]{2,1,0:T(8,128)S(1)} %all_to_all.20), channel_id=1, source_target_pairs={{0,4},{4,0},{1,5},{5,1},{2,6},{6,2},{3,7},{7,3},{8,12},{12,8},{9,1... | collective-permute-start | bytes 1966088 | tf_op jit(solution)/shard_map/ppermute | solution.py:565
  54.1 1.7 collective-permute-done.9
  55.8 0.0 copy-start.1
  55.8 0.0 copy-start.10
  55.8 0.0 copy-start.11
  55.8 0.0 copy-start.3
  55.8 5.8 %all-to-all-start.2 = ((f32[64,128,128]{2,1,0:T(8,128)}), f32[64,128,128]{2,1,0:T(8,128)}, u32[]{:S(2)}, u32[]{:S(2)}) async-start(f32[64,128,128]{2,1,0:T(8,128)} %get-tuple-element.45), calls=%async_computation.2 | async-start | bytes 8388608 | tf_op jit(solution)/shard_map/all_to_all | solution.py:536
  61.6 0.0 copy-done.1
  61.6 0.1 convert_reduce_fusion.1
  61.8 0.7 reduce_max.9
  63.1 0.1 pad.3.clone
  63.2 0.7 convert_reduce_fusion.starts_ref
  63.9 0.0 copy-done.10
  63.9 0.0 copy-done.11
  63.9 0.1 maximum_maximum_fusion.facts_ref
  64.0 0.0 copy-done.4
  64.0 0.0 copy-done.3
  64.0 10.7 %observations.1 = (bf16[1152,1152]{1,0:T(8,128)(2,1)S(1)}, bf16[1040,1280]{1,0:T(8,128)(2,1)S(1)}) custom-call(s32[4]{0:T(128)S(1)} %pad_add_fusion.position_ref, s32[1,1024]{1,0:T(1,128)S(1)} %bitcast.16, f32[8,1024]{1,0:T(8,128)S(1)} %maximum_maximum_fusion.facts_ref, f32[1280,128]{1,0:T(8,128)S(1)} %bitcast.14, f32[1280,128]{1,0:T(8,128)S(1)} %bitcast.17), custom_call_target="tpu_custom_call" | custom-call | flops 20000000000 | bytes 8388608 | tf_op jit(solution)/shard_map/observations/pallas_call | solution.py:347
  74.7 0.0 copy-start.7
  74.7 1.5 copy-done.7
  76.2 0.0 copy-start.9
  76.2 1.6 copy-done.9
  77.8 37.6 %all-to-all-done.2.block_ref.refs_8_ = f32[64,128,128]{2,1,0:T(8,128)} async-done(((f32[64,128,128]{2,1,0:T(8,128)}), f32[64,128,128]{2,1,0:T(8,128)}, u32[]{:S(2)}, u32[]{:S(2)}) %all-to-all-start.2) | async-done | bytes 4194336 | tf_op jit(solution)/shard_map/all_to_all | solution.py:536
  115.4 0.0 copy-start.5
  115.4 0.0 copy-start.6
  115.4 5.9 %covariances.1 = (f32[160,128]{1,0:T(8,128)}, f32[160,128]{1,0:T(8,128)}, f32[160,128]{1,0:T(8,128)}, f32[160,128]{1,0:T(8,128)}, f32[96,128]{1,0:T(8,128)S(1)},...) custom-call(s32[4]{0:T(128)} %copy-done.4, s32[17]{0:T(128)} %convert_reduce_fusion.starts_ref, ...), custom_call_target="tpu_custom_call" | custom-call | flops 3000000000 | bytes 7340032 | tf_op jit(solution)/shard_map/covariances/pallas_call | solution.py:463
  121.3 1.3 collective-permute-start.10
  122.6 2.6 %collective-permute-start.11 = (f32[160,128]{1,0:T(8,128)}, f32[160,128]{1,0:T(8,128)S(1)}, u32[]{:S(2)}, u32[]{:S(2)}) collective-permute-start(f32[160,128]{1,0:T(8,128)} %get-tuple-element.50), channel_id=1, source_target_pairs={{0,32},{16,48},{32,0},{48,16},{1,33},{17,49},{33,1},{49,17},{2,34}... | collective-permute-start | bytes 245768 | tf_op jit(solution)/shard_map/ppermute | solution.py:540
  125.3 1.8 collective-permute-start.12
  127.0 0.0 collective-permute-done.10
  127.1 3.1 %collective-permute-done.11 = f32[160,128]{1,0:T(8,128)S(1)} collective-permute-done((f32[160,128]{1,0:T(8,128)}, f32[160,128]{1,0:T(8,128)S(1)}, u32[]{:S(2)}, u32[]{:S(2)}) %collective-permute-start.11) | collective-permute-done | bytes 81952 | tf_op jit(solution)/shard_map/ppermute | solution.py:540
  130.1 4.4 %collective-permute-done.12 = f32[160,128]{1,0:T(8,128)S(1)} collective-permute-done((f32[160,128]{1,0:T(8,128)}, f32[160,128]{1,0:T(8,128)S(1)}, u32[]{:S(2)}, u32[]{:S(2)}) %collective-permute-start.12) | collective-permute-done | bytes 81952 | tf_op jit(solution)/shard_map/ppermute | solution.py:540
  134.5 0.9 add_add_fusion.1.refs_0_
  135.4 0.1 collective-permute-start.15
  135.5 2.9 %collective-permute-start.14 = (f32[160,128]{1,0:T(8,128)S(1)}, f32[160,128]{1,0:T(8,128)S(1)}, u32[]{:S(2)}, u32[]{:S(2)}) collective-permute-start(f32[160,128]{1,0:T(8,128)S(1)} %add_add_fusion.1.refs_0_), channel_id=1, source_target_pairs={{0,32},{16,48},{32,0},{48,16},{1,33},{17,49},{33,1},{49,17},{2,34}... | collective-permute-start | bytes 245768 | tf_op jit(solution)/shard_map/ppermute | solution.py:540
  138.5 2.7 %collective-permute-start.13 = (f32[160,128]{1,0:T(8,128)S(1)}, f32[160,128]{1,0:T(8,128)S(1)}, u32[]{:S(2)}, u32[]{:S(2)}) collective-permute-start(f32[160,128]{1,0:T(8,128)S(1)} %add_add_fusion.1.refs_0_), channel_id=1, source_target_pairs={{0,16},{16,0},{32,48},{48,32},{1,17},{17,1},{33,49},{49,33},{2,18}... | collective-permute-start | bytes 245768 | tf_op jit(solution)/shard_map/ppermute | solution.py:540
  141.2 0.0 collective-permute-done.15.refs_3_
  141.2 1.7 collective-permute-done.14.refs_2_
  142.9 0.4 collective-permute-done.13.refs_1_
  143.3 0.0 copy-done.5
  143.3 0.0 copy-done.6
  143.3 0.0 copy-done.8
  143.3 6.5 %updated.1 = f32[64,128,128]{2,1,0:T(8,128)S(1)} custom-call(s32[4]{0:T(128)S(1)} %copy-done.5, s32[17]{0:T(128)S(1)} %copy-done.6, f32[160,128]{1,0:T(8,128)S(1)} %add_add_fusion.1.refs_0_, f32[160,128]{1,0:T(8,128)S(1)} %collective-permute-done.13.refs_1_, f32[160,128]{1,0:T(8,128)S(1)} %collective-permute-done.14.refs_2_, ...), custom_call_target="tpu_custom_call" | custom-call | flops 4000000000 | bytes 8388608 | tf_op jit(solution)/shard_map/updated/pallas_call | solution.py:518
  149.8 63.9 %all_to_all.21.in_ref = f32[64,128,128]{2,1,0:T(8,128)} all-to-all(f32[64,128,128]{2,1,0:T(8,128)S(1)} %updated.1), channel_id=1, replica_groups=mesh['y'=4,'h'=4,'l'=2,'c'=2,'x'=4] {'c','y','l','x'}, dimensions={0} | all-to-all | bytes 8388608 | tf_op jit(solution)/shard_map/all_to_all | solution.py:536
  213.8 4.1 %collect.1 = f32[128,64,128]{2,1,0:T(8,128)} custom-call(f32[64,128,128]{2,1,0:T(8,128)} %all_to_all.21.in_ref), custom_call_target="tpu_custom_call" | custom-call | flops 1000000 | bytes 8388608 | tf_op jit(solution)/shard_map/collect/pallas_call | solution.py:200
  (12 shorter events, 0.1 us)
Async XLA Ops:
  0.1 63.9 %copy-start.4 = (s32[4]{0:T(128)}, s32[4]{0:T(128)S(1)}, u32[]{:S(2)}) copy-start(s32[4]{0:T(128)S(1)} %pad_add_fusion.position_ref) | copy-start | bytes 52
  0.1 0.7 copy-start
  0.8 0.8 copy-start.2
  2.7 17.1 %all-to-all-start = ((f32[32,4,128]{2,1,0:T(4,128)}), f32[32,4,128]{2,1,0:T(4,128)S(1)}, u32[]{:S(2)}, u32[]{:S(2)}) async-start(f32[32,4,128]{2,1,0:T(4,128)} %bitcast.6), calls=%async_computation | async-start | bytes 131072 | tf_op jit(solution)/shard_map/all_to_all | solution.py:536
  20.5 7.2 %collective-permute-start.8 = (f32[12,128]{1,0:T(8,128)S(1)}, f32[12,128]{1,0:T(8,128)S(1)}, u32[]{:S(2)}, u32[]{:S(2)}) collective-permute-start(f32[12,128]{1,0:T(8,128)S(1)} %pad_maximum_fusion), channel_id=1, source_target_pairs={{0,48},{16,32},{32,16},{48,0},{1,49},{17,33},{33,17},{49,1},{2,50}... | collective-permute-start | bytes 18440 | tf_op jit(solution)/shard_map/ppermute | solution.py:540
  25.7 6.4 %collective-permute-start.7 = (f32[12,128]{1,0:T(8,128)S(1)}, f32[12,128]{1,0:T(8,128)S(1)}, u32[]{:S(2)}, u32[]{:S(2)}) collective-permute-start(f32[12,128]{1,0:T(8,128)S(1)} %pad_maximum_fusion), channel_id=1, source_target_pairs={{0,32},{16,48},{32,0},{48,16},{1,33},{17,49},{33,1},{49,17},{2,34}... | collective-permute-start | bytes 18440 | tf_op jit(solution)/shard_map/ppermute | solution.py:540
  26.8 5.3 %collective-permute-start.6 = (f32[12,128]{1,0:T(8,128)S(1)}, f32[12,128]{1,0:T(8,128)S(1)}, u32[]{:S(2)}, u32[]{:S(2)}) collective-permute-start(f32[12,128]{1,0:T(8,128)S(1)} %pad_maximum_fusion), channel_id=1, source_target_pairs={{0,16},{16,0},{32,48},{48,32},{1,17},{17,1},{33,49},{49,33},{2,18}... | collective-permute-start | bytes 18440 | tf_op jit(solution)/shard_map/ppermute | solution.py:540
  50.1 5.7 %collective-permute-start.9 = (f32[32,40,128]{2,1,0:T(8,128)S(1)}, f32[32,40,128]{2,1,0:T(8,128)S(1)}, u32[]{:S(2)}, u32[]{:S(2)}) collective-permute-start(f32[32,40,128]{2,1,0:T(8,128)S(1)} %all_to_all.20), channel_id=1, source_target_pairs={{0,4},{4,0},{1,5},{5,1},{2,6},{6,2},{3,7},{7,3},{8,12},{12,8},{9,1... | collective-permute-start | bytes 1966088 | tf_op jit(solution)/shard_map/ppermute | solution.py:565
  55.8 5.8 %copy-start.1 = (s32[1024]{0:T(1024)S(1)}, s32[1024]{0:T(1024)}, u32[]{:S(2)}) copy-start(s32[1024]{0:T(1024)} %locations_ref.1) | copy-start | bytes 12292
  55.8 8.1 %copy-start.10 = (f32[1024]{0:T(1024)S(1)}, f32[1024]{0:T(1024)}, u32[]{:S(2)}) copy-start(f32[1024]{0:T(1024)} %param.13) | copy-start | bytes 12292
  55.8 8.1 %copy-start.11 = (f32[1024]{0:T(1024)S(1)}, f32[1024]{0:T(1024)}, u32[]{:S(2)}) copy-start(f32[1024]{0:T(1024)} %param.12) | copy-start | bytes 12292
  55.8 8.2 %copy-start.3 = (s32[1024]{0:T(1024)S(1)}, s32[1024]{0:T(1024)}, u32[]{:S(2)}) copy-start(s32[1024]{0:T(1024)} %plan_ref.1) | copy-start | bytes 12292
  55.8 59.6 %all-to-all-start.2 = ((f32[64,128,128]{2,1,0:T(8,128)}), f32[64,128,128]{2,1,0:T(8,128)}, u32[]{:S(2)}, u32[]{:S(2)}) async-start(f32[64,128,128]{2,1,0:T(8,128)} %get-tuple-element.45), calls=%async_computation.2 | async-start | bytes 8388608 | tf_op jit(solution)/shard_map/all_to_all | solution.py:536
  74.7 1.5 copy-start.7
  76.2 1.6 copy-start.9
  115.4 27.9 %copy-start.5 = (s32[4]{0:T(128)S(1)}, s32[4]{0:T(128)}, u32[]{:S(2)}) copy-start(s32[4]{0:T(128)} %copy-done.4) | copy-start | bytes 52
  115.4 27.9 %copy-start.6 = (s32[17]{0:T(128)S(1)}, s32[17]{0:T(128)}, u32[]{:S(2)}) copy-start(s32[17]{0:T(128)} %convert_reduce_fusion.starts_ref) | copy-start | bytes 208
  115.4 27.9 %copy-start.8 = (bf16[1040,1280]{1,0:T(8,128)(2,1)S(1)}, bf16[1040,1280]{1,0:T(8,128)(2,1)}, u32[]{:S(2)}) copy-start(bf16[1040,1280]{1,0:T(8,128)(2,1)} %copy-done.7) | copy-start | bytes 7987204
  121.3 5.7 %collective-permute-start.10 = (f32[160,128]{1,0:T(8,128)}, f32[160,128]{1,0:T(8,128)S(1)}, u32[]{:S(2)}, u32[]{:S(2)}) collective-permute-start(f32[160,128]{1,0:T(8,128)} %get-tuple-element.49), channel_id=1, source_target_pairs={{0,16},{16,0},{32,48},{48,32},{1,17},{17,1},{33,49},{49,33},{2,18}... | collective-permute-start | bytes 245768 | tf_op jit(solution)/shard_map/ppermute | solution.py:540
  122.6 7.5 %collective-permute-start.11 = (f32[160,128]{1,0:T(8,128)}, f32[160,128]{1,0:T(8,128)S(1)}, u32[]{:S(2)}, u32[]{:S(2)}) collective-permute-start(f32[160,128]{1,0:T(8,128)} %get-tuple-element.50), channel_id=1, source_target_pairs={{0,32},{16,48},{32,0},{48,16},{1,33},{17,49},{33,1},{49,17},{2,34}... | collective-permute-start | bytes 245768 | tf_op jit(solution)/shard_map/ppermute | solution.py:540
  125.3 9.3 %collective-permute-start.12 = (f32[160,128]{1,0:T(8,128)}, f32[160,128]{1,0:T(8,128)S(1)}, u32[]{:S(2)}, u32[]{:S(2)}) collective-permute-start(f32[160,128]{1,0:T(8,128)} %get-tuple-element.51), channel_id=1, source_target_pairs={{0,48},{16,32},{32,16},{48,0},{1,49},{17,33},{33,17},{49,1},{2,50}... | collective-permute-start | bytes 245768 | tf_op jit(solution)/shard_map/ppermute | solution.py:540
  135.4 5.7 %collective-permute-start.15 = (f32[160,128]{1,0:T(8,128)S(1)}, f32[160,128]{1,0:T(8,128)S(1)}, u32[]{:S(2)}, u32[]{:S(2)}) collective-permute-start(f32[160,128]{1,0:T(8,128)S(1)} %add_add_fusion.1.refs_0_), channel_id=1, source_target_pairs={{0,48},{16,32},{32,16},{48,0},{1,49},{17,33},{33,17},{49,1},{2,50}... | collective-permute-start | bytes 245768 | tf_op jit(solution)/shard_map/ppermute | solution.py:540
  135.5 7.4 %collective-permute-start.14 = (f32[160,128]{1,0:T(8,128)S(1)}, f32[160,128]{1,0:T(8,128)S(1)}, u32[]{:S(2)}, u32[]{:S(2)}) collective-permute-start(f32[160,128]{1,0:T(8,128)S(1)} %add_add_fusion.1.refs_0_), channel_id=1, source_target_pairs={{0,32},{16,48},{32,0},{48,16},{1,33},{17,49},{33,1},{49,17},{2,34}... | collective-permute-start | bytes 245768 | tf_op jit(solution)/shard_map/ppermute | solution.py:540
  138.5 4.9 %collective-permute-start.13 = (f32[160,128]{1,0:T(8,128)S(1)}, f32[160,128]{1,0:T(8,128)S(1)}, u32[]{:S(2)}, u32[]{:S(2)}) collective-permute-start(f32[160,128]{1,0:T(8,128)S(1)} %add_add_fusion.1.refs_0_), channel_id=1, source_target_pairs={{0,16},{16,0},{32,48},{48,32},{1,17},{17,1},{33,49},{49,33},{2,18}... | collective-permute-start | bytes 245768 | tf_op jit(solution)/shard_map/ppermute | solution.py:540

commit v11 on v8

--- a/solution.py
+++ b/solution.py
@@ -86,7 +86,15 @@
     return dot_parts(*two_parts(a), *two_parts(b))
 
 
-def masks_kernel(position_ref, locations_ref, tile_mask_ref, out_ref):
+def masks_kernel(position_ref, locations_in_ref, tile_mask_in_ref, out_ref, locations_ref, tile_mask_ref, sems):
+    copies = [
+        pltpu.make_async_copy(locations_in_ref, locations_ref, sems.at[0]),
+        pltpu.make_async_copy(tile_mask_in_ref, tile_mask_ref, sems.at[1]),
+    ]
+    for copy in copies:
+        copy.start()
+    for copy in copies:
+        copy.wait()
     tiles_here = tile_mask_ref.shape[0]
     first = position_ref[3] * tiles_here
     per_row = NOBS // LANES
@@ -108,9 +116,12 @@
     return pl.pallas_call(
         masks_kernel,
         out_shape=struct((16 * NOBS // LANES, LANES)),
-        in_specs=[SMEM, VMEM, VMEM],
+        in_specs=[SMEM, ANY, ANY],
         out_specs=VMEM,
-        compiler_params=kernel_params(4),
+        scratch_shapes=[
+            pltpu.VMEM(locations.shape, i32), pltpu.VMEM(tile_mask.shape, i32), pltpu.SemaphoreType.DMA((2,))
+        ],
+        compiler_params=kernel_params(60),
         cost_estimate=pl.CostEstimate(flops=10**5, bytes_accessed=10**5, transcendentals=0),
         name="own_masks",
     )(position, locations, tile_mask)

time: 217 us -> 217 us (level)
    unnamed x34 -> x30, local copies, waits for them, and re-layouts: 12.3 us -> 10.9 us
where the time goes in v11:
time: 217 us
  blocking collectives  60.2 us (28%)
  waiting for transfers between devices  54.5 us (25%)
  starting transfers between devices  50.8 us (23%)
  Pallas kernels  35.1 us (16%)
  local copies, waits for them, and re-layouts  11.9 us (5%)
  other arithmetic  3.16 us (1%)
    all_to_all x1, blocking collectives, exchange(): return lax.all_to_all(value, axes, 0, 0, tiled=True)  60.2 us
    all_to_all x3, waiting for transfers between devices, exchange(): return lax.all_to_all(value, axes, 0, 0, tiled=True)  41.1 us
    ppermute x9, starting transfers between devices, passed_along(): return lax.ppermute(value, 'h', [(i, (i + by) % SUMS) for i in range(SUMS)])  24.9 us
    all_to_all x3, starting transfers between devices, exchange(): return lax.all_to_all(value, axes, 0, 0, tiled=True)  21.9 us
    ppermute x9, waiting for transfers between devices, passed_along(): return lax.ppermute(value, 'h', [(i, (i + by) % SUMS) for i in range(SUMS)])  11.6 us
    unnamed x30, local copies, waits for them, and re-layouts  10.9 us
    pallas_call x1, Pallas kernels, observations(): pl.pallas_call(observation_kernel, out_shape=(columns, factors), in_specs...  10.7 us
    pallas_call x1, Pallas kernels, updated(): pl.pallas_call(update_kernel, out_shape=struct((GROUP, OWN_TILES, LANES))...  6.51 us
  transfers between devices with their start and end apart: 13, of which 8 were waited for; matrix products, arithmetic and copies ran while one was open for 1% of the time, Pallas kernels for 8%

profile of v11, /device:TPU:1, one launch (start us, length us, event | category | flops | bytes accessed | tf_op | source)
XLA Modules:
  0.0 216.6 jit_solution(9768588776184061242)
XLA Ops:
  0.0 0.6 pad_add_fusion.position_ref
  0.6 2.1 own_masks.1
  2.7 9.2 %all-to-all-start = ((f32[32,4,128]{2,1,0:T(4,128)}), f32[32,4,128]{2,1,0:T(4,128)S(1)}, u32[]{:S(2)}, u32[]{:S(2)}) async-start(f32[32,4,128]{2,1,0:T(4,128)} %bitcast.20), calls=%async_computation | async-start | bytes 131072 | tf_op jit(solution)/shard_map/all_to_all | solution.py:544
  12.0 0.0 copy-start
  12.0 2.2 %copy-done = f32[1,1048576]{1,0:T(1,128)S(1)} copy-done((f32[1,1048576]{1,0:T(1,128)S(1)}, f32[1,1048576]{1,0:T(1,128)}, u32[]{:S(2)}) %copy-start) | copy-done | bytes 4194328
  14.2 0.0 copy-start.3
  14.2 0.7 copy-done.3
  14.8 0.0 copy-start.5
  14.9 0.7 copy-done.5
  15.5 3.1 %own_columns.1 = f32[8,128]{1,0:T(8,128)S(1)} custom-call(s32[1024]{0:T(1024)S(1)} %copy-done.5, s32[1024]{0:T(1024)S(1)} %copy-done.3, f32[8192,128]{1,0:T(8,128)S(1)} %bitcast.14), custom_call_target="tpu_custom_call" | custom-call | flops 1000000 | bytes 8388608 | tf_op jit(solution)/shard_map/own_columns/pallas_call | solution.py:153
  18.6 0.7 all-to-all-done
  19.4 5.2 %collective-permute-start.8 = (f32[12,128]{1,0:T(8,128)S(1)}, f32[12,128]{1,0:T(8,128)S(1)}, u32[]{:S(2)}, u32[]{:S(2)}) collective-permute-start(f32[12,128]{1,0:T(8,128)S(1)} %pad_maximum_fusion), channel_id=1, source_target_pairs={{0,48},{16,0},{32,16},{48,32},{1,49},{17,1},{33,17},{49,33},{2,50}... | collective-permute-start | bytes 18440 | tf_op jit(solution)/shard_map/ppermute | solution.py:548
  24.5 1.2 collective-permute-start.7
  25.7 2.1 collective-permute-start.6
  27.8 0.0 collective-permute-done.8
  27.8 3.1 %collective-permute-done.7 = f32[12,128]{1,0:T(8,128)S(1)} collective-permute-done((f32[12,128]{1,0:T(8,128)S(1)}, f32[12,128]{1,0:T(8,128)S(1)}, u32[]{:S(2)}, u32[]{:S(2)}) %collective-permute-start.7) | collective-permute-done | bytes 6176 | tf_op jit(solution)/shard_map/ppermute | solution.py:548
  31.0 0.0 collective-permute-done.6
  31.0 0.9 broadcast_in_dim.34
  31.9 7.1 %all-to-all-start.1 = ((f32[32,40,128]{2,1,0:T(8,128)}), f32[32,40,128]{2,1,0:T(8,128)S(1)}, u32[]{:S(2)}, u32[]{:S(2)}) async-start(f32[32,40,128]{2,1,0:T(8,128)} %broadcast_in_dim.34), calls=%async_computation.1 | async-start | bytes 1310720 | tf_op jit(solution)/shard_map/all_to_all | solution.py:544
  39.0 0.0 copy-start.1
  39.0 2.2 %copy-done.1 = f32[1,1048576]{1,0:T(1,128)S(1)} copy-done((f32[1,1048576]{1,0:T(1,128)S(1)}, f32[1,1048576]{1,0:T(1,128)}, u32[]{:S(2)}) %copy-start.1) | copy-done | bytes 4194328
  41.1 2.8 %spread_out.1 = f32[64,128,128]{2,1,0:T(8,128)S(1)} custom-call(f32[8192,128]{1,0:T(8,128)S(1)} %bitcast.15), custom_call_target="tpu_custom_call" | custom-call | flops 1000000 | bytes 8388608 | tf_op jit(solution)/shard_map/spread_out/pallas_call | solution.py:171
  43.9 0.0 copy-start.2
  44.0 2.0 copy-done.2
  46.0 0.0 copy-start.7
  46.0 2.7 %all-to-all-done.1 = f32[32,40,128]{2,1,0:T(8,128)S(1)} async-done(((f32[32,40,128]{2,1,0:T(8,128)}), f32[32,40,128]{2,1,0:T(8,128)S(1)}, u32[]{:S(2)}, u32[]{:S(2)}) %all-to-all-start.1) | async-done | bytes 655392 | tf_op jit(solution)/shard_map/all_to_all | solution.py:544
  48.7 4.0 %collective-permute-start.9 = (f32[32,40,128]{2,1,0:T(8,128)S(1)}, f32[32,40,128]{2,1,0:T(8,128)S(1)}, u32[]{:S(2)}, u32[]{:S(2)}) collective-permute-start(f32[32,40,128]{2,1,0:T(8,128)S(1)} %all-to-all-done.1), channel_id=1, source_target_pairs={{0,4},{4,0},{1,5},{5,1},{2,6},{6,2},{3,7},{7,3},{8,12},{12,8},{9,1... | collective-permute-start | bytes 1966088 | tf_op jit(solution)/shard_map/ppermute | solution.py:575
  52.6 1.7 collective-permute-done.9
  54.4 5.6 %all-to-all-start.2 = ((f32[64,128,128]{2,1,0:T(8,128)}), f32[64,128,128]{2,1,0:T(8,128)}, u32[]{:S(2)}, u32[]{:S(2)}) async-start(f32[64,128,128]{2,1,0:T(8,128)} %copy-done.2), calls=%async_computation.2 | async-start | bytes 8388608 | tf_op jit(solution)/shard_map/all_to_all | solution.py:544
  60.0 0.0 copy-done.4
  60.0 0.1 convert_reduce_fusion.1
  60.2 0.6 reduce_max.9
  61.3 0.1 pad.3.clone
  61.4 0.8 convert_reduce_fusion.starts_ref
  62.2 0.0 copy-done.13
  62.2 0.0 copy-done.14
  62.2 0.1 maximum_maximum_fusion.facts_ref
  62.2 0.0 copy-done.6
  62.2 0.0 copy-done.7
  62.2 10.7 %observations.1 = (bf16[1152,1152]{1,0:T(8,128)(2,1)S(1)}, bf16[1040,1280]{1,0:T(8,128)(2,1)S(1)}) custom-call(s32[4]{0:T(128)S(1)} %copy-done.7, s32[1,1024]{1,0:T(1,128)S(1)} %bitcast.18, f32[8,1024]{1,0:T(8,128)S(1)} %maximum_maximum_fusion.facts_ref, f32[1280,128]{1,0:T(8,128)S(1)} %bitcast.16, f32[1280,128]{1,0:T(8,128)S(1)} %bitcast.19), custom_call_target="tpu_custom_call" | custom-call | flops 20000000000 | bytes 8388608 | tf_op jit(solution)/shard_map/observations/pallas_call | solution.py:355
  73.0 0.0 copy-start.10
  73.0 1.5 copy-done.10
  74.5 1.6 copy-done.12
  76.1 37.8 %all-to-all-done.2.block_ref.refs_8_ = f32[64,128,128]{2,1,0:T(8,128)} async-done(((f32[64,128,128]{2,1,0:T(8,128)}), f32[64,128,128]{2,1,0:T(8,128)}, u32[]{:S(2)}, u32[]{:S(2)}) %all-to-all-start.2) | async-done | bytes 4194336 | tf_op jit(solution)/shard_map/all_to_all | solution.py:544
  113.8 5.9 %covariances.1 = (f32[160,128]{1,0:T(8,128)}, f32[160,128]{1,0:T(8,128)}, f32[160,128]{1,0:T(8,128)}, f32[160,128]{1,0:T(8,128)}, f32[96,128]{1,0:T(8,128)S(1)},...) custom-call(s32[4]{0:T(128)} %pad_add_fusion.position_ref, s32[17]{0:T(128)} %convert_reduce_fusion.starts_ref, ...), custom_call_target="tpu_custom_call" | custom-call | flops 3000000000 | bytes 7340032 | tf_op jit(solution)/shard_map/covariances/pallas_call | solution.py:471
  119.7 0.5 collective-permute-start.10
  120.2 3.4 %collective-permute-start.11 = (f32[160,128]{1,0:T(8,128)}, f32[160,128]{1,0:T(8,128)S(1)}, u32[]{:S(2)}, u32[]{:S(2)}) collective-permute-start(f32[160,128]{1,0:T(8,128)} %get-tuple-element.50), channel_id=1, source_target_pairs={{0,32},{16,48},{32,0},{48,16},{1,33},{17,49},{33,1},{49,17},{2,34}... | collective-permute-start | bytes 245768 | tf_op jit(solution)/shard_map/ppermute | solution.py:548
  123.7 3.5 %collective-permute-start.12 = (f32[160,128]{1,0:T(8,128)}, f32[160,128]{1,0:T(8,128)S(1)}, u32[]{:S(2)}, u32[]{:S(2)}) collective-permute-start(f32[160,128]{1,0:T(8,128)} %get-tuple-element.51), channel_id=1, source_target_pairs={{0,48},{16,0},{32,16},{48,32},{1,49},{17,1},{33,17},{49,33},{2,50}... | collective-permute-start | bytes 245768 | tf_op jit(solution)/shard_map/ppermute | solution.py:548
  127.2 0.0 collective-permute-done.10
  127.2 0.5 collective-permute-done.11
  127.7 1.3 collective-permute-done.12
  129.0 0.9 add_add_fusion.1.refs_0_
  129.9 6.6 %collective-permute-start.15 = (f32[160,128]{1,0:T(8,128)S(1)}, f32[160,128]{1,0:T(8,128)S(1)}, u32[]{:S(2)}, u32[]{:S(2)}) collective-permute-start(f32[160,128]{1,0:T(8,128)S(1)} %add_add_fusion.1.refs_0_), channel_id=1, source_target_pairs={{0,48},{16,0},{32,16},{48,32},{1,49},{17,1},{33,17},{49,33},{2,50}... | collective-permute-start | bytes 245768 | tf_op jit(solution)/shard_map/ppermute | solution.py:548
  136.5 2.4 %collective-permute-start.14 = (f32[160,128]{1,0:T(8,128)S(1)}, f32[160,128]{1,0:T(8,128)S(1)}, u32[]{:S(2)}, u32[]{:S(2)}) collective-permute-start(f32[160,128]{1,0:T(8,128)S(1)} %add_add_fusion.1.refs_0_), channel_id=1, source_target_pairs={{0,32},{16,48},{32,0},{48,16},{1,33},{17,49},{33,1},{49,17},{2,34}... | collective-permute-start | bytes 245768 | tf_op jit(solution)/shard_map/ppermute | solution.py:548
  138.9 0.0 collective-permute-start.13
  138.9 0.0 collective-permute-done.15.refs_3_
  138.9 6.7 %collective-permute-done.14.refs_2_ = f32[160,128]{1,0:T(8,128)S(1)} collective-permute-done((f32[160,128]{1,0:T(8,128)S(1)}, f32[160,128]{1,0:T(8,128)S(1)}, u32[]{:S(2)}, u32[]{:S(2)}) %collective-permute-start.14) | collective-permute-done | bytes 81952 | tf_op jit(solution)/shard_map/ppermute | solution.py:548
  145.6 0.0 collective-permute-done.13.refs_1_
  145.6 0.0 copy-done.8
  145.6 0.0 copy-done.9
  145.6 0.0 copy-done.11
  145.6 6.5 %updated.1 = f32[64,128,128]{2,1,0:T(8,128)S(1)} custom-call(s32[4]{0:T(128)S(1)} %copy-done.8, s32[17]{0:T(128)S(1)} %copy-done.9, f32[160,128]{1,0:T(8,128)S(1)} %add_add_fusion.1.refs_0_, f32[160,128]{1,0:T(8,128)S(1)} %collective-permute-done.13.refs_1_, f32[160,128]{1,0:T(8,128)S(1)} %collective-permute-done.14.refs_2_, ...), custom_call_target="tpu_custom_call" | custom-call | flops 4000000000 | bytes 8388608 | tf_op jit(solution)/shard_map/updated/pallas_call | solution.py:526
  152.1 60.2 %all_to_all.20.in_ref = f32[64,128,128]{2,1,0:T(8,128)} all-to-all(f32[64,128,128]{2,1,0:T(8,128)S(1)} %updated.1), channel_id=1, replica_groups=mesh['y'=4,'h'=4,'l'=2,'c'=2,'x'=4] {'c','y','l','x'}, dimensions={0} | all-to-all | bytes 8388608 | tf_op jit(solution)/shard_map/all_to_all | solution.py:544
  212.4 4.1 %collect.1 = f32[128,64,128]{2,1,0:T(8,128)} custom-call(f32[64,128,128]{2,1,0:T(8,128)} %all_to_all.20.in_ref), custom_call_target="tpu_custom_call" | custom-call | flops 1000000 | bytes 8388608 | tf_op jit(solution)/shard_map/collect/pallas_call | solution.py:208
  (20 shorter events, 0.1 us)
Async XLA Ops:
  2.7 16.6 %all-to-all-start = ((f32[32,4,128]{2,1,0:T(4,128)}), f32[32,4,128]{2,1,0:T(4,128)S(1)}, u32[]{:S(2)}, u32[]{:S(2)}) async-start(f32[32,4,128]{2,1,0:T(4,128)} %bitcast.20), calls=%async_computation | async-start | bytes 131072 | tf_op jit(solution)/shard_map/all_to_all | solution.py:544
  12.0 2.2 %copy-start = (f32[1,1048576]{1,0:T(1,128)S(1)}, f32[1,1048576]{1,0:T(1,128)}, u32[]{:S(2)}) copy-start(f32[1,1048576]{1,0:T(1,128)} %param.8) | copy-start | bytes 12582916
  14.2 0.7 copy-start.3
  14.8 0.7 copy-start.5
  19.4 8.5 %collective-permute-start.8 = (f32[12,128]{1,0:T(8,128)S(1)}, f32[12,128]{1,0:T(8,128)S(1)}, u32[]{:S(2)}, u32[]{:S(2)}) collective-permute-start(f32[12,128]{1,0:T(8,128)S(1)} %pad_maximum_fusion), channel_id=1, source_target_pairs={{0,48},{16,0},{32,16},{48,32},{1,49},{17,1},{33,17},{49,33},{2,50}... | collective-permute-start | bytes 18440 | tf_op jit(solution)/shard_map/ppermute | solution.py:548
  24.5 6.4 %collective-permute-start.7 = (f32[12,128]{1,0:T(8,128)S(1)}, f32[12,128]{1,0:T(8,128)S(1)}, u32[]{:S(2)}, u32[]{:S(2)}) collective-permute-start(f32[12,128]{1,0:T(8,128)S(1)} %pad_maximum_fusion), channel_id=1, source_target_pairs={{0,32},{16,48},{32,0},{48,16},{1,33},{17,49},{33,1},{49,17},{2,34}... | collective-permute-start | bytes 18440 | tf_op jit(solution)/shard_map/ppermute | solution.py:548
  25.7 5.3 %collective-permute-start.6 = (f32[12,128]{1,0:T(8,128)S(1)}, f32[12,128]{1,0:T(8,128)S(1)}, u32[]{:S(2)}, u32[]{:S(2)}) collective-permute-start(f32[12,128]{1,0:T(8,128)S(1)} %pad_maximum_fusion), channel_id=1, source_target_pairs={{0,16},{16,32},{32,48},{48,0},{1,17},{17,33},{33,49},{49,1},{2,18}... | collective-permute-start | bytes 18440 | tf_op jit(solution)/shard_map/ppermute | solution.py:548
  31.9 16.8 %all-to-all-start.1 = ((f32[32,40,128]{2,1,0:T(8,128)}), f32[32,40,128]{2,1,0:T(8,128)S(1)}, u32[]{:S(2)}, u32[]{:S(2)}) async-start(f32[32,40,128]{2,1,0:T(8,128)} %broadcast_in_dim.34), calls=%async_computation.1 | async-start | bytes 1310720 | tf_op jit(solution)/shard_map/all_to_all | solution.py:544
  39.0 2.2 %copy-start.1 = (f32[1,1048576]{1,0:T(1,128)S(1)}, f32[1,1048576]{1,0:T(1,128)}, u32[]{:S(2)}) copy-start(f32[1,1048576]{1,0:T(1,128)} %param.8) | copy-start | bytes 12582916
  43.9 2.0 copy-start.2
  46.0 14.0 %copy-start.4 = (s32[1024]{0:T(1024)S(1)}, s32[1024]{0:T(1024)}, u32[]{:S(2)}) copy-start(s32[1024]{0:T(1024)} %locations_ref.1) | copy-start | bytes 12292
  46.0 16.2 %copy-start.13 = (f32[1024]{0:T(1024)S(1)}, f32[1024]{0:T(1024)}, u32[]{:S(2)}) copy-start(f32[1024]{0:T(1024)} %param.13) | copy-start | bytes 12292
  46.0 16.2 %copy-start.14 = (f32[1024]{0:T(1024)S(1)}, f32[1024]{0:T(1024)}, u32[]{:S(2)}) copy-start(f32[1024]{0:T(1024)} %param.12) | copy-start | bytes 12292
  46.0 16.3 %copy-start.6 = (s32[1024]{0:T(1024)S(1)}, s32[1024]{0:T(1024)}, u32[]{:S(2)}) copy-start(s32[1024]{0:T(1024)} %plan_ref.1) | copy-start | bytes 12292
  46.0 16.3 %copy-start.7 = (s32[4]{0:T(128)S(1)}, s32[4]{0:T(128)}, u32[]{:S(2)}) copy-start(s32[4]{0:T(128)} %pad_add_fusion.position_ref) | copy-start | bytes 52
  48.7 5.7 %collective-permute-start.9 = (f32[32,40,128]{2,1,0:T(8,128)S(1)}, f32[32,40,128]{2,1,0:T(8,128)S(1)}, u32[]{:S(2)}, u32[]{:S(2)}) collective-permute-start(f32[32,40,128]{2,1,0:T(8,128)S(1)} %all-to-all-done.1), channel_id=1, source_target_pairs={{0,4},{4,0},{1,5},{5,1},{2,6},{6,2},{3,7},{7,3},{8,12},{12,8},{9,1... | collective-permute-start | bytes 1966088 | tf_op jit(solution)/shard_map/ppermute | solution.py:575
  54.4 59.5 %all-to-all-start.2 = ((f32[64,128,128]{2,1,0:T(8,128)}), f32[64,128,128]{2,1,0:T(8,128)}, u32[]{:S(2)}, u32[]{:S(2)}) async-start(f32[64,128,128]{2,1,0:T(8,128)} %copy-done.2), calls=%async_computation.2 | async-start | bytes 8388608 | tf_op jit(solution)/shard_map/all_to_all | solution.py:544
  73.0 1.5 copy-start.10
  74.5 1.6 copy-start.12
  113.8 31.8 %copy-start.8 = (s32[4]{0:T(128)S(1)}, s32[4]{0:T(128)}, u32[]{:S(2)}) copy-start(s32[4]{0:T(128)} %pad_add_fusion.position_ref) | copy-start | bytes 52
  113.8 31.8 %copy-start.9 = (s32[17]{0:T(128)S(1)}, s32[17]{0:T(128)}, u32[]{:S(2)}) copy-start(s32[17]{0:T(128)} %convert_reduce_fusion.starts_ref) | copy-start | bytes 208
  113.8 31.8 %copy-start.11 = (bf16[1040,1280]{1,0:T(8,128)(2,1)S(1)}, bf16[1040,1280]{1,0:T(8,128)(2,1)}, u32[]{:S(2)}) copy-start(bf16[1040,1280]{1,0:T(8,128)(2,1)} %copy-done.10) | copy-start | bytes 7987204
  119.7 7.4 %collective-permute-start.10 = (f32[160,128]{1,0:T(8,128)}, f32[160,128]{1,0:T(8,128)S(1)}, u32[]{:S(2)}, u32[]{:S(2)}) collective-permute-start(f32[160,128]{1,0:T(8,128)} %get-tuple-element.49), channel_id=1, source_target_pairs={{0,16},{16,32},{32,48},{48,0},{1,17},{17,33},{33,49},{49,1},{2,18}... | collective-permute-start | bytes 245768 | tf_op jit(solution)/shard_map/ppermute | solution.py:548
  120.2 7.4 %collective-permute-start.11 = (f32[160,128]{1,0:T(8,128)}, f32[160,128]{1,0:T(8,128)S(1)}, u32[]{:S(2)}, u32[]{:S(2)}) collective-permute-start(f32[160,128]{1,0:T(8,128)} %get-tuple-element.50), channel_id=1, source_target_pairs={{0,32},{16,48},{32,0},{48,16},{1,33},{17,49},{33,1},{49,17},{2,34}... | collective-permute-start | bytes 245768 | tf_op jit(solution)/shard_map/ppermute | solution.py:548
  123.7 5.3 %collective-permute-start.12 = (f32[160,128]{1,0:T(8,128)}, f32[160,128]{1,0:T(8,128)S(1)}, u32[]{:S(2)}, u32[]{:S(2)}) collective-permute-start(f32[160,128]{1,0:T(8,128)} %get-tuple-element.51), channel_id=1, source_target_pairs={{0,48},{16,0},{32,16},{48,32},{1,49},{17,1},{33,17},{49,33},{2,50}... | collective-permute-start | bytes 245768 | tf_op jit(solution)/shard_map/ppermute | solution.py:548
  129.9 9.1 %collective-permute-start.15 = (f32[160,128]{1,0:T(8,128)S(1)}, f32[160,128]{1,0:T(8,128)S(1)}, u32[]{:S(2)}, u32[]{:S(2)}) collective-permute-start(f32[160,128]{1,0:T(8,128)S(1)} %add_add_fusion.1.refs_0_), channel_id=1, source_target_pairs={{0,48},{16,0},{32,16},{48,32},{1,49},{17,1},{33,17},{49,33},{2,50}... | collective-permute-start | bytes 245768 | tf_op jit(solution)/shard_map/ppermute | solution.py:548
  136.5 9.1 %collective-permute-start.14 = (f32[160,128]{1,0:T(8,128)S(1)}, f32[160,128]{1,0:T(8,128)S(1)}, u32[]{:S(2)}, u32[]{:S(2)}) collective-permute-start(f32[160,128]{1,0:T(8,128)S(1)} %add_add_fusion.1.refs_0_), channel_id=1, source_target_pairs={{0,32},{16,48},{32,0},{48,16},{1,33},{17,49},{33,1},{49,17},{2,34}... | collective-permute-start | bytes 245768 | tf_op jit(solution)/shard_map/ppermute | solution.py:548
  138.9 6.7 %collective-permute-start.13 = (f32[160,128]{1,0:T(8,128)S(1)}, f32[160,128]{1,0:T(8,128)S(1)}, u32[]{:S(2)}, u32[]{:S(2)}) collective-permute-start(f32[160,128]{1,0:T(8,128)S(1)} %add_add_fusion.1.refs_0_), channel_id=1, source_target_pairs={{0,16},{16,32},{32,48},{48,0},{1,17},{17,33},{33,49},{49,1},{2,18}... | collective-permute-start | bytes 245768 | tf_op jit(solution)/shard_map/ppermute | solution.py:548
